TPU v7x, 128 devices: a whole 4x4x4 slice. The times are simulated.
128 devices in a mesh: grp: 4 (over y_lo, core), dev: 32 (over z, x, y_hi).
Axes of the slice: x: 4, y: 4 (y_hi: 2, y_lo: 2; y = y_hi * 2 + y_lo), z: 4, core: 2. Of those that a mesh axis runs over, the one named last changes fastest.
Arguments:
- voltage_real: bfloat16 [2048, 110592], P(('grp', 'dev')), may hold values from -6 to 6
- voltage_imaginary: bfloat16 [2048, 110592], P(('grp', 'dev')), may hold values from -6 to 6
- filter_taps: float32 [16, 4096], replicated, may hold values from -1.5 to 1.5
- weights_re: float32 [32, 2048, 512], P('dev'), may hold values from -0.0625 to 0.0625
- weights_im: float32 [32, 2048, 512], P('dev'), may hold values from -0.0625 to 0.0625
- owners: int32 [2], replicated, may hold values from 0 to 31
- antenna_map: int32 [2048], replicated, may hold values from 0 to 2047, each once
Outputs:
- beam_power: float32 [2, 4096, 512], P(None, ('grp', 'dev'))
Inputs may be any that keep to these rules, and one draw needn't show every extreme that they name: `owners`: the index along dev of the device whose calibration serves each step. A permutation: voltage slot j carries antenna antenna_map[j].
All inputs are finite; a program needn't handle non-finite values.
Results may differ from a plain program's by a relative error of at most 0.0022.
Values may be sent and summed in bfloat16 or wider, within the bound.
No kernel may reach another device: no remote copies, remote signals or barrier semaphores. Data moves between devices by JAX's collectives and lax.ppermute only.
A program may use at most 192 MiB of HBM per device.

v0:
```python
import math

import jax
import jax.numpy as jnp
import numpy as np
from jax import lax
from jax.experimental import pallas as pl
from jax.experimental.pallas import tpu as pltpu
from jax.sharding import PartitionSpec as P

CHANNELS = 4096
TAPS = 16
SPECTRA = 6
STEPS = 2
FRAMES = STEPS * SPECTRA
BLOCKS = FRAMES + TAPS - 1
OUTER = 32
INNER = 128
SLOTS = 16
DEVICES = 128
ALL = ("grp", "dev")
MIB = 1 << 20


def twist_tables():
    products = np.outer(np.arange(OUTER), np.arange(INNER)) % CHANNELS
    angles = products * (2.0 * math.pi / CHANNELS)
    return np.cos(angles).astype(np.float32), np.sin(angles).astype(np.float32)


def inner_matrix():
    products = np.outer(np.arange(INNER), np.arange(INNER)) % INNER
    angles = products * (2.0 * math.pi / INNER)
    norm = CHANNELS ** (-0.5)
    c, s = np.cos(angles) * norm, np.sin(angles) * norm
    return np.block([[c, s], [-s, c]]).astype(np.float32)


def small_fft(points):
    count = len(points)
    if count == 1:
        return points
    even = small_fft(points[0::2])
    odd = small_fft(points[1::2])
    half = count // 2
    result = [None] * count
    for k in range(half):
        er, ei = even[k]
        xr, xi = odd[k]
        if k == 0:
            tr, ti = xr, xi
        elif 4 * k == count:
            tr, ti = xi, -xr
        elif 8 * k == count:
            r = math.sqrt(0.5)
            tr, ti = (xr + xi) * r, (xi - xr) * r
        elif 8 * k == 3 * count:
            r = math.sqrt(0.5)
            tr, ti = (xi - xr) * r, (xr + xi) * (-r)
        else:
            c = math.cos(2.0 * math.pi * k / count)
            s = math.sin(2.0 * math.pi * k / count)
            tr, ti = xr * c + xi * s, xi * c - xr * s
        result[k] = (er + tr, ei + ti)
        result[k + half] = (er - tr, ei - ti)
    return result


def spectra_kernel(vre, vim, taps, cos_t, sin_t, mat, out, frames, turned, packed):
    def fir(n1, _):
        rows = [taps[k : k + 1, pl.ds(pl.multiple_of(n1 * INNER, INNER), INNER)] for k in range(TAPS)]
        for c, volts in ((0, vre), (1, vim)):
            window = [
                volts[:, pl.ds(pl.multiple_of(b * CHANNELS + n1 * INNER, INNER), INNER)].astype(jnp.float32)
                for b in range(BLOCKS)
            ]
            for u in range(FRAMES):
                total = window[u] * rows[0]
                for k in range(1, TAPS):
                    total = total + window[u + k] * rows[k]
                frames[c, u, n1] = total
        return 0

    lax.fori_loop(0, OUTER, fir, 0)

    def outer(i, _):
        u = i // 2
        low = pl.multiple_of((i % 2) * 8, 8)
        s = u // SPECTRA
        t = u % SPECTRA
        place = jnp.where(t < 4, s * 128 + t * 32, 256 + s * 64 + (t - 4) * 32)
        points = [
            (frames[0, u, n1, pl.ds(low, 8), :], frames[1, u, n1, pl.ds(low, 8), :]) for n1 in range(OUTER)
        ]
        points = small_fft(points)
        for f1 in range(OUTER):
            re, im = points[f1]
            if f1:
                c, d = cos_t[f1 : f1 + 1, :], sin_t[f1 : f1 + 1, :]
                re, im = re * c + im * d, im * c - re * d
            at = low * 384 + place + f1
            turned[0, pl.ds(at, 8, stride=384), :] = re
            turned[1, pl.ds(at, 8, stride=384), :] = im
        return 0

    lax.fori_loop(0, 2 * FRAMES, outer, 0)

    matrix = mat[...]
    lane = lax.broadcasted_iota(jnp.int32, (32, INNER), 1)

    def inner(a, _):
        base = pl.multiple_of(a * 384, 128)
        rows = jnp.concatenate(
            [turned[0, pl.ds(base, 384), :], turned[1, pl.ds(base, 384), :]], axis=1
        ).astype(jnp.bfloat16)
        spec = lax.dot_general(
            matrix, rows, (((1,), (1,)), ((), ())), preferred_element_type=jnp.float32
        )
        for y in range(2):
            for c in range(2):
                mixed = []
                for pair in range(2):
                    f2 = c * 128 + (y * 2 + pair) * 32
                    for s in range(2):
                        to = (y * 2 + s) * 32 * SLOTS + a
                        packed[c * 3 + pair, pl.ds(to, 32, stride=SLOTS), :] = spec[
                            f2 : f2 + 32, s * 128 : s * 128 + 128
                        ]
                    mixed.append(spec[f2 : f2 + 32, 256:384])
                first = jnp.where(lane < 64, mixed[0], pltpu.roll(mixed[1], 64, 1))
                second = jnp.where(lane < 64, pltpu.roll(mixed[0], 64, 1), mixed[1])
                packed[c * 3 + 2, pl.ds(y * 64 * SLOTS + a, 32, stride=SLOTS), :] = first
                packed[c * 3 + 2, pl.ds((y * 2 + 1) * 32 * SLOTS + a, 32, stride=SLOTS), :] = second
        return 0

    lax.fori_loop(0, SLOTS, inner, 0)

    def emit(p, _):
        for tile in range(6):
            out[p, :, tile * INNER : (tile + 1) * INNER] = packed[
                tile, pl.ds(pl.multiple_of(p * SLOTS, SLOTS), SLOTS), :
            ].astype(jnp.bfloat16)
        return 0

    lax.fori_loop(0, DEVICES, emit, 0, unroll=4)


def spectra_of(vre, vim, taps, interpret=False):
    cos_t, sin_t = twist_tables()
    mat = inner_matrix().astype(jnp.bfloat16)
    return pl.pallas_call(
        spectra_kernel,
        out_shape=jax.ShapeDtypeStruct((DEVICES, SLOTS, 6 * INNER), jnp.bfloat16),
        in_specs=[pl.BlockSpec(memory_space=pltpu.VMEM)] * 6,
        out_specs=pl.BlockSpec(memory_space=pltpu.VMEM),
        scratch_shapes=[
            pltpu.VMEM((2, FRAMES, OUTER, SLOTS, INNER), jnp.float32),
            pltpu.VMEM((2, SLOTS * 384, INNER), jnp.float32),
            pltpu.VMEM((6, DEVICES * SLOTS, INNER), jnp.float32),
        ],
        compiler_params=pltpu.CompilerParams(vmem_limit_bytes=52 * MIB),
        cost_estimate=pl.CostEstimate(flops=2 * 10**9, bytes_accessed=60 * 10**6, transcendentals=0),
        interpret=interpret,
        name="spectra",
    )(vre, vim, taps, jnp.asarray(cos_t), jnp.asarray(sin_t), jnp.asarray(mat))


def quarter_kernel(where, wre, wim, slots, out, total):
    step = pl.program_id(0)
    rows = jnp.where(where[0] == 0, wre[...], wim[...]).astype(jnp.bfloat16)
    antenna = lax.broadcasted_iota(jnp.int32, (rows.shape[0], slots.shape[2]), 0) + step * rows.shape[0]
    chosen = jnp.where(antenna == slots[0], 1.0, 0.0).astype(jnp.bfloat16)
    part = lax.dot_general(rows, chosen, (((0,), (0,)), ((), ())), preferred_element_type=jnp.float32)

    @pl.when(step == 0)
    def _():
        total[...] = part

    @pl.when(step > 0)
    def _():
        total[...] = total[...] + part

    @pl.when(step == pl.num_programs(0) - 1)
    def _():
        out[...] = total[...].astype(jnp.bfloat16)


def quarter_of(y_lo, core, wre, wim, antenna_map, interpret=False):
    antennas, beams = wre.shape
    depth = 256
    half = antennas // 2
    grid_spec = pltpu.PrefetchScalarGridSpec(
        num_scalar_prefetch=1,
        grid=(antennas // depth,),
        in_specs=[
            pl.BlockSpec((depth, beams), lambda i, w: (jnp.where(w[0] == 0, i, 0), 0)),
            pl.BlockSpec((depth, beams), lambda i, w: (jnp.where(w[0] == 0, 0, i), 0)),
            pl.BlockSpec((1, 1, half), lambda i, w: (w[1], 0, 0)),
        ],
        out_specs=pl.BlockSpec((beams, half), lambda i, w: (0, 0)),
        scratch_shapes=[pltpu.VMEM((beams, half), jnp.float32)],
    )
    return pl.pallas_call(
        quarter_kernel,
        grid_spec=grid_spec,
        out_shape=jax.ShapeDtypeStruct((beams, half), jnp.bfloat16),
        compiler_params=pltpu.CompilerParams(vmem_limit_bytes=32 * MIB),
        cost_estimate=pl.CostEstimate(flops=2 * 10**9, bytes_accessed=6 * 10**6, transcendentals=0),
        interpret=interpret,
        name="quarter",
    )(jnp.stack([y_lo, core]).astype(jnp.int32), wre, wim, antenna_map.reshape(2, 1, half))


def choose_matrix():
    chosen = np.zeros((2, 32, 3, 4, 32), np.float32)
    for pair in range(2):
        for f1 in range(32):
            chosen[pair, f1, pair, :, f1] = 1.0
            chosen[pair, f1, 2, 2 * pair : 2 * pair + 2, f1] = 1.0
    return chosen.reshape(64, 384)


def beams_kernel(places, w0, w1, w2, w3, spectra, choose, out, sums):
    spec = spectra[...]
    for k3, part in enumerate((w0, w1, w2, w3)):
        result = jnp.dot(part[...], spec, preferred_element_type=jnp.float32)
        for k in range(16):
            at = pl.multiple_of(places[k3 * 16 + k], 16)
            sums[pl.ds(at, 16), :] = result[k * 16 : (k + 1) * 16, :]
    beams = sums.shape[0] // 2
    re = sums[:beams, :384] - sums[beams:, 384:]
    im = sums[beams:, :384] + sums[:beams, 384:]
    power = re * re + im * im
    total = lax.dot_general(
        choose[...],
        power,
        (((1,), (1,)), ((), ())),
        preferred_element_type=jnp.float32,
        precision=lax.Precision.HIGHEST,
    )
    out[...] = total * (1.0 / SPECTRA)


def beams_of(places, parts, spectra, interpret=False):
    rows = sum(p.shape[0] for p in parts)
    return pl.pallas_call(
        beams_kernel,
        out_shape=jax.ShapeDtypeStruct((64, rows // 2), jnp.float32),
        in_specs=[pl.BlockSpec(memory_space=pltpu.SMEM)] + [pl.BlockSpec(memory_space=pltpu.VMEM)] * 6,
        out_specs=pl.BlockSpec(memory_space=pltpu.VMEM),
        scratch_shapes=[pltpu.VMEM((rows, 768), jnp.float32)],
        compiler_params=pltpu.CompilerParams(vmem_limit_bytes=40 * MIB),
        cost_estimate=pl.CostEstimate(flops=33 * 10**8, bytes_accessed=8 * 10**6, transcendentals=0),
        interpret=interpret,
        name="beams",
    )(places, *parts, spectra, jnp.asarray(choose_matrix()))


def index_of(z, x, y, core):
    return ((y % 2) * 2 + core) * 32 + (z % 4) * 8 + (x % 4) * 2 + (y % 4) // 2


EVERY = [(z, x, y, c) for z in range(4) for x in range(4) for y in range(4) for c in range(2)]
ORDER = (("y", "x", "z"), ("z", "y", "x"))
SHIFTS = (0, -1, 1, 2)


def permutation(stage, shift):
    pairs = []
    for z, x, y, core in EVERY:
        axis = ORDER[core][stage]
        source = {"z": z, "x": x, "y": y}
        source[axis] += shift
        pairs.append((index_of(source["z"], source["x"], source["y"], core), index_of(z, x, y, core)))
    return pairs


def gather_stage(block, stage):
    return [block] + [lax.ppermute(block, ALL, permutation(stage, shift)) for shift in SHIFTS[1:]]


def block_places(grp, dev):
    core = grp % 2
    z, x, y = dev // 8, dev // 2 % 4, dev % 2 * 2 + grp // 2
    k = np.arange(64)
    shift = np.array(SHIFTS)
    first, second, third = shift[k % 4], shift[k // 4 % 4], shift[k // 16]
    by_core = []
    for order in ORDER:
        moved = dict(zip(order, (first, second, third)))
        by_core.append([moved[axis] for axis in "zxy"])
    is_first = core == 0
    mz, mx, my = [jnp.where(is_first, jnp.asarray(a), jnp.asarray(b)) for a, b in zip(*by_core)]
    fz, fx, fy = (z + mz + 4) % 4, (x + mx + 4) % 4, (y + my + 4) % 4
    return (((fy % 2) * 32 + fz * 8 + fx * 2 + fy // 2) * 16).astype(jnp.int32)


SWAP = [(0, 1), (1, 0), (2, 3), (3, 2)]


def on_device(voltage_real, voltage_imaginary, filter_taps, weights_re, weights_im, owners, antenna_map):
    grp, dev = lax.axis_index("grp"), lax.axis_index("dev")
    y_lo, core = grp // 2, grp % 2

    quarter = quarter_of(y_lo, core, weights_re[0], weights_im[0], antenna_map)
    offers = lax.all_to_all(quarter.reshape(32, 16, -1), "dev", split_axis=0, concat_axis=0, tiled=True)

    spectra = spectra_of(voltage_real, voltage_imaginary, filter_taps)
    spectra = lax.all_to_all(spectra, ALL, split_axis=0, concat_axis=0, tiled=True)

    mine = lax.dynamic_index_in_dim(offers, owners[core], 0, keepdims=False)
    other = lax.dynamic_index_in_dim(offers, owners[1 - core], 0, keepdims=False)
    other = lax.ppermute(other, "grp", SWAP)
    block = jnp.where(
        core == 0,
        jnp.concatenate([mine, other], axis=1),
        jnp.concatenate([other, mine], axis=1),
    )
    block = jnp.concatenate(gather_stage(block, 0), axis=0)
    block = jnp.concatenate(gather_stage(block, 1), axis=0)
    parts = gather_stage(block, 2)

    power = beams_of(block_places(grp, dev), parts, spectra.reshape(DEVICES * SLOTS, -1))
    power = power.reshape(2, 32, -1)
    own = lax.dynamic_index_in_dim(power, core, 0, keepdims=False)
    given = lax.dynamic_index_in_dim(power, 1 - core, 0, keepdims=False)
    taken = lax.ppermute(given, "grp", SWAP)
    return jnp.where(core == 0, jnp.stack([own, taken]), jnp.stack([taken, own]))


def solution(mesh):
    return jax.shard_map(
        on_device,
        mesh=mesh,
        in_specs=(
            P(("grp", "dev"), None),
            P(("grp", "dev"), None),
            P(),
            P("dev", None, None),
            P("dev", None, None),
            P(),
            P(),
        ),
        out_specs=P(None, ("grp", "dev"), None),
        check_vma=False,
    )
```

profile of v0, /device:TPU:1, one launch (start us, length us, event | category | flops | bytes accessed | tf_op | source)
XLA Modules:
  0.0 150.6 jit_solution(5953822052340792451)
XLA Ops:
  0.0 0.1 pad_add_fusion.where
  0.1 0.0 copy-start
  0.1 2.2 %copy-done = f32[1,2048,512]{2,1,0:T(8,128)S(1)} copy-done((f32[1,2048,512]{2,1,0:T(8,128)S(1)}, f32[1,2048,512]{2,1,0:T(8,128)}, u32[]{:S(2)}) %copy-start) | copy-done | bytes 4194328
  2.3 0.0 copy-start.1
  2.3 2.2 %copy-done.1 = f32[1,2048,512]{2,1,0:T(8,128)S(1)} copy-done((f32[1,2048,512]{2,1,0:T(8,128)S(1)}, f32[1,2048,512]{2,1,0:T(8,128)}, u32[]{:S(2)}) %copy-start.1) | copy-done | bytes 4194328
  4.5 0.0 copy-start.6
  4.5 0.7 copy-done.6
  5.2 0.0 copy-start.2
  5.2 0.0 copy-start.3
  5.2 0.0 copy-start.4
  5.2 0.0 copy-start.5
  5.2 7.2 %quarter.1 = bf16[512,1024]{1,0:T(8,128)(2,1)} custom-call(s32[2]{0:T(128)S(1)} %pad_add_fusion.where, f32[2048,512]{1,0:T(8,128)S(1)} %bitcast.17, f32[2048,512]{1,0:T(8,128)S(1)} %bitcast.18, s32[2,1,1024]{2,1,0:T(1,128)S(1)} %bitcast.21), custom_call_target="tpu_custom_call" | custom-call | flops 2000000000 | bytes 6000000 | tf_op jit(solution)/shard_map/quarter/pallas_call | solution.py:203
  12.4 11.3 %all-to-all-start = ((bf16[32,16,1024]{2,1,0:T(8,128)(2,1)}), bf16[32,16,1024]{2,1,0:T(8,128)(2,1)S(1)}, u32[]{:S(2)}, u32[]{:S(2)}) async-start(bf16[32,16,1024]{2,1,0:T(8,128)(2,1)} %bitcast.5), calls=%async_computation | async-start | bytes 2097152 | tf_op jit(solution)/shard_map/all_to_all | solution.py:306
  23.7 0.0 copy-done.2
  23.8 0.0 copy-done.3
  23.8 0.0 copy-done.4
  23.8 0.0 copy-done.5
  23.8 26.2 %spectra.1 = bf16[128,16,768]{2,1,0:T(8,128)(2,1)} custom-call(bf16[16,110592]{1,0:T(8,128)(2,1)} %vre.1, bf16[16,110592]{1,0:T(8,128)(2,1)} %vim.1, f32[16,4096]{1,0:T(8,128)S(1)} %copy-done.2, f32[32,128]{1,0:T(8,128)S(1)} %copy-done.5, f32[32,128]{1,0:T(8,128)S(1)} %copy-done.4, bf16[256,256]{1,0:T(8,128)(2,1)S(1)} %copy-done.3), custom_call_target="tpu_custom_call" | custom-call | flops 2000000000 | bytes 60000000 | tf_op jit(solution)/shard_map/spectra/pallas_call | solution.py:151
  50.0 0.0 copy-start.9
  50.0 0.0 copy-start.10
  50.0 0.0 copy-start.7
  50.0 0.0 all-to-all-done
  50.0 0.0 copy-start.8
  50.0 1.0 copy-done.8
  51.0 9.9 %all-to-all-start.1 = ((bf16[128,16,768]{2,1,0:T(8,128)(2,1)}), bf16[128,16,768]{2,1,0:T(8,128)(2,1)S(1)}, u32[]{:S(2)}, u32[]{:S(2)}) async-start(bf16[128,16,768]{2,1,0:T(8,128)(2,1)} %spectra.1), calls=%async_computation.1 | async-start | bytes 6291456 | tf_op jit(solution)/shard_map/all_to_all | solution.py:309
  60.9 0.0 copy-done.9
  60.9 0.7 fusion.16
  65.1 0.8 dynamic-slice_bitcast_fusion.1
  65.9 1.1 collective-permute-start
  67.0 0.9 collective-permute-done
  67.8 0.6 constant_dynamic-update-slice_fusion.6
  68.5 2.6 %collective-permute-start.3 = (bf16[16,2048]{1,0:T(8,128)(2,1)S(1)}, bf16[16,2048]{1,0:T(8,128)(2,1)S(1)}, u32[]{:S(2)}, u32[]{:S(2)}) collective-permute-start(bf16[16,2048]{1,0:T(8,128)(2,1)S(1)} %get-tuple-element.6), channel_id=1, source_target_pairs={{1,0},{48,32},{65,64},{112,96},{0,1},{49,33},{64,65},{113,97},{3,2... | collective-permute-start | bytes 196616 | tf_op jit(solution)/shard_map/ppermute | solution.py:279
  71.0 0.6 collective-permute-start.2
  71.7 0.8 collective-permute-start.1
  72.5 11.7 %collective-permute-done.3 = bf16[16,2048]{1,0:T(8,128)(2,1)S(1)} collective-permute-done((bf16[16,2048]{1,0:T(8,128)(2,1)S(1)}, bf16[16,2048]{1,0:T(8,128)(2,1)S(1)}, u32[]{:S(2)}, u32[]{:S(2)}) %collective-permute-start.3) | collective-permute-done | bytes 65568 | tf_op jit(solution)/shard_map/ppermute | solution.py:279
  84.2 15.0 %collective-permute-done.2 = bf16[16,2048]{1,0:T(8,128)(2,1)S(1)} collective-permute-done((bf16[16,2048]{1,0:T(8,128)(2,1)S(1)}, bf16[16,2048]{1,0:T(8,128)(2,1)S(1)}, u32[]{:S(2)}, u32[]{:S(2)}) %collective-permute-start.2) | collective-permute-done | bytes 65568 | tf_op jit(solution)/shard_map/ppermute | solution.py:279
  99.3 0.0 collective-permute-done.1
  99.3 2.0 %collective-permute-start.6 = (bf16[64,2048]{1,0:T(8,128)(2,1)S(1)}, bf16[64,2048]{1,0:T(8,128)(2,1)S(1)}, u32[]{:S(2)}, u32[]{:S(2)}) collective-permute-start(bf16[64,2048]{1,0:T(8,128)(2,1)S(1)} %pad_maximum_fusion), channel_id=1, source_target_pairs={{4,0},{33,32},{68,64},{97,96},{5,1},{32,33},{69,65},{96,97},{6,2},... | collective-permute-start | bytes 786440 | tf_op jit(solution)/shard_map/ppermute | solution.py:279
  101.2 0.2 collective-permute-start.5
  101.5 1.2 collective-permute-start.4
  102.7 0.6 constant_dynamic-update-slice_fusion.5
  103.3 0.6 constant_dynamic-update-slice_fusion.4
  103.9 0.6 constant_dynamic-update-slice_fusion.3
  104.6 4.6 %collective-permute-done.4 = bf16[64,2048]{1,0:T(8,128)(2,1)S(1)} collective-permute-done((bf16[64,2048]{1,0:T(8,128)(2,1)S(1)}, bf16[64,2048]{1,0:T(8,128)(2,1)S(1)}, u32[]{:S(2)}, u32[]{:S(2)}) %collective-permute-start.4) | collective-permute-done | bytes 262176 | tf_op jit(solution)/shard_map/ppermute | solution.py:279
  109.2 0.7 constant_dynamic-update-slice_fusion.2
  109.9 0.0 collective-permute-done.5
  109.9 0.7 constant_dynamic-update-slice_fusion.1
  110.6 0.0 collective-permute-done.6
  110.7 0.7 constant_dynamic-update-slice_fusion.w0
  111.4 3.5 %collective-permute-start.9 = (bf16[256,2048]{1,0:T(8,128)(2,1)}, bf16[256,2048]{1,0:T(8,128)(2,1)}, u32[]{:S(2)}, u32[]{:S(2)}) collective-permute-start(bf16[256,2048]{1,0:T(8,128)(2,1)} %constant_dynamic-update-slice_fusion.w0), channel_id=1, source_target_pairs={{16,0},{36,32},{80,64},{100,96},{17,1},{37,33},{81,65},{101,97},{1... | collective-permute-start | bytes 3145736 | tf_op jit(solution)/shard_map/ppermute | solution.py:279
  114.8 0.0 collective-permute-start.8
  114.8 1.5 collective-permute-start.7
  116.3 0.0 copy-done.10
  116.3 0.0 copy-done.11
  116.3 0.0 copy-done.12
  116.3 11.3 %collective-permute-done.9.w3 = bf16[256,2048]{1,0:T(8,128)(2,1)} collective-permute-done((bf16[256,2048]{1,0:T(8,128)(2,1)}, bf16[256,2048]{1,0:T(8,128)(2,1)}, u32[]{:S(2)}, u32[]{:S(2)}) %collective-permute-start.9) | collective-permute-done | bytes 1048608 | tf_op jit(solution)/shard_map/ppermute | solution.py:279
  127.7 11.7 %collective-permute-done.8.w2 = bf16[256,2048]{1,0:T(8,128)(2,1)} collective-permute-done((bf16[256,2048]{1,0:T(8,128)(2,1)}, bf16[256,2048]{1,0:T(8,128)(2,1)}, u32[]{:S(2)}, u32[]{:S(2)}) %collective-permute-start.8) | collective-permute-done | bytes 1048608 | tf_op jit(solution)/shard_map/ppermute | solution.py:279
  139.4 0.0 collective-permute-done.7.w1
  139.4 0.0 all-to-all-done.1
  139.4 0.0 copy-done.7
  139.4 6.5 %beams.1 = f32[64,512]{1,0:T(8,128)S(1)} custom-call(s32[64]{0:T(128)S(1)} %fusion.15.places, bf16[256,2048]{1,0:T(8,128)(2,1)} %constant_dynamic-update-slice_fusion.w0, bf16[256,2048]{1,0:T(8,128)(2,1)} %collective-permute-done.7.w1, bf16[256,2048]{1,0:T(8,128)(2,1)} %collective-permute-done.8.w2, bf16[256,2048]{1,0:T(8,128)(2,1)} %collective-permute-done.9.w3, ...), custom_call_target="tpu_custom_call" | custom-call | flops 3300000000 | bytes 8000000 | tf_op jit(solution)/shard_map/beams/pallas_call | solution.py:246
  146.0 3.0 %collective-permute-start.10 = (f32[32,512]{1,0:T(8,128)S(1)}, f32[32,512]{1,0:T(8,128)S(1)}, u32[]{:S(2)}, u32[]{:S(2)}) collective-permute-start(f32[32,512]{1,0:T(8,128)S(1)} %get-tuple-element.10), channel_id=1, source_target_pairs={{0,32},{32,0},{64,96},{96,64},{1,33},{33,1},{65,97},{97,65},{2,34}... | collective-permute-start | bytes 196616 | tf_op jit(solution)/shard_map/ppermute | solution.py:327
  149.0 0.9 collective-permute-done.10
  149.9 0.7 maximum_select_fusion
  (5 shorter events, 0.1 us)
Async XLA Ops:
  0.1 2.2 %copy-start = (f32[1,2048,512]{2,1,0:T(8,128)S(1)}, f32[1,2048,512]{2,1,0:T(8,128)}, u32[]{:S(2)}) copy-start(f32[1,2048,512]{2,1,0:T(8,128)} %param.17) | copy-start | bytes 12582916
  2.3 2.2 %copy-start.1 = (f32[1,2048,512]{2,1,0:T(8,128)S(1)}, f32[1,2048,512]{2,1,0:T(8,128)}, u32[]{:S(2)}) copy-start(f32[1,2048,512]{2,1,0:T(8,128)} %param.18) | copy-start | bytes 12582916
  4.5 0.7 copy-start.6
  5.2 18.6 %copy-start.2 = (f32[16,4096]{1,0:T(8,128)S(1)}, f32[16,4096]{1,0:T(8,128)}, u32[]{:S(2)}) copy-start(f32[16,4096]{1,0:T(8,128)} %taps.1) | copy-start | bytes 786436
  5.2 18.6 %copy-start.3 = (bf16[256,256]{1,0:T(8,128)(2,1)S(1)}, bf16[256,256]{1,0:T(8,128)(2,1)}, u32[]{:S(2)}) copy-start(bf16[256,256]{1,0:T(8,128)(2,1)} %constant.139.clone.mat) | copy-start | bytes 393220
  5.2 18.6 %copy-start.4 = (f32[32,128]{1,0:T(8,128)S(1)}, f32[32,128]{1,0:T(8,128)}, u32[]{:S(2)}) copy-start(f32[32,128]{1,0:T(8,128)} %constant.138.clone.sin_t) | copy-start | bytes 49156
  5.2 18.6 %copy-start.5 = (f32[32,128]{1,0:T(8,128)S(1)}, f32[32,128]{1,0:T(8,128)}, u32[]{:S(2)}) copy-start(f32[32,128]{1,0:T(8,128)} %constant.137.clone.cos_t) | copy-start | bytes 49156
  12.4 37.6 %all-to-all-start = ((bf16[32,16,1024]{2,1,0:T(8,128)(2,1)}), bf16[32,16,1024]{2,1,0:T(8,128)(2,1)S(1)}, u32[]{:S(2)}, u32[]{:S(2)}) async-start(bf16[32,16,1024]{2,1,0:T(8,128)(2,1)} %bitcast.5), calls=%async_computation | async-start | bytes 2097152 | tf_op jit(solution)/shard_map/all_to_all | solution.py:306
  50.0 11.0 %copy-start.9 = (s32[2]{0:T(128)S(1)}, s32[2]{0:T(128)}, u32[]{:S(2)}) copy-start(s32[2]{0:T(128)} %param.19) | copy-start | bytes 28
  50.0 66.3 %copy-start.10 = (s32[64]{0:T(128)S(1)}, s32[64]{0:T(128)}, u32[]{:S(2)}) copy-start(s32[64]{0:T(128)} %constant.142.clone) | copy-start | bytes 772
  50.0 66.3 %copy-start.11 = (s32[64]{0:T(128)S(1)}, s32[64]{0:T(128)}, u32[]{:S(2)}) copy-start(s32[64]{0:T(128)} %constant.141.clone) | copy-start | bytes 772
  50.0 66.3 %copy-start.12 = (s32[64]{0:T(128)S(1)}, s32[64]{0:T(128)}, u32[]{:S(2)}) copy-start(s32[64]{0:T(128)} %constant.140.clone) | copy-start | bytes 772
  50.0 89.4 %copy-start.7 = (f32[64,384]{1,0:T(8,128)S(1)}, f32[64,384]{1,0:T(8,128)}, u32[]{:S(2)}) copy-start(f32[64,384]{1,0:T(8,128)} %constant.143.clone.choose) | copy-start | bytes 294916
  50.0 1.0 copy-start.8
  51.0 88.4 %all-to-all-start.1 = ((bf16[128,16,768]{2,1,0:T(8,128)(2,1)}), bf16[128,16,768]{2,1,0:T(8,128)(2,1)S(1)}, u32[]{:S(2)}, u32[]{:S(2)}) async-start(bf16[128,16,768]{2,1,0:T(8,128)(2,1)} %spectra.1), calls=%async_computation.1 | async-start | bytes 6291456 | tf_op jit(solution)/shard_map/all_to_all | solution.py:309
  65.9 1.9 %collective-permute-start = (bf16[16,1024]{1,0:T(8,128)(2,1)S(1)}, bf16[16,1024]{1,0:T(8,128)(2,1)S(1)}, u32[]{:S(2)}, u32[]{:S(2)}) collective-permute-start(bf16[16,1024]{1,0:T(8,128)(2,1)S(1)} %get-tuple-element.7), channel_id=1, source_target_pairs={{0,32},{32,0},{64,96},{96,64},{1,33},{33,1},{65,97},{97,65},{2,34}... | collective-permute-start | bytes 98312 | tf_op jit(solution)/shard_map/ppermute | solution.py:313
  68.5 15.8 %collective-permute-start.3 = (bf16[16,2048]{1,0:T(8,128)(2,1)S(1)}, bf16[16,2048]{1,0:T(8,128)(2,1)S(1)}, u32[]{:S(2)}, u32[]{:S(2)}) collective-permute-start(bf16[16,2048]{1,0:T(8,128)(2,1)S(1)} %get-tuple-element.6), channel_id=1, source_target_pairs={{1,0},{48,32},{65,64},{112,96},{0,1},{49,33},{64,65},{113,97},{3,2... | collective-permute-start | bytes 196616 | tf_op jit(solution)/shard_map/ppermute | solution.py:279
  71.0 28.2 %collective-permute-start.2 = (bf16[16,2048]{1,0:T(8,128)(2,1)S(1)}, bf16[16,2048]{1,0:T(8,128)(2,1)S(1)}, u32[]{:S(2)}, u32[]{:S(2)}) collective-permute-start(bf16[16,2048]{1,0:T(8,128)(2,1)S(1)} %get-tuple-element.6), channel_id=1, source_target_pairs={{64,0},{40,32},{1,64},{104,96},{65,1},{41,33},{0,65},{105,97},{66,... | collective-permute-start | bytes 196616 | tf_op jit(solution)/shard_map/ppermute | solution.py:279
  71.7 27.6 %collective-permute-start.1 = (bf16[16,2048]{1,0:T(8,128)(2,1)S(1)}, bf16[16,2048]{1,0:T(8,128)(2,1)S(1)}, u32[]{:S(2)}, u32[]{:S(2)}) collective-permute-start(bf16[16,2048]{1,0:T(8,128)(2,1)S(1)} %get-tuple-element.6), channel_id=1, source_target_pairs={{65,0},{56,32},{0,64},{120,96},{64,1},{57,33},{1,65},{121,97},{67,... | collective-permute-start | bytes 196616 | tf_op jit(solution)/shard_map/ppermute | solution.py:279
  99.3 11.4 %collective-permute-start.6 = (bf16[64,2048]{1,0:T(8,128)(2,1)S(1)}, bf16[64,2048]{1,0:T(8,128)(2,1)S(1)}, u32[]{:S(2)}, u32[]{:S(2)}) collective-permute-start(bf16[64,2048]{1,0:T(8,128)(2,1)S(1)} %pad_maximum_fusion), channel_id=1, source_target_pairs={{4,0},{33,32},{68,64},{97,96},{5,1},{32,33},{69,65},{96,97},{6,2},... | collective-permute-start | bytes 786440 | tf_op jit(solution)/shard_map/ppermute | solution.py:279
  101.2 8.7 %collective-permute-start.5 = (bf16[64,2048]{1,0:T(8,128)(2,1)S(1)}, bf16[64,2048]{1,0:T(8,128)(2,1)S(1)}, u32[]{:S(2)}, u32[]{:S(2)}) collective-permute-start(bf16[64,2048]{1,0:T(8,128)(2,1)S(1)} %pad_maximum_fusion), channel_id=1, source_target_pairs={{2,0},{96,32},{66,64},{33,96},{3,1},{97,33},{67,65},{32,97},{4,2},... | collective-permute-start | bytes 786440 | tf_op jit(solution)/shard_map/ppermute | solution.py:279
  101.5 7.7 %collective-permute-start.4 = (bf16[64,2048]{1,0:T(8,128)(2,1)S(1)}, bf16[64,2048]{1,0:T(8,128)(2,1)S(1)}, u32[]{:S(2)}, u32[]{:S(2)}) collective-permute-start(bf16[64,2048]{1,0:T(8,128)(2,1)S(1)} %pad_maximum_fusion), channel_id=1, source_target_pairs={{6,0},{97,32},{70,64},{32,96},{7,1},{96,33},{71,65},{33,97},{0,2},... | collective-permute-start | bytes 786440 | tf_op jit(solution)/shard_map/ppermute | solution.py:279
  111.4 16.3 %collective-permute-start.9 = (bf16[256,2048]{1,0:T(8,128)(2,1)}, bf16[256,2048]{1,0:T(8,128)(2,1)}, u32[]{:S(2)}, u32[]{:S(2)}) collective-permute-start(bf16[256,2048]{1,0:T(8,128)(2,1)} %constant_dynamic-update-slice_fusion.w0), channel_id=1, source_target_pairs={{16,0},{36,32},{80,64},{100,96},{17,1},{37,33},{81,65},{101,97},{1... | collective-permute-start | bytes 3145736 | tf_op jit(solution)/shard_map/ppermute | solution.py:279
  114.8 24.6 %collective-permute-start.8 = (bf16[256,2048]{1,0:T(8,128)(2,1)}, bf16[256,2048]{1,0:T(8,128)(2,1)}, u32[]{:S(2)}, u32[]{:S(2)}) collective-permute-start(bf16[256,2048]{1,0:T(8,128)(2,1)} %constant_dynamic-update-slice_fusion.w0), channel_id=1, source_target_pairs={{8,0},{34,32},{72,64},{98,96},{9,1},{35,33},{73,65},{99,97},{10,2}... | collective-permute-start | bytes 3145736 | tf_op jit(solution)/shard_map/ppermute | solution.py:279
  114.8 24.6 %collective-permute-start.7 = (bf16[256,2048]{1,0:T(8,128)(2,1)}, bf16[256,2048]{1,0:T(8,128)(2,1)}, u32[]{:S(2)}, u32[]{:S(2)}) collective-permute-start(bf16[256,2048]{1,0:T(8,128)(2,1)} %constant_dynamic-update-slice_fusion.w0), channel_id=1, source_target_pairs={{24,0},{38,32},{88,64},{102,96},{25,1},{39,33},{89,65},{103,97},{2... | collective-permute-start | bytes 3145736 | tf_op jit(solution)/shard_map/ppermute | solution.py:279
  146.0 3.9 %collective-permute-start.10 = (f32[32,512]{1,0:T(8,128)S(1)}, f32[32,512]{1,0:T(8,128)S(1)}, u32[]{:S(2)}, u32[]{:S(2)}) collective-permute-start(f32[32,512]{1,0:T(8,128)S(1)} %get-tuple-element.10), channel_id=1, source_target_pairs={{0,32},{32,0},{64,96},{96,64},{1,33},{33,1},{65,97},{97,65},{2,34}... | collective-permute-start | bytes 196616 | tf_op jit(solution)/shard_map/ppermute | solution.py:327
where the time goes:
time: 151 us
  waiting for transfers between devices  56.2 us (37%)
  Pallas kernels  39.9 us (26%)
  starting transfers between devices  37.7 us (25%)
  local copies, waits for them, and re-layouts  11.5 us (8%)
  between operations  3.69 us (2%)
    ppermute x9, waiting for transfers between devices, gather_stage(): lax.ppermute(block, ALL, permutation(stage, shift))  54.4 us
    pallas_call x1, Pallas kernels, spectra_of(): pl.pallas_call(spectra_kernel, out_shape=jax.ShapeDtypeStruct((DEVICES, S...  26.2 us
    ppermute x9, starting transfers between devices, gather_stage(): lax.ppermute(block, ALL, permutation(stage, shift))  12.4 us
    all_to_all x1, starting transfers between devices, on_device(): lax.all_to_all(quarter.reshape(32, 16, -1), 'dev', split_axis=0, concat_a...  11.3 us
    all_to_all x1, starting transfers between devices, on_device(): lax.all_to_all(spectra, ALL, split_axis=0, concat_axis=0, tiled=True)  9.93 us
    unnamed x31, local copies, waits for them, and re-layouts  9.38 us
    pallas_call x1, Pallas kernels, quarter_of(): pl.pallas_call(quarter_kernel, grid_spec=grid_spec, out_shape=jax.ShapeDt...  7.23 us
    pallas_call x1, Pallas kernels, beams_of(): pl.pallas_call(beams_kernel, out_shape=jax.ShapeDtypeStruct((64, rows //...  6.53 us
  transfers between devices with their start and end apart: 13, of which 7 were waited for; matrix products, arithmetic and copies ran while one was open for 4% of the time, Pallas kernels for 17%

commit v1 on v0

--- a/solution.py
+++ b/solution.py
@@ -1,3 +1,4 @@
+import functools
 import math
 
 import jax
@@ -18,6 +19,8 @@
 INNER = 128
 SLOTS = 16
 DEVICES = 128
+ROW_STRIDE = 24
+PARTS = ((0, 1, 2, 3, 6, 7, 8, 9), (4, 5, 10, 11))
 ALL = ("grp", "dev")
 MIB = 1 << 20
 
@@ -66,19 +69,24 @@
     return result
 
 
-def spectra_kernel(vre, vim, taps, cos_t, sin_t, mat, out, frames, turned, packed):
+def spectra_kernel(part, vre, vim, taps, cos_t, sin_t, mat, out, frames, turned, packed):
+    chosen = PARTS[part]
+    first, last = min(chosen), max(chosen) + TAPS
+    rows_per_slot = 32 * len(chosen)
+    slot_stride = rows_per_slot + 8
+
     def fir(n1, _):
         rows = [taps[k : k + 1, pl.ds(pl.multiple_of(n1 * INNER, INNER), INNER)] for k in range(TAPS)]
         for c, volts in ((0, vre), (1, vim)):
-            window = [
-                volts[:, pl.ds(pl.multiple_of(b * CHANNELS + n1 * INNER, INNER), INNER)].astype(jnp.float32)
-                for b in range(BLOCKS)
-            ]
-            for u in range(FRAMES):
+            window = {
+                b: volts[:, pl.ds(pl.multiple_of(b * CHANNELS + n1 * INNER, INNER), INNER)].astype(jnp.float32)
+                for b in range(first, last)
+            }
+            for i, u in enumerate(chosen):
                 total = window[u] * rows[0]
                 for k in range(1, TAPS):
                     total = total + window[u + k] * rows[k]
-                frames[c, u, n1] = total
+                frames[c, i, n1] = total
         return 0
 
     lax.fori_loop(0, OUTER, fir, 0)
@@ -86,9 +94,6 @@
     def outer(i, _):
         u = i // 2
         low = pl.multiple_of((i % 2) * 8, 8)
-        s = u // SPECTRA
-        t = u % SPECTRA
-        place = jnp.where(t < 4, s * 128 + t * 32, 256 + s * 64 + (t - 4) * 32)
         points = [
             (frames[0, u, n1, pl.ds(low, 8), :], frames[1, u, n1, pl.ds(low, 8), :]) for n1 in range(OUTER)
         ]
@@ -98,70 +103,69 @@
             if f1:
                 c, d = cos_t[f1 : f1 + 1, :], sin_t[f1 : f1 + 1, :]
                 re, im = re * c + im * d, im * c - re * d
-            at = low * 384 + place + f1
-            turned[0, pl.ds(at, 8, stride=384), :] = re
-            turned[1, pl.ds(at, 8, stride=384), :] = im
+            at = low * slot_stride + u * 32 + f1
+            turned[0, pl.ds(at, 8, stride=slot_stride), :] = re
+            turned[1, pl.ds(at, 8, stride=slot_stride), :] = im
         return 0
 
-    lax.fori_loop(0, 2 * FRAMES, outer, 0)
+    lax.fori_loop(0, 2 * len(chosen), outer, 0)
 
     matrix = mat[...]
     lane = lax.broadcasted_iota(jnp.int32, (32, INNER), 1)
 
     def inner(a, _):
-        base = pl.multiple_of(a * 384, 128)
+        base = pl.multiple_of(a * slot_stride, 8)
         rows = jnp.concatenate(
-            [turned[0, pl.ds(base, 384), :], turned[1, pl.ds(base, 384), :]], axis=1
+            [turned[0, pl.ds(base, rows_per_slot), :], turned[1, pl.ds(base, rows_per_slot), :]], axis=1
         ).astype(jnp.bfloat16)
         spec = lax.dot_general(
             matrix, rows, (((1,), (1,)), ((), ())), preferred_element_type=jnp.float32
         )
         for y in range(2):
             for c in range(2):
-                mixed = []
-                for pair in range(2):
-                    f2 = c * 128 + (y * 2 + pair) * 32
-                    for s in range(2):
-                        to = (y * 2 + s) * 32 * SLOTS + a
-                        packed[c * 3 + pair, pl.ds(to, 32, stride=SLOTS), :] = spec[
-                            f2 : f2 + 32, s * 128 : s * 128 + 128
-                        ]
-                    mixed.append(spec[f2 : f2 + 32, 256:384])
-                first = jnp.where(lane < 64, mixed[0], pltpu.roll(mixed[1], 64, 1))
-                second = jnp.where(lane < 64, pltpu.roll(mixed[0], 64, 1), mixed[1])
-                packed[c * 3 + 2, pl.ds(y * 64 * SLOTS + a, 32, stride=SLOTS), :] = first
-                packed[c * 3 + 2, pl.ds((y * 2 + 1) * 32 * SLOTS + a, 32, stride=SLOTS), :] = second
+                to = [pl.ds((y * 2 + s) * 32 * ROW_STRIDE + a, 32, stride=ROW_STRIDE) for s in range(2)]
+                at = [c * 128 + (y * 2 + pair) * 32 for pair in range(2)]
+                if part == 0:
+                    for pair in range(2):
+                        for s in range(2):
+                            packed[c * 2 + pair, to[s], :] = spec[at[pair] : at[pair] + 32, s * 128 : s * 128 + 128]
+                else:
+                    mixed = [spec[f2 : f2 + 32, :] for f2 in at]
+                    packed[c, to[0], :] = jnp.where(lane < 64, mixed[0], pltpu.roll(mixed[1], 64, 1))
+                    packed[c, to[1], :] = jnp.where(lane < 64, pltpu.roll(mixed[0], 64, 1), mixed[1])
         return 0
 
     lax.fori_loop(0, SLOTS, inner, 0)
 
     def emit(p, _):
-        for tile in range(6):
+        for tile in range(packed.shape[0]):
             out[p, :, tile * INNER : (tile + 1) * INNER] = packed[
-                tile, pl.ds(pl.multiple_of(p * SLOTS, SLOTS), SLOTS), :
+                tile, pl.ds(pl.multiple_of(p * ROW_STRIDE, 8), SLOTS), :
             ].astype(jnp.bfloat16)
         return 0
 
     lax.fori_loop(0, DEVICES, emit, 0, unroll=4)
 
 
-def spectra_of(vre, vim, taps, interpret=False):
+def spectra_of(part, vre, vim, taps, interpret=False):
     cos_t, sin_t = twist_tables()
     mat = inner_matrix().astype(jnp.bfloat16)
+    count = len(PARTS[part])
+    tiles = count // 2
     return pl.pallas_call(
-        spectra_kernel,
-        out_shape=jax.ShapeDtypeStruct((DEVICES, SLOTS, 6 * INNER), jnp.bfloat16),
+        functools.partial(spectra_kernel, part),
+        out_shape=jax.ShapeDtypeStruct((DEVICES, SLOTS, tiles * INNER), jnp.bfloat16),
         in_specs=[pl.BlockSpec(memory_space=pltpu.VMEM)] * 6,
         out_specs=pl.BlockSpec(memory_space=pltpu.VMEM),
         scratch_shapes=[
-            pltpu.VMEM((2, FRAMES, OUTER, SLOTS, INNER), jnp.float32),
-            pltpu.VMEM((2, SLOTS * 384, INNER), jnp.float32),
-            pltpu.VMEM((6, DEVICES * SLOTS, INNER), jnp.float32),
+            pltpu.VMEM((2, count, OUTER, SLOTS, INNER), jnp.float32),
+            pltpu.VMEM((2, SLOTS * (32 * count + 8), INNER), jnp.float32),
+            pltpu.VMEM((tiles, DEVICES * ROW_STRIDE, INNER), jnp.float32),
         ],
-        compiler_params=pltpu.CompilerParams(vmem_limit_bytes=52 * MIB),
-        cost_estimate=pl.CostEstimate(flops=2 * 10**9, bytes_accessed=60 * 10**6, transcendentals=0),
+        compiler_params=pltpu.CompilerParams(vmem_limit_bytes=32 * MIB),
+        cost_estimate=pl.CostEstimate(flops=2 * 10**8 * count, bytes_accessed=4 * 10**6 * count, transcendentals=0),
         interpret=interpret,
-        name="spectra",
+        name="spectra" + "ab"[part],
     )(vre, vim, taps, jnp.asarray(cos_t), jnp.asarray(sin_t), jnp.asarray(mat))
 
 
@@ -187,7 +191,7 @@
 
 def quarter_of(y_lo, core, wre, wim, antenna_map, interpret=False):
     antennas, beams = wre.shape
-    depth = 256
+    depth = 512
     half = antennas // 2
     grid_spec = pltpu.PrefetchScalarGridSpec(
         num_scalar_prefetch=1,
@@ -204,7 +208,7 @@
         quarter_kernel,
         grid_spec=grid_spec,
         out_shape=jax.ShapeDtypeStruct((beams, half), jnp.bfloat16),
-        compiler_params=pltpu.CompilerParams(vmem_limit_bytes=32 * MIB),
+        compiler_params=pltpu.CompilerParams(vmem_limit_bytes=57 * MIB),
         cost_estimate=pl.CostEstimate(flops=2 * 10**9, bytes_accessed=6 * 10**6, transcendentals=0),
         interpret=interpret,
         name="quarter",
@@ -220,20 +224,52 @@
     return chosen.reshape(64, 384)
 
 
-def beams_kernel(places, w0, w1, w2, w3, spectra, choose, out, sums):
-    spec = spectra[...]
-    for k3, part in enumerate((w0, w1, w2, w3)):
-        result = jnp.dot(part[...], spec, preferred_element_type=jnp.float32)
+def early_kernel(w0, w1, za, zb, out):
+    for i, part in enumerate((w0, w1)):
+        w = part[...]
+        n = w.shape[0]
+        out[i * n : (i + 1) * n, :512] = jnp.dot(w, za[...], preferred_element_type=jnp.float32)
+        out[i * n : (i + 1) * n, 512:] = jnp.dot(w, zb[...], preferred_element_type=jnp.float32)
+
+
+def early_of(w0, w1, za, zb, interpret=False):
+    return pl.pallas_call(
+        early_kernel,
+        out_shape=jax.ShapeDtypeStruct((2 * w0.shape[0], 768), jnp.float32),
+        in_specs=[pl.BlockSpec(memory_space=pltpu.VMEM)] * 4,
+        out_specs=pl.BlockSpec(memory_space=pltpu.VMEM),
+        compiler_params=pltpu.CompilerParams(vmem_limit_bytes=24 * MIB),
+        cost_estimate=pl.CostEstimate(flops=17 * 10**8, bytes_accessed=8 * 10**6, transcendentals=0),
+        interpret=interpret,
+        name="early",
+    )(w0, w1, za, zb)
+
+
+def beams_kernel(places, early, w2, w3, za, zb, choose, out, sums):
+    for k in range(32):
+        at = pl.multiple_of(places[k], 16)
+        sums[pl.ds(at, 16), :] = early[k * 16 : (k + 1) * 16, :]
+    for i, part in enumerate((w2, w3)):
+        w = part[...]
+        first = jnp.dot(w, za[...], preferred_element_type=jnp.float32)
+        second = jnp.dot(w, zb[...], preferred_element_type=jnp.float32)
         for k in range(16):
-            at = pl.multiple_of(places[k3 * 16 + k], 16)
-            sums[pl.ds(at, 16), :] = result[k * 16 : (k + 1) * 16, :]
+            at = pl.multiple_of(places[(i + 2) * 16 + k], 16)
+            sums[pl.ds(at, 16), :512] = first[k * 16 : (k + 1) * 16, :]
+            sums[pl.ds(at, 16), 512:] = second[k * 16 : (k + 1) * 16, :]
     beams = sums.shape[0] // 2
-    re = sums[:beams, :384] - sums[beams:, 384:]
-    im = sums[beams:, :384] + sums[:beams, 384:]
-    power = re * re + im * im
+
+    def power(re_lanes, im_lanes):
+        re = sums[:beams, re_lanes] - sums[beams:, im_lanes]
+        im = sums[beams:, re_lanes] + sums[:beams, im_lanes]
+        return re * re + im * im
+
+    powers = jnp.concatenate(
+        [power(slice(0, 256), slice(256, 512)), power(slice(512, 640), slice(640, 768))], axis=1
+    )
     total = lax.dot_general(
         choose[...],
-        power,
+        powers,
         (((1,), (1,)), ((), ())),
         preferred_element_type=jnp.float32,
         precision=lax.Precision.HIGHEST,
@@ -241,19 +277,19 @@
     out[...] = total * (1.0 / SPECTRA)
 
 
-def beams_of(places, parts, spectra, interpret=False):
-    rows = sum(p.shape[0] for p in parts)
+def beams_of(places, early, w2, w3, za, zb, interpret=False):
+    rows = early.shape[0] + 2 * w2.shape[0]
     return pl.pallas_call(
         beams_kernel,
         out_shape=jax.ShapeDtypeStruct((64, rows // 2), jnp.float32),
         in_specs=[pl.BlockSpec(memory_space=pltpu.SMEM)] + [pl.BlockSpec(memory_space=pltpu.VMEM)] * 6,
         out_specs=pl.BlockSpec(memory_space=pltpu.VMEM),
         scratch_shapes=[pltpu.VMEM((rows, 768), jnp.float32)],
-        compiler_params=pltpu.CompilerParams(vmem_limit_bytes=40 * MIB),
-        cost_estimate=pl.CostEstimate(flops=33 * 10**8, bytes_accessed=8 * 10**6, transcendentals=0),
+        compiler_params=pltpu.CompilerParams(vmem_limit_bytes=32 * MIB),
+        cost_estimate=pl.CostEstimate(flops=17 * 10**8, bytes_accessed=8 * 10**6, transcendentals=0),
         interpret=interpret,
         name="beams",
-    )(places, *parts, spectra, jnp.asarray(choose_matrix()))
+    )(places, early, w2, w3, za, zb, jnp.asarray(choose_matrix()))
 
 
 def index_of(z, x, y, core):
@@ -305,8 +341,11 @@
     quarter = quarter_of(y_lo, core, weights_re[0], weights_im[0], antenna_map)
     offers = lax.all_to_all(quarter.reshape(32, 16, -1), "dev", split_axis=0, concat_axis=0, tiled=True)
 
-    spectra = spectra_of(voltage_real, voltage_imaginary, filter_taps)
-    spectra = lax.all_to_all(spectra, ALL, split_axis=0, concat_axis=0, tiled=True)
+    moved = []
+    for part in range(2):
+        rows = spectra_of(part, voltage_real, voltage_imaginary, filter_taps)
+        rows = lax.all_to_all(rows, ALL, split_axis=0, concat_axis=0, tiled=True)
+        moved.append(rows.reshape(DEVICES * SLOTS, -1))
 
     mine = lax.dynamic_index_in_dim(offers, owners[core], 0, keepdims=False)
     other = lax.dynamic_index_in_dim(offers, owners[1 - core], 0, keepdims=False)
@@ -320,7 +359,10 @@
     block = jnp.concatenate(gather_stage(block, 1), axis=0)
     parts = gather_stage(block, 2)
 
-    power = beams_of(block_places(grp, dev), parts, spectra.reshape(DEVICES * SLOTS, -1))
+    early = early_of(parts[0], parts[3], *moved)
+    places = block_places(grp, dev)
+    places = jnp.concatenate([places[:16], places[48:], places[16:48]])
+    power = beams_of(places, early, parts[1], parts[2], *moved)
     power = power.reshape(2, 32, -1)
     own = lax.dynamic_index_in_dim(power, core, 0, keepdims=False)
     given = lax.dynamic_index_in_dim(power, 1 - core, 0, keepdims=False)

time: 151 us -> 148 us (0.980)
  waiting for transfers between devices: 56.2 us -> 41.2 us
  local copies, waits for them, and re-layouts: 11.5 us -> 18.5 us
  starting transfers between devices: 37.7 us -> 44.2 us
  Pallas kernels: 39.9 us -> 36.1 us
    ppermute x9, waiting for transfers between devices: 54.4 us -> 13.7 us  [gather_stage(): lax.ppermute(block, ALL, permutation(stage, shift))]
    all_to_all x1 -> x2, waiting for transfers between devices: 0.01 us -> 21.6 us  [on_device(): rows = lax.all_to_all(rows, ALL, split_axis=0, concat_axis=0, tiled=True)]
    unnamed x31 -> x45, local copies, waits for them, and re-layouts: 9.38 us -> 14.8 us
    all_to_all x1 -> x2, starting transfers between devices: 9.93 us -> 14.8 us  [on_device(): rows = lax.all_to_all(rows, ALL, split_axis=0, concat_axis=0, tiled=True)]
    all_to_all x1, waiting for transfers between devices: 0.01 us -> 3.91 us  [on_device(): lax.all_to_all(quarter.reshape(32, 16, -1), 'dev', split_axis=0, concat_a...]
    pallas_call x1 -> x3, Pallas kernels: 26.2 us -> 23.9 us  [the longest x2 20.2 us: spectra_of(): pl.pallas_call(functools.partial(spectra_kernel, part), out_shape=jax.Sha...]
    pallas_call x1, Pallas kernels: 6.53 us -> 4.3 us  [beams_of(): pl.pallas_call(beams_kernel, out_shape=jax.ShapeDtypeStruct((64, rows //...]
    ppermute x9, starting transfers between devices: 12.4 us -> 13.9 us  [gather_stage(): lax.ppermute(block, ALL, permutation(stage, shift))]
  transfers between devices with their start and end apart: 13 -> 14, of which waited for: 7 -> 6; matrix products, arithmetic and copies ran while one was open for 4% -> 6% of each run, Pallas kernels for 17% -> 16%
where the time goes in v1:
time: 148 us; the launch traced here: 147 us
  starting transfers between devices  44.2 us (30%)
  waiting for transfers between devices  41.2 us (28%)
  Pallas kernels  36.1 us (24%)
  local copies, waits for them, and re-layouts  18.5 us (12%)
  between operations  4.16 us (3%)
  other arithmetic  2.85 us (2%)
    all_to_all x2, waiting for transfers between devices, on_device(): rows = lax.all_to_all(rows, ALL, split_axis=0, concat_axis=0, tiled=True)  21.6 us
    pallas_call x2, Pallas kernels, spectra_of(): pl.pallas_call(functools.partial(spectra_kernel, part), out_shape=jax.Sha...  20.2 us
    unnamed x45, local copies, waits for them, and re-layouts  14.8 us
    all_to_all x2, starting transfers between devices, on_device(): rows = lax.all_to_all(rows, ALL, split_axis=0, concat_axis=0, tiled=True)  14.8 us
    ppermute x9, starting transfers between devices, gather_stage(): lax.ppermute(block, ALL, permutation(stage, shift))  13.9 us
    ppermute x9, waiting for transfers between devices, gather_stage(): lax.ppermute(block, ALL, permutation(stage, shift))  13.7 us
    all_to_all x1, starting transfers between devices, on_device(): lax.all_to_all(quarter.reshape(32, 16, -1), 'dev', split_axis=0, concat_a...  11.5 us
    pallas_call x1, Pallas kernels, quarter_of(): pl.pallas_call(quarter_kernel, grid_spec=grid_spec, out_shape=jax.ShapeDt...  7.94 us
  transfers between devices with their start and end apart: 14, of which 6 were waited for; matrix products, arithmetic and copies ran while one was open for 6% of the time, Pallas kernels for 16%

profile of v1, /device:TPU:1, one launch (start us, length us, event | category | flops | bytes accessed | tf_op | source)
XLA Modules:
  0.0 147.1 jit_solution(6129152660056217292)
XLA Ops:
  0.0 0.6 pad_add_fusion.1.where
  0.6 7.9 %quarter.1 = bf16[512,1024]{1,0:T(8,128)(2,1)} custom-call(s32[2]{0:T(128)} %pad_add_fusion.1.where, f32[2048,512]{1,0:T(8,128)} %bitcast.21, f32[2048,512]{1,0:T(8,128)} %bitcast.22, s32[2,1,1024]{2,1,0:T(1,128)} %bitcast.25), custom_call_target="tpu_custom_call" | custom-call | flops 2000000000 | bytes 6000000 | tf_op jit(solution)/shard_map/quarter/pallas_call | solution.py:207
  8.5 11.5 %all-to-all-start = ((bf16[32,16,1024]{2,1,0:T(8,128)(2,1)}), bf16[32,16,1024]{2,1,0:T(8,128)(2,1)}, u32[]{:S(2)}, u32[]{:S(2)}) async-start(bf16[32,16,1024]{2,1,0:T(8,128)(2,1)} %bitcast.23), calls=%async_computation | async-start | bytes 2097152 | tf_op jit(solution)/shard_map/all_to_all | solution.py:342
  20.0 0.0 copy-done
  20.0 0.0 copy-done.10
  20.0 0.0 copy-start.1
  20.0 2.0 %copy-done.1 = bf16[16,110592]{1,0:T(8,128)(2,1)S(1)} copy-done((bf16[16,110592]{1,0:T(8,128)(2,1)S(1)}, bf16[16,110592]{1,0:T(8,128)(2,1)}, u32[]{:S(2)}) %copy-start.1) | copy-done | bytes 3538968
  22.0 0.9 copy-done.5
  23.0 0.9 copy-done.7
  23.9 0.7 copy-done.11
  24.6 8.6 %spectrab.1 = bf16[128,16,256]{2,1,0:T(8,128)(2,1)S(1)} custom-call(bf16[16,110592]{1,0:T(8,128)(2,1)S(1)} %copy-done, bf16[16,110592]{1,0:T(8,128)(2,1)S(1)} %copy-done.1, f32[16,4096]{1,0:T(8,128)S(1)} %copy-done.5, f32[32,128]{1,0:T(8,128)S(1)} %copy-done.10, f32[32,128]{1,0:T(8,128)S(1)} %copy-done.11, bf16[256,256]{1,0:T(8,128)(2,1)S(1)} %copy-done.7), custom_call_target="tpu_custom_call" | custom-call | flops 800000000 | bytes 16000000 | tf_op jit(solution)/shard_map/spectrab/pallas_call | solution.py:155
  33.2 1.0 copy-done.4
  34.2 3.9 %all-to-all-done = bf16[32,16,1024]{2,1,0:T(8,128)(2,1)} async-done(((bf16[32,16,1024]{2,1,0:T(8,128)(2,1)}), bf16[32,16,1024]{2,1,0:T(8,128)(2,1)}, u32[]{:S(2)}, u32[]{:S(2)}) %all-to-all-start) | async-done | bytes 1048608 | tf_op jit(solution)/shard_map/all_to_all | solution.py:342
  38.1 6.6 %all-to-all-start.2 = ((bf16[128,16,256]{2,1,0:T(8,128)(2,1)}), bf16[128,16,256]{2,1,0:T(8,128)(2,1)}, u32[]{:S(2)}, u32[]{:S(2)}) async-start(bf16[128,16,256]{2,1,0:T(8,128)(2,1)} %copy-done.4), calls=%async_computation.2 | async-start | bytes 2097152 | tf_op jit(solution)/shard_map/all_to_all | solution.py:347
  44.8 1.4 fusion.16
  50.1 1.4 dynamic-slice_bitcast_fusion.1
  51.5 1.3 collective-permute-start
  52.8 1.2 collective-permute-done
  54.0 1.5 constant_dynamic-update-slice_fusion.6
  55.5 0.7 collective-permute-start.1
  56.2 1.9 %collective-permute-start.2 = (bf16[16,2048]{1,0:T(8,128)(2,1)S(1)}, bf16[16,2048]{1,0:T(8,128)(2,1)S(1)}, u32[]{:S(2)}, u32[]{:S(2)}) collective-permute-start(bf16[16,2048]{1,0:T(8,128)(2,1)S(1)} %get-tuple-element.6), channel_id=1, source_target_pairs={{64,0},{40,32},{1,64},{104,96},{65,1},{41,33},{0,65},{105,97},{66,... | collective-permute-start | bytes 196616 | tf_op jit(solution)/shard_map/ppermute | solution.py:315
  58.2 1.3 collective-permute-start.3
  59.4 2.0 %copy-done.2 = bf16[16,110592]{1,0:T(8,128)(2,1)S(1)} copy-done((bf16[16,110592]{1,0:T(8,128)(2,1)S(1)}, bf16[16,110592]{1,0:T(8,128)(2,1)}, u32[]{:S(2)}) %copy-start.2) | copy-done | bytes 3538968
  61.5 0.9 copy-done.6
  62.4 0.9 copy-done.8
  63.3 0.7 copy-done.12
  64.0 11.6 %spectraa.1 = bf16[128,16,512]{2,1,0:T(8,128)(2,1)S(1)} custom-call(bf16[16,110592]{1,0:T(8,128)(2,1)S(1)} %copy-done, bf16[16,110592]{1,0:T(8,128)(2,1)S(1)} %copy-done.2, f32[16,4096]{1,0:T(8,128)S(1)} %copy-done.6, f32[32,128]{1,0:T(8,128)S(1)} %copy-done.10, f32[32,128]{1,0:T(8,128)S(1)} %copy-done.12, bf16[256,256]{1,0:T(8,128)(2,1)S(1)} %copy-done.8), custom_call_target="tpu_custom_call" | custom-call | flops 1600000000 | bytes 32000000 | tf_op jit(solution)/shard_map/spectraa/pallas_call | solution.py:155
  75.7 1.3 copy-done.3
  77.0 0.0 collective-permute-done.1
  77.0 0.0 collective-permute-done.2
  77.0 0.0 copy-start.13
  77.0 0.0 collective-permute-done.3
  77.1 0.0 copy-start.15
  77.1 1.3 collective-permute-start.4
  78.4 1.4 collective-permute-start.5
  79.8 1.6 %collective-permute-start.6 = (bf16[64,2048]{1,0:T(8,128)(2,1)S(1)}, bf16[64,2048]{1,0:T(8,128)(2,1)S(1)}, u32[]{:S(2)}, u32[]{:S(2)}) collective-permute-start(bf16[64,2048]{1,0:T(8,128)(2,1)S(1)} %pad_maximum_fusion), channel_id=1, source_target_pairs={{4,0},{33,32},{68,64},{97,96},{5,1},{32,33},{69,65},{96,97},{6,2},... | collective-permute-start | bytes 786440 | tf_op jit(solution)/shard_map/ppermute | solution.py:315
  81.5 0.0 copy-done.15
  81.5 0.6 constant_dynamic-update-slice_fusion.5
  82.1 0.0 all-to-all-done.2
  82.1 8.1 %all-to-all-start.1 = ((bf16[128,16,512]{2,1,0:T(8,128)(2,1)}), bf16[128,16,512]{2,1,0:T(8,128)(2,1)S(1)}, u32[]{:S(2)}, u32[]{:S(2)}) async-start(bf16[128,16,512]{2,1,0:T(8,128)(2,1)} %copy-done.3), calls=%async_computation.1 | async-start | bytes 4194304 | tf_op jit(solution)/shard_map/all_to_all | solution.py:347
  90.3 0.6 constant_dynamic-update-slice_fusion.4
  90.9 0.6 constant_dynamic-update-slice_fusion.3
  91.5 0.0 collective-permute-done.4
  91.5 0.7 constant_dynamic-update-slice_fusion.2
  92.2 0.0 collective-permute-done.5
  92.2 0.7 constant_dynamic-update-slice_fusion.1
  93.0 0.0 collective-permute-done.6
  93.0 0.7 constant_dynamic-update-slice_fusion.w0
  93.7 2.9 %collective-permute-start.7 = (bf16[256,2048]{1,0:T(8,128)(2,1)}, bf16[256,2048]{1,0:T(8,128)(2,1)}, u32[]{:S(2)}, u32[]{:S(2)}) collective-permute-start(bf16[256,2048]{1,0:T(8,128)(2,1)} %constant_dynamic-update-slice_fusion.w0), channel_id=1, source_target_pairs={{16,0},{36,32},{80,64},{100,96},{17,1},{37,33},{81,65},{101,97},{1... | collective-permute-start | bytes 3145736 | tf_op jit(solution)/shard_map/ppermute | solution.py:315
  96.6 0.3 collective-permute-start.8
  96.9 2.4 %collective-permute-start.9 = (bf16[256,2048]{1,0:T(8,128)(2,1)}, bf16[256,2048]{1,0:T(8,128)(2,1)}, u32[]{:S(2)}, u32[]{:S(2)}) collective-permute-start(bf16[256,2048]{1,0:T(8,128)(2,1)} %constant_dynamic-update-slice_fusion.w0), channel_id=1, source_target_pairs={{8,0},{34,32},{72,64},{98,96},{9,1},{35,33},{73,65},{99,97},{10,2}... | collective-permute-start | bytes 3145736 | tf_op jit(solution)/shard_map/ppermute | solution.py:315
  99.3 0.1 slice.11
  99.4 0.1 fusion.17
  99.4 0.1 pad_add_fusion.places
  99.5 21.6 %all-to-all-done.1 = bf16[128,16,512]{2,1,0:T(8,128)(2,1)S(1)} async-done(((bf16[128,16,512]{2,1,0:T(8,128)(2,1)}), bf16[128,16,512]{2,1,0:T(8,128)(2,1)S(1)}, u32[]{:S(2)}, u32[]{:S(2)}) %all-to-all-start.1) | async-done | bytes 2097184 | tf_op jit(solution)/shard_map/all_to_all | solution.py:347
  121.1 6.5 %collective-permute-done.7.w1 = bf16[256,2048]{1,0:T(8,128)(2,1)} collective-permute-done((bf16[256,2048]{1,0:T(8,128)(2,1)}, bf16[256,2048]{1,0:T(8,128)(2,1)}, u32[]{:S(2)}, u32[]{:S(2)}) %collective-permute-start.7) | collective-permute-done | bytes 1048608 | tf_op jit(solution)/shard_map/ppermute | solution.py:315
  127.5 3.6 %early.1 = f32[512,768]{1,0:T(8,128)S(1)} custom-call(bf16[256,2048]{1,0:T(8,128)(2,1)} %constant_dynamic-update-slice_fusion.w0, bf16[256,2048]{1,0:T(8,128)(2,1)} %collective-permute-done.7.w1, bf16[2048,512]{1,0:T(8,128)(2,1)S(1)} %bitcast.18, bf16[2048,256]{1,0:T(8,128)(2,1)} %bitcast.11.zb), custom_call_target="tpu_custom_call" | custom-call | flops 1700000000 | bytes 8000000 | tf_op jit(solution)/shard_map/early/pallas_call | solution.py:236
  131.2 7.2 %collective-permute-done.8.w2 = bf16[256,2048]{1,0:T(8,128)(2,1)S(1)} collective-permute-done((bf16[256,2048]{1,0:T(8,128)(2,1)}, bf16[256,2048]{1,0:T(8,128)(2,1)S(1)}, u32[]{:S(2)}, u32[]{:S(2)}) %collective-permute-start.8) | collective-permute-done | bytes 1048608 | tf_op jit(solution)/shard_map/ppermute | solution.py:315
  138.4 0.0 collective-permute-done.9.w3
  138.4 0.0 copy-done.9
  138.4 4.3 %beams.1 = f32[64,512]{1,0:T(8,128)S(1)} custom-call(s32[64]{0:T(128)S(1)} %pad_add_fusion.places, f32[512,768]{1,0:T(8,128)S(1)} %early.1, bf16[256,2048]{1,0:T(8,128)(2,1)S(1)} %collective-permute-done.8.w2, bf16[256,2048]{1,0:T(8,128)(2,1)} %collective-permute-done.9.w3, bf16[2048,512]{1,0:T(8,128)(2,1)S(1)} %bitcast.19, bf16[2048,256]{1,0:T(8,128)(2,1)} %bitcast.11.zb, ...), custom_call_target="tpu_custom_call" | custom-call | flops 1700000000 | bytes 8000000 | tf_op jit(solution)/shard_map/beams/pallas_call | solution.py:282
  142.7 2.8 %collective-permute-start.10 = (f32[32,512]{1,0:T(8,128)S(1)}, f32[32,512]{1,0:T(8,128)S(1)}, u32[]{:S(2)}, u32[]{:S(2)}) collective-permute-start(f32[32,512]{1,0:T(8,128)S(1)} %get-tuple-element.10), channel_id=1, source_target_pairs={{0,32},{32,0},{64,96},{96,64},{1,33},{33,1},{65,97},{97,65},{2,34}... | collective-permute-start | bytes 196616 | tf_op jit(solution)/shard_map/ppermute | solution.py:369
  145.5 0.9 collective-permute-done.10
  146.4 0.7 maximum_select_fusion
  (26 shorter events, 0.1 us)
Async XLA Ops:
  0.6 19.4 %copy-start = (bf16[16,110592]{1,0:T(8,128)(2,1)S(1)}, bf16[16,110592]{1,0:T(8,128)(2,1)}, u32[]{:S(2)}) copy-start(bf16[16,110592]{1,0:T(8,128)(2,1)} %vre.3) | copy-start | bytes 10616836
  0.6 19.4 %copy-start.10 = (f32[32,128]{1,0:T(8,128)S(1)}, f32[32,128]{1,0:T(8,128)}, u32[]{:S(2)}) copy-start(f32[32,128]{1,0:T(8,128)} %constant.137.clone.cos_t) | copy-start | bytes 49156
  8.5 29.6 %all-to-all-start = ((bf16[32,16,1024]{2,1,0:T(8,128)(2,1)}), bf16[32,16,1024]{2,1,0:T(8,128)(2,1)}, u32[]{:S(2)}, u32[]{:S(2)}) async-start(bf16[32,16,1024]{2,1,0:T(8,128)(2,1)} %bitcast.23), calls=%async_computation | async-start | bytes 2097152 | tf_op jit(solution)/shard_map/all_to_all | solution.py:342
  20.0 2.0 %copy-start.1 = (bf16[16,110592]{1,0:T(8,128)(2,1)S(1)}, bf16[16,110592]{1,0:T(8,128)(2,1)}, u32[]{:S(2)}) copy-start(bf16[16,110592]{1,0:T(8,128)(2,1)} %vim.3) | copy-start | bytes 10616836
  22.0 0.9 copy-start.5
  23.0 0.9 copy-start.7
  23.9 0.7 copy-start.11
  33.2 1.0 copy-start.4
  38.1 44.0 %all-to-all-start.2 = ((bf16[128,16,256]{2,1,0:T(8,128)(2,1)}), bf16[128,16,256]{2,1,0:T(8,128)(2,1)}, u32[]{:S(2)}, u32[]{:S(2)}) async-start(bf16[128,16,256]{2,1,0:T(8,128)(2,1)} %copy-done.4), calls=%async_computation.2 | async-start | bytes 2097152 | tf_op jit(solution)/shard_map/all_to_all | solution.py:347
  51.5 2.5 %collective-permute-start = (bf16[16,1024]{1,0:T(8,128)(2,1)}, bf16[16,1024]{1,0:T(8,128)(2,1)}, u32[]{:S(2)}, u32[]{:S(2)}) collective-permute-start(bf16[16,1024]{1,0:T(8,128)(2,1)} %get-tuple-element.7), channel_id=1, source_target_pairs={{0,32},{32,0},{64,96},{96,64},{1,33},{33,1},{65,97},{97,65},{2,34}... | collective-permute-start | bytes 98312 | tf_op jit(solution)/shard_map/ppermute | solution.py:352
  55.5 21.5 %collective-permute-start.1 = (bf16[16,2048]{1,0:T(8,128)(2,1)S(1)}, bf16[16,2048]{1,0:T(8,128)(2,1)S(1)}, u32[]{:S(2)}, u32[]{:S(2)}) collective-permute-start(bf16[16,2048]{1,0:T(8,128)(2,1)S(1)} %get-tuple-element.6), channel_id=1, source_target_pairs={{65,0},{56,32},{0,64},{120,96},{64,1},{57,33},{1,65},{121,97},{67,... | collective-permute-start | bytes 196616 | tf_op jit(solution)/shard_map/ppermute | solution.py:315
  56.2 20.8 %collective-permute-start.2 = (bf16[16,2048]{1,0:T(8,128)(2,1)S(1)}, bf16[16,2048]{1,0:T(8,128)(2,1)S(1)}, u32[]{:S(2)}, u32[]{:S(2)}) collective-permute-start(bf16[16,2048]{1,0:T(8,128)(2,1)S(1)} %get-tuple-element.6), channel_id=1, source_target_pairs={{64,0},{40,32},{1,64},{104,96},{65,1},{41,33},{0,65},{105,97},{66,... | collective-permute-start | bytes 196616 | tf_op jit(solution)/shard_map/ppermute | solution.py:315
  58.2 18.9 %collective-permute-start.3 = (bf16[16,2048]{1,0:T(8,128)(2,1)S(1)}, bf16[16,2048]{1,0:T(8,128)(2,1)S(1)}, u32[]{:S(2)}, u32[]{:S(2)}) collective-permute-start(bf16[16,2048]{1,0:T(8,128)(2,1)S(1)} %get-tuple-element.6), channel_id=1, source_target_pairs={{1,0},{48,32},{65,64},{112,96},{0,1},{49,33},{64,65},{113,97},{3,2... | collective-permute-start | bytes 196616 | tf_op jit(solution)/shard_map/ppermute | solution.py:315
  59.4 2.0 %copy-start.2 = (bf16[16,110592]{1,0:T(8,128)(2,1)S(1)}, bf16[16,110592]{1,0:T(8,128)(2,1)}, u32[]{:S(2)}) copy-start(bf16[16,110592]{1,0:T(8,128)(2,1)} %vim.3) | copy-start | bytes 10616836
  61.4 0.9 copy-start.6
  62.4 0.9 copy-start.8
  63.3 0.7 copy-start.12
  75.7 1.4 copy-start.3
  77.0 22.2 %copy-start.17 = (s32[64]{0:T(128)S(1)}, s32[64]{0:T(128)}, u32[]{:S(2)}) copy-start(s32[64]{0:T(128)} %constant.142.clone) | copy-start | bytes 772
  77.0 22.2 %copy-start.18 = (s32[64]{0:T(128)S(1)}, s32[64]{0:T(128)}, u32[]{:S(2)}) copy-start(s32[64]{0:T(128)} %constant.140.clone) | copy-start | bytes 772
  77.0 22.2 %copy-start.19 = (s32[64]{0:T(128)S(1)}, s32[64]{0:T(128)}, u32[]{:S(2)}) copy-start(s32[64]{0:T(128)} %constant.141.clone) | copy-start | bytes 772
  77.0 4.4 %copy-start.13 = (bf16[16,2048]{1,0:T(8,128)(2,1)}, bf16[16,2048]{1,0:T(8,128)(2,1)S(1)}, u32[]{:S(2)}) copy-start(bf16[16,2048]{1,0:T(8,128)(2,1)S(1)} %collective-permute-done.2) | copy-start | bytes 196612
  77.1 4.4 %copy-start.15 = (bf16[16,2048]{1,0:T(8,128)(2,1)}, bf16[16,2048]{1,0:T(8,128)(2,1)S(1)}, u32[]{:S(2)}) copy-start(bf16[16,2048]{1,0:T(8,128)(2,1)S(1)} %collective-permute-done.3) | copy-start | bytes 196612
  77.1 14.4 %collective-permute-start.4 = (bf16[64,2048]{1,0:T(8,128)(2,1)S(1)}, bf16[64,2048]{1,0:T(8,128)(2,1)S(1)}, u32[]{:S(2)}, u32[]{:S(2)}) collective-permute-start(bf16[64,2048]{1,0:T(8,128)(2,1)S(1)} %pad_maximum_fusion), channel_id=1, source_target_pairs={{6,0},{97,32},{70,64},{32,96},{7,1},{96,33},{71,65},{33,97},{0,2},... | collective-permute-start | bytes 786440 | tf_op jit(solution)/shard_map/ppermute | solution.py:315
  78.4 13.8 %collective-permute-start.5 = (bf16[64,2048]{1,0:T(8,128)(2,1)S(1)}, bf16[64,2048]{1,0:T(8,128)(2,1)S(1)}, u32[]{:S(2)}, u32[]{:S(2)}) collective-permute-start(bf16[64,2048]{1,0:T(8,128)(2,1)S(1)} %pad_maximum_fusion), channel_id=1, source_target_pairs={{2,0},{96,32},{66,64},{33,96},{3,1},{97,33},{67,65},{32,97},{4,2},... | collective-permute-start | bytes 786440 | tf_op jit(solution)/shard_map/ppermute | solution.py:315
  79.8 13.1 %collective-permute-start.6 = (bf16[64,2048]{1,0:T(8,128)(2,1)S(1)}, bf16[64,2048]{1,0:T(8,128)(2,1)S(1)}, u32[]{:S(2)}, u32[]{:S(2)}) collective-permute-start(bf16[64,2048]{1,0:T(8,128)(2,1)S(1)} %pad_maximum_fusion), channel_id=1, source_target_pairs={{4,0},{33,32},{68,64},{97,96},{5,1},{32,33},{69,65},{96,97},{6,2},... | collective-permute-start | bytes 786440 | tf_op jit(solution)/shard_map/ppermute | solution.py:315
  81.5 8.8 %copy-start.14 = (bf16[16,2048]{1,0:T(8,128)(2,1)S(1)}, bf16[16,2048]{1,0:T(8,128)(2,1)}, u32[]{:S(2)}) copy-start(bf16[16,2048]{1,0:T(8,128)(2,1)} %copy-done.13) | copy-start | bytes 196612
  82.1 8.8 %copy-start.16 = (bf16[16,2048]{1,0:T(8,128)(2,1)S(1)}, bf16[16,2048]{1,0:T(8,128)(2,1)}, u32[]{:S(2)}) copy-start(bf16[16,2048]{1,0:T(8,128)(2,1)} %copy-done.15) | copy-start | bytes 196612
  82.1 39.0 %all-to-all-start.1 = ((bf16[128,16,512]{2,1,0:T(8,128)(2,1)}), bf16[128,16,512]{2,1,0:T(8,128)(2,1)S(1)}, u32[]{:S(2)}, u32[]{:S(2)}) async-start(bf16[128,16,512]{2,1,0:T(8,128)(2,1)} %copy-done.3), calls=%async_computation.1 | async-start | bytes 4194304 | tf_op jit(solution)/shard_map/all_to_all | solution.py:347
  93.7 44.7 %copy-start.9 = (f32[64,384]{1,0:T(8,128)S(1)}, f32[64,384]{1,0:T(8,128)}, u32[]{:S(2)}) copy-start(f32[64,384]{1,0:T(8,128)} %constant.143.clone.choose) | copy-start | bytes 294916
  93.7 33.8 %collective-permute-start.7 = (bf16[256,2048]{1,0:T(8,128)(2,1)}, bf16[256,2048]{1,0:T(8,128)(2,1)}, u32[]{:S(2)}, u32[]{:S(2)}) collective-permute-start(bf16[256,2048]{1,0:T(8,128)(2,1)} %constant_dynamic-update-slice_fusion.w0), channel_id=1, source_target_pairs={{16,0},{36,32},{80,64},{100,96},{17,1},{37,33},{81,65},{101,97},{1... | collective-permute-start | bytes 3145736 | tf_op jit(solution)/shard_map/ppermute | solution.py:315
  96.6 41.8 %collective-permute-start.8 = (bf16[256,2048]{1,0:T(8,128)(2,1)}, bf16[256,2048]{1,0:T(8,128)(2,1)S(1)}, u32[]{:S(2)}, u32[]{:S(2)}) collective-permute-start(bf16[256,2048]{1,0:T(8,128)(2,1)} %constant_dynamic-update-slice_fusion.w0), channel_id=1, source_target_pairs={{24,0},{38,32},{88,64},{102,96},{25,1},{39,33},{89,65},{103,97},{2... | collective-permute-start | bytes 3145736 | tf_op jit(solution)/shard_map/ppermute | solution.py:315
  96.9 41.5 %collective-permute-start.9 = (bf16[256,2048]{1,0:T(8,128)(2,1)}, bf16[256,2048]{1,0:T(8,128)(2,1)}, u32[]{:S(2)}, u32[]{:S(2)}) collective-permute-start(bf16[256,2048]{1,0:T(8,128)(2,1)} %constant_dynamic-update-slice_fusion.w0), channel_id=1, source_target_pairs={{8,0},{34,32},{72,64},{98,96},{9,1},{35,33},{73,65},{99,97},{10,2}... | collective-permute-start | bytes 3145736 | tf_op jit(solution)/shard_map/ppermute | solution.py:315
  142.7 3.7 %collective-permute-start.10 = (f32[32,512]{1,0:T(8,128)S(1)}, f32[32,512]{1,0:T(8,128)S(1)}, u32[]{:S(2)}, u32[]{:S(2)}) collective-permute-start(f32[32,512]{1,0:T(8,128)S(1)} %get-tuple-element.10), channel_id=1, source_target_pairs={{0,32},{32,0},{64,96},{96,64},{1,33},{33,1},{65,97},{97,65},{2,34}... | collective-permute-start | bytes 196616 | tf_op jit(solution)/shard_map/ppermute | solution.py:369

commit v2 on v1

--- a/solution.py
+++ b/solution.py
@@ -20,7 +20,8 @@
 SLOTS = 16
 DEVICES = 128
 ROW_STRIDE = 24
-PARTS = ((0, 1, 2, 3, 6, 7, 8, 9), (4, 5, 10, 11))
+GROUPS = ((0, 1, 6, 7), (2, 3, 8, 9), (4, 5, 10, 11))
+MESSAGES = ((0, 1), (2,))
 ALL = ("grp", "dev")
 MIB = 1 << 20
 
@@ -69,27 +70,48 @@
     return result
 
 
-def spectra_kernel(part, vre, vim, taps, cos_t, sin_t, mat, out, frames, turned, packed):
-    chosen = PARTS[part]
+def spectra_kernel(messages, *refs):
+    groups = [group for message in messages for group in message]
+    count = len(groups)
+    sources, outs = refs[:6], refs[6 : 6 + len(messages)]
+    vre, vim, taps, cos_t, sin_t, mat, frames, turned, packed, ready, sems = refs[6 + len(messages) :]
+    chosen = [u for group in groups for u in GROUPS[group]]
     first, last = min(chosen), max(chosen) + TAPS
     rows_per_slot = 32 * len(chosen)
     slot_stride = rows_per_slot + 8
 
-    def fir(n1, _):
-        rows = [taps[k : k + 1, pl.ds(pl.multiple_of(n1 * INNER, INNER), INNER)] for k in range(TAPS)]
-        for c, volts in ((0, vre), (1, vim)):
+    loads = []
+    for i in (2, 0, 1, 3, 4, 5):
+        source = sources[i]
+        if i < 2:
+            source = source.at[:, first * CHANNELS : last * CHANNELS]
+        loads.append(pltpu.make_async_copy(source, (vre, vim, taps, cos_t, sin_t, mat)[i], sems.at[i]))
+        loads[-1].start()
+    loads[0].wait()
+
+    for c, volts in ((0, vre), (1, vim)):
+        loads[1 + c].wait()
+
+        def fir(n1, _, c=c, volts=volts):
+            rows = [taps[k : k + 1, pl.ds(pl.multiple_of(n1 * INNER, INNER), INNER)] for k in range(TAPS)]
+            needed = sorted({u + k for u in chosen for k in range(TAPS)})
             window = {
-                b: volts[:, pl.ds(pl.multiple_of(b * CHANNELS + n1 * INNER, INNER), INNER)].astype(jnp.float32)
-                for b in range(first, last)
+                b: volts[
+                    :, pl.ds(pl.multiple_of((b - first) * CHANNELS + n1 * INNER, INNER), INNER)
+                ].astype(jnp.float32)
+                for b in needed
             }
             for i, u in enumerate(chosen):
                 total = window[u] * rows[0]
                 for k in range(1, TAPS):
                     total = total + window[u + k] * rows[k]
                 frames[c, i, n1] = total
-        return 0
-
-    lax.fori_loop(0, OUTER, fir, 0)
+            return 0
+
+        lax.fori_loop(0, OUTER, fir, 0)
+
+    for load in loads[3:]:
+        load.wait()
 
     def outer(i, _):
         u = i // 2
@@ -121,51 +143,74 @@
         spec = lax.dot_general(
             matrix, rows, (((1,), (1,)), ((), ())), preferred_element_type=jnp.float32
         )
-        for y in range(2):
-            for c in range(2):
-                to = [pl.ds((y * 2 + s) * 32 * ROW_STRIDE + a, 32, stride=ROW_STRIDE) for s in range(2)]
-                at = [c * 128 + (y * 2 + pair) * 32 for pair in range(2)]
-                if part == 0:
-                    for pair in range(2):
-                        for s in range(2):
-                            packed[c * 2 + pair, to[s], :] = spec[at[pair] : at[pair] + 32, s * 128 : s * 128 + 128]
-                else:
-                    mixed = [spec[f2 : f2 + 32, :] for f2 in at]
-                    packed[c, to[0], :] = jnp.where(lane < 64, mixed[0], pltpu.roll(mixed[1], 64, 1))
-                    packed[c, to[1], :] = jnp.where(lane < 64, pltpu.roll(mixed[0], 64, 1), mixed[1])
+        for g in range(count):
+            for y in range(2):
+                for c in range(2):
+                    to = [pl.ds((y * 2 + s) * 32 * ROW_STRIDE + a, 32, stride=ROW_STRIDE) for s in range(2)]
+                    at = [c * 128 + (y * 2 + pair) * 32 for pair in range(2)]
+                    mixed = [spec[f2 : f2 + 32, g * INNER : (g + 1) * INNER] for f2 in at]
+                    packed[g * 2 + c, to[0], :] = jnp.where(lane < 64, mixed[0], pltpu.roll(mixed[1], 64, 1))
+                    packed[g * 2 + c, to[1], :] = jnp.where(lane < 64, pltpu.roll(mixed[0], 64, 1), mixed[1])
         return 0
 
     lax.fori_loop(0, SLOTS, inner, 0)
 
-    def emit(p, _):
-        for tile in range(packed.shape[0]):
-            out[p, :, tile * INNER : (tile + 1) * INNER] = packed[
-                tile, pl.ds(pl.multiple_of(p * ROW_STRIDE, 8), SLOTS), :
-            ].astype(jnp.bfloat16)
-        return 0
-
-    lax.fori_loop(0, DEVICES, emit, 0, unroll=4)
-
-
-def spectra_of(part, vre, vim, taps, interpret=False):
+    stores = []
+    tile = 0
+    for message, to in zip(messages, outs):
+        for quarter in range(4):
+
+            def emit(p, _, tile=tile, wide=2 * len(message)):
+                for i in range(tile, tile + wide):
+                    ready[p, :, i * INNER : (i + 1) * INNER] = packed[
+                        i, pl.ds(pl.multiple_of(p * ROW_STRIDE, 8), SLOTS), :
+                    ].astype(jnp.bfloat16)
+                return 0
+
+            lax.fori_loop(quarter * 32, quarter * 32 + 32, emit, 0, unroll=4)
+            part = pl.ds(quarter * 32, 32)
+            lanes = slice(tile * INNER, (tile + 2 * len(message)) * INNER)
+            stores.append(
+                pltpu.make_async_copy(ready.at[part, :, lanes], to.at[part], sems.at[6 + len(stores)])
+            )
+            stores[-1].start()
+        tile += 2 * len(message)
+    for store in stores:
+        store.wait()
+
+
+def spectra_of(messages, vre, vim, taps, interpret=False):
     cos_t, sin_t = twist_tables()
     mat = inner_matrix().astype(jnp.bfloat16)
-    count = len(PARTS[part])
-    tiles = count // 2
-    return pl.pallas_call(
-        functools.partial(spectra_kernel, part),
-        out_shape=jax.ShapeDtypeStruct((DEVICES, SLOTS, tiles * INNER), jnp.bfloat16),
-        in_specs=[pl.BlockSpec(memory_space=pltpu.VMEM)] * 6,
-        out_specs=pl.BlockSpec(memory_space=pltpu.VMEM),
+    groups = [group for message in messages for group in message]
+    count = len(groups)
+    many = 4 * count
+    chosen = [u for group in groups for u in GROUPS[group]]
+    samples = (max(chosen) + TAPS - min(chosen)) * CHANNELS
+    return pl.pallas_call(
+        functools.partial(spectra_kernel, messages),
+        out_shape=[jax.ShapeDtypeStruct((DEVICES, SLOTS, 2 * INNER * len(m)), jnp.bfloat16) for m in messages],
+        in_specs=[pl.BlockSpec(memory_space=pltpu.HBM)] * 6,
+        out_specs=[pl.BlockSpec(memory_space=pltpu.HBM)] * len(messages),
         scratch_shapes=[
-            pltpu.VMEM((2, count, OUTER, SLOTS, INNER), jnp.float32),
-            pltpu.VMEM((2, SLOTS * (32 * count + 8), INNER), jnp.float32),
-            pltpu.VMEM((tiles, DEVICES * ROW_STRIDE, INNER), jnp.float32),
+            pltpu.VMEM((SLOTS, samples), jnp.bfloat16),
+            pltpu.VMEM((SLOTS, samples), jnp.bfloat16),
+            pltpu.VMEM((TAPS, CHANNELS), jnp.float32),
+            pltpu.VMEM((OUTER, INNER), jnp.float32),
+            pltpu.VMEM((OUTER, INNER), jnp.float32),
+            pltpu.VMEM((256, 256), jnp.bfloat16),
+            pltpu.VMEM((2, many, OUTER, SLOTS, INNER), jnp.float32),
+            pltpu.VMEM((2, SLOTS * (32 * many + 8), INNER), jnp.float32),
+            pltpu.VMEM((2 * count, DEVICES * ROW_STRIDE, INNER), jnp.float32),
+            pltpu.VMEM((DEVICES, SLOTS, 2 * count * INNER), jnp.bfloat16),
+            pltpu.SemaphoreType.DMA((6 + 4 * len(messages),)),
         ],
-        compiler_params=pltpu.CompilerParams(vmem_limit_bytes=32 * MIB),
-        cost_estimate=pl.CostEstimate(flops=2 * 10**8 * count, bytes_accessed=4 * 10**6 * count, transcendentals=0),
-        interpret=interpret,
-        name="spectra" + "ab"[part],
+        compiler_params=pltpu.CompilerParams(vmem_limit_bytes=58 * MIB),
+        cost_estimate=pl.CostEstimate(
+            flops=8 * 10**8 * count, bytes_accessed=16 * 10**6 * count, transcendentals=0
+        ),
+        interpret=interpret,
+        name="spectra",
     )(vre, vim, taps, jnp.asarray(cos_t), jnp.asarray(sin_t), jnp.asarray(mat))
 
 
@@ -189,7 +234,7 @@
         out[...] = total[...].astype(jnp.bfloat16)
 
 
-def quarter_of(y_lo, core, wre, wim, antenna_map, interpret=False):
+def quarter_of(info, wre, wim, antenna_map, interpret=False):
     antennas, beams = wre.shape
     depth = 512
     half = antennas // 2
@@ -208,68 +253,120 @@
         quarter_kernel,
         grid_spec=grid_spec,
         out_shape=jax.ShapeDtypeStruct((beams, half), jnp.bfloat16),
-        compiler_params=pltpu.CompilerParams(vmem_limit_bytes=57 * MIB),
+        compiler_params=pltpu.CompilerParams(vmem_limit_bytes=58 * MIB),
         cost_estimate=pl.CostEstimate(flops=2 * 10**9, bytes_accessed=6 * 10**6, transcendentals=0),
         interpret=interpret,
         name="quarter",
-    )(jnp.stack([y_lo, core]).astype(jnp.int32), wre, wim, antenna_map.reshape(2, 1, half))
+    )(info, wre, wim, antenna_map.reshape(2, 1, half))
+
+
+def pick_kernel(info, first, second, mine, other):
+    mine[...] = first[0]
+    other[...] = second[0]
+
+
+def pick_of(info, offers, interpret=False):
+    _, rows, columns = offers.shape
+    return pl.pallas_call(
+        pick_kernel,
+        grid_spec=pltpu.PrefetchScalarGridSpec(
+            num_scalar_prefetch=1,
+            grid=(1,),
+            in_specs=[
+                pl.BlockSpec((1, rows, columns), lambda i, w: (w[2], 0, 0)),
+                pl.BlockSpec((1, rows, columns), lambda i, w: (w[3], 0, 0)),
+            ],
+            out_specs=[pl.BlockSpec((rows, columns), lambda i, w: (0, 0))] * 2,
+        ),
+        out_shape=[jax.ShapeDtypeStruct((rows, columns), offers.dtype)] * 2,
+        interpret=interpret,
+        name="pick",
+    )(info, offers, offers)
+
+
+def join_kernel(*refs):
+    parts, out = refs[:-1], refs[-1]
+    at = 0
+    for part in parts:
+        rows = part.shape[0]
+        out[at : at + rows, :] = part[...]
+        at += rows
+
+
+def join_of(parts, interpret=False):
+    rows = sum(p.shape[0] for p in parts)
+    return pl.pallas_call(
+        join_kernel,
+        out_shape=jax.ShapeDtypeStruct((rows, parts[0].shape[1]), parts[0].dtype),
+        in_specs=[pl.BlockSpec(memory_space=pltpu.VMEM)] * len(parts),
+        out_specs=pl.BlockSpec(memory_space=pltpu.VMEM),
+        compiler_params=pltpu.CompilerParams(vmem_limit_bytes=8 * MIB),
+        interpret=interpret,
+        name="join",
+    )(*parts)
 
 
 def choose_matrix():
-    chosen = np.zeros((2, 32, 3, 4, 32), np.float32)
+    chosen = np.zeros((2, 32, 3, 2, 2, 32), np.float32)
     for pair in range(2):
         for f1 in range(32):
-            chosen[pair, f1, pair, :, f1] = 1.0
-            chosen[pair, f1, 2, 2 * pair : 2 * pair + 2, f1] = 1.0
+            chosen[pair, f1, :, pair, :, f1] = 1.0
     return chosen.reshape(64, 384)
 
 
-def early_kernel(w0, w1, za, zb, out):
+def products(core, part, spectra):
+    half = part.shape[1] // 2
+    near = pl.ds(pl.multiple_of(core * half, half), half)
+    far = pl.ds(pl.multiple_of((1 - core) * half, half), half)
+    left, right = part[:, :half], part[:, half:]
+    return [
+        jnp.dot(left, z[near, :], preferred_element_type=jnp.float32)
+        + jnp.dot(right, z[far, :], preferred_element_type=jnp.float32)
+        for z in spectra
+    ]
+
+
+def early_kernel(info, w0, w1, za, zb, out):
     for i, part in enumerate((w0, w1)):
-        w = part[...]
-        n = w.shape[0]
-        out[i * n : (i + 1) * n, :512] = jnp.dot(w, za[...], preferred_element_type=jnp.float32)
-        out[i * n : (i + 1) * n, 512:] = jnp.dot(w, zb[...], preferred_element_type=jnp.float32)
-
-
-def early_of(w0, w1, za, zb, interpret=False):
+        n = part.shape[0]
+        first, second = products(info[1], part, (za, zb))
+        out[i * n : (i + 1) * n, :512] = first
+        out[i * n : (i + 1) * n, 512:] = second
+
+
+def early_of(info, w0, w1, spectra, interpret=False):
     return pl.pallas_call(
         early_kernel,
         out_shape=jax.ShapeDtypeStruct((2 * w0.shape[0], 768), jnp.float32),
-        in_specs=[pl.BlockSpec(memory_space=pltpu.VMEM)] * 4,
+        in_specs=[pl.BlockSpec(memory_space=pltpu.SMEM)] + [pl.BlockSpec(memory_space=pltpu.VMEM)] * 4,
         out_specs=pl.BlockSpec(memory_space=pltpu.VMEM),
         compiler_params=pltpu.CompilerParams(vmem_limit_bytes=24 * MIB),
         cost_estimate=pl.CostEstimate(flops=17 * 10**8, bytes_accessed=8 * 10**6, transcendentals=0),
         interpret=interpret,
         name="early",
-    )(w0, w1, za, zb)
-
-
-def beams_kernel(places, early, w2, w3, za, zb, choose, out, sums):
+    )(info, w0, w1, *spectra)
+
+
+def beams_kernel(info, places, early, w2, w3, za, zb, choose, out, sums):
     for k in range(32):
         at = pl.multiple_of(places[k], 16)
         sums[pl.ds(at, 16), :] = early[k * 16 : (k + 1) * 16, :]
     for i, part in enumerate((w2, w3)):
-        w = part[...]
-        first = jnp.dot(w, za[...], preferred_element_type=jnp.float32)
-        second = jnp.dot(w, zb[...], preferred_element_type=jnp.float32)
+        first, second = products(info[1], part, (za, zb))
         for k in range(16):
             at = pl.multiple_of(places[(i + 2) * 16 + k], 16)
             sums[pl.ds(at, 16), :512] = first[k * 16 : (k + 1) * 16, :]
             sums[pl.ds(at, 16), 512:] = second[k * 16 : (k + 1) * 16, :]
     beams = sums.shape[0] // 2
-
-    def power(re_lanes, im_lanes):
+    powers = []
+    for g in range(3):
+        re_lanes, im_lanes = slice(g * 256, g * 256 + 128), slice(g * 256 + 128, g * 256 + 256)
         re = sums[:beams, re_lanes] - sums[beams:, im_lanes]
         im = sums[beams:, re_lanes] + sums[:beams, im_lanes]
-        return re * re + im * im
-
-    powers = jnp.concatenate(
-        [power(slice(0, 256), slice(256, 512)), power(slice(512, 640), slice(640, 768))], axis=1
-    )
+        powers.append(re * re + im * im)
     total = lax.dot_general(
         choose[...],
-        powers,
+        jnp.concatenate(powers, axis=1),
         (((1,), (1,)), ((), ())),
         preferred_element_type=jnp.float32,
         precision=lax.Precision.HIGHEST,
@@ -277,19 +374,19 @@
     out[...] = total * (1.0 / SPECTRA)
 
 
-def beams_of(places, early, w2, w3, za, zb, interpret=False):
+def beams_of(info, places, early, w2, w3, spectra, interpret=False):
     rows = early.shape[0] + 2 * w2.shape[0]
     return pl.pallas_call(
         beams_kernel,
         out_shape=jax.ShapeDtypeStruct((64, rows // 2), jnp.float32),
-        in_specs=[pl.BlockSpec(memory_space=pltpu.SMEM)] + [pl.BlockSpec(memory_space=pltpu.VMEM)] * 6,
+        in_specs=[pl.BlockSpec(memory_space=pltpu.SMEM)] * 2 + [pl.BlockSpec(memory_space=pltpu.VMEM)] * 6,
         out_specs=pl.BlockSpec(memory_space=pltpu.VMEM),
         scratch_shapes=[pltpu.VMEM((rows, 768), jnp.float32)],
         compiler_params=pltpu.CompilerParams(vmem_limit_bytes=32 * MIB),
         cost_estimate=pl.CostEstimate(flops=17 * 10**8, bytes_accessed=8 * 10**6, transcendentals=0),
         interpret=interpret,
         name="beams",
-    )(places, early, w2, w3, za, zb, jnp.asarray(choose_matrix()))
+    )(info, places, early, w2, w3, *spectra, jnp.asarray(choose_matrix()))
 
 
 def index_of(z, x, y, core):
@@ -336,36 +433,38 @@
 
 def on_device(voltage_real, voltage_imaginary, filter_taps, weights_re, weights_im, owners, antenna_map):
     grp, dev = lax.axis_index("grp"), lax.axis_index("dev")
-    y_lo, core = grp // 2, grp % 2
-
-    quarter = quarter_of(y_lo, core, weights_re[0], weights_im[0], antenna_map)
+    core = grp % 2
+    ordered = jnp.where(core == 0, owners, owners[::-1])
+    info = jnp.concatenate([jnp.stack([grp // 2, core]).astype(jnp.int32), ordered])
+
+    quarter = quarter_of(info, weights_re[0], weights_im[0], antenna_map)
     offers = lax.all_to_all(quarter.reshape(32, 16, -1), "dev", split_axis=0, concat_axis=0, tiled=True)
 
-    moved = []
-    for part in range(2):
-        rows = spectra_of(part, voltage_real, voltage_imaginary, filter_taps)
-        rows = lax.all_to_all(rows, ALL, split_axis=0, concat_axis=0, tiled=True)
-        moved.append(rows.reshape(DEVICES * SLOTS, -1))
-
-    mine = lax.dynamic_index_in_dim(offers, owners[core], 0, keepdims=False)
-    other = lax.dynamic_index_in_dim(offers, owners[1 - core], 0, keepdims=False)
+    volts = (voltage_real, voltage_imaginary, filter_taps)
+    quarter, *volts = lax.optimization_barrier((quarter, *volts))
+    messages = spectra_of(MESSAGES, *volts)
+    def turn(message):
+        moved = lax.all_to_all(message, ALL, split_axis=0, concat_axis=0, tiled=True)
+        return moved.reshape(DEVICES * SLOTS, -1)
+
+    message, offers = lax.optimization_barrier((messages[0], offers))
+    spectra = [turn(message)]
+    mine, other = pick_of(info, offers)
     other = lax.ppermute(other, "grp", SWAP)
-    block = jnp.where(
-        core == 0,
-        jnp.concatenate([mine, other], axis=1),
-        jnp.concatenate([other, mine], axis=1),
-    )
-    block = jnp.concatenate(gather_stage(block, 0), axis=0)
-    block = jnp.concatenate(gather_stage(block, 1), axis=0)
+    block = jnp.concatenate([mine, other], axis=1)
+    block = join_of(gather_stage(block, 0))
+    block, message, spectra[0] = lax.optimization_barrier((block, messages[1], spectra[0]))
+    spectra.append(turn(message))
+    block = join_of(gather_stage(block, 1))
     parts = gather_stage(block, 2)
 
-    early = early_of(parts[0], parts[3], *moved)
+    early = early_of(info, parts[0], parts[3], spectra)
     places = block_places(grp, dev)
     places = jnp.concatenate([places[:16], places[48:], places[16:48]])
-    power = beams_of(places, early, parts[1], parts[2], *moved)
+    power = beams_of(info, places, early, parts[1], parts[2], spectra)
     power = power.reshape(2, 32, -1)
-    own = lax.dynamic_index_in_dim(power, core, 0, keepdims=False)
-    given = lax.dynamic_index_in_dim(power, 1 - core, 0, keepdims=False)
+    own = jnp.where(core == 0, power[0], power[1])
+    given = jnp.where(core == 0, power[1], power[0])
     taken = lax.ppermute(given, "grp", SWAP)
     return jnp.where(core == 0, jnp.stack([own, taken]), jnp.stack([taken, own]))
 

time: 148 us -> 140 us (0.946)
  local copies, waits for them, and re-layouts: 18.5 us -> 1.69 us
  waiting for transfers between devices: 41.2 us -> 52.7 us
  between operations: 4.16 us -> 0.14 us
  Pallas kernels: 36.1 us -> 38.8 us
    ppermute x9, waiting for transfers between devices: 13.7 us -> 31.6 us  [gather_stage(): lax.ppermute(block, ALL, permutation(stage, shift))]
    unnamed x45 -> x13, local copies, waits for them, and re-layouts: 14.8 us -> 0.8 us
    all_to_all x2, starting transfers between devices: 14.8 us -> 19.3 us  [turn(): lax.all_to_all(message, ALL, split_axis=0, concat_axis=0, tiled=True)]
    all_to_all x1, waiting for transfers between devices: 3.91 us -> 0.01 us  [on_device(): lax.all_to_all(quarter.reshape(32, 16, -1), 'dev', split_axis=0, concat_a...]
    ppermute x9, starting transfers between devices: 13.9 us -> 10.1 us  [gather_stage(): lax.ppermute(block, ALL, permutation(stage, shift))]
    pallas_call x2 -> x4, Pallas kernels: 20.2 us -> 23.6 us  [the longest x1 20.3 us: spectra_of(): pl.pallas_call(functools.partial(spectra_kernel, messages), out_shape=[ja...]
    all_to_all x2, waiting for transfers between devices: 21.6 us -> 19.9 us  [turn(): lax.all_to_all(message, ALL, split_axis=0, concat_axis=0, tiled=True)]
  transfers between devices with their start and end apart: 14 -> 14, of which waited for: 6 -> 11; matrix products, arithmetic and copies ran while one was open for 6% -> 1% of each run, Pallas kernels for 16% -> 19%
where the time goes in v2:
time: 140 us; the launch traced here: 139 us
  waiting for transfers between devices  52.7 us (38%)
  starting transfers between devices  44.4 us (32%)
  Pallas kernels  38.8 us (28%)
  local copies, waits for them, and re-layouts  1.69 us (1%)
    ppermute x9, waiting for transfers between devices, gather_stage(): lax.ppermute(block, ALL, permutation(stage, shift))  31.6 us
    pallas_call x1, Pallas kernels, spectra_of(): pl.pallas_call(functools.partial(spectra_kernel, messages), out_shape=[ja...  20.3 us
    all_to_all x2, waiting for transfers between devices, turn(): lax.all_to_all(message, ALL, split_axis=0, concat_axis=0, tiled=True)  19.9 us
    all_to_all x2, starting transfers between devices, turn(): lax.all_to_all(message, ALL, split_axis=0, concat_axis=0, tiled=True)  19.3 us
    all_to_all x1, starting transfers between devices, on_device(): lax.all_to_all(quarter.reshape(32, 16, -1), 'dev', split_axis=0, concat_a...  11.3 us
    ppermute x9, starting transfers between devices, gather_stage(): lax.ppermute(block, ALL, permutation(stage, shift))  10.1 us
    pallas_call x1, Pallas kernels, quarter_of(): pl.pallas_call(quarter_kernel, grid_spec=grid_spec, out_shape=jax.ShapeDt...  7.53 us
    pallas_call x1, Pallas kernels, beams_of(): pl.pallas_call(beams_kernel, out_shape=jax.ShapeDtypeStruct((64, rows //...  4.37 us
  transfers between devices with their start and end apart: 14, of which 11 were waited for; matrix products, arithmetic and copies ran while one was open for 1% of the time, Pallas kernels for 19%

profile of v2, /device:TPU:1, one launch (start us, length us, event | category | flops | bytes accessed | tf_op | source)
XLA Modules:
  0.0 139.1 jit_solution(10635347944947970214)
XLA Ops:
  0.0 0.7 rev.3
  0.8 0.6 pad_add_fusion.where.info
  1.4 7.5 %quarter.1 = bf16[512,1024]{1,0:T(8,128)(2,1)} custom-call(s32[4]{0:T(128)} %pad_add_fusion.where.info, f32[2048,512]{1,0:T(8,128)} %bitcast.15, f32[2048,512]{1,0:T(8,128)} %bitcast.16, s32[2,1,1024]{2,1,0:T(1,128)} %bitcast.19), custom_call_target="tpu_custom_call" | custom-call | flops 2000000000 | bytes 6000000 | tf_op jit(solution)/shard_map/quarter/pallas_call | solution.py:252
  8.9 11.3 %all-to-all-start = ((bf16[32,16,1024]{2,1,0:T(8,128)(2,1)}), bf16[32,16,1024]{2,1,0:T(8,128)(2,1)S(1)}, u32[]{:S(2)}, u32[]{:S(2)}) async-start(bf16[32,16,1024]{2,1,0:T(8,128)(2,1)} %bitcast.17), calls=%async_computation | async-start | bytes 2097152 | tf_op jit(solution)/shard_map/all_to_all | solution.py:441
  20.2 20.3 %spectra.1 = (bf16[128,16,512]{2,1,0:T(8,128)(2,1)}, bf16[128,16,256]{2,1,0:T(8,128)(2,1)}) custom-call(bf16[16,110592]{1,0:T(8,128)(2,1)} %refs_0_, bf16[16,110592]{1,0:T(8,128)(2,1)} %refs_1_, f32[16,4096]{1,0:T(8,128)} %refs_2_, f32[32,128]{1,0:T(8,128)} %constant.123.clone.refs_3_, f32[32,128]{1,0:T(8,128)} %constant.124.clone.refs_4_, ...), custom_call_target="tpu_custom_call" | custom-call | flops 2400000000 | bytes 48000000 | tf_op jit(solution)/shard_map/spectra/pallas_call | solution.py:190
  40.5 0.0 all-to-all-done.first.second
  40.5 0.0 copy-start.2
  40.5 10.6 %all-to-all-start.1 = ((bf16[128,16,512]{2,1,0:T(8,128)(2,1)}), bf16[128,16,512]{2,1,0:T(8,128)(2,1)S(1)}, u32[]{:S(2)}, u32[]{:S(2)}) async-start(bf16[128,16,512]{2,1,0:T(8,128)(2,1)} %get-tuple-element.25), calls=%async_computation.1 | async-start | bytes 4194304 | tf_op jit(solution)/shard_map/all_to_all | solution.py:447
  51.1 0.0 copy-done.2
  51.1 0.0 copy-start.3
  51.1 0.0 copy-start.4
  51.2 0.0 copy-start.5
  51.2 0.0 copy-start.1
  51.2 2.2 %pick.1 = (bf16[16,1024]{1,0:T(8,128)(2,1)}, bf16[16,1024]{1,0:T(8,128)(2,1)}) custom-call(s32[4]{0:T(128)} %pad_add_fusion.where.info, bf16[32,16,1024]{2,1,0:T(8,128)(2,1)} %copy-done.2, bf16[32,16,1024]{2,1,0:T(8,128)(2,1)} %copy-done.2), custom_call_target="tpu_custom_call" | custom-call | tf_op jit(solution)/shard_map/pick/pallas_call | solution.py:270
  53.4 1.1 collective-permute-start
  54.5 0.8 constant_dynamic-update-slice_fusion.1
  55.2 0.3 collective-permute-done
  55.5 0.8 collective-permute-start.1
  56.3 1.9 %collective-permute-start.2 = (bf16[16,2048]{1,0:T(8,128)(2,1)S(1)}, bf16[16,2048]{1,0:T(8,128)(2,1)S(1)}, u32[]{:S(2)}, u32[]{:S(2)}) collective-permute-start(bf16[16,2048]{1,0:T(8,128)(2,1)S(1)} %constant_dynamic-update-slice_fusion.refs_0_), channel_id=1, source_target_pairs={{64,0},{40,32},{1,64},{104,96},{65,1},{41,33},{0,65},{105,97},{66,... | collective-permute-start | bytes 196616 | tf_op jit(solution)/shard_map/ppermute | solution.py:412
  58.2 1.4 collective-permute-start.3
  59.6 7.6 %collective-permute-done.1.refs_1_ = bf16[16,2048]{1,0:T(8,128)(2,1)S(1)} collective-permute-done((bf16[16,2048]{1,0:T(8,128)(2,1)S(1)}, bf16[16,2048]{1,0:T(8,128)(2,1)S(1)}, u32[]{:S(2)}, u32[]{:S(2)}) %collective-permute-start.1) | collective-permute-done | bytes 65568 | tf_op jit(solution)/shard_map/ppermute | solution.py:412
  67.1 9.6 %collective-permute-done.2.refs_2_ = bf16[16,2048]{1,0:T(8,128)(2,1)S(1)} collective-permute-done((bf16[16,2048]{1,0:T(8,128)(2,1)S(1)}, bf16[16,2048]{1,0:T(8,128)(2,1)S(1)}, u32[]{:S(2)}, u32[]{:S(2)}) %collective-permute-start.2) | collective-permute-done | bytes 65568 | tf_op jit(solution)/shard_map/ppermute | solution.py:412
  76.8 1.7 %collective-permute-done.3.refs_3_ = bf16[16,2048]{1,0:T(8,128)(2,1)S(1)} collective-permute-done((bf16[16,2048]{1,0:T(8,128)(2,1)S(1)}, bf16[16,2048]{1,0:T(8,128)(2,1)S(1)}, u32[]{:S(2)}, u32[]{:S(2)}) %collective-permute-start.3) | collective-permute-done | bytes 65568 | tf_op jit(solution)/shard_map/ppermute | solution.py:412
  78.5 3.1 %all-to-all-done.1 = bf16[128,16,512]{2,1,0:T(8,128)(2,1)S(1)} async-done(((bf16[128,16,512]{2,1,0:T(8,128)(2,1)}), bf16[128,16,512]{2,1,0:T(8,128)(2,1)S(1)}, u32[]{:S(2)}, u32[]{:S(2)}) %all-to-all-start.1) | async-done | bytes 2097184 | tf_op jit(solution)/shard_map/all_to_all | solution.py:447
  81.5 0.2 collective-permute-start.4
  81.7 2.5 %collective-permute-start.5 = (bf16[64,2048]{1,0:T(8,128)(2,1)S(1)}, bf16[64,2048]{1,0:T(8,128)(2,1)S(1)}, u32[]{:S(2)}, u32[]{:S(2)}) collective-permute-start(bf16[64,2048]{1,0:T(8,128)(2,1)S(1)} %join.2.refs_0_), channel_id=1, source_target_pairs={{2,0},{96,32},{66,64},{33,96},{3,1},{97,33},{67,65},{32,97},{4,2},... | collective-permute-start | bytes 786440 | tf_op jit(solution)/shard_map/ppermute | solution.py:412
  84.2 0.0 collective-permute-start.6
  84.2 4.0 %collective-permute-done.4.refs_1_ = bf16[64,2048]{1,0:T(8,128)(2,1)S(1)} collective-permute-done((bf16[64,2048]{1,0:T(8,128)(2,1)S(1)}, bf16[64,2048]{1,0:T(8,128)(2,1)S(1)}, u32[]{:S(2)}, u32[]{:S(2)}) %collective-permute-start.4) | collective-permute-done | bytes 262176 | tf_op jit(solution)/shard_map/ppermute | solution.py:412
  88.3 2.1 %collective-permute-done.5.refs_2_ = bf16[64,2048]{1,0:T(8,128)(2,1)S(1)} collective-permute-done((bf16[64,2048]{1,0:T(8,128)(2,1)S(1)}, bf16[64,2048]{1,0:T(8,128)(2,1)S(1)}, u32[]{:S(2)}, u32[]{:S(2)}) %collective-permute-start.5) | collective-permute-done | bytes 262176 | tf_op jit(solution)/shard_map/ppermute | solution.py:412
  90.3 0.9 collective-permute-done.6.refs_3_
  91.2 1.1 join.3.w0
  92.3 0.6 collective-permute-start.7
  92.9 8.7 %all-to-all-start.2 = ((bf16[128,16,256]{2,1,0:T(8,128)(2,1)}), bf16[128,16,256]{2,1,0:T(8,128)(2,1)S(1)}, u32[]{:S(2)}, u32[]{:S(2)}) async-start(bf16[128,16,256]{2,1,0:T(8,128)(2,1)} %get-tuple-element.28), calls=%async_computation.2 | async-start | bytes 2097152 | tf_op jit(solution)/shard_map/all_to_all | solution.py:447
  101.6 0.0 copy-start
  101.6 1.5 %collective-permute-start.8 = (bf16[256,2048]{1,0:T(8,128)(2,1)}, bf16[256,2048]{1,0:T(8,128)(2,1)}, u32[]{:S(2)}, u32[]{:S(2)}) collective-permute-start(bf16[256,2048]{1,0:T(8,128)(2,1)} %join.3.w0), channel_id=1, source_target_pairs={{24,0},{38,32},{88,64},{102,96},{25,1},{39,33},{89,65},{103,97},{2... | collective-permute-start | bytes 3145736 | tf_op jit(solution)/shard_map/ppermute | solution.py:412
  103.1 1.3 collective-permute-start.9
  104.4 0.0 copy-done.3
  104.4 0.0 copy-done.4
  104.4 0.0 copy-done.5
  104.4 0.1 slice.21
  104.5 0.1 fusion.16
  104.5 0.1 pad_add_fusion.1.places
  104.6 16.9 %all-to-all-done.2 = bf16[128,16,256]{2,1,0:T(8,128)(2,1)S(1)} async-done(((bf16[128,16,256]{2,1,0:T(8,128)(2,1)}), bf16[128,16,256]{2,1,0:T(8,128)(2,1)S(1)}, u32[]{:S(2)}, u32[]{:S(2)}) %all-to-all-start.2) | async-done | bytes 1048608 | tf_op jit(solution)/shard_map/all_to_all | solution.py:447
  121.5 0.0 collective-permute-done.7.w1
  121.5 0.0 copy-done.1
  121.5 3.3 %early.1 = f32[512,768]{1,0:T(8,128)S(1)} custom-call(s32[4]{0:T(128)S(1)} %copy-done.1, bf16[256,2048]{1,0:T(8,128)(2,1)} %join.3.w0, bf16[256,2048]{1,0:T(8,128)(2,1)} %collective-permute-done.7.w1, bf16[2048,512]{1,0:T(8,128)(2,1)S(1)} %bitcast.11, bf16[2048,256]{1,0:T(8,128)(2,1)S(1)} %bitcast.13), custom_call_target="tpu_custom_call" | custom-call | flops 1700000000 | bytes 8000000 | tf_op jit(solution)/shard_map/early/pallas_call | solution.py:338
  124.9 5.7 %collective-permute-done.8.w2 = bf16[256,2048]{1,0:T(8,128)(2,1)} collective-permute-done((bf16[256,2048]{1,0:T(8,128)(2,1)}, bf16[256,2048]{1,0:T(8,128)(2,1)}, u32[]{:S(2)}, u32[]{:S(2)}) %collective-permute-start.8) | collective-permute-done | bytes 1048608 | tf_op jit(solution)/shard_map/ppermute | solution.py:412
  130.6 0.0 collective-permute-done.9.w3
  130.6 0.0 copy-done
  130.6 4.4 %beams.1 = f32[64,512]{1,0:T(8,128)S(1)} custom-call(s32[4]{0:T(128)S(1)} %copy-done.1, s32[64]{0:T(128)S(1)} %pad_add_fusion.1.places, f32[512,768]{1,0:T(8,128)S(1)} %early.1, bf16[256,2048]{1,0:T(8,128)(2,1)} %collective-permute-done.8.w2, bf16[256,2048]{1,0:T(8,128)(2,1)} %collective-permute-done.9.w3, bf16[2048,512]{1,0:T(8,128)(2,1)S(1)} %bitcast.12, ...), custom_call_target="tpu_custom_call" | custom-call | flops 1700000000 | bytes 8000000 | tf_op jit(solution)/shard_map/beams/pallas_call | solution.py:379
  134.9 2.6 %collective-permute-start.10 = (f32[32,512]{1,0:T(8,128)S(1)}, f32[32,512]{1,0:T(8,128)S(1)}, u32[]{:S(2)}, u32[]{:S(2)}) collective-permute-start(f32[32,512]{1,0:T(8,128)S(1)} %get-tuple-element.30), channel_id=1, source_target_pairs={{0,32},{32,0},{64,96},{96,64},{1,33},{33,1},{65,97},{97,65},{2,34}... | collective-permute-start | bytes 196616 | tf_op jit(solution)/shard_map/ppermute | solution.py:468
  137.6 0.9 collective-permute-done.10
  138.5 0.7 maximum_select_fusion
  (5 shorter events, 0.1 us)
Async XLA Ops:
  8.9 31.6 %all-to-all-start = ((bf16[32,16,1024]{2,1,0:T(8,128)(2,1)}), bf16[32,16,1024]{2,1,0:T(8,128)(2,1)S(1)}, u32[]{:S(2)}, u32[]{:S(2)}) async-start(bf16[32,16,1024]{2,1,0:T(8,128)(2,1)} %bitcast.17), calls=%async_computation | async-start | bytes 2097152 | tf_op jit(solution)/shard_map/all_to_all | solution.py:441
  40.5 10.6 %copy-start.2 = (bf16[32,16,1024]{2,1,0:T(8,128)(2,1)}, bf16[32,16,1024]{2,1,0:T(8,128)(2,1)S(1)}, u32[]{:S(2)}) copy-start(bf16[32,16,1024]{2,1,0:T(8,128)(2,1)S(1)} %all-to-all-done.first.second) | copy-start | bytes 3145732
  40.5 41.0 %all-to-all-start.1 = ((bf16[128,16,512]{2,1,0:T(8,128)(2,1)}), bf16[128,16,512]{2,1,0:T(8,128)(2,1)S(1)}, u32[]{:S(2)}, u32[]{:S(2)}) async-start(bf16[128,16,512]{2,1,0:T(8,128)(2,1)} %get-tuple-element.25), calls=%async_computation.1 | async-start | bytes 4194304 | tf_op jit(solution)/shard_map/all_to_all | solution.py:447
  51.1 53.2 %copy-start.3 = (s32[64]{0:T(128)S(1)}, s32[64]{0:T(128)}, u32[]{:S(2)}) copy-start(s32[64]{0:T(128)} %constant.128.clone) | copy-start | bytes 772
  51.1 53.2 %copy-start.4 = (s32[64]{0:T(128)S(1)}, s32[64]{0:T(128)}, u32[]{:S(2)}) copy-start(s32[64]{0:T(128)} %constant.126.clone) | copy-start | bytes 772
  51.2 53.2 %copy-start.5 = (s32[64]{0:T(128)S(1)}, s32[64]{0:T(128)}, u32[]{:S(2)}) copy-start(s32[64]{0:T(128)} %constant.127.clone) | copy-start | bytes 772
  51.2 70.3 %copy-start.1 = (s32[4]{0:T(128)S(1)}, s32[4]{0:T(128)}, u32[]{:S(2)}) copy-start(s32[4]{0:T(128)} %pad_add_fusion.where.info) | copy-start | bytes 52
  53.4 2.1 %collective-permute-start = (bf16[16,1024]{1,0:T(8,128)(2,1)}, bf16[16,1024]{1,0:T(8,128)(2,1)S(1)}, u32[]{:S(2)}, u32[]{:S(2)}) collective-permute-start(bf16[16,1024]{1,0:T(8,128)(2,1)} %get-tuple-element.23), channel_id=1, source_target_pairs={{0,32},{32,0},{64,96},{96,64},{1,33},{33,1},{65,97},{97,65},{2,34}... | collective-permute-start | bytes 98312 | tf_op jit(solution)/shard_map/ppermute | solution.py:453
  55.5 11.6 %collective-permute-start.1 = (bf16[16,2048]{1,0:T(8,128)(2,1)S(1)}, bf16[16,2048]{1,0:T(8,128)(2,1)S(1)}, u32[]{:S(2)}, u32[]{:S(2)}) collective-permute-start(bf16[16,2048]{1,0:T(8,128)(2,1)S(1)} %constant_dynamic-update-slice_fusion.refs_0_), channel_id=1, source_target_pairs={{65,0},{56,32},{0,64},{120,96},{64,1},{57,33},{1,65},{121,97},{67,... | collective-permute-start | bytes 196616 | tf_op jit(solution)/shard_map/ppermute | solution.py:412
  56.3 20.4 %collective-permute-start.2 = (bf16[16,2048]{1,0:T(8,128)(2,1)S(1)}, bf16[16,2048]{1,0:T(8,128)(2,1)S(1)}, u32[]{:S(2)}, u32[]{:S(2)}) collective-permute-start(bf16[16,2048]{1,0:T(8,128)(2,1)S(1)} %constant_dynamic-update-slice_fusion.refs_0_), channel_id=1, source_target_pairs={{64,0},{40,32},{1,64},{104,96},{65,1},{41,33},{0,65},{105,97},{66,... | collective-permute-start | bytes 196616 | tf_op jit(solution)/shard_map/ppermute | solution.py:412
  58.2 20.2 %collective-permute-start.3 = (bf16[16,2048]{1,0:T(8,128)(2,1)S(1)}, bf16[16,2048]{1,0:T(8,128)(2,1)S(1)}, u32[]{:S(2)}, u32[]{:S(2)}) collective-permute-start(bf16[16,2048]{1,0:T(8,128)(2,1)S(1)} %constant_dynamic-update-slice_fusion.refs_0_), channel_id=1, source_target_pairs={{1,0},{48,32},{65,64},{112,96},{0,1},{49,33},{64,65},{113,97},{3,2... | collective-permute-start | bytes 196616 | tf_op jit(solution)/shard_map/ppermute | solution.py:412
  81.5 6.7 %collective-permute-start.4 = (bf16[64,2048]{1,0:T(8,128)(2,1)S(1)}, bf16[64,2048]{1,0:T(8,128)(2,1)S(1)}, u32[]{:S(2)}, u32[]{:S(2)}) collective-permute-start(bf16[64,2048]{1,0:T(8,128)(2,1)S(1)} %join.2.refs_0_), channel_id=1, source_target_pairs={{6,0},{97,32},{70,64},{32,96},{7,1},{96,33},{71,65},{33,97},{0,2},... | collective-permute-start | bytes 786440 | tf_op jit(solution)/shard_map/ppermute | solution.py:412
  81.7 8.6 %collective-permute-start.5 = (bf16[64,2048]{1,0:T(8,128)(2,1)S(1)}, bf16[64,2048]{1,0:T(8,128)(2,1)S(1)}, u32[]{:S(2)}, u32[]{:S(2)}) collective-permute-start(bf16[64,2048]{1,0:T(8,128)(2,1)S(1)} %join.2.refs_0_), channel_id=1, source_target_pairs={{2,0},{96,32},{66,64},{33,96},{3,1},{97,33},{67,65},{32,97},{4,2},... | collective-permute-start | bytes 786440 | tf_op jit(solution)/shard_map/ppermute | solution.py:412
  84.2 7.0 %collective-permute-start.6 = (bf16[64,2048]{1,0:T(8,128)(2,1)S(1)}, bf16[64,2048]{1,0:T(8,128)(2,1)S(1)}, u32[]{:S(2)}, u32[]{:S(2)}) collective-permute-start(bf16[64,2048]{1,0:T(8,128)(2,1)S(1)} %join.2.refs_0_), channel_id=1, source_target_pairs={{4,0},{33,32},{68,64},{97,96},{5,1},{32,33},{69,65},{96,97},{6,2},... | collective-permute-start | bytes 786440 | tf_op jit(solution)/shard_map/ppermute | solution.py:412
  92.3 29.2 %collective-permute-start.7 = (bf16[256,2048]{1,0:T(8,128)(2,1)}, bf16[256,2048]{1,0:T(8,128)(2,1)}, u32[]{:S(2)}, u32[]{:S(2)}) collective-permute-start(bf16[256,2048]{1,0:T(8,128)(2,1)} %join.3.w0), channel_id=1, source_target_pairs={{16,0},{36,32},{80,64},{100,96},{17,1},{37,33},{81,65},{101,97},{1... | collective-permute-start | bytes 3145736 | tf_op jit(solution)/shard_map/ppermute | solution.py:412
  92.9 28.6 %all-to-all-start.2 = ((bf16[128,16,256]{2,1,0:T(8,128)(2,1)}), bf16[128,16,256]{2,1,0:T(8,128)(2,1)S(1)}, u32[]{:S(2)}, u32[]{:S(2)}) async-start(bf16[128,16,256]{2,1,0:T(8,128)(2,1)} %get-tuple-element.28), calls=%async_computation.2 | async-start | bytes 2097152 | tf_op jit(solution)/shard_map/all_to_all | solution.py:447
  101.6 29.0 %copy-start = (f32[64,384]{1,0:T(8,128)S(1)}, f32[64,384]{1,0:T(8,128)}, u32[]{:S(2)}) copy-start(f32[64,384]{1,0:T(8,128)} %constant.129.clone.choose) | copy-start | bytes 294916
  101.6 28.9 %collective-permute-start.8 = (bf16[256,2048]{1,0:T(8,128)(2,1)}, bf16[256,2048]{1,0:T(8,128)(2,1)}, u32[]{:S(2)}, u32[]{:S(2)}) collective-permute-start(bf16[256,2048]{1,0:T(8,128)(2,1)} %join.3.w0), channel_id=1, source_target_pairs={{24,0},{38,32},{88,64},{102,96},{25,1},{39,33},{89,65},{103,97},{2... | collective-permute-start | bytes 3145736 | tf_op jit(solution)/shard_map/ppermute | solution.py:412
  103.1 27.5 %collective-permute-start.9 = (bf16[256,2048]{1,0:T(8,128)(2,1)}, bf16[256,2048]{1,0:T(8,128)(2,1)}, u32[]{:S(2)}, u32[]{:S(2)}) collective-permute-start(bf16[256,2048]{1,0:T(8,128)(2,1)} %join.3.w0), channel_id=1, source_target_pairs={{8,0},{34,32},{72,64},{98,96},{9,1},{35,33},{73,65},{99,97},{10,2}... | collective-permute-start | bytes 3145736 | tf_op jit(solution)/shard_map/ppermute | solution.py:412
  134.9 3.5 %collective-permute-start.10 = (f32[32,512]{1,0:T(8,128)S(1)}, f32[32,512]{1,0:T(8,128)S(1)}, u32[]{:S(2)}, u32[]{:S(2)}) collective-permute-start(f32[32,512]{1,0:T(8,128)S(1)} %get-tuple-element.30), channel_id=1, source_target_pairs={{0,32},{32,0},{64,96},{96,64},{1,33},{33,1},{65,97},{97,65},{2,34}... | collective-permute-start | bytes 196616 | tf_op jit(solution)/shard_map/ppermute | solution.py:468

commit v3 on v2

--- a/solution.py
+++ b/solution.py
@@ -21,7 +21,7 @@
 DEVICES = 128
 ROW_STRIDE = 24
 GROUPS = ((0, 1, 6, 7), (2, 3, 8, 9), (4, 5, 10, 11))
-MESSAGES = ((0, 1), (2,))
+MESSAGES = ((2,), (0, 1))
 ALL = ("grp", "dev")
 MIB = 1 << 20
 
@@ -153,7 +153,7 @@
                     packed[g * 2 + c, to[1], :] = jnp.where(lane < 64, pltpu.roll(mixed[0], 64, 1), mixed[1])
         return 0
 
-    lax.fori_loop(0, SLOTS, inner, 0)
+    lax.fori_loop(0, SLOTS, inner, 0, unroll=4)
 
     stores = []
     tile = 0
@@ -214,90 +214,108 @@
     )(vre, vim, taps, jnp.asarray(cos_t), jnp.asarray(sin_t), jnp.asarray(mat))
 
 
-def quarter_kernel(where, wre, wim, slots, out, total):
-    step = pl.program_id(0)
-    rows = jnp.where(where[0] == 0, wre[...], wim[...]).astype(jnp.bfloat16)
-    antenna = lax.broadcasted_iota(jnp.int32, (rows.shape[0], slots.shape[2]), 0) + step * rows.shape[0]
-    chosen = jnp.where(antenna == slots[0], 1.0, 0.0).astype(jnp.bfloat16)
-    part = lax.dot_general(rows, chosen, (((0,), (0,)), ((), ())), preferred_element_type=jnp.float32)
-
-    @pl.when(step == 0)
-    def _():
-        total[...] = part
-
-    @pl.when(step > 0)
-    def _():
-        total[...] = total[...] + part
-
-    @pl.when(step == pl.num_programs(0) - 1)
-    def _():
-        out[...] = total[...].astype(jnp.bfloat16)
-
-
-def quarter_of(info, wre, wim, antenna_map, interpret=False):
+def quarter_kernel(wre, wim, slots, out, buf, names, chosen, sems):
+    grp = lax.axis_index("grp")
+    y_lo, core = grp // 2, grp % 2
     antennas, beams = wre.shape
-    depth = 512
     half = antennas // 2
-    grid_spec = pltpu.PrefetchScalarGridSpec(
-        num_scalar_prefetch=1,
-        grid=(antennas // depth,),
-        in_specs=[
-            pl.BlockSpec((depth, beams), lambda i, w: (jnp.where(w[0] == 0, i, 0), 0)),
-            pl.BlockSpec((depth, beams), lambda i, w: (jnp.where(w[0] == 0, 0, i), 0)),
-            pl.BlockSpec((1, 1, half), lambda i, w: (w[1], 0, 0)),
-        ],
-        out_specs=pl.BlockSpec((beams, half), lambda i, w: (0, 0)),
-        scratch_shapes=[pltpu.VMEM((beams, half), jnp.float32)],
-    )
+    name_copy = pltpu.make_async_copy(slots.at[core], names, sems.at[4])
+    name_copy.start()
+    for y, source in ((0, wre), (1, wim)):
+
+        @pl.when(y_lo == y)
+        def _():
+            for i in range(4):
+                part = pl.ds(i * half // 2, half // 2)
+                pltpu.make_async_copy(source.at[part], buf.at[part], sems.at[i]).start()
+    name_copy.wait()
+    row = names[...]
+
+    def build(i, _):
+        antenna = lax.broadcasted_iota(jnp.int32, (16, half), 0) + i * 16
+        chosen[pl.ds(pl.multiple_of(i * 16, 16), 16), :] = jnp.where(antenna == row, 1.0, 0.0).astype(jnp.bfloat16)
+        return 0
+    lax.fori_loop(0, antennas // 16, build, 0, unroll=4)
+    for y, source in ((0, wre), (1, wim)):
+
+        @pl.when(y_lo == y)
+        def _():
+            for i in range(4):
+                part = pl.ds(i * half // 2, half // 2)
+                pltpu.make_async_copy(source.at[part], buf.at[part], sems.at[i]).wait()
+    for j in range(0, beams, 256):
+        w = buf[:, j : j + 256].astype(jnp.bfloat16)
+        for k in range(0, half, 512):
+            out[j : j + 256, k : k + 512] = lax.dot_general(
+                w, chosen[:, k : k + 512], (((0,), (0,)), ((), ())), preferred_element_type=jnp.float32
+            ).astype(jnp.bfloat16)
+
+
+def quarter_of(wre, wim, antenna_map, interpret=False):
+    antennas, beams = wre.shape
+    half = antennas // 2
     return pl.pallas_call(
         quarter_kernel,
-        grid_spec=grid_spec,
+        in_specs=[pl.BlockSpec(memory_space=pltpu.HBM)] * 3,
+        out_specs=pl.BlockSpec(memory_space=pltpu.VMEM),
         out_shape=jax.ShapeDtypeStruct((beams, half), jnp.bfloat16),
+        scratch_shapes=[
+            pltpu.VMEM((antennas, beams), jnp.float32),
+            pltpu.VMEM((1, half), jnp.int32),
+            pltpu.VMEM((antennas, half), jnp.bfloat16),
+            pltpu.SemaphoreType.DMA((5,)),
+        ],
         compiler_params=pltpu.CompilerParams(vmem_limit_bytes=58 * MIB),
         cost_estimate=pl.CostEstimate(flops=2 * 10**9, bytes_accessed=6 * 10**6, transcendentals=0),
         interpret=interpret,
         name="quarter",
-    )(info, wre, wim, antenna_map.reshape(2, 1, half))
-
-
-def pick_kernel(info, first, second, mine, other):
-    mine[...] = first[0]
-    other[...] = second[0]
-
-
-def pick_of(info, offers, interpret=False):
+    )(wre, wim, antenna_map.reshape(2, 1, half))
+
+
+def pick_kernel(owners, offers, mine, other, sems):
+    core = lax.axis_index("grp") % 2
+    copies = [
+        pltpu.make_async_copy(offers.at[owners[core]], mine, sems.at[0]),
+        pltpu.make_async_copy(offers.at[owners[1 - core]], other, sems.at[1]),
+    ]
+    for copy in copies:
+        copy.start()
+    for copy in copies:
+        copy.wait()
+
+
+def pick_of(owners, offers, interpret=False):
     _, rows, columns = offers.shape
     return pl.pallas_call(
         pick_kernel,
-        grid_spec=pltpu.PrefetchScalarGridSpec(
-            num_scalar_prefetch=1,
-            grid=(1,),
-            in_specs=[
-                pl.BlockSpec((1, rows, columns), lambda i, w: (w[2], 0, 0)),
-                pl.BlockSpec((1, rows, columns), lambda i, w: (w[3], 0, 0)),
-            ],
-            out_specs=[pl.BlockSpec((rows, columns), lambda i, w: (0, 0))] * 2,
-        ),
+        in_specs=[pl.BlockSpec(memory_space=pltpu.SMEM), pl.BlockSpec(memory_space=pltpu.HBM)],
+        out_specs=[pl.BlockSpec(memory_space=pltpu.VMEM)] * 2,
         out_shape=[jax.ShapeDtypeStruct((rows, columns), offers.dtype)] * 2,
+        scratch_shapes=[pltpu.SemaphoreType.DMA((2,))],
+        compiler_params=pltpu.CompilerParams(vmem_limit_bytes=58 * MIB),
         interpret=interpret,
         name="pick",
-    )(info, offers, offers)
-
-
-def join_kernel(*refs):
+    )(owners, offers)
+
+
+def join_kernel(axis, *refs):
     parts, out = refs[:-1], refs[-1]
     at = 0
     for part in parts:
-        rows = part.shape[0]
-        out[at : at + rows, :] = part[...]
-        at += rows
-
-
-def join_of(parts, interpret=False):
-    rows = sum(p.shape[0] for p in parts)
+        size = part.shape[axis]
+        if axis == 0:
+            out[at : at + size, :] = part[...]
+        else:
+            out[:, at : at + size] = part[...]
+        at += size
+
+
+def join_of(parts, axis, interpret=False):
+    shape = list(parts[0].shape)
+    shape[axis] = sum(p.shape[axis] for p in parts)
     return pl.pallas_call(
-        join_kernel,
-        out_shape=jax.ShapeDtypeStruct((rows, parts[0].shape[1]), parts[0].dtype),
+        functools.partial(join_kernel, axis),
+        out_shape=jax.ShapeDtypeStruct(tuple(shape), parts[0].dtype),
         in_specs=[pl.BlockSpec(memory_space=pltpu.VMEM)] * len(parts),
         out_specs=pl.BlockSpec(memory_space=pltpu.VMEM),
         compiler_params=pltpu.CompilerParams(vmem_limit_bytes=8 * MIB),
@@ -326,37 +344,41 @@
     ]
 
 
-def early_kernel(info, w0, w1, za, zb, out):
+def early_kernel(w0, w1, za, zb, out):
+    core = lax.axis_index("grp") % 2
+    wide = za.shape[1]
     for i, part in enumerate((w0, w1)):
         n = part.shape[0]
-        first, second = products(info[1], part, (za, zb))
-        out[i * n : (i + 1) * n, :512] = first
-        out[i * n : (i + 1) * n, 512:] = second
-
-
-def early_of(info, w0, w1, spectra, interpret=False):
+        first, second = products(core, part, (za, zb))
+        out[i * n : (i + 1) * n, :wide] = first
+        out[i * n : (i + 1) * n, wide:] = second
+
+
+def early_of(w0, w1, spectra, interpret=False):
     return pl.pallas_call(
         early_kernel,
         out_shape=jax.ShapeDtypeStruct((2 * w0.shape[0], 768), jnp.float32),
-        in_specs=[pl.BlockSpec(memory_space=pltpu.SMEM)] + [pl.BlockSpec(memory_space=pltpu.VMEM)] * 4,
+        in_specs=[pl.BlockSpec(memory_space=pltpu.VMEM)] * 4,
         out_specs=pl.BlockSpec(memory_space=pltpu.VMEM),
         compiler_params=pltpu.CompilerParams(vmem_limit_bytes=24 * MIB),
         cost_estimate=pl.CostEstimate(flops=17 * 10**8, bytes_accessed=8 * 10**6, transcendentals=0),
         interpret=interpret,
         name="early",
-    )(info, w0, w1, *spectra)
-
-
-def beams_kernel(info, places, early, w2, w3, za, zb, choose, out, sums):
+    )(w0, w1, *spectra)
+
+
+def beams_kernel(places, early, w2, w3, za, zb, choose, out, sums):
     for k in range(32):
         at = pl.multiple_of(places[k], 16)
         sums[pl.ds(at, 16), :] = early[k * 16 : (k + 1) * 16, :]
+    core = lax.axis_index("grp") % 2
+    wide = za.shape[1]
     for i, part in enumerate((w2, w3)):
-        first, second = products(info[1], part, (za, zb))
+        first, second = products(core, part, (za, zb))
         for k in range(16):
             at = pl.multiple_of(places[(i + 2) * 16 + k], 16)
-            sums[pl.ds(at, 16), :512] = first[k * 16 : (k + 1) * 16, :]
-            sums[pl.ds(at, 16), 512:] = second[k * 16 : (k + 1) * 16, :]
+            sums[pl.ds(at, 16), :wide] = first[k * 16 : (k + 1) * 16, :]
+            sums[pl.ds(at, 16), wide:] = second[k * 16 : (k + 1) * 16, :]
     beams = sums.shape[0] // 2
     powers = []
     for g in range(3):
@@ -374,19 +396,19 @@
     out[...] = total * (1.0 / SPECTRA)
 
 
-def beams_of(info, places, early, w2, w3, spectra, interpret=False):
+def beams_of(places, early, w2, w3, spectra, interpret=False):
     rows = early.shape[0] + 2 * w2.shape[0]
     return pl.pallas_call(
         beams_kernel,
         out_shape=jax.ShapeDtypeStruct((64, rows // 2), jnp.float32),
-        in_specs=[pl.BlockSpec(memory_space=pltpu.SMEM)] * 2 + [pl.BlockSpec(memory_space=pltpu.VMEM)] * 6,
+        in_specs=[pl.BlockSpec(memory_space=pltpu.SMEM)] + [pl.BlockSpec(memory_space=pltpu.VMEM)] * 6,
         out_specs=pl.BlockSpec(memory_space=pltpu.VMEM),
         scratch_shapes=[pltpu.VMEM((rows, 768), jnp.float32)],
         compiler_params=pltpu.CompilerParams(vmem_limit_bytes=32 * MIB),
         cost_estimate=pl.CostEstimate(flops=17 * 10**8, bytes_accessed=8 * 10**6, transcendentals=0),
         interpret=interpret,
         name="beams",
-    )(info, places, early, w2, w3, *spectra, jnp.asarray(choose_matrix()))
+    )(places, early, w2, w3, *spectra, jnp.asarray(choose_matrix()))
 
 
 def index_of(z, x, y, core):
@@ -434,34 +456,33 @@
 def on_device(voltage_real, voltage_imaginary, filter_taps, weights_re, weights_im, owners, antenna_map):
     grp, dev = lax.axis_index("grp"), lax.axis_index("dev")
     core = grp % 2
-    ordered = jnp.where(core == 0, owners, owners[::-1])
-    info = jnp.concatenate([jnp.stack([grp // 2, core]).astype(jnp.int32), ordered])
-
-    quarter = quarter_of(info, weights_re[0], weights_im[0], antenna_map)
+
+    quarter = quarter_of(weights_re[0], weights_im[0], antenna_map)
     offers = lax.all_to_all(quarter.reshape(32, 16, -1), "dev", split_axis=0, concat_axis=0, tiled=True)
 
     volts = (voltage_real, voltage_imaginary, filter_taps)
     quarter, *volts = lax.optimization_barrier((quarter, *volts))
     messages = spectra_of(MESSAGES, *volts)
+
     def turn(message):
         moved = lax.all_to_all(message, ALL, split_axis=0, concat_axis=0, tiled=True)
         return moved.reshape(DEVICES * SLOTS, -1)
 
     message, offers = lax.optimization_barrier((messages[0], offers))
     spectra = [turn(message)]
-    mine, other = pick_of(info, offers)
+    mine, other = pick_of(owners, offers)
     other = lax.ppermute(other, "grp", SWAP)
-    block = jnp.concatenate([mine, other], axis=1)
-    block = join_of(gather_stage(block, 0))
+    block = join_of([mine, other], 1)
+    block = join_of(gather_stage(block, 0), 0)
     block, message, spectra[0] = lax.optimization_barrier((block, messages[1], spectra[0]))
     spectra.append(turn(message))
-    block = join_of(gather_stage(block, 1))
+    block = join_of(gather_stage(block, 1), 0)
     parts = gather_stage(block, 2)
 
-    early = early_of(info, parts[0], parts[3], spectra)
+    early = early_of(parts[0], parts[3], spectra)
     places = block_places(grp, dev)
     places = jnp.concatenate([places[:16], places[48:], places[16:48]])
-    power = beams_of(info, places, early, parts[1], parts[2], spectra)
+    power = beams_of(places, early, parts[1], parts[2], spectra)
     power = power.reshape(2, 32, -1)
     own = jnp.where(core == 0, power[0], power[1])
     given = jnp.where(core == 0, power[1], power[0])

time: 140 us -> 137 us (0.979)
  waiting for transfers between devices: 52.7 us -> 58.1 us
  Pallas kernels: 38.8 us -> 34 us
  starting transfers between devices: 44.4 us -> 42.1 us
    ppermute x9, waiting for transfers between devices: 31.6 us -> 53.3 us  [gather_stage(): lax.ppermute(block, ALL, permutation(stage, shift))]
    all_to_all x2, waiting for transfers between devices: 19.9 us -> 2.34 us  [turn(): lax.all_to_all(message, ALL, split_axis=0, concat_axis=0, tiled=True)]
    all_to_all x2, starting transfers between devices: 19.3 us -> 13.9 us  [turn(): lax.all_to_all(message, ALL, split_axis=0, concat_axis=0, tiled=True)]
    ppermute x9, starting transfers between devices: 10.1 us -> 13.6 us  [gather_stage(): lax.ppermute(block, ALL, permutation(stage, shift))]
    pallas_call x1, Pallas kernels: 20.3 us -> 17.6 us  [spectra_of(): pl.pallas_call(functools.partial(spectra_kernel, messages), out_shape=[ja...]
    pallas_call x4 -> x5, Pallas kernels: 10.8 us -> 8.73 us  [the longest x1 5.56 us: quarter_of(): pl.pallas_call(quarter_kernel, in_specs=[pl.BlockSpec(memory_space=pltpu....]
  transfers between devices with their start and end apart: 14 -> 14, of which waited for: 11 -> 10; matrix products, arithmetic and copies ran while one was open for 1% -> 0% of each run, Pallas kernels for 19% -> 18%
where the time goes in v3:
time: 137 us; the launch traced here: 136 us
  waiting for transfers between devices  58.1 us (42%)
  starting transfers between devices  42.1 us (31%)
  Pallas kernels  34 us (25%)
    ppermute x9, waiting for transfers between devices, gather_stage(): lax.ppermute(block, ALL, permutation(stage, shift))  53.3 us
    pallas_call x1, Pallas kernels, spectra_of(): pl.pallas_call(functools.partial(spectra_kernel, messages), out_shape=[ja...  17.6 us
    all_to_all x2, starting transfers between devices, turn(): lax.all_to_all(message, ALL, split_axis=0, concat_axis=0, tiled=True)  13.9 us
    ppermute x9, starting transfers between devices, gather_stage(): lax.ppermute(block, ALL, permutation(stage, shift))  13.6 us
    all_to_all x1, starting transfers between devices, on_device(): lax.all_to_all(quarter.reshape(32, 16, -1), 'dev', split_axis=0, concat_a...  11.4 us
    pallas_call x1, Pallas kernels, quarter_of(): pl.pallas_call(quarter_kernel, in_specs=[pl.BlockSpec(memory_space=pltpu....  5.56 us
    pallas_call x1, Pallas kernels, beams_of(): pl.pallas_call(beams_kernel, out_shape=jax.ShapeDtypeStruct((64, rows //...  4.33 us
    pallas_call x1, Pallas kernels, early_of(): pl.pallas_call(early_kernel, out_shape=jax.ShapeDtypeStruct((2 * w0.shape...  3.33 us
  transfers between devices with their start and end apart: 14, of which 10 were waited for; matrix products, arithmetic and copies ran while one was open for 0% of the time, Pallas kernels for 18%

profile of v3, /device:TPU:1, one launch (start us, length us, event | category | flops | bytes accessed | tf_op | source)
XLA Modules:
  0.0 136.0 jit_solution(10971849922675412338)
XLA Ops:
  0.0 5.6 %quarter.1 = bf16[512,1024]{1,0:T(8,128)(2,1)} custom-call(f32[2048,512]{1,0:T(8,128)} %bitcast.13, f32[2048,512]{1,0:T(8,128)} %bitcast.14, s32[2,1,1024]{2,1,0:T(1,128)} %bitcast.17), custom_call_target="tpu_custom_call" | custom-call | flops 2000000000 | bytes 6000000 | tf_op jit(solution)/shard_map/quarter/pallas_call | solution.py:257
  5.6 11.4 %all-to-all-start = ((bf16[32,16,1024]{2,1,0:T(8,128)(2,1)}), bf16[32,16,1024]{2,1,0:T(8,128)(2,1)S(1)}, u32[]{:S(2)}, u32[]{:S(2)}) async-start(bf16[32,16,1024]{2,1,0:T(8,128)(2,1)} %bitcast.15), calls=%async_computation | async-start | bytes 2097152 | tf_op jit(solution)/shard_map/all_to_all | solution.py:461
  16.9 17.6 %spectra.1 = (bf16[128,16,256]{2,1,0:T(8,128)(2,1)}, bf16[128,16,512]{2,1,0:T(8,128)(2,1)}) custom-call(bf16[16,110592]{1,0:T(8,128)(2,1)} %refs_0_, bf16[16,110592]{1,0:T(8,128)(2,1)} %refs_1_, f32[16,4096]{1,0:T(8,128)} %refs_2_, f32[32,128]{1,0:T(8,128)} %constant.121.clone.refs_3_, f32[32,128]{1,0:T(8,128)} %constant.122.clone.refs_4_, ...), custom_call_target="tpu_custom_call" | custom-call | flops 2400000000 | bytes 48000000 | tf_op jit(solution)/shard_map/spectra/pallas_call | solution.py:190
  34.6 0.5 all-to-all-done.offers
  35.1 0.0 copy-start.2
  35.1 9.5 %all-to-all-start.1 = ((bf16[128,16,256]{2,1,0:T(8,128)(2,1)}), bf16[128,16,256]{2,1,0:T(8,128)(2,1)S(1)}, u32[]{:S(2)}, u32[]{:S(2)}) async-start(bf16[128,16,256]{2,1,0:T(8,128)(2,1)} %get-tuple-element.25), calls=%async_computation.1 | async-start | bytes 2097152 | tf_op jit(solution)/shard_map/all_to_all | solution.py:468
  44.5 0.0 copy-done.2
  44.5 2.1 %pick.1 = (bf16[16,1024]{1,0:T(8,128)(2,1)}, bf16[16,1024]{1,0:T(8,128)(2,1)}) custom-call(s32[2]{0:T(128)} %owners.1, bf16[32,16,1024]{2,1,0:T(8,128)(2,1)} %copy-done.2), custom_call_target="tpu_custom_call" | custom-call | tf_op jit(solution)/shard_map/pick/pallas_call | solution.py:289
  46.6 1.1 collective-permute-start
  47.8 1.1 collective-permute-done.refs_1_
  48.9 0.0 copy-start.1
  48.9 0.8 copy-done.1
  49.6 0.0 copy-start.3
  49.6 0.0 copy-start.4
  49.6 0.0 copy-start.5
  49.6 0.9 collective-permute-start.1
  50.5 1.9 %collective-permute-start.2 = (bf16[16,2048]{1,0:T(8,128)(2,1)S(1)}, bf16[16,2048]{1,0:T(8,128)(2,1)S(1)}, u32[]{:S(2)}, u32[]{:S(2)}) collective-permute-start(bf16[16,2048]{1,0:T(8,128)(2,1)S(1)} %join.3.refs_0_), channel_id=1, source_target_pairs={{64,0},{40,32},{1,64},{104,96},{65,1},{41,33},{0,65},{105,97},{66,... | collective-permute-start | bytes 196616 | tf_op jit(solution)/shard_map/ppermute | solution.py:434
  52.4 1.4 %collective-permute-start.3 = (bf16[16,2048]{1,0:T(8,128)(2,1)S(1)}, bf16[16,2048]{1,0:T(8,128)(2,1)S(1)}, u32[]{:S(2)}, u32[]{:S(2)}) collective-permute-start(bf16[16,2048]{1,0:T(8,128)(2,1)S(1)} %join.3.refs_0_), channel_id=1, source_target_pairs={{1,0},{48,32},{65,64},{112,96},{0,1},{49,33},{64,65},{113,97},{3,2... | collective-permute-start | bytes 196616 | tf_op jit(solution)/shard_map/ppermute | solution.py:434
  53.8 6.9 %collective-permute-done.1.refs_1_ = bf16[16,2048]{1,0:T(8,128)(2,1)S(1)} collective-permute-done((bf16[16,2048]{1,0:T(8,128)(2,1)S(1)}, bf16[16,2048]{1,0:T(8,128)(2,1)S(1)}, u32[]{:S(2)}, u32[]{:S(2)}) %collective-permute-start.1) | collective-permute-done | bytes 65568 | tf_op jit(solution)/shard_map/ppermute | solution.py:434
  60.7 0.0 collective-permute-done.2.refs_2_
  60.7 0.9 collective-permute-done.3.refs_3_
  61.6 2.3 %all-to-all-done.1 = bf16[128,16,256]{2,1,0:T(8,128)(2,1)S(1)} async-done(((bf16[128,16,256]{2,1,0:T(8,128)(2,1)}), bf16[128,16,256]{2,1,0:T(8,128)(2,1)S(1)}, u32[]{:S(2)}, u32[]{:S(2)}) %all-to-all-start.1) | async-done | bytes 1048608 | tf_op jit(solution)/shard_map/all_to_all | solution.py:468
  63.9 4.4 %all-to-all-start.2 = ((bf16[128,16,512]{2,1,0:T(8,128)(2,1)}), bf16[128,16,512]{2,1,0:T(8,128)(2,1)S(1)}, u32[]{:S(2)}, u32[]{:S(2)}) async-start(bf16[128,16,512]{2,1,0:T(8,128)(2,1)} %get-tuple-element.28), calls=%async_computation.2 | async-start | bytes 4194304 | tf_op jit(solution)/shard_map/all_to_all | solution.py:468
  68.4 1.5 %collective-permute-start.4 = (bf16[64,2048]{1,0:T(8,128)(2,1)S(1)}, bf16[64,2048]{1,0:T(8,128)(2,1)S(1)}, u32[]{:S(2)}, u32[]{:S(2)}) collective-permute-start(bf16[64,2048]{1,0:T(8,128)(2,1)S(1)} %join.4.refs_0_), channel_id=1, source_target_pairs={{6,0},{97,32},{70,64},{32,96},{7,1},{96,33},{71,65},{33,97},{0,2},... | collective-permute-start | bytes 786440 | tf_op jit(solution)/shard_map/ppermute | solution.py:434
  69.8 1.3 collective-permute-start.5
  71.2 1.6 %collective-permute-start.6 = (bf16[64,2048]{1,0:T(8,128)(2,1)S(1)}, bf16[64,2048]{1,0:T(8,128)(2,1)S(1)}, u32[]{:S(2)}, u32[]{:S(2)}) collective-permute-start(bf16[64,2048]{1,0:T(8,128)(2,1)S(1)} %join.4.refs_0_), channel_id=1, source_target_pairs={{4,0},{33,32},{68,64},{97,96},{5,1},{32,33},{69,65},{96,97},{6,2},... | collective-permute-start | bytes 786440 | tf_op jit(solution)/shard_map/ppermute | solution.py:434
  72.8 24.1 %collective-permute-done.4.refs_1_ = bf16[64,2048]{1,0:T(8,128)(2,1)S(1)} collective-permute-done((bf16[64,2048]{1,0:T(8,128)(2,1)S(1)}, bf16[64,2048]{1,0:T(8,128)(2,1)S(1)}, u32[]{:S(2)}, u32[]{:S(2)}) %collective-permute-start.4) | collective-permute-done | bytes 262176 | tf_op jit(solution)/shard_map/ppermute | solution.py:434
  96.9 0.0 collective-permute-done.5.refs_2_
  96.9 3.0 %collective-permute-done.6.refs_3_ = bf16[64,2048]{1,0:T(8,128)(2,1)S(1)} collective-permute-done((bf16[64,2048]{1,0:T(8,128)(2,1)S(1)}, bf16[64,2048]{1,0:T(8,128)(2,1)S(1)}, u32[]{:S(2)}, u32[]{:S(2)}) %collective-permute-start.6) | collective-permute-done | bytes 262176 | tf_op jit(solution)/shard_map/ppermute | solution.py:434
  99.9 1.0 join.5.w0
  101.0 0.0 copy-start
  101.0 2.4 %collective-permute-start.7 = (bf16[256,2048]{1,0:T(8,128)(2,1)}, bf16[256,2048]{1,0:T(8,128)(2,1)}, u32[]{:S(2)}, u32[]{:S(2)}) collective-permute-start(bf16[256,2048]{1,0:T(8,128)(2,1)} %join.5.w0), channel_id=1, source_target_pairs={{16,0},{36,32},{80,64},{100,96},{17,1},{37,33},{81,65},{101,97},{1... | collective-permute-start | bytes 3145736 | tf_op jit(solution)/shard_map/ppermute | solution.py:434
  103.4 0.3 collective-permute-start.8
  103.7 2.4 %collective-permute-start.9 = (bf16[256,2048]{1,0:T(8,128)(2,1)}, bf16[256,2048]{1,0:T(8,128)(2,1)}, u32[]{:S(2)}, u32[]{:S(2)}) collective-permute-start(bf16[256,2048]{1,0:T(8,128)(2,1)} %join.5.w0), channel_id=1, source_target_pairs={{8,0},{34,32},{72,64},{98,96},{9,1},{35,33},{73,65},{99,97},{10,2}... | collective-permute-start | bytes 3145736 | tf_op jit(solution)/shard_map/ppermute | solution.py:434
  106.1 0.0 copy-done.3
  106.1 0.0 copy-done.4
  106.1 0.0 copy-done.5
  106.1 0.1 slice.21
  106.2 0.1 fusion.16
  106.3 0.1 pad_add_fusion.places
  106.3 10.5 %collective-permute-done.7.w1 = bf16[256,2048]{1,0:T(8,128)(2,1)} collective-permute-done((bf16[256,2048]{1,0:T(8,128)(2,1)}, bf16[256,2048]{1,0:T(8,128)(2,1)}, u32[]{:S(2)}, u32[]{:S(2)}) %collective-permute-start.7) | collective-permute-done | bytes 1048608 | tf_op jit(solution)/shard_map/ppermute | solution.py:434
  116.8 0.0 all-to-all-done.2
  116.8 3.3 %early.1 = f32[512,768]{1,0:T(8,128)S(1)} custom-call(bf16[256,2048]{1,0:T(8,128)(2,1)} %join.5.w0, bf16[256,2048]{1,0:T(8,128)(2,1)} %collective-permute-done.7.w1, bf16[2048,256]{1,0:T(8,128)(2,1)S(1)} %bitcast.11, bf16[2048,512]{1,0:T(8,128)(2,1)S(1)} %bitcast.9), custom_call_target="tpu_custom_call" | custom-call | flops 1700000000 | bytes 8000000 | tf_op jit(solution)/shard_map/early/pallas_call | solution.py:358
  120.1 7.8 %collective-permute-done.8.w2 = bf16[256,2048]{1,0:T(8,128)(2,1)} collective-permute-done((bf16[256,2048]{1,0:T(8,128)(2,1)}, bf16[256,2048]{1,0:T(8,128)(2,1)}, u32[]{:S(2)}, u32[]{:S(2)}) %collective-permute-start.8) | collective-permute-done | bytes 1048608 | tf_op jit(solution)/shard_map/ppermute | solution.py:434
  128.0 0.0 collective-permute-done.9.w3
  128.0 0.0 copy-done
  128.0 4.3 %beams.1 = f32[64,512]{1,0:T(8,128)S(1)} custom-call(s32[64]{0:T(128)S(1)} %pad_add_fusion.places, f32[512,768]{1,0:T(8,128)S(1)} %early.1, bf16[256,2048]{1,0:T(8,128)(2,1)} %collective-permute-done.8.w2, bf16[256,2048]{1,0:T(8,128)(2,1)} %collective-permute-done.9.w3, bf16[2048,256]{1,0:T(8,128)(2,1)S(1)} %bitcast.12, bf16[2048,512]{1,0:T(8,128)(2,1)S(1)} %bitcast.10, ...), custom_call_target="tpu_custom_call" | custom-call | flops 1700000000 | bytes 8000000 | tf_op jit(solution)/shard_map/beams/pallas_call | solution.py:401
  132.3 2.1 %collective-permute-start.10 = (f32[32,512]{1,0:T(8,128)S(1)}, f32[32,512]{1,0:T(8,128)S(1)}, u32[]{:S(2)}, u32[]{:S(2)}) collective-permute-start(f32[32,512]{1,0:T(8,128)S(1)} %get-tuple-element.30), channel_id=1, source_target_pairs={{0,32},{32,0},{64,96},{96,64},{1,33},{33,1},{65,97},{97,65},{2,34}... | collective-permute-start | bytes 196616 | tf_op jit(solution)/shard_map/ppermute | solution.py:489
  134.4 0.9 collective-permute-done.10
  135.3 0.7 maximum_select_fusion
  (4 shorter events, 0.1 us)
Async XLA Ops:
  5.6 29.5 %all-to-all-start = ((bf16[32,16,1024]{2,1,0:T(8,128)(2,1)}), bf16[32,16,1024]{2,1,0:T(8,128)(2,1)S(1)}, u32[]{:S(2)}, u32[]{:S(2)}) async-start(bf16[32,16,1024]{2,1,0:T(8,128)(2,1)} %bitcast.15), calls=%async_computation | async-start | bytes 2097152 | tf_op jit(solution)/shard_map/all_to_all | solution.py:461
  35.1 9.5 %copy-start.2 = (bf16[32,16,1024]{2,1,0:T(8,128)(2,1)}, bf16[32,16,1024]{2,1,0:T(8,128)(2,1)S(1)}, u32[]{:S(2)}) copy-start(bf16[32,16,1024]{2,1,0:T(8,128)(2,1)S(1)} %all-to-all-done.offers) | copy-start | bytes 3145732
  35.1 28.9 %all-to-all-start.1 = ((bf16[128,16,256]{2,1,0:T(8,128)(2,1)}), bf16[128,16,256]{2,1,0:T(8,128)(2,1)S(1)}, u32[]{:S(2)}, u32[]{:S(2)}) async-start(bf16[128,16,256]{2,1,0:T(8,128)(2,1)} %get-tuple-element.25), calls=%async_computation.1 | async-start | bytes 2097152 | tf_op jit(solution)/shard_map/all_to_all | solution.py:468
  46.6 2.2 %collective-permute-start = (bf16[16,1024]{1,0:T(8,128)(2,1)}, bf16[16,1024]{1,0:T(8,128)(2,1)S(1)}, u32[]{:S(2)}, u32[]{:S(2)}) collective-permute-start(bf16[16,1024]{1,0:T(8,128)(2,1)} %get-tuple-element.23), channel_id=1, source_target_pairs={{0,32},{32,0},{64,96},{96,64},{1,33},{33,1},{65,97},{97,65},{2,34}... | collective-permute-start | bytes 98312 | tf_op jit(solution)/shard_map/ppermute | solution.py:474
  48.9 0.8 copy-start.1
  49.6 56.4 %copy-start.3 = (s32[64]{0:T(128)S(1)}, s32[64]{0:T(128)}, u32[]{:S(2)}) copy-start(s32[64]{0:T(128)} %constant.124.clone) | copy-start | bytes 772
  49.6 56.4 %copy-start.4 = (s32[64]{0:T(128)S(1)}, s32[64]{0:T(128)}, u32[]{:S(2)}) copy-start(s32[64]{0:T(128)} %constant.125.clone) | copy-start | bytes 772
  49.6 56.4 %copy-start.5 = (s32[64]{0:T(128)S(1)}, s32[64]{0:T(128)}, u32[]{:S(2)}) copy-start(s32[64]{0:T(128)} %constant.126.clone) | copy-start | bytes 772
  49.6 11.0 %collective-permute-start.1 = (bf16[16,2048]{1,0:T(8,128)(2,1)S(1)}, bf16[16,2048]{1,0:T(8,128)(2,1)S(1)}, u32[]{:S(2)}, u32[]{:S(2)}) collective-permute-start(bf16[16,2048]{1,0:T(8,128)(2,1)S(1)} %join.3.refs_0_), channel_id=1, source_target_pairs={{65,0},{56,32},{0,64},{120,96},{64,1},{57,33},{1,65},{121,97},{67,... | collective-permute-start | bytes 196616 | tf_op jit(solution)/shard_map/ppermute | solution.py:434
  50.5 10.1 %collective-permute-start.2 = (bf16[16,2048]{1,0:T(8,128)(2,1)S(1)}, bf16[16,2048]{1,0:T(8,128)(2,1)S(1)}, u32[]{:S(2)}, u32[]{:S(2)}) collective-permute-start(bf16[16,2048]{1,0:T(8,128)(2,1)S(1)} %join.3.refs_0_), channel_id=1, source_target_pairs={{64,0},{40,32},{1,64},{104,96},{65,1},{41,33},{0,65},{105,97},{66,... | collective-permute-start | bytes 196616 | tf_op jit(solution)/shard_map/ppermute | solution.py:434
  52.4 9.2 %collective-permute-start.3 = (bf16[16,2048]{1,0:T(8,128)(2,1)S(1)}, bf16[16,2048]{1,0:T(8,128)(2,1)S(1)}, u32[]{:S(2)}, u32[]{:S(2)}) collective-permute-start(bf16[16,2048]{1,0:T(8,128)(2,1)S(1)} %join.3.refs_0_), channel_id=1, source_target_pairs={{1,0},{48,32},{65,64},{112,96},{0,1},{49,33},{64,65},{113,97},{3,2... | collective-permute-start | bytes 196616 | tf_op jit(solution)/shard_map/ppermute | solution.py:434
  63.9 52.9 %all-to-all-start.2 = ((bf16[128,16,512]{2,1,0:T(8,128)(2,1)}), bf16[128,16,512]{2,1,0:T(8,128)(2,1)S(1)}, u32[]{:S(2)}, u32[]{:S(2)}) async-start(bf16[128,16,512]{2,1,0:T(8,128)(2,1)} %get-tuple-element.28), calls=%async_computation.2 | async-start | bytes 4194304 | tf_op jit(solution)/shard_map/all_to_all | solution.py:468
  68.4 28.5 %collective-permute-start.4 = (bf16[64,2048]{1,0:T(8,128)(2,1)S(1)}, bf16[64,2048]{1,0:T(8,128)(2,1)S(1)}, u32[]{:S(2)}, u32[]{:S(2)}) collective-permute-start(bf16[64,2048]{1,0:T(8,128)(2,1)S(1)} %join.4.refs_0_), channel_id=1, source_target_pairs={{6,0},{97,32},{70,64},{32,96},{7,1},{96,33},{71,65},{33,97},{0,2},... | collective-permute-start | bytes 786440 | tf_op jit(solution)/shard_map/ppermute | solution.py:434
  69.8 27.1 %collective-permute-start.5 = (bf16[64,2048]{1,0:T(8,128)(2,1)S(1)}, bf16[64,2048]{1,0:T(8,128)(2,1)S(1)}, u32[]{:S(2)}, u32[]{:S(2)}) collective-permute-start(bf16[64,2048]{1,0:T(8,128)(2,1)S(1)} %join.4.refs_0_), channel_id=1, source_target_pairs={{2,0},{96,32},{66,64},{33,96},{3,1},{97,33},{67,65},{32,97},{4,2},... | collective-permute-start | bytes 786440 | tf_op jit(solution)/shard_map/ppermute | solution.py:434
  71.2 28.8 %collective-permute-start.6 = (bf16[64,2048]{1,0:T(8,128)(2,1)S(1)}, bf16[64,2048]{1,0:T(8,128)(2,1)S(1)}, u32[]{:S(2)}, u32[]{:S(2)}) collective-permute-start(bf16[64,2048]{1,0:T(8,128)(2,1)S(1)} %join.4.refs_0_), channel_id=1, source_target_pairs={{4,0},{33,32},{68,64},{97,96},{5,1},{32,33},{69,65},{96,97},{6,2},... | collective-permute-start | bytes 786440 | tf_op jit(solution)/shard_map/ppermute | solution.py:434
  101.0 27.0 %copy-start = (f32[64,384]{1,0:T(8,128)S(1)}, f32[64,384]{1,0:T(8,128)}, u32[]{:S(2)}) copy-start(f32[64,384]{1,0:T(8,128)} %constant.127.clone.choose) | copy-start | bytes 294916
  101.0 15.8 %collective-permute-start.7 = (bf16[256,2048]{1,0:T(8,128)(2,1)}, bf16[256,2048]{1,0:T(8,128)(2,1)}, u32[]{:S(2)}, u32[]{:S(2)}) collective-permute-start(bf16[256,2048]{1,0:T(8,128)(2,1)} %join.5.w0), channel_id=1, source_target_pairs={{16,0},{36,32},{80,64},{100,96},{17,1},{37,33},{81,65},{101,97},{1... | collective-permute-start | bytes 3145736 | tf_op jit(solution)/shard_map/ppermute | solution.py:434
  103.4 24.6 %collective-permute-start.8 = (bf16[256,2048]{1,0:T(8,128)(2,1)}, bf16[256,2048]{1,0:T(8,128)(2,1)}, u32[]{:S(2)}, u32[]{:S(2)}) collective-permute-start(bf16[256,2048]{1,0:T(8,128)(2,1)} %join.5.w0), channel_id=1, source_target_pairs={{24,0},{38,32},{88,64},{102,96},{25,1},{39,33},{89,65},{103,97},{2... | collective-permute-start | bytes 3145736 | tf_op jit(solution)/shard_map/ppermute | solution.py:434
  103.7 24.3 %collective-permute-start.9 = (bf16[256,2048]{1,0:T(8,128)(2,1)}, bf16[256,2048]{1,0:T(8,128)(2,1)}, u32[]{:S(2)}, u32[]{:S(2)}) collective-permute-start(bf16[256,2048]{1,0:T(8,128)(2,1)} %join.5.w0), channel_id=1, source_target_pairs={{8,0},{34,32},{72,64},{98,96},{9,1},{35,33},{73,65},{99,97},{10,2}... | collective-permute-start | bytes 3145736 | tf_op jit(solution)/shard_map/ppermute | solution.py:434
  132.3 3.0 %collective-permute-start.10 = (f32[32,512]{1,0:T(8,128)S(1)}, f32[32,512]{1,0:T(8,128)S(1)}, u32[]{:S(2)}, u32[]{:S(2)}) collective-permute-start(f32[32,512]{1,0:T(8,128)S(1)} %get-tuple-element.30), channel_id=1, source_target_pairs={{0,32},{32,0},{64,96},{96,64},{1,33},{33,1},{65,97},{97,65},{2,34}... | collective-permute-start | bytes 196616 | tf_op jit(solution)/shard_map/ppermute | solution.py:489

commit v4 on v3

--- a/solution.py
+++ b/solution.py
@@ -214,7 +214,15 @@
     )(vre, vim, taps, jnp.asarray(cos_t), jnp.asarray(sin_t), jnp.asarray(mat))
 
 
-def quarter_kernel(wre, wim, slots, out, buf, names, chosen, sems):
+SHIFTS = (0, -1, 1, 2)
+
+
+def place():
+    grp, dev = lax.axis_index("grp"), lax.axis_index("dev")
+    return grp % 2, {"z": dev // 8, "x": dev // 2 % 4, "y": dev % 2 * 2 + grp // 2}
+
+
+def quarter_kernel(wre, wim, slots, out0, out1, out2, out3, buf, names, chosen, turned, sems):
     grp = lax.axis_index("grp")
     y_lo, core = grp // 2, grp % 2
     antennas, beams = wre.shape
@@ -246,9 +254,20 @@
     for j in range(0, beams, 256):
         w = buf[:, j : j + 256].astype(jnp.bfloat16)
         for k in range(0, half, 512):
-            out[j : j + 256, k : k + 512] = lax.dot_general(
+            turned[j : j + 256, k : k + 512] = lax.dot_general(
                 w, chosen[:, k : k + 512], (((0,), (0,)), ((), ())), preferred_element_type=jnp.float32
             ).astype(jnp.bfloat16)
+    quarter_finish(turned, (out0, out1, out2, out3))
+
+
+def quarter_finish(turned, outs):
+    core, coordinate = place()
+    mine = jnp.where(core == 0, coordinate["z"], coordinate["x"])
+    for shift, out in zip(SHIFTS, outs):
+        block = (mine - shift + 4) % 4
+        for j in range(4):
+            at = jnp.where(core == 0, block * 128 + j * 32, j * 128 + block * 32)
+            out[j * 32 : j * 32 + 32, :] = turned[pl.ds(pl.multiple_of(at, 32), 32), :]
 
 
 def quarter_of(wre, wim, antenna_map, interpret=False):
@@ -257,12 +276,13 @@
     return pl.pallas_call(
         quarter_kernel,
         in_specs=[pl.BlockSpec(memory_space=pltpu.HBM)] * 3,
-        out_specs=pl.BlockSpec(memory_space=pltpu.VMEM),
-        out_shape=jax.ShapeDtypeStruct((beams, half), jnp.bfloat16),
+        out_specs=[pl.BlockSpec(memory_space=pltpu.VMEM)] * 4,
+        out_shape=[jax.ShapeDtypeStruct((beams // 4, half), jnp.bfloat16)] * 4,
         scratch_shapes=[
             pltpu.VMEM((antennas, beams), jnp.float32),
             pltpu.VMEM((1, half), jnp.int32),
             pltpu.VMEM((antennas, half), jnp.bfloat16),
+            pltpu.VMEM((beams, half), jnp.bfloat16),
             pltpu.SemaphoreType.DMA((5,)),
         ],
         compiler_params=pltpu.CompilerParams(vmem_limit_bytes=58 * MIB),
@@ -272,30 +292,62 @@
     )(wre, wim, antenna_map.reshape(2, 1, half))
 
 
-def pick_kernel(owners, offers, mine, other, sems):
-    core = lax.axis_index("grp") % 2
-    copies = [
-        pltpu.make_async_copy(offers.at[owners[core]], mine, sems.at[0]),
-        pltpu.make_async_copy(offers.at[owners[1 - core]], other, sems.at[1]),
-    ]
-    for copy in copies:
-        copy.start()
-    for copy in copies:
-        copy.wait()
-
-
-def pick_of(owners, offers, interpret=False):
-    _, rows, columns = offers.shape
+def pick_kernel(kind, owners, *refs):
+    inputs, outs = refs[:4], refs[4:]
+    core, here = place()
+
+    def copy_from(coordinate, position, copy):
+        for shift, source in zip(SHIFTS, inputs):
+
+            @pl.when((coordinate - position - shift + 8) % 4 == 0)
+            def _():
+                copy(source)
+
+    for i in range(2):
+        step = (core + i) % 2 if kind == "third" else i
+        owner = owners[step]
+        there = {"z": owner // 8, "x": owner // 2 % 4}
+        if kind == "first":
+
+            def copy(source):
+                mine = jnp.where(core == 0, here["x"], here["z"])
+                for shift, out in zip(SHIFTS, outs):
+                    at = pl.multiple_of((mine - shift + 4) % 4 * 32, 32)
+                    out[i * 32 : i * 32 + 32, :] = source[pl.ds(at, 32), :]
+
+            copy_from(
+                jnp.where(core == 0, there["z"], there["x"]), jnp.where(core == 0, here["z"], here["x"]), copy
+            )
+        elif kind == "second":
+
+            def copy(source):
+                outs[0][i * 32 : i * 32 + 32, :] = source[i * 32 : i * 32 + 32, :]
+
+            copy_from(
+                jnp.where(core == 0, there["x"], there["z"]), jnp.where(core == 0, here["x"], here["z"]), copy
+            )
+        else:
+            for y_lo in range(2):
+
+                def copy(source):
+                    at = pl.multiple_of(step * 32, 32)
+                    outs[i][y_lo * 32 : y_lo * 32 + 32, :] = source[pl.ds(at, 32), :]
+
+                copy_from(owner % 2 * 2 + y_lo, here["y"], copy)
+
+
+def pick_of(kind, owners, parts, interpret=False):
+    columns = parts[0].shape[1]
+    count = {"first": 4, "second": 1, "third": 2}[kind]
     return pl.pallas_call(
-        pick_kernel,
-        in_specs=[pl.BlockSpec(memory_space=pltpu.SMEM), pl.BlockSpec(memory_space=pltpu.HBM)],
-        out_specs=[pl.BlockSpec(memory_space=pltpu.VMEM)] * 2,
-        out_shape=[jax.ShapeDtypeStruct((rows, columns), offers.dtype)] * 2,
-        scratch_shapes=[pltpu.SemaphoreType.DMA((2,))],
-        compiler_params=pltpu.CompilerParams(vmem_limit_bytes=58 * MIB),
+        functools.partial(pick_kernel, kind),
+        in_specs=[pl.BlockSpec(memory_space=pltpu.SMEM)] + [pl.BlockSpec(memory_space=pltpu.VMEM)] * 4,
+        out_specs=[pl.BlockSpec(memory_space=pltpu.VMEM)] * count,
+        out_shape=[jax.ShapeDtypeStruct((64, columns), parts[0].dtype)] * count,
+        compiler_params=pltpu.CompilerParams(vmem_limit_bytes=8 * MIB),
         interpret=interpret,
-        name="pick",
-    )(owners, offers)
+        name="pick_" + kind,
+    )(owners, *parts)
 
 
 def join_kernel(axis, *refs):
@@ -367,18 +419,25 @@
     )(w0, w1, *spectra)
 
 
-def beams_kernel(places, early, w2, w3, za, zb, choose, out, sums):
-    for k in range(32):
-        at = pl.multiple_of(places[k], 16)
-        sums[pl.ds(at, 16), :] = early[k * 16 : (k + 1) * 16, :]
-    core = lax.axis_index("grp") % 2
+def beams_kernel(early, w2, w3, za, zb, choose, out, sums):
+    core, here = place()
     wide = za.shape[1]
-    for i, part in enumerate((w2, w3)):
-        first, second = products(core, part, (za, zb))
-        for k in range(16):
-            at = pl.multiple_of(places[(i + 2) * 16 + k], 16)
-            sums[pl.ds(at, 16), :wide] = first[k * 16 : (k + 1) * 16, :]
-            sums[pl.ds(at, 16), wide:] = second[k * 16 : (k + 1) * 16, :]
+
+    def row_of(part, k):
+        first, y_lo = SHIFTS[k // 2], k % 2
+        second = SHIFTS[part]
+        z = (here["z"] + jnp.where(core == 0, second, first) + 4) % 4
+        x = (here["x"] + jnp.where(core == 0, first, second) + 4) % 4
+        return pl.ds(pl.multiple_of(y_lo * 512 + z * 128 + x * 32, 32), 32)
+
+    for part in range(2):
+        for k in range(8):
+            sums[row_of(part, k), :] = early[part * 256 + k * 32 : part * 256 + (k + 1) * 32, :]
+    for part, w in ((2, w2), (3, w3)):
+        first, second = products(core, w, (za, zb))
+        for k in range(8):
+            sums[row_of(part, k), :wide] = first[k * 32 : (k + 1) * 32, :]
+            sums[row_of(part, k), wide:] = second[k * 32 : (k + 1) * 32, :]
     beams = sums.shape[0] // 2
     powers = []
     for g in range(3):
@@ -396,19 +455,19 @@
     out[...] = total * (1.0 / SPECTRA)
 
 
-def beams_of(places, early, w2, w3, spectra, interpret=False):
+def beams_of(early, w2, w3, spectra, interpret=False):
     rows = early.shape[0] + 2 * w2.shape[0]
     return pl.pallas_call(
         beams_kernel,
         out_shape=jax.ShapeDtypeStruct((64, rows // 2), jnp.float32),
-        in_specs=[pl.BlockSpec(memory_space=pltpu.SMEM)] + [pl.BlockSpec(memory_space=pltpu.VMEM)] * 6,
+        in_specs=[pl.BlockSpec(memory_space=pltpu.VMEM)] * 6,
         out_specs=pl.BlockSpec(memory_space=pltpu.VMEM),
         scratch_shapes=[pltpu.VMEM((rows, 768), jnp.float32)],
         compiler_params=pltpu.CompilerParams(vmem_limit_bytes=32 * MIB),
         cost_estimate=pl.CostEstimate(flops=17 * 10**8, bytes_accessed=8 * 10**6, transcendentals=0),
         interpret=interpret,
         name="beams",
-    )(places, early, w2, w3, *spectra, jnp.asarray(choose_matrix()))
+    )(early, w2, w3, *spectra, jnp.asarray(choose_matrix()))
 
 
 def index_of(z, x, y, core):
@@ -416,73 +475,62 @@
 
 
 EVERY = [(z, x, y, c) for z in range(4) for x in range(4) for y in range(4) for c in range(2)]
-ORDER = (("y", "x", "z"), ("z", "y", "x"))
-SHIFTS = (0, -1, 1, 2)
+AXES = (("z", "x", "y", "x", "z"), ("x", "z", "y", "z", "x"))
 
 
 def permutation(stage, shift):
     pairs = []
     for z, x, y, core in EVERY:
-        axis = ORDER[core][stage]
+        axis = AXES[core][stage]
         source = {"z": z, "x": x, "y": y}
         source[axis] += shift
         pairs.append((index_of(source["z"], source["x"], source["y"], core), index_of(z, x, y, core)))
     return pairs
 
 
-def gather_stage(block, stage):
-    return [block] + [lax.ppermute(block, ALL, permutation(stage, shift)) for shift in SHIFTS[1:]]
-
-
-def block_places(grp, dev):
-    core = grp % 2
-    z, x, y = dev // 8, dev // 2 % 4, dev % 2 * 2 + grp // 2
-    k = np.arange(64)
-    shift = np.array(SHIFTS)
-    first, second, third = shift[k % 4], shift[k // 4 % 4], shift[k // 16]
-    by_core = []
-    for order in ORDER:
-        moved = dict(zip(order, (first, second, third)))
-        by_core.append([moved[axis] for axis in "zxy"])
-    is_first = core == 0
-    mz, mx, my = [jnp.where(is_first, jnp.asarray(a), jnp.asarray(b)) for a, b in zip(*by_core)]
-    fz, fx, fy = (z + mz + 4) % 4, (x + mx + 4) % 4, (y + my + 4) % 4
-    return (((fy % 2) * 32 + fz * 8 + fx * 2 + fy // 2) * 16).astype(jnp.int32)
+def exchange(blocks, stage):
+    return [blocks[0]] + [
+        lax.ppermute(block, ALL, permutation(stage, shift)) for block, shift in zip(blocks[1:], SHIFTS[1:])
+    ]
 
 
 SWAP = [(0, 1), (1, 0), (2, 3), (3, 2)]
 
 
 def on_device(voltage_real, voltage_imaginary, filter_taps, weights_re, weights_im, owners, antenna_map):
-    grp, dev = lax.axis_index("grp"), lax.axis_index("dev")
-    core = grp % 2
-
-    quarter = quarter_of(weights_re[0], weights_im[0], antenna_map)
-    offers = lax.all_to_all(quarter.reshape(32, 16, -1), "dev", split_axis=0, concat_axis=0, tiled=True)
-
-    volts = (voltage_real, voltage_imaginary, filter_taps)
-    quarter, *volts = lax.optimization_barrier((quarter, *volts))
-    messages = spectra_of(MESSAGES, *volts)
+    core = lax.axis_index("grp") % 2
+    tie = lax.optimization_barrier
 
     def turn(message):
         moved = lax.all_to_all(message, ALL, split_axis=0, concat_axis=0, tiled=True)
         return moved.reshape(DEVICES * SLOTS, -1)
 
-    message, offers = lax.optimization_barrier((messages[0], offers))
-    spectra = [turn(message)]
-    mine, other = pick_of(owners, offers)
+    volts = (voltage_real, voltage_imaginary, filter_taps)
+    blocks = quarter_of(weights_re[0], weights_im[0], antenna_map)
+    blocks, volts = tie((blocks, volts))
+    blocks = exchange(blocks, 0)
+    (late,) = spectra_of(((2,),), *volts)
+    blocks, late, volts = tie((blocks, late, volts))
+    blocks = pick_of("first", owners, blocks)
+    blocks, late, volts = tie((blocks, late, volts))
+    blocks = exchange(blocks, 1)
+    late = turn(late)
+    (soon,) = spectra_of(((0, 1),), *volts)
+    blocks, soon, late = tie((blocks, soon, late))
+    (block,) = pick_of("second", owners, blocks)
+    blocks = exchange([block] * 4, 2)
+    blocks, soon = tie((blocks, soon))
+    soon = turn(soon)
+    mine, other = pick_of("third", owners, blocks)
     other = lax.ppermute(other, "grp", SWAP)
     block = join_of([mine, other], 1)
-    block = join_of(gather_stage(block, 0), 0)
-    block, message, spectra[0] = lax.optimization_barrier((block, messages[1], spectra[0]))
-    spectra.append(turn(message))
-    block = join_of(gather_stage(block, 1), 0)
-    parts = gather_stage(block, 2)
-
-    early = early_of(parts[0], parts[3], spectra)
-    places = block_places(grp, dev)
-    places = jnp.concatenate([places[:16], places[48:], places[16:48]])
-    power = beams_of(places, early, parts[1], parts[2], spectra)
+    block = join_of(exchange([block] * 4, 3), 0)
+    block, soon = tie((block, soon))
+    parts = exchange([block] * 4, 4)
+
+    spectra = (soon, late)
+    early = early_of(parts[0], parts[1], spectra)
+    power = beams_of(early, parts[2], parts[3], spectra)
     power = power.reshape(2, 32, -1)
     own = jnp.where(core == 0, power[0], power[1])
     given = jnp.where(core == 0, power[1], power[0])

time: 137 us -> 137 us (level)
  waiting for transfers between devices: 58.1 us -> 53.6 us
  Pallas kernels: 34 us -> 37.3 us
  local copies, waits for them, and re-layouts: 0.92 us -> 3.78 us
  starting transfers between devices: 42.1 us -> 40.5 us
    all_to_all x1 -> x0, starting transfers between devices: 11.4 us -> none  [on_device(): lax.all_to_all(quarter.reshape(32, 16, -1), 'dev', split_axis=0, concat_a...]
    ppermute x9 -> x15, starting transfers between devices: 13.6 us -> 20.6 us  [exchange(): lax.ppermute(block, ALL, permutation(stage, shift))]
    pallas_call x1 -> x2, Pallas kernels: 17.6 us -> 22.2 us  [spectra_of(): pl.pallas_call(functools.partial(spectra_kernel, messages), out_shape=[ja...]
    all_to_all x2, starting transfers between devices: 13.9 us -> 18.2 us  [turn(): lax.all_to_all(message, ALL, split_axis=0, concat_axis=0, tiled=True)]
    unnamed x12 -> x14, local copies, waits for them, and re-layouts: 0.78 us -> 3.78 us
    ppermute x9 -> x15, waiting for transfers between devices: 53.3 us -> 50.7 us  [exchange(): lax.ppermute(block, ALL, permutation(stage, shift))]
    ppermute x1, starting transfers between devices: 2.06 us -> 0.47 us  [on_device(): taken = lax.ppermute(given, 'grp', SWAP)]
  transfers between devices with their start and end apart: 14 -> 19, of which waited for: 10 -> 12; matrix products, arithmetic and copies ran while one was open for 0% -> 0% of each run, Pallas kernels for 18% -> 19%
where the time goes in v4:
time: 137 us; the launch traced here: 136 us
  waiting for transfers between devices  53.6 us (39%)
  starting transfers between devices  40.5 us (30%)
  Pallas kernels  37.3 us (27%)
  local copies, waits for them, and re-layouts  3.78 us (3%)
    ppermute x15, waiting for transfers between devices, exchange(): lax.ppermute(block, ALL, permutation(stage, shift))  50.7 us
    pallas_call x2, Pallas kernels, spectra_of(): pl.pallas_call(functools.partial(spectra_kernel, messages), out_shape=[ja...  22.2 us
    ppermute x15, starting transfers between devices, exchange(): lax.ppermute(block, ALL, permutation(stage, shift))  20.6 us
    all_to_all x2, starting transfers between devices, turn(): lax.all_to_all(message, ALL, split_axis=0, concat_axis=0, tiled=True)  18.2 us
    pallas_call x1, Pallas kernels, quarter_of(): pl.pallas_call(quarter_kernel, in_specs=[pl.BlockSpec(memory_space=pltpu....  5.6 us
    pallas_call x1, Pallas kernels, beams_of(): pl.pallas_call(beams_kernel, out_shape=jax.ShapeDtypeStruct((64, rows //...  4.33 us
    unnamed x14, local copies, waits for them, and re-layouts  3.78 us
    pallas_call x1, Pallas kernels, early_of(): pl.pallas_call(early_kernel, out_shape=jax.ShapeDtypeStruct((2 * w0.shape...  3.01 us
  transfers between devices with their start and end apart: 19, of which 12 were waited for; matrix products, arithmetic and copies ran while one was open for 0% of the time, Pallas kernels for 19%

profile of v4, /device:TPU:1, one launch (start us, length us, event | category | flops | bytes accessed | tf_op | source)
XLA Modules:
  0.0 136.1 jit_solution(9343334612939898243)
XLA Ops:
  0.0 5.6 %quarter.1 = (bf16[128,1024]{1,0:T(8,128)(2,1)}, bf16[128,1024]{1,0:T(8,128)(2,1)}, bf16[128,1024]{1,0:T(8,128)(2,1)}, bf16[128,1024]{1,0:T(8,128)(2,1)}) custom-call(f32[2048,512]{1,0:T(8,128)} %bitcast.12, f32[2048,512]{1,0:T(8,128)} %bitcast.13, s32[2,1,1024]{2,1,0:T(1,128)} %bitcast.15), custom_call_target="tpu_custom_call" | custom-call | flops 2000000000 | bytes 6000000 | tf_op jit(solution)/shard_map/quarter/pallas_call | solution.py:276
  5.6 0.0 copy-start.2
  5.6 0.0 copy-start.6
  5.6 2.1 %collective-permute-start = (bf16[128,1024]{1,0:T(8,128)(2,1)}, bf16[128,1024]{1,0:T(8,128)(2,1)S(1)}, u32[]{:S(2)}, u32[]{:S(2)}) collective-permute-start(bf16[128,1024]{1,0:T(8,128)(2,1)} %get-tuple-element.56), channel_id=1, source_target_pairs={{24,0},{38,32},{88,64},{102,96},{25,1},{39,33},{89,65},{103,97},{2... | collective-permute-start | bytes 786440 | tf_op jit(solution)/shard_map/ppermute | solution.py:493
  7.7 1.4 collective-permute-start.1
  9.1 1.6 %collective-permute-start.2 = (bf16[128,1024]{1,0:T(8,128)(2,1)}, bf16[128,1024]{1,0:T(8,128)(2,1)S(1)}, u32[]{:S(2)}, u32[]{:S(2)}) collective-permute-start(bf16[128,1024]{1,0:T(8,128)(2,1)} %get-tuple-element.58), channel_id=1, source_target_pairs={{16,0},{36,32},{80,64},{100,96},{17,1},{37,33},{81,65},{101,97},{1... | collective-permute-start | bytes 786440 | tf_op jit(solution)/shard_map/ppermute | solution.py:493
  10.7 8.9 %spectra.2 = bf16[128,16,256]{2,1,0:T(8,128)(2,1)} custom-call(bf16[16,110592]{1,0:T(8,128)(2,1)} %refs_0_.1, bf16[16,110592]{1,0:T(8,128)(2,1)} %refs_1_.1, f32[16,4096]{1,0:T(8,128)} %refs_2_.1, f32[32,128]{1,0:T(8,128)} %constant.28.clone.refs_3_, f32[32,128]{1,0:T(8,128)} %constant.29.clone.refs_4_, bf16[256,256]{1,0:T(8,128)(2,1)} %constant.30.clone.refs_5_), custom_call_target="tpu_custom_call" | custom-call | flops 800000000 | bytes 16000000 | tf_op jit(solution)/shard_map/spectra/pallas_call | solution.py:190
  19.7 0.0 collective-permute-done.refs_1_
  19.7 0.0 collective-permute-done.1.refs_2_
  19.7 0.0 collective-permute-done.2.refs_3_
  19.7 0.0 copy-done.2
  19.7 0.0 copy-done.6
  19.7 0.7 pick_first.1
  20.4 10.1 %all-to-all-start = ((bf16[128,16,256]{2,1,0:T(8,128)(2,1)}), bf16[128,16,256]{2,1,0:T(8,128)(2,1)S(1)}, u32[]{:S(2)}, u32[]{:S(2)}) async-start(bf16[128,16,256]{2,1,0:T(8,128)(2,1)} %spectra.2), calls=%async_computation | async-start | bytes 2097152 | tf_op jit(solution)/shard_map/all_to_all | solution.py:505
  30.5 1.6 %collective-permute-start.3 = (bf16[64,1024]{1,0:T(8,128)(2,1)S(1)}, bf16[64,1024]{1,0:T(8,128)(2,1)S(1)}, u32[]{:S(2)}, u32[]{:S(2)}) collective-permute-start(bf16[64,1024]{1,0:T(8,128)(2,1)S(1)} %get-tuple-element.75), channel_id=1, source_target_pairs={{6,0},{56,32},{70,64},{120,96},{7,1},{57,33},{71,65},{121,97},{0,2... | collective-permute-start | bytes 393224 | tf_op jit(solution)/shard_map/ppermute | solution.py:493
  32.1 1.8 %collective-permute-start.4 = (bf16[64,1024]{1,0:T(8,128)(2,1)S(1)}, bf16[64,1024]{1,0:T(8,128)(2,1)S(1)}, u32[]{:S(2)}, u32[]{:S(2)}) collective-permute-start(bf16[64,1024]{1,0:T(8,128)(2,1)S(1)} %get-tuple-element.76), channel_id=1, source_target_pairs={{2,0},{40,32},{66,64},{104,96},{3,1},{41,33},{67,65},{105,97},{4,2... | collective-permute-start | bytes 393224 | tf_op jit(solution)/shard_map/ppermute | solution.py:493
  33.9 1.4 %collective-permute-start.5 = (bf16[64,1024]{1,0:T(8,128)(2,1)S(1)}, bf16[64,1024]{1,0:T(8,128)(2,1)S(1)}, u32[]{:S(2)}, u32[]{:S(2)}) collective-permute-start(bf16[64,1024]{1,0:T(8,128)(2,1)S(1)} %get-tuple-element.77), channel_id=1, source_target_pairs={{4,0},{48,32},{68,64},{112,96},{5,1},{49,33},{69,65},{113,97},{6,2... | collective-permute-start | bytes 393224 | tf_op jit(solution)/shard_map/ppermute | solution.py:493
  35.3 13.3 %spectra.3 = bf16[128,16,512]{2,1,0:T(8,128)(2,1)} custom-call(bf16[16,110592]{1,0:T(8,128)(2,1)} %refs_0_.1, bf16[16,110592]{1,0:T(8,128)(2,1)} %refs_1_.1, f32[16,4096]{1,0:T(8,128)} %refs_2_.1, f32[32,128]{1,0:T(8,128)} %constant.28.clone.refs_3_, f32[32,128]{1,0:T(8,128)} %constant.29.clone.refs_4_, bf16[256,256]{1,0:T(8,128)(2,1)} %constant.30.clone.refs_5_), custom_call_target="tpu_custom_call" | custom-call | flops 1600000000 | bytes 32000000 | tf_op jit(solution)/shard_map/spectra/pallas_call | solution.py:190
  48.6 0.0 collective-permute-done.3.refs_1_
  48.6 0.0 collective-permute-done.4.refs_2_
  48.6 0.3 collective-permute-done.5.refs_3_
  48.9 1.0 all-to-all-done
  49.9 0.7 pick_second.1.refs_0_
  50.6 0.3 collective-permute-start.6
  50.9 2.4 %collective-permute-start.7 = (bf16[64,1024]{1,0:T(8,128)(2,1)S(1)}, bf16[64,1024]{1,0:T(8,128)(2,1)S(1)}, u32[]{:S(2)}, u32[]{:S(2)}) collective-permute-start(bf16[64,1024]{1,0:T(8,128)(2,1)S(1)} %pick_second.1.refs_0_), channel_id=1, source_target_pairs={{64,0},{96,32},{1,64},{33,96},{65,1},{97,33},{0,65},{32,97},{66,2}... | collective-permute-start | bytes 393224 | tf_op jit(solution)/shard_map/ppermute | solution.py:493
  53.3 0.4 collective-permute-start.8
  53.7 3.1 %collective-permute-done.6.refs_1_ = bf16[64,1024]{1,0:T(8,128)(2,1)S(1)} collective-permute-done((bf16[64,1024]{1,0:T(8,128)(2,1)S(1)}, bf16[64,1024]{1,0:T(8,128)(2,1)S(1)}, u32[]{:S(2)}, u32[]{:S(2)}) %collective-permute-start.6) | collective-permute-done | bytes 131104 | tf_op jit(solution)/shard_map/ppermute | solution.py:493
  56.8 1.9 %collective-permute-done.7.refs_2_ = bf16[64,1024]{1,0:T(8,128)(2,1)S(1)} collective-permute-done((bf16[64,1024]{1,0:T(8,128)(2,1)S(1)}, bf16[64,1024]{1,0:T(8,128)(2,1)S(1)}, u32[]{:S(2)}, u32[]{:S(2)}) %collective-permute-start.7) | collective-permute-done | bytes 131104 | tf_op jit(solution)/shard_map/ppermute | solution.py:493
  58.6 0.5 collective-permute-done.8.refs_3_
  59.1 0.0 copy-start.3
  59.1 0.7 copy-done.3
  59.7 8.2 %all-to-all-start.1 = ((bf16[128,16,512]{2,1,0:T(8,128)(2,1)}), bf16[128,16,512]{2,1,0:T(8,128)(2,1)S(1)}, u32[]{:S(2)}, u32[]{:S(2)}) async-start(bf16[128,16,512]{2,1,0:T(8,128)(2,1)} %spectra.3), calls=%async_computation.1 | async-start | bytes 4194304 | tf_op jit(solution)/shard_map/all_to_all | solution.py:505
  67.9 0.0 copy-start.4
  67.9 0.9 copy-done.4
  68.8 0.8 pick_third.1
  69.6 1.1 collective-permute-start.9
  70.7 1.0 collective-permute-done.9.refs_1_
  71.7 0.9 collective-permute-start.10
  72.6 1.9 %collective-permute-start.11 = (bf16[64,2048]{1,0:T(8,128)(2,1)S(1)}, bf16[64,2048]{1,0:T(8,128)(2,1)S(1)}, u32[]{:S(2)}, u32[]{:S(2)}) collective-permute-start(bf16[64,2048]{1,0:T(8,128)(2,1)S(1)} %join.2.refs_0_), channel_id=1, source_target_pairs={{2,0},{40,32},{66,64},{104,96},{3,1},{41,33},{67,65},{105,97},{4,2... | collective-permute-start | bytes 786440 | tf_op jit(solution)/shard_map/ppermute | solution.py:493
  74.5 1.4 %collective-permute-start.12 = (bf16[64,2048]{1,0:T(8,128)(2,1)S(1)}, bf16[64,2048]{1,0:T(8,128)(2,1)S(1)}, u32[]{:S(2)}, u32[]{:S(2)}) collective-permute-start(bf16[64,2048]{1,0:T(8,128)(2,1)S(1)} %join.2.refs_0_), channel_id=1, source_target_pairs={{4,0},{48,32},{68,64},{112,96},{5,1},{49,33},{69,65},{113,97},{6,2... | collective-permute-start | bytes 786440 | tf_op jit(solution)/shard_map/ppermute | solution.py:493
  75.8 22.4 %collective-permute-done.10.refs_1_ = bf16[64,2048]{1,0:T(8,128)(2,1)S(1)} collective-permute-done((bf16[64,2048]{1,0:T(8,128)(2,1)S(1)}, bf16[64,2048]{1,0:T(8,128)(2,1)S(1)}, u32[]{:S(2)}, u32[]{:S(2)}) %collective-permute-start.10) | collective-permute-done | bytes 262176 | tf_op jit(solution)/shard_map/ppermute | solution.py:493
  98.3 0.0 collective-permute-done.11.refs_2_
  98.3 2.9 %collective-permute-done.12.refs_3_ = bf16[64,2048]{1,0:T(8,128)(2,1)S(1)} collective-permute-done((bf16[64,2048]{1,0:T(8,128)(2,1)S(1)}, bf16[64,2048]{1,0:T(8,128)(2,1)S(1)}, u32[]{:S(2)}, u32[]{:S(2)}) %collective-permute-start.12) | collective-permute-done | bytes 262176 | tf_op jit(solution)/shard_map/ppermute | solution.py:493
  101.2 0.0 copy-start.5
  101.2 0.1 join.3.w0
  101.2 0.0 copy-start
  101.2 1.0 copy-done
  102.2 0.0 all-to-all-done.1
  102.2 0.3 collective-permute-start.13
  102.5 2.4 %collective-permute-start.14 = (bf16[256,2048]{1,0:T(8,128)(2,1)}, bf16[256,2048]{1,0:T(8,128)(2,1)}, u32[]{:S(2)}, u32[]{:S(2)}) collective-permute-start(bf16[256,2048]{1,0:T(8,128)(2,1)} %copy-done), channel_id=1, source_target_pairs={{8,0},{34,32},{72,64},{98,96},{9,1},{35,33},{73,65},{99,97},{10,2}... | collective-permute-start | bytes 3145736 | tf_op jit(solution)/shard_map/ppermute | solution.py:493
  104.9 0.8 collective-permute-start.15
  105.7 11.7 %collective-permute-done.13.w1 = bf16[256,2048]{1,0:T(8,128)(2,1)} collective-permute-done((bf16[256,2048]{1,0:T(8,128)(2,1)}, bf16[256,2048]{1,0:T(8,128)(2,1)}, u32[]{:S(2)}, u32[]{:S(2)}) %collective-permute-start.13) | collective-permute-done | bytes 1048608 | tf_op jit(solution)/shard_map/ppermute | solution.py:493
  117.4 0.0 copy-start.1
  117.4 1.2 copy-done.1
  118.6 3.0 %early.1 = f32[512,768]{1,0:T(8,128)S(1)} custom-call(bf16[256,2048]{1,0:T(8,128)(2,1)S(1)} %copy-done.1, bf16[256,2048]{1,0:T(8,128)(2,1)} %collective-permute-done.13.w1, bf16[2048,512]{1,0:T(8,128)(2,1)S(1)} %bitcast.8, bf16[2048,256]{1,0:T(8,128)(2,1)S(1)} %bitcast.10), custom_call_target="tpu_custom_call" | custom-call | flops 1700000000 | bytes 8000000 | tf_op jit(solution)/shard_map/early/pallas_call | solution.py:410
  121.6 6.6 %collective-permute-done.14.w2 = bf16[256,2048]{1,0:T(8,128)(2,1)} collective-permute-done((bf16[256,2048]{1,0:T(8,128)(2,1)}, bf16[256,2048]{1,0:T(8,128)(2,1)}, u32[]{:S(2)}, u32[]{:S(2)}) %collective-permute-start.14) | collective-permute-done | bytes 1048608 | tf_op jit(solution)/shard_map/ppermute | solution.py:493
  128.2 1.5 %collective-permute-done.15.w3 = bf16[256,2048]{1,0:T(8,128)(2,1)} collective-permute-done((bf16[256,2048]{1,0:T(8,128)(2,1)}, bf16[256,2048]{1,0:T(8,128)(2,1)}, u32[]{:S(2)}, u32[]{:S(2)}) %collective-permute-start.15) | collective-permute-done | bytes 1048608 | tf_op jit(solution)/shard_map/ppermute | solution.py:493
  129.7 0.0 copy-done.5
  129.7 4.3 %beams.1 = f32[64,512]{1,0:T(8,128)S(1)} custom-call(f32[512,768]{1,0:T(8,128)S(1)} %early.1, bf16[256,2048]{1,0:T(8,128)(2,1)} %collective-permute-done.14.w2, bf16[256,2048]{1,0:T(8,128)(2,1)} %collective-permute-done.15.w3, bf16[2048,512]{1,0:T(8,128)(2,1)S(1)} %bitcast.9, bf16[2048,256]{1,0:T(8,128)(2,1)S(1)} %bitcast.11, f32[64,384]{1,0:T(8,128)S(1)} %copy-done.5), custom_call_target="tpu_custom_call" | custom-call | flops 1700000000 | bytes 8000000 | tf_op jit(solution)/shard_map/beams/pallas_call | solution.py:460
  134.0 0.5 collective-permute-start.16
  134.5 0.9 collective-permute-done.16
  135.4 0.7 maximum_select_fusion
  (2 shorter events, 0.0 us)
Async XLA Ops:
  5.6 14.1 %copy-start.2 = (bf16[128,1024]{1,0:T(8,128)(2,1)S(1)}, bf16[128,1024]{1,0:T(8,128)(2,1)}, u32[]{:S(2)}) copy-start(bf16[128,1024]{1,0:T(8,128)(2,1)} %get-tuple-element.62.refs_0_) | copy-start | bytes 786436
  5.6 14.1 %copy-start.6 = (s32[2]{0:T(128)S(1)}, s32[2]{0:T(128)}, u32[]{:S(2)}) copy-start(s32[2]{0:T(128)} %owners.5) | copy-start | bytes 28
  5.6 14.0 %collective-permute-start = (bf16[128,1024]{1,0:T(8,128)(2,1)}, bf16[128,1024]{1,0:T(8,128)(2,1)S(1)}, u32[]{:S(2)}, u32[]{:S(2)}) collective-permute-start(bf16[128,1024]{1,0:T(8,128)(2,1)} %get-tuple-element.56), channel_id=1, source_target_pairs={{24,0},{38,32},{88,64},{102,96},{25,1},{39,33},{89,65},{103,97},{2... | collective-permute-start | bytes 786440 | tf_op jit(solution)/shard_map/ppermute | solution.py:493
  7.7 11.9 %collective-permute-start.1 = (bf16[128,1024]{1,0:T(8,128)(2,1)}, bf16[128,1024]{1,0:T(8,128)(2,1)S(1)}, u32[]{:S(2)}, u32[]{:S(2)}) collective-permute-start(bf16[128,1024]{1,0:T(8,128)(2,1)} %get-tuple-element.57), channel_id=1, source_target_pairs={{8,0},{34,32},{72,64},{98,96},{9,1},{35,33},{73,65},{99,97},{10,2}... | collective-permute-start | bytes 786440 | tf_op jit(solution)/shard_map/ppermute | solution.py:493
  9.1 10.6 %collective-permute-start.2 = (bf16[128,1024]{1,0:T(8,128)(2,1)}, bf16[128,1024]{1,0:T(8,128)(2,1)S(1)}, u32[]{:S(2)}, u32[]{:S(2)}) collective-permute-start(bf16[128,1024]{1,0:T(8,128)(2,1)} %get-tuple-element.58), channel_id=1, source_target_pairs={{16,0},{36,32},{80,64},{100,96},{17,1},{37,33},{81,65},{101,97},{1... | collective-permute-start | bytes 786440 | tf_op jit(solution)/shard_map/ppermute | solution.py:493
  20.4 29.5 %all-to-all-start = ((bf16[128,16,256]{2,1,0:T(8,128)(2,1)}), bf16[128,16,256]{2,1,0:T(8,128)(2,1)S(1)}, u32[]{:S(2)}, u32[]{:S(2)}) async-start(bf16[128,16,256]{2,1,0:T(8,128)(2,1)} %spectra.2), calls=%async_computation | async-start | bytes 2097152 | tf_op jit(solution)/shard_map/all_to_all | solution.py:505
  30.5 18.1 %collective-permute-start.3 = (bf16[64,1024]{1,0:T(8,128)(2,1)S(1)}, bf16[64,1024]{1,0:T(8,128)(2,1)S(1)}, u32[]{:S(2)}, u32[]{:S(2)}) collective-permute-start(bf16[64,1024]{1,0:T(8,128)(2,1)S(1)} %get-tuple-element.75), channel_id=1, source_target_pairs={{6,0},{56,32},{70,64},{120,96},{7,1},{57,33},{71,65},{121,97},{0,2... | collective-permute-start | bytes 393224 | tf_op jit(solution)/shard_map/ppermute | solution.py:493
  32.1 16.5 %collective-permute-start.4 = (bf16[64,1024]{1,0:T(8,128)(2,1)S(1)}, bf16[64,1024]{1,0:T(8,128)(2,1)S(1)}, u32[]{:S(2)}, u32[]{:S(2)}) collective-permute-start(bf16[64,1024]{1,0:T(8,128)(2,1)S(1)} %get-tuple-element.76), channel_id=1, source_target_pairs={{2,0},{40,32},{66,64},{104,96},{3,1},{41,33},{67,65},{105,97},{4,2... | collective-permute-start | bytes 393224 | tf_op jit(solution)/shard_map/ppermute | solution.py:493
  33.9 15.0 %collective-permute-start.5 = (bf16[64,1024]{1,0:T(8,128)(2,1)S(1)}, bf16[64,1024]{1,0:T(8,128)(2,1)S(1)}, u32[]{:S(2)}, u32[]{:S(2)}) collective-permute-start(bf16[64,1024]{1,0:T(8,128)(2,1)S(1)} %get-tuple-element.77), channel_id=1, source_target_pairs={{4,0},{48,32},{68,64},{112,96},{5,1},{49,33},{69,65},{113,97},{6,2... | collective-permute-start | bytes 393224 | tf_op jit(solution)/shard_map/ppermute | solution.py:493
  50.6 6.2 %collective-permute-start.6 = (bf16[64,1024]{1,0:T(8,128)(2,1)S(1)}, bf16[64,1024]{1,0:T(8,128)(2,1)S(1)}, u32[]{:S(2)}, u32[]{:S(2)}) collective-permute-start(bf16[64,1024]{1,0:T(8,128)(2,1)S(1)} %pick_second.1.refs_0_), channel_id=1, source_target_pairs={{65,0},{97,32},{0,64},{32,96},{64,1},{96,33},{1,65},{33,97},{67,2}... | collective-permute-start | bytes 393224 | tf_op jit(solution)/shard_map/ppermute | solution.py:493
  50.9 7.7 %collective-permute-start.7 = (bf16[64,1024]{1,0:T(8,128)(2,1)S(1)}, bf16[64,1024]{1,0:T(8,128)(2,1)S(1)}, u32[]{:S(2)}, u32[]{:S(2)}) collective-permute-start(bf16[64,1024]{1,0:T(8,128)(2,1)S(1)} %pick_second.1.refs_0_), channel_id=1, source_target_pairs={{64,0},{96,32},{1,64},{33,96},{65,1},{97,33},{0,65},{32,97},{66,2}... | collective-permute-start | bytes 393224 | tf_op jit(solution)/shard_map/ppermute | solution.py:493
  53.3 5.7 %collective-permute-start.8 = (bf16[64,1024]{1,0:T(8,128)(2,1)S(1)}, bf16[64,1024]{1,0:T(8,128)(2,1)S(1)}, u32[]{:S(2)}, u32[]{:S(2)}) collective-permute-start(bf16[64,1024]{1,0:T(8,128)(2,1)S(1)} %pick_second.1.refs_0_), channel_id=1, source_target_pairs={{1,0},{33,32},{65,64},{97,96},{0,1},{32,33},{64,65},{96,97},{3,2},... | collective-permute-start | bytes 393224 | tf_op jit(solution)/shard_map/ppermute | solution.py:493
  59.1 0.7 copy-start.3
  59.7 42.5 %all-to-all-start.1 = ((bf16[128,16,512]{2,1,0:T(8,128)(2,1)}), bf16[128,16,512]{2,1,0:T(8,128)(2,1)S(1)}, u32[]{:S(2)}, u32[]{:S(2)}) async-start(bf16[128,16,512]{2,1,0:T(8,128)(2,1)} %spectra.3), calls=%async_computation.1 | async-start | bytes 4194304 | tf_op jit(solution)/shard_map/all_to_all | solution.py:505
  67.9 0.9 copy-start.4
  69.6 2.1 %collective-permute-start.9 = (bf16[64,1024]{1,0:T(8,128)(2,1)S(1)}, bf16[64,1024]{1,0:T(8,128)(2,1)S(1)}, u32[]{:S(2)}, u32[]{:S(2)}) collective-permute-start(bf16[64,1024]{1,0:T(8,128)(2,1)S(1)} %get-tuple-element.92), channel_id=1, source_target_pairs={{0,32},{32,0},{64,96},{96,64},{1,33},{33,1},{65,97},{97,65},{2,34}... | collective-permute-start | bytes 393224 | tf_op jit(solution)/shard_map/ppermute | solution.py:525
  71.7 26.6 %collective-permute-start.10 = (bf16[64,2048]{1,0:T(8,128)(2,1)S(1)}, bf16[64,2048]{1,0:T(8,128)(2,1)S(1)}, u32[]{:S(2)}, u32[]{:S(2)}) collective-permute-start(bf16[64,2048]{1,0:T(8,128)(2,1)S(1)} %join.2.refs_0_), channel_id=1, source_target_pairs={{6,0},{56,32},{70,64},{120,96},{7,1},{57,33},{71,65},{121,97},{0,2... | collective-permute-start | bytes 786440 | tf_op jit(solution)/shard_map/ppermute | solution.py:493
  72.6 25.7 %collective-permute-start.11 = (bf16[64,2048]{1,0:T(8,128)(2,1)S(1)}, bf16[64,2048]{1,0:T(8,128)(2,1)S(1)}, u32[]{:S(2)}, u32[]{:S(2)}) collective-permute-start(bf16[64,2048]{1,0:T(8,128)(2,1)S(1)} %join.2.refs_0_), channel_id=1, source_target_pairs={{2,0},{40,32},{66,64},{104,96},{3,1},{41,33},{67,65},{105,97},{4,2... | collective-permute-start | bytes 786440 | tf_op jit(solution)/shard_map/ppermute | solution.py:493
  74.5 26.7 %collective-permute-start.12 = (bf16[64,2048]{1,0:T(8,128)(2,1)S(1)}, bf16[64,2048]{1,0:T(8,128)(2,1)S(1)}, u32[]{:S(2)}, u32[]{:S(2)}) collective-permute-start(bf16[64,2048]{1,0:T(8,128)(2,1)S(1)} %join.2.refs_0_), channel_id=1, source_target_pairs={{4,0},{48,32},{68,64},{112,96},{5,1},{49,33},{69,65},{113,97},{6,2... | collective-permute-start | bytes 786440 | tf_op jit(solution)/shard_map/ppermute | solution.py:493
  101.2 28.5 %copy-start.5 = (f32[64,384]{1,0:T(8,128)S(1)}, f32[64,384]{1,0:T(8,128)}, u32[]{:S(2)}) copy-start(f32[64,384]{1,0:T(8,128)} %constant.31.clone.choose) | copy-start | bytes 294916
  101.2 1.0 copy-start
  102.2 15.2 %collective-permute-start.13 = (bf16[256,2048]{1,0:T(8,128)(2,1)}, bf16[256,2048]{1,0:T(8,128)(2,1)}, u32[]{:S(2)}, u32[]{:S(2)}) collective-permute-start(bf16[256,2048]{1,0:T(8,128)(2,1)} %copy-done), channel_id=1, source_target_pairs={{24,0},{38,32},{88,64},{102,96},{25,1},{39,33},{89,65},{103,97},{2... | collective-permute-start | bytes 3145736 | tf_op jit(solution)/shard_map/ppermute | solution.py:493
  102.5 25.8 %collective-permute-start.14 = (bf16[256,2048]{1,0:T(8,128)(2,1)}, bf16[256,2048]{1,0:T(8,128)(2,1)}, u32[]{:S(2)}, u32[]{:S(2)}) collective-permute-start(bf16[256,2048]{1,0:T(8,128)(2,1)} %copy-done), channel_id=1, source_target_pairs={{8,0},{34,32},{72,64},{98,96},{9,1},{35,33},{73,65},{99,97},{10,2}... | collective-permute-start | bytes 3145736 | tf_op jit(solution)/shard_map/ppermute | solution.py:493
  104.9 24.8 %collective-permute-start.15 = (bf16[256,2048]{1,0:T(8,128)(2,1)}, bf16[256,2048]{1,0:T(8,128)(2,1)}, u32[]{:S(2)}, u32[]{:S(2)}) collective-permute-start(bf16[256,2048]{1,0:T(8,128)(2,1)} %copy-done), channel_id=1, source_target_pairs={{16,0},{36,32},{80,64},{100,96},{17,1},{37,33},{81,65},{101,97},{1... | collective-permute-start | bytes 3145736 | tf_op jit(solution)/shard_map/ppermute | solution.py:493
  117.4 1.2 copy-start.1
  134.0 1.4 %collective-permute-start.16 = (f32[32,512]{1,0:T(8,128)S(1)}, f32[32,512]{1,0:T(8,128)S(1)}, u32[]{:S(2)}, u32[]{:S(2)}) collective-permute-start(f32[32,512]{1,0:T(8,128)S(1)} %get-tuple-element.98), channel_id=1, source_target_pairs={{0,32},{32,0},{64,96},{96,64},{1,33},{33,1},{65,97},{97,65},{2,34}... | collective-permute-start | bytes 196616 | tf_op jit(solution)/shard_map/ppermute | solution.py:537

commit v5 on v4

--- a/solution.py
+++ b/solution.py
@@ -396,32 +396,31 @@
     ]
 
 
-def early_kernel(w0, w1, za, zb, out):
-    core = lax.axis_index("grp") % 2
-    wide = za.shape[1]
-    for i, part in enumerate((w0, w1)):
-        n = part.shape[0]
-        first, second = products(core, part, (za, zb))
-        out[i * n : (i + 1) * n, :wide] = first
-        out[i * n : (i + 1) * n, wide:] = second
-
-
-def early_of(w0, w1, spectra, interpret=False):
+def early_kernel(*refs):
+    *weights, za, zb, zc, out = refs
+    core, _ = place()
+    rows = jnp.concatenate([w[...] for w in weights], axis=0)
+    for g, result in enumerate(products(core, rows, (za, zb, zc))):
+        out[:, g * 256 : (g + 1) * 256] = result
+
+
+def early_of(weights, spectra, interpret=False):
+    rows = sum(w.shape[0] for w in weights)
     return pl.pallas_call(
         early_kernel,
-        out_shape=jax.ShapeDtypeStruct((2 * w0.shape[0], 768), jnp.float32),
-        in_specs=[pl.BlockSpec(memory_space=pltpu.VMEM)] * 4,
+        out_shape=jax.ShapeDtypeStruct((rows, 768), jnp.float32),
+        in_specs=[pl.BlockSpec(memory_space=pltpu.VMEM)] * 7,
         out_specs=pl.BlockSpec(memory_space=pltpu.VMEM),
-        compiler_params=pltpu.CompilerParams(vmem_limit_bytes=24 * MIB),
+        compiler_params=pltpu.CompilerParams(vmem_limit_bytes=28 * MIB),
         cost_estimate=pl.CostEstimate(flops=17 * 10**8, bytes_accessed=8 * 10**6, transcendentals=0),
         interpret=interpret,
         name="early",
-    )(w0, w1, *spectra)
-
-
-def beams_kernel(early, w2, w3, za, zb, choose, out, sums):
+    )(*weights, *spectra)
+
+
+def beams_kernel(early, *refs):
+    *weights, za, zb, zc, choose, own, given, sums = refs
     core, here = place()
-    wide = za.shape[1]
 
     def row_of(part, k):
         first, y_lo = SHIFTS[k // 2], k % 2
@@ -430,14 +429,12 @@
         x = (here["x"] + jnp.where(core == 0, first, second) + 4) % 4
         return pl.ds(pl.multiple_of(y_lo * 512 + z * 128 + x * 32, 32), 32)
 
-    for part in range(2):
-        for k in range(8):
-            sums[row_of(part, k), :] = early[part * 256 + k * 32 : part * 256 + (k + 1) * 32, :]
-    for part, w in ((2, w2), (3, w3)):
-        first, second = products(core, w, (za, zb))
-        for k in range(8):
-            sums[row_of(part, k), :wide] = first[k * 32 : (k + 1) * 32, :]
-            sums[row_of(part, k), wide:] = second[k * 32 : (k + 1) * 32, :]
+    for k in range(16):
+        sums[row_of(k // 8, k % 8), :] = early[k * 32 : (k + 1) * 32, :]
+    rows = jnp.concatenate([w[...] for w in weights], axis=0)
+    for g, result in enumerate(products(core, rows, (za, zb, zc))):
+        for k in range(16):
+            sums[row_of(2 + k // 8, k % 8), g * 256 : (g + 1) * 256] = result[k * 32 : (k + 1) * 32, :]
     beams = sums.shape[0] // 2
     powers = []
     for g in range(3):
@@ -451,23 +448,24 @@
         (((1,), (1,)), ((), ())),
         preferred_element_type=jnp.float32,
         precision=lax.Precision.HIGHEST,
-    )
-    out[...] = total * (1.0 / SPECTRA)
-
-
-def beams_of(early, w2, w3, spectra, interpret=False):
-    rows = early.shape[0] + 2 * w2.shape[0]
+    ) * (1.0 / SPECTRA)
+    own[...] = jnp.where(core == 0, total[:32], total[32:])
+    given[...] = jnp.where(core == 0, total[32:], total[:32])
+
+
+def beams_of(early, weights, spectra, interpret=False):
+    beams = early.shape[0]
     return pl.pallas_call(
         beams_kernel,
-        out_shape=jax.ShapeDtypeStruct((64, rows // 2), jnp.float32),
-        in_specs=[pl.BlockSpec(memory_space=pltpu.VMEM)] * 6,
-        out_specs=pl.BlockSpec(memory_space=pltpu.VMEM),
-        scratch_shapes=[pltpu.VMEM((rows, 768), jnp.float32)],
-        compiler_params=pltpu.CompilerParams(vmem_limit_bytes=32 * MIB),
+        out_shape=[jax.ShapeDtypeStruct((32, beams), jnp.float32)] * 2,
+        in_specs=[pl.BlockSpec(memory_space=pltpu.VMEM)] * 9,
+        out_specs=[pl.BlockSpec(memory_space=pltpu.VMEM)] * 2,
+        scratch_shapes=[pltpu.VMEM((2 * beams, 768), jnp.float32)],
+        compiler_params=pltpu.CompilerParams(vmem_limit_bytes=28 * MIB),
         cost_estimate=pl.CostEstimate(flops=17 * 10**8, bytes_accessed=8 * 10**6, transcendentals=0),
         interpret=interpret,
         name="beams",
-    )(early, w2, w3, *spectra, jnp.asarray(choose_matrix()))
+    )(early, *weights, *spectra, jnp.asarray(choose_matrix()))
 
 
 def index_of(z, x, y, core):
@@ -515,25 +513,25 @@
     blocks, late, volts = tie((blocks, late, volts))
     blocks = exchange(blocks, 1)
     late = turn(late)
-    (soon,) = spectra_of(((0, 1),), *volts)
-    blocks, soon, late = tie((blocks, soon, late))
+    soon, last = spectra_of(((0,), (1,)), *volts)
+    blocks, soon, last, late = tie((blocks, soon, last, late))
     (block,) = pick_of("second", owners, blocks)
+    block, soon = tie((block, soon))
+    soon = turn(soon)
     blocks = exchange([block] * 4, 2)
-    blocks, soon = tie((blocks, soon))
-    soon = turn(soon)
     mine, other = pick_of("third", owners, blocks)
     other = lax.ppermute(other, "grp", SWAP)
     block = join_of([mine, other], 1)
-    block = join_of(exchange([block] * 4, 3), 0)
-    block, soon = tie((block, soon))
-    parts = exchange([block] * 4, 4)
-
-    spectra = (soon, late)
-    early = early_of(parts[0], parts[1], spectra)
-    power = beams_of(early, parts[2], parts[3], spectra)
-    power = power.reshape(2, 32, -1)
-    own = jnp.where(core == 0, power[0], power[1])
-    given = jnp.where(core == 0, power[1], power[0])
+    near = exchange([block] * 4, 3)
+    first = exchange([block] * 4, 4)
+    block = join_of(near[1:], 0)
+    block, first, last, soon = tie((block, first, last, soon))
+    last = turn(last)
+    second = exchange([block] * 4, 4)
+
+    spectra = (soon, last, late)
+    early = early_of([first[0], second[0], first[1], second[1]], spectra)
+    own, given = beams_of(early, [first[2], second[2], first[3], second[3]], spectra)
     taken = lax.ppermute(given, "grp", SWAP)
     return jnp.where(core == 0, jnp.stack([own, taken]), jnp.stack([taken, own]))
 

time: 137 us -> 149 us (1.088)
  starting transfers between devices: 40.5 us -> 57.9 us
  waiting for transfers between devices: 53.6 us -> 44.5 us
  local copies, waits for them, and re-layouts: 3.78 us -> 7.14 us
    ppermute x15 -> x18, waiting for transfers between devices: 50.7 us -> 41.6 us  [exchange(): lax.ppermute(block, ALL, permutation(stage, shift))]
    ppermute x15 -> x18, starting transfers between devices: 20.6 us -> 28.8 us  [exchange(): lax.ppermute(block, ALL, permutation(stage, shift))]
    all_to_all x2 -> x3, starting transfers between devices: 18.2 us -> 25.8 us  [turn(): lax.all_to_all(message, ALL, split_axis=0, concat_axis=0, tiled=True)]
    unnamed x14 -> x26, local copies, waits for them, and re-layouts: 3.78 us -> 7.14 us
    ppermute x1, starting transfers between devices: 0.47 us -> 2.34 us  [on_device(): taken = lax.ppermute(given, 'grp', SWAP)]
  transfers between devices with their start and end apart: 19 -> 23, of which waited for: 12 -> 12; matrix products, arithmetic and copies ran while one was open for 0% -> 0% of each run, Pallas kernels for 19% -> 17%
where the time goes in v5:
time: 149 us; the launch traced here: 147 us
  starting transfers between devices  57.9 us (39%)
  waiting for transfers between devices  44.5 us (30%)
  Pallas kernels  36.8 us (25%)
  local copies, waits for them, and re-layouts  7.14 us (5%)
    ppermute x18, waiting for transfers between devices, exchange(): lax.ppermute(block, ALL, permutation(stage, shift))  41.6 us
    ppermute x18, starting transfers between devices, exchange(): lax.ppermute(block, ALL, permutation(stage, shift))  28.8 us
    all_to_all x3, starting transfers between devices, turn(): lax.all_to_all(message, ALL, split_axis=0, concat_axis=0, tiled=True)  25.8 us
    pallas_call x2, Pallas kernels, spectra_of(): pl.pallas_call(functools.partial(spectra_kernel, messages), out_shape=[ja...  22.1 us
    unnamed x26, local copies, waits for them, and re-layouts  7.14 us
    pallas_call x1, Pallas kernels, quarter_of(): pl.pallas_call(quarter_kernel, in_specs=[pl.BlockSpec(memory_space=pltpu....  5.61 us
    pallas_call x1, Pallas kernels, beams_of(): pl.pallas_call(beams_kernel, out_shape=[jax.ShapeDtypeStruct((32, beams),...  5.08 us
  transfers between devices with their start and end apart: 23, of which 12 were waited for; matrix products, arithmetic and copies ran while one was open for 0% of the time, Pallas kernels for 17%

profile of v5, /device:TPU:1, one launch (start us, length us, event | category | flops | bytes accessed | tf_op | source)
XLA Modules:
  0.0 147.2 jit_solution(2469622106438020082)
XLA Ops:
  0.0 5.6 %quarter.1 = (bf16[128,1024]{1,0:T(8,128)(2,1)}, bf16[128,1024]{1,0:T(8,128)(2,1)}, bf16[128,1024]{1,0:T(8,128)(2,1)}, bf16[128,1024]{1,0:T(8,128)(2,1)}) custom-call(f32[2048,512]{1,0:T(8,128)} %bitcast.15, f32[2048,512]{1,0:T(8,128)} %bitcast.16, s32[2,1,1024]{2,1,0:T(1,128)} %bitcast.18), custom_call_target="tpu_custom_call" | custom-call | flops 2000000000 | bytes 6000000 | tf_op jit(solution)/shard_map/quarter/pallas_call | solution.py:276
  5.6 0.0 copy-start.12
  5.6 2.1 %collective-permute-start = (bf16[128,1024]{1,0:T(8,128)(2,1)}, bf16[128,1024]{1,0:T(8,128)(2,1)S(1)}, u32[]{:S(2)}, u32[]{:S(2)}) collective-permute-start(bf16[128,1024]{1,0:T(8,128)(2,1)} %get-tuple-element.63), channel_id=1, source_target_pairs={{24,0},{38,32},{88,64},{102,96},{25,1},{39,33},{89,65},{103,97},{2... | collective-permute-start | bytes 786440 | tf_op jit(solution)/shard_map/ppermute | solution.py:491
  7.7 1.4 collective-permute-start.1
  9.1 1.6 %collective-permute-start.2 = (bf16[128,1024]{1,0:T(8,128)(2,1)}, bf16[128,1024]{1,0:T(8,128)(2,1)S(1)}, u32[]{:S(2)}, u32[]{:S(2)}) collective-permute-start(bf16[128,1024]{1,0:T(8,128)(2,1)} %get-tuple-element.65), channel_id=1, source_target_pairs={{16,0},{36,32},{80,64},{100,96},{17,1},{37,33},{81,65},{101,97},{1... | collective-permute-start | bytes 786440 | tf_op jit(solution)/shard_map/ppermute | solution.py:491
  10.7 8.9 %spectra.2 = bf16[128,16,256]{2,1,0:T(8,128)(2,1)} custom-call(bf16[16,110592]{1,0:T(8,128)(2,1)} %refs_0_.1, bf16[16,110592]{1,0:T(8,128)(2,1)} %refs_1_.1, f32[16,4096]{1,0:T(8,128)} %refs_2_.1, f32[32,128]{1,0:T(8,128)} %constant.28.clone.refs_3_, f32[32,128]{1,0:T(8,128)} %constant.29.clone.refs_4_, bf16[256,256]{1,0:T(8,128)(2,1)} %constant.30.clone.refs_5_), custom_call_target="tpu_custom_call" | custom-call | flops 800000000 | bytes 16000000 | tf_op jit(solution)/shard_map/spectra/pallas_call | solution.py:190
  19.6 0.0 collective-permute-done.refs_1_
  19.7 0.0 collective-permute-done.1.refs_2_
  19.7 0.0 collective-permute-done.2.refs_3_
  19.7 0.7 pick_first.1
  20.4 10.1 %all-to-all-start = ((bf16[128,16,256]{2,1,0:T(8,128)(2,1)}), bf16[128,16,256]{2,1,0:T(8,128)(2,1)S(1)}, u32[]{:S(2)}, u32[]{:S(2)}) async-start(bf16[128,16,256]{2,1,0:T(8,128)(2,1)} %spectra.2), calls=%async_computation | async-start | bytes 2097152 | tf_op jit(solution)/shard_map/all_to_all | solution.py:503
  30.5 1.6 %collective-permute-start.3 = (bf16[64,1024]{1,0:T(8,128)(2,1)S(1)}, bf16[64,1024]{1,0:T(8,128)(2,1)S(1)}, u32[]{:S(2)}, u32[]{:S(2)}) collective-permute-start(bf16[64,1024]{1,0:T(8,128)(2,1)S(1)} %get-tuple-element.82), channel_id=1, source_target_pairs={{6,0},{56,32},{70,64},{120,96},{7,1},{57,33},{71,65},{121,97},{0,2... | collective-permute-start | bytes 393224 | tf_op jit(solution)/shard_map/ppermute | solution.py:491
  32.1 1.8 %collective-permute-start.4 = (bf16[64,1024]{1,0:T(8,128)(2,1)S(1)}, bf16[64,1024]{1,0:T(8,128)(2,1)S(1)}, u32[]{:S(2)}, u32[]{:S(2)}) collective-permute-start(bf16[64,1024]{1,0:T(8,128)(2,1)S(1)} %get-tuple-element.83), channel_id=1, source_target_pairs={{2,0},{40,32},{66,64},{104,96},{3,1},{41,33},{67,65},{105,97},{4,2... | collective-permute-start | bytes 393224 | tf_op jit(solution)/shard_map/ppermute | solution.py:491
  33.9 1.4 collective-permute-start.5
  35.3 13.3 %spectra.3 = (bf16[128,16,256]{2,1,0:T(8,128)(2,1)}, bf16[128,16,256]{2,1,0:T(8,128)(2,1)}) custom-call(bf16[16,110592]{1,0:T(8,128)(2,1)} %refs_0_.1, bf16[16,110592]{1,0:T(8,128)(2,1)} %refs_1_.1, f32[16,4096]{1,0:T(8,128)} %refs_2_.1, f32[32,128]{1,0:T(8,128)} %constant.28.clone.refs_3_, f32[32,128]{1,0:T(8,128)} %constant.29.clone.refs_4_, ...), custom_call_target="tpu_custom_call" | custom-call | flops 1600000000 | bytes 32000000 | tf_op jit(solution)/shard_map/spectra/pallas_call | solution.py:190
  48.6 0.0 collective-permute-done.3.refs_1_
  48.6 0.0 collective-permute-done.4.refs_2_
  48.6 0.3 collective-permute-done.5.refs_3_
  48.9 1.0 all-to-all-done
  49.9 0.7 pick_second.1.refs_0_
  50.6 7.5 %all-to-all-start.1 = ((bf16[128,16,256]{2,1,0:T(8,128)(2,1)}), bf16[128,16,256]{2,1,0:T(8,128)(2,1)S(1)}, u32[]{:S(2)}, u32[]{:S(2)}) async-start(bf16[128,16,256]{2,1,0:T(8,128)(2,1)} %get-tuple-element.100), calls=%async_computation.1 | async-start | bytes 2097152 | tf_op jit(solution)/shard_map/all_to_all | solution.py:503
  58.1 1.5 collective-permute-start.6
  59.5 1.3 collective-permute-start.7
  60.9 1.6 %collective-permute-start.8 = (bf16[64,1024]{1,0:T(8,128)(2,1)S(1)}, bf16[64,1024]{1,0:T(8,128)(2,1)S(1)}, u32[]{:S(2)}, u32[]{:S(2)}) collective-permute-start(bf16[64,1024]{1,0:T(8,128)(2,1)S(1)} %pick_second.1.refs_0_), channel_id=1, source_target_pairs={{1,0},{33,32},{65,64},{97,96},{0,1},{32,33},{64,65},{96,97},{3,2},... | collective-permute-start | bytes 393224 | tf_op jit(solution)/shard_map/ppermute | solution.py:491
  62.5 12.5 %collective-permute-done.6.refs_1_ = bf16[64,1024]{1,0:T(8,128)(2,1)S(1)} collective-permute-done((bf16[64,1024]{1,0:T(8,128)(2,1)S(1)}, bf16[64,1024]{1,0:T(8,128)(2,1)S(1)}, u32[]{:S(2)}, u32[]{:S(2)}) %collective-permute-start.6) | collective-permute-done | bytes 131104 | tf_op jit(solution)/shard_map/ppermute | solution.py:491
  75.0 0.0 collective-permute-done.7.refs_2_
  75.0 3.0 %collective-permute-done.8.refs_3_ = bf16[64,1024]{1,0:T(8,128)(2,1)S(1)} collective-permute-done((bf16[64,1024]{1,0:T(8,128)(2,1)S(1)}, bf16[64,1024]{1,0:T(8,128)(2,1)S(1)}, u32[]{:S(2)}, u32[]{:S(2)}) %collective-permute-start.8) | collective-permute-done | bytes 131104 | tf_op jit(solution)/shard_map/ppermute | solution.py:491
  77.9 0.8 pick_third.1
  78.7 1.0 collective-permute-start.9
  79.7 1.0 collective-permute-done.9.refs_1_
  80.7 1.5 %collective-permute-start.10 = (bf16[64,2048]{1,0:T(8,128)(2,1)S(1)}, bf16[64,2048]{1,0:T(8,128)(2,1)S(1)}, u32[]{:S(2)}, u32[]{:S(2)}) collective-permute-start(bf16[64,2048]{1,0:T(8,128)(2,1)S(1)} %join.2.refs_0_), channel_id=1, source_target_pairs={{6,0},{56,32},{70,64},{120,96},{7,1},{57,33},{71,65},{121,97},{0,2... | collective-permute-start | bytes 786440 | tf_op jit(solution)/shard_map/ppermute | solution.py:491
  82.2 1.8 %collective-permute-start.11 = (bf16[64,2048]{1,0:T(8,128)(2,1)S(1)}, bf16[64,2048]{1,0:T(8,128)(2,1)S(1)}, u32[]{:S(2)}, u32[]{:S(2)}) collective-permute-start(bf16[64,2048]{1,0:T(8,128)(2,1)S(1)} %join.2.refs_0_), channel_id=1, source_target_pairs={{2,0},{40,32},{66,64},{104,96},{3,1},{41,33},{67,65},{105,97},{4,2... | collective-permute-start | bytes 786440 | tf_op jit(solution)/shard_map/ppermute | solution.py:491
  84.0 1.4 collective-permute-start.12
  85.4 1.2 collective-permute-start.13
  86.6 1.5 %collective-permute-start.14 = (bf16[64,2048]{1,0:T(8,128)(2,1)S(1)}, bf16[64,2048]{1,0:T(8,128)(2,1)S(1)}, u32[]{:S(2)}, u32[]{:S(2)}) collective-permute-start(bf16[64,2048]{1,0:T(8,128)(2,1)S(1)} %join.2.refs_0_), channel_id=1, source_target_pairs={{8,0},{34,32},{72,64},{98,96},{9,1},{35,33},{73,65},{99,97},{10,2}... | collective-permute-start | bytes 786440 | tf_op jit(solution)/shard_map/ppermute | solution.py:491
  88.1 0.0 collective-permute-done.10.refs_0_
  88.1 2.4 %collective-permute-start.15 = (bf16[64,2048]{1,0:T(8,128)(2,1)S(1)}, bf16[64,2048]{1,0:T(8,128)(2,1)S(1)}, u32[]{:S(2)}, u32[]{:S(2)}) collective-permute-start(bf16[64,2048]{1,0:T(8,128)(2,1)S(1)} %join.2.refs_0_), channel_id=1, source_target_pairs={{16,0},{36,32},{80,64},{100,96},{17,1},{37,33},{81,65},{101,97},{1... | collective-permute-start | bytes 786440 | tf_op jit(solution)/shard_map/ppermute | solution.py:491
  90.5 0.0 collective-permute-done.11.refs_1_
  90.5 1.4 collective-permute-done.12.refs_2_
  92.0 0.1 join.3.refs_1_
  92.0 0.9 copy-done
  92.9 1.9 %collective-permute-done.13.refs_2_ = bf16[64,2048]{1,0:T(8,128)(2,1)S(1)} collective-permute-done((bf16[64,2048]{1,0:T(8,128)(2,1)S(1)}, bf16[64,2048]{1,0:T(8,128)(2,1)S(1)}, u32[]{:S(2)}, u32[]{:S(2)}) %collective-permute-start.13) | collective-permute-done | bytes 262176 | tf_op jit(solution)/shard_map/ppermute | solution.py:491
  94.8 0.7 copy-done.9
  95.5 0.8 collective-permute-done.14.refs_0_
  96.3 0.7 copy-done.5
  96.9 0.7 collective-permute-done.15.refs_2_
  97.6 0.7 copy-done.7
  98.3 0.0 all-to-all-done.1
  98.4 8.2 %all-to-all-start.2 = ((bf16[128,16,256]{2,1,0:T(8,128)(2,1)}), bf16[128,16,256]{2,1,0:T(8,128)(2,1)S(1)}, u32[]{:S(2)}, u32[]{:S(2)}) async-start(bf16[128,16,256]{2,1,0:T(8,128)(2,1)} %get-tuple-element.105), calls=%async_computation.2 | async-start | bytes 2097152 | tf_op jit(solution)/shard_map/all_to_all | solution.py:503
  106.5 1.6 %collective-permute-start.16 = (bf16[192,2048]{1,0:T(8,128)(2,1)}, bf16[192,2048]{1,0:T(8,128)(2,1)S(1)}, u32[]{:S(2)}, u32[]{:S(2)}) collective-permute-start(bf16[192,2048]{1,0:T(8,128)(2,1)} %copy-done), channel_id=1, source_target_pairs={{24,0},{38,32},{88,64},{102,96},{25,1},{39,33},{89,65},{103,97},{2... | collective-permute-start | bytes 2359304 | tf_op jit(solution)/shard_map/ppermute | solution.py:491
  108.2 1.3 collective-permute-start.17
  109.5 1.7 %collective-permute-start.18 = (bf16[192,2048]{1,0:T(8,128)(2,1)}, bf16[192,2048]{1,0:T(8,128)(2,1)}, u32[]{:S(2)}, u32[]{:S(2)}) collective-permute-start(bf16[192,2048]{1,0:T(8,128)(2,1)} %copy-done), channel_id=1, source_target_pairs={{16,0},{36,32},{80,64},{100,96},{17,1},{37,33},{81,65},{101,97},{1... | collective-permute-start | bytes 2359304 | tf_op jit(solution)/shard_map/ppermute | solution.py:491
  111.1 18.2 %collective-permute-done.16.refs_3_ = bf16[192,2048]{1,0:T(8,128)(2,1)S(1)} collective-permute-done((bf16[192,2048]{1,0:T(8,128)(2,1)}, bf16[192,2048]{1,0:T(8,128)(2,1)S(1)}, u32[]{:S(2)}, u32[]{:S(2)}) %collective-permute-start.16) | collective-permute-done | bytes 786464 | tf_op jit(solution)/shard_map/ppermute | solution.py:491
  129.4 0.9 copy-done.2
  130.3 0.0 all-to-all-done.2
  130.3 1.1 copy-done.1
  131.4 1.1 copy-done.3
  132.6 0.9 copy-done.10
  133.5 1.8 %early.1 = f32[512,768]{1,0:T(8,128)S(1)} custom-call(bf16[64,2048]{1,0:T(8,128)(2,1)S(1)} %join.2.refs_0_, bf16[192,2048]{1,0:T(8,128)(2,1)S(1)} %copy-done.1, bf16[64,2048]{1,0:T(8,128)(2,1)S(1)} %copy-done.10, bf16[192,2048]{1,0:T(8,128)(2,1)S(1)} %copy-done.3, bf16[2048,256]{1,0:T(8,128)(2,1)S(1)} %bitcast.10, bf16[2048,256]{1,0:T(8,128)(2,1)S(1)} %bitcast.12, ...), custom_call_target="tpu_custom_call" | custom-call | flops 1700000000 | bytes 8000000 | tf_op jit(solution)/shard_map/early/pallas_call | solution.py:409
  135.3 2.9 %collective-permute-done.18.refs_3_ = bf16[192,2048]{1,0:T(8,128)(2,1)} collective-permute-done((bf16[192,2048]{1,0:T(8,128)(2,1)}, bf16[192,2048]{1,0:T(8,128)(2,1)}, u32[]{:S(2)}, u32[]{:S(2)}) %collective-permute-start.18) | collective-permute-done | bytes 786464 | tf_op jit(solution)/shard_map/ppermute | solution.py:491
  138.2 5.1 %beams.1 = (f32[32,512]{1,0:T(8,128)S(1)}, f32[32,512]{1,0:T(8,128)S(1)}) custom-call(f32[512,768]{1,0:T(8,128)S(1)} %early.1, bf16[64,2048]{1,0:T(8,128)(2,1)S(1)} %copy-done.6, bf16[192,2048]{1,0:T(8,128)(2,1)} %collective-permute-done.17.refs_1_, bf16[64,2048]{1,0:T(8,128)(2,1)S(1)} %copy-done.8, bf16[192,2048]{1,0:T(8,128)(2,1)} %collective-permute-done.18.refs_3_, ...), custom_call_target="tpu_custom_call" | custom-call | flops 1700000000 | bytes 8000000 | tf_op jit(solution)/shard_map/beams/pallas_call | solution.py:458
  143.3 2.3 %collective-permute-start.19 = (f32[32,512]{1,0:T(8,128)S(1)}, f32[32,512]{1,0:T(8,128)S(1)}, u32[]{:S(2)}, u32[]{:S(2)}) collective-permute-start(f32[32,512]{1,0:T(8,128)S(1)} %get-tuple-element.110), channel_id=1, source_target_pairs={{0,32},{32,0},{64,96},{96,64},{1,33},{33,1},{65,97},{97,65},{2,34}... | collective-permute-start | bytes 196616 | tf_op jit(solution)/shard_map/ppermute | solution.py:535
  145.6 0.9 collective-permute-done.19
  146.5 0.7 maximum_select_fusion
  (19 shorter events, 0.1 us)
Async XLA Ops:
  5.6 14.1 %copy-start.4 = (bf16[128,1024]{1,0:T(8,128)(2,1)S(1)}, bf16[128,1024]{1,0:T(8,128)(2,1)}, u32[]{:S(2)}) copy-start(bf16[128,1024]{1,0:T(8,128)(2,1)} %get-tuple-element.69.refs_0_) | copy-start | bytes 786436
  5.6 14.1 %copy-start.12 = (s32[2]{0:T(128)S(1)}, s32[2]{0:T(128)}, u32[]{:S(2)}) copy-start(s32[2]{0:T(128)} %owners.5) | copy-start | bytes 28
  5.6 14.0 %collective-permute-start = (bf16[128,1024]{1,0:T(8,128)(2,1)}, bf16[128,1024]{1,0:T(8,128)(2,1)S(1)}, u32[]{:S(2)}, u32[]{:S(2)}) collective-permute-start(bf16[128,1024]{1,0:T(8,128)(2,1)} %get-tuple-element.63), channel_id=1, source_target_pairs={{24,0},{38,32},{88,64},{102,96},{25,1},{39,33},{89,65},{103,97},{2... | collective-permute-start | bytes 786440 | tf_op jit(solution)/shard_map/ppermute | solution.py:491
  7.7 11.9 %collective-permute-start.1 = (bf16[128,1024]{1,0:T(8,128)(2,1)}, bf16[128,1024]{1,0:T(8,128)(2,1)S(1)}, u32[]{:S(2)}, u32[]{:S(2)}) collective-permute-start(bf16[128,1024]{1,0:T(8,128)(2,1)} %get-tuple-element.64), channel_id=1, source_target_pairs={{8,0},{34,32},{72,64},{98,96},{9,1},{35,33},{73,65},{99,97},{10,2}... | collective-permute-start | bytes 786440 | tf_op jit(solution)/shard_map/ppermute | solution.py:491
  9.1 10.6 %collective-permute-start.2 = (bf16[128,1024]{1,0:T(8,128)(2,1)}, bf16[128,1024]{1,0:T(8,128)(2,1)S(1)}, u32[]{:S(2)}, u32[]{:S(2)}) collective-permute-start(bf16[128,1024]{1,0:T(8,128)(2,1)} %get-tuple-element.65), channel_id=1, source_target_pairs={{16,0},{36,32},{80,64},{100,96},{17,1},{37,33},{81,65},{101,97},{1... | collective-permute-start | bytes 786440 | tf_op jit(solution)/shard_map/ppermute | solution.py:491
  20.4 29.5 %all-to-all-start = ((bf16[128,16,256]{2,1,0:T(8,128)(2,1)}), bf16[128,16,256]{2,1,0:T(8,128)(2,1)S(1)}, u32[]{:S(2)}, u32[]{:S(2)}) async-start(bf16[128,16,256]{2,1,0:T(8,128)(2,1)} %spectra.2), calls=%async_computation | async-start | bytes 2097152 | tf_op jit(solution)/shard_map/all_to_all | solution.py:503
  30.5 18.1 %collective-permute-start.3 = (bf16[64,1024]{1,0:T(8,128)(2,1)S(1)}, bf16[64,1024]{1,0:T(8,128)(2,1)S(1)}, u32[]{:S(2)}, u32[]{:S(2)}) collective-permute-start(bf16[64,1024]{1,0:T(8,128)(2,1)S(1)} %get-tuple-element.82), channel_id=1, source_target_pairs={{6,0},{56,32},{70,64},{120,96},{7,1},{57,33},{71,65},{121,97},{0,2... | collective-permute-start | bytes 393224 | tf_op jit(solution)/shard_map/ppermute | solution.py:491
  32.1 16.5 %collective-permute-start.4 = (bf16[64,1024]{1,0:T(8,128)(2,1)S(1)}, bf16[64,1024]{1,0:T(8,128)(2,1)S(1)}, u32[]{:S(2)}, u32[]{:S(2)}) collective-permute-start(bf16[64,1024]{1,0:T(8,128)(2,1)S(1)} %get-tuple-element.83), channel_id=1, source_target_pairs={{2,0},{40,32},{66,64},{104,96},{3,1},{41,33},{67,65},{105,97},{4,2... | collective-permute-start | bytes 393224 | tf_op jit(solution)/shard_map/ppermute | solution.py:491
  33.9 15.0 %collective-permute-start.5 = (bf16[64,1024]{1,0:T(8,128)(2,1)S(1)}, bf16[64,1024]{1,0:T(8,128)(2,1)S(1)}, u32[]{:S(2)}, u32[]{:S(2)}) collective-permute-start(bf16[64,1024]{1,0:T(8,128)(2,1)S(1)} %get-tuple-element.84), channel_id=1, source_target_pairs={{4,0},{48,32},{68,64},{112,96},{5,1},{49,33},{69,65},{113,97},{6,2... | collective-permute-start | bytes 393224 | tf_op jit(solution)/shard_map/ppermute | solution.py:491
  50.6 47.8 %all-to-all-start.1 = ((bf16[128,16,256]{2,1,0:T(8,128)(2,1)}), bf16[128,16,256]{2,1,0:T(8,128)(2,1)S(1)}, u32[]{:S(2)}, u32[]{:S(2)}) async-start(bf16[128,16,256]{2,1,0:T(8,128)(2,1)} %get-tuple-element.100), calls=%async_computation.1 | async-start | bytes 2097152 | tf_op jit(solution)/shard_map/all_to_all | solution.py:503
  58.1 16.9 %collective-permute-start.6 = (bf16[64,1024]{1,0:T(8,128)(2,1)S(1)}, bf16[64,1024]{1,0:T(8,128)(2,1)S(1)}, u32[]{:S(2)}, u32[]{:S(2)}) collective-permute-start(bf16[64,1024]{1,0:T(8,128)(2,1)S(1)} %pick_second.1.refs_0_), channel_id=1, source_target_pairs={{65,0},{97,32},{0,64},{32,96},{64,1},{96,33},{1,65},{33,97},{67,2}... | collective-permute-start | bytes 393224 | tf_op jit(solution)/shard_map/ppermute | solution.py:491
  59.5 15.4 %collective-permute-start.7 = (bf16[64,1024]{1,0:T(8,128)(2,1)S(1)}, bf16[64,1024]{1,0:T(8,128)(2,1)S(1)}, u32[]{:S(2)}, u32[]{:S(2)}) collective-permute-start(bf16[64,1024]{1,0:T(8,128)(2,1)S(1)} %pick_second.1.refs_0_), channel_id=1, source_target_pairs={{64,0},{96,32},{1,64},{33,96},{65,1},{97,33},{0,65},{32,97},{66,2}... | collective-permute-start | bytes 393224 | tf_op jit(solution)/shard_map/ppermute | solution.py:491
  60.9 17.1 %collective-permute-start.8 = (bf16[64,1024]{1,0:T(8,128)(2,1)S(1)}, bf16[64,1024]{1,0:T(8,128)(2,1)S(1)}, u32[]{:S(2)}, u32[]{:S(2)}) collective-permute-start(bf16[64,1024]{1,0:T(8,128)(2,1)S(1)} %pick_second.1.refs_0_), channel_id=1, source_target_pairs={{1,0},{33,32},{65,64},{97,96},{0,1},{32,33},{64,65},{96,97},{3,2},... | collective-permute-start | bytes 393224 | tf_op jit(solution)/shard_map/ppermute | solution.py:491
  78.7 1.9 %collective-permute-start.9 = (bf16[64,1024]{1,0:T(8,128)(2,1)S(1)}, bf16[64,1024]{1,0:T(8,128)(2,1)S(1)}, u32[]{:S(2)}, u32[]{:S(2)}) collective-permute-start(bf16[64,1024]{1,0:T(8,128)(2,1)S(1)} %get-tuple-element.98), channel_id=1, source_target_pairs={{0,32},{32,0},{64,96},{96,64},{1,33},{33,1},{65,97},{97,65},{2,34}... | collective-permute-start | bytes 393224 | tf_op jit(solution)/shard_map/ppermute | solution.py:523
  80.7 7.4 %collective-permute-start.10 = (bf16[64,2048]{1,0:T(8,128)(2,1)S(1)}, bf16[64,2048]{1,0:T(8,128)(2,1)S(1)}, u32[]{:S(2)}, u32[]{:S(2)}) collective-permute-start(bf16[64,2048]{1,0:T(8,128)(2,1)S(1)} %join.2.refs_0_), channel_id=1, source_target_pairs={{6,0},{56,32},{70,64},{120,96},{7,1},{57,33},{71,65},{121,97},{0,2... | collective-permute-start | bytes 786440 | tf_op jit(solution)/shard_map/ppermute | solution.py:491
  82.2 8.4 %collective-permute-start.11 = (bf16[64,2048]{1,0:T(8,128)(2,1)S(1)}, bf16[64,2048]{1,0:T(8,128)(2,1)S(1)}, u32[]{:S(2)}, u32[]{:S(2)}) collective-permute-start(bf16[64,2048]{1,0:T(8,128)(2,1)S(1)} %join.2.refs_0_), channel_id=1, source_target_pairs={{2,0},{40,32},{66,64},{104,96},{3,1},{41,33},{67,65},{105,97},{4,2... | collective-permute-start | bytes 786440 | tf_op jit(solution)/shard_map/ppermute | solution.py:491
  84.0 8.0 %collective-permute-start.12 = (bf16[64,2048]{1,0:T(8,128)(2,1)S(1)}, bf16[64,2048]{1,0:T(8,128)(2,1)S(1)}, u32[]{:S(2)}, u32[]{:S(2)}) collective-permute-start(bf16[64,2048]{1,0:T(8,128)(2,1)S(1)} %join.2.refs_0_), channel_id=1, source_target_pairs={{4,0},{48,32},{68,64},{112,96},{5,1},{49,33},{69,65},{113,97},{6,2... | collective-permute-start | bytes 786440 | tf_op jit(solution)/shard_map/ppermute | solution.py:491
  85.4 9.4 %collective-permute-start.13 = (bf16[64,2048]{1,0:T(8,128)(2,1)S(1)}, bf16[64,2048]{1,0:T(8,128)(2,1)S(1)}, u32[]{:S(2)}, u32[]{:S(2)}) collective-permute-start(bf16[64,2048]{1,0:T(8,128)(2,1)S(1)} %join.2.refs_0_), channel_id=1, source_target_pairs={{24,0},{38,32},{88,64},{102,96},{25,1},{39,33},{89,65},{103,97},{2... | collective-permute-start | bytes 786440 | tf_op jit(solution)/shard_map/ppermute | solution.py:491
  86.6 9.6 %collective-permute-start.14 = (bf16[64,2048]{1,0:T(8,128)(2,1)S(1)}, bf16[64,2048]{1,0:T(8,128)(2,1)S(1)}, u32[]{:S(2)}, u32[]{:S(2)}) collective-permute-start(bf16[64,2048]{1,0:T(8,128)(2,1)S(1)} %join.2.refs_0_), channel_id=1, source_target_pairs={{8,0},{34,32},{72,64},{98,96},{9,1},{35,33},{73,65},{99,97},{10,2}... | collective-permute-start | bytes 786440 | tf_op jit(solution)/shard_map/ppermute | solution.py:491
  88.1 9.6 %collective-permute-start.15 = (bf16[64,2048]{1,0:T(8,128)(2,1)S(1)}, bf16[64,2048]{1,0:T(8,128)(2,1)S(1)}, u32[]{:S(2)}, u32[]{:S(2)}) collective-permute-start(bf16[64,2048]{1,0:T(8,128)(2,1)S(1)} %join.2.refs_0_), channel_id=1, source_target_pairs={{16,0},{36,32},{80,64},{100,96},{17,1},{37,33},{81,65},{101,97},{1... | collective-permute-start | bytes 786440 | tf_op jit(solution)/shard_map/ppermute | solution.py:491
  92.0 0.9 copy-start
  94.8 0.7 copy-start.9
  96.3 0.7 copy-start.5
  97.6 0.7 copy-start.7
  98.4 39.8 %copy-start.11 = (f32[64,384]{1,0:T(8,128)S(1)}, f32[64,384]{1,0:T(8,128)}, u32[]{:S(2)}) copy-start(f32[64,384]{1,0:T(8,128)} %constant.31.clone.refs_7_) | copy-start | bytes 294916
  98.4 31.9 %all-to-all-start.2 = ((bf16[128,16,256]{2,1,0:T(8,128)(2,1)}), bf16[128,16,256]{2,1,0:T(8,128)(2,1)S(1)}, u32[]{:S(2)}, u32[]{:S(2)}) async-start(bf16[128,16,256]{2,1,0:T(8,128)(2,1)} %get-tuple-element.105), calls=%async_computation.2 | async-start | bytes 2097152 | tf_op jit(solution)/shard_map/all_to_all | solution.py:503
  106.5 22.8 %collective-permute-start.16 = (bf16[192,2048]{1,0:T(8,128)(2,1)}, bf16[192,2048]{1,0:T(8,128)(2,1)S(1)}, u32[]{:S(2)}, u32[]{:S(2)}) collective-permute-start(bf16[192,2048]{1,0:T(8,128)(2,1)} %copy-done), channel_id=1, source_target_pairs={{24,0},{38,32},{88,64},{102,96},{25,1},{39,33},{89,65},{103,97},{2... | collective-permute-start | bytes 2359304 | tf_op jit(solution)/shard_map/ppermute | solution.py:491
  108.2 27.1 %collective-permute-start.17 = (bf16[192,2048]{1,0:T(8,128)(2,1)}, bf16[192,2048]{1,0:T(8,128)(2,1)}, u32[]{:S(2)}, u32[]{:S(2)}) collective-permute-start(bf16[192,2048]{1,0:T(8,128)(2,1)} %copy-done), channel_id=1, source_target_pairs={{8,0},{34,32},{72,64},{98,96},{9,1},{35,33},{73,65},{99,97},{10,2}... | collective-permute-start | bytes 2359304 | tf_op jit(solution)/shard_map/ppermute | solution.py:491
  109.5 28.7 %collective-permute-start.18 = (bf16[192,2048]{1,0:T(8,128)(2,1)}, bf16[192,2048]{1,0:T(8,128)(2,1)}, u32[]{:S(2)}, u32[]{:S(2)}) collective-permute-start(bf16[192,2048]{1,0:T(8,128)(2,1)} %copy-done), channel_id=1, source_target_pairs={{16,0},{36,32},{80,64},{100,96},{17,1},{37,33},{81,65},{101,97},{1... | collective-permute-start | bytes 2359304 | tf_op jit(solution)/shard_map/ppermute | solution.py:491
  129.4 0.9 copy-start.2
  130.3 1.1 copy-start.1
  131.4 1.1 copy-start.3
  132.6 0.9 copy-start.10
  133.5 4.7 %copy-start.6 = (bf16[64,2048]{1,0:T(8,128)(2,1)S(1)}, bf16[64,2048]{1,0:T(8,128)(2,1)}, u32[]{:S(2)}) copy-start(bf16[64,2048]{1,0:T(8,128)(2,1)} %copy-done.5) | copy-start | bytes 786436
  133.5 4.7 %copy-start.8 = (bf16[64,2048]{1,0:T(8,128)(2,1)S(1)}, bf16[64,2048]{1,0:T(8,128)(2,1)}, u32[]{:S(2)}) copy-start(bf16[64,2048]{1,0:T(8,128)(2,1)} %copy-done.7) | copy-start | bytes 786436
  143.3 3.2 %collective-permute-start.19 = (f32[32,512]{1,0:T(8,128)S(1)}, f32[32,512]{1,0:T(8,128)S(1)}, u32[]{:S(2)}, u32[]{:S(2)}) collective-permute-start(f32[32,512]{1,0:T(8,128)S(1)} %get-tuple-element.110), channel_id=1, source_target_pairs={{0,32},{32,0},{64,96},{96,64},{1,33},{33,1},{65,97},{97,65},{2,34}... | collective-permute-start | bytes 196616 | tf_op jit(solution)/shard_map/ppermute | solution.py:535

commit v6 on v4

--- a/solution.py
+++ b/solution.py
@@ -519,13 +519,12 @@
     blocks, soon, late = tie((blocks, soon, late))
     (block,) = pick_of("second", owners, blocks)
     blocks = exchange([block] * 4, 2)
-    blocks, soon = tie((blocks, soon))
-    soon = turn(soon)
     mine, other = pick_of("third", owners, blocks)
     other = lax.ppermute(other, "grp", SWAP)
     block = join_of([mine, other], 1)
     block = join_of(exchange([block] * 4, 3), 0)
     block, soon = tie((block, soon))
+    soon = turn(soon)
     parts = exchange([block] * 4, 4)
 
     spectra = (soon, late)

time: 137 us -> 139 us (1.015)
  starting transfers between devices: 40.5 us -> 42.9 us
  local copies, waits for them, and re-layouts: 3.78 us -> 2.22 us
  waiting for transfers between devices: 53.6 us -> 55 us
    unnamed x14 -> x10, local copies, waits for them, and re-layouts: 3.78 us -> 2.22 us
    ppermute x1, starting transfers between devices: 0.47 us -> 1.94 us  [on_device(): taken = lax.ppermute(given, 'grp', SWAP)]
  transfers between devices with their start and end apart: 19 -> 19, of which waited for: 12 -> 12; matrix products, arithmetic and copies ran while one was open for 0% -> 0% of each run, Pallas kernels for 19% -> 18%
where the time goes in v6:
time: 139 us; the launch traced here: 138 us
  waiting for transfers between devices  55 us (40%)
  starting transfers between devices  42.9 us (31%)
  Pallas kernels  37.3 us (27%)
  local copies, waits for them, and re-layouts  2.22 us (2%)
    ppermute x15, waiting for transfers between devices, exchange(): lax.ppermute(block, ALL, permutation(stage, shift))  52.1 us
    pallas_call x2, Pallas kernels, spectra_of(): pl.pallas_call(functools.partial(spectra_kernel, messages), out_shape=[ja...  22.2 us
    ppermute x15, starting transfers between devices, exchange(): lax.ppermute(block, ALL, permutation(stage, shift))  21.3 us
    all_to_all x2, starting transfers between devices, turn(): lax.all_to_all(message, ALL, split_axis=0, concat_axis=0, tiled=True)  18 us
    pallas_call x1, Pallas kernels, quarter_of(): pl.pallas_call(quarter_kernel, in_specs=[pl.BlockSpec(memory_space=pltpu....  5.61 us
    pallas_call x1, Pallas kernels, beams_of(): pl.pallas_call(beams_kernel, out_shape=jax.ShapeDtypeStruct((64, rows //...  4.32 us
    pallas_call x1, Pallas kernels, early_of(): pl.pallas_call(early_kernel, out_shape=jax.ShapeDtypeStruct((2 * w0.shape...  3.01 us
  transfers between devices with their start and end apart: 19, of which 12 were waited for; matrix products, arithmetic and copies ran while one was open for 0% of the time, Pallas kernels for 18%

profile of v6, /device:TPU:1, one launch (start us, length us, event | category | flops | bytes accessed | tf_op | source)
XLA Modules:
  0.0 138.3 jit_solution(13407677229540882116)
XLA Ops:
  0.0 5.6 %quarter.1 = (bf16[128,1024]{1,0:T(8,128)(2,1)}, bf16[128,1024]{1,0:T(8,128)(2,1)}, bf16[128,1024]{1,0:T(8,128)(2,1)}, bf16[128,1024]{1,0:T(8,128)(2,1)}) custom-call(f32[2048,512]{1,0:T(8,128)} %bitcast.12, f32[2048,512]{1,0:T(8,128)} %bitcast.13, s32[2,1,1024]{2,1,0:T(1,128)} %bitcast.15), custom_call_target="tpu_custom_call" | custom-call | flops 2000000000 | bytes 6000000 | tf_op jit(solution)/shard_map/quarter/pallas_call | solution.py:276
  5.6 0.0 copy-start.2
  5.6 0.0 copy-start.4
  5.6 2.1 %collective-permute-start = (bf16[128,1024]{1,0:T(8,128)(2,1)}, bf16[128,1024]{1,0:T(8,128)(2,1)S(1)}, u32[]{:S(2)}, u32[]{:S(2)}) collective-permute-start(bf16[128,1024]{1,0:T(8,128)(2,1)} %get-tuple-element.51), channel_id=1, source_target_pairs={{24,0},{38,32},{88,64},{102,96},{25,1},{39,33},{89,65},{103,97},{2... | collective-permute-start | bytes 786440 | tf_op jit(solution)/shard_map/ppermute | solution.py:493
  7.7 1.4 collective-permute-start.1
  9.1 1.6 %collective-permute-start.2 = (bf16[128,1024]{1,0:T(8,128)(2,1)}, bf16[128,1024]{1,0:T(8,128)(2,1)S(1)}, u32[]{:S(2)}, u32[]{:S(2)}) collective-permute-start(bf16[128,1024]{1,0:T(8,128)(2,1)} %get-tuple-element.53), channel_id=1, source_target_pairs={{16,0},{36,32},{80,64},{100,96},{17,1},{37,33},{81,65},{101,97},{1... | collective-permute-start | bytes 786440 | tf_op jit(solution)/shard_map/ppermute | solution.py:493
  10.8 8.9 %spectra.2 = bf16[128,16,256]{2,1,0:T(8,128)(2,1)} custom-call(bf16[16,110592]{1,0:T(8,128)(2,1)} %refs_0_.1, bf16[16,110592]{1,0:T(8,128)(2,1)} %refs_1_.1, f32[16,4096]{1,0:T(8,128)} %refs_2_.1, f32[32,128]{1,0:T(8,128)} %constant.28.clone.refs_3_, f32[32,128]{1,0:T(8,128)} %constant.29.clone.refs_4_, bf16[256,256]{1,0:T(8,128)(2,1)} %constant.30.clone.refs_5_), custom_call_target="tpu_custom_call" | custom-call | flops 800000000 | bytes 16000000 | tf_op jit(solution)/shard_map/spectra/pallas_call | solution.py:190
  19.7 0.0 collective-permute-done.refs_1_
  19.7 0.0 collective-permute-done.1.refs_2_
  19.7 0.0 collective-permute-done.2.refs_3_
  19.7 0.0 copy-done.2
  19.7 0.0 copy-done.4
  19.7 0.7 pick_first.1
  20.4 10.1 %all-to-all-start = ((bf16[128,16,256]{2,1,0:T(8,128)(2,1)}), bf16[128,16,256]{2,1,0:T(8,128)(2,1)S(1)}, u32[]{:S(2)}, u32[]{:S(2)}) async-start(bf16[128,16,256]{2,1,0:T(8,128)(2,1)} %spectra.2), calls=%async_computation | async-start | bytes 2097152 | tf_op jit(solution)/shard_map/all_to_all | solution.py:505
  30.5 1.6 %collective-permute-start.3 = (bf16[64,1024]{1,0:T(8,128)(2,1)S(1)}, bf16[64,1024]{1,0:T(8,128)(2,1)S(1)}, u32[]{:S(2)}, u32[]{:S(2)}) collective-permute-start(bf16[64,1024]{1,0:T(8,128)(2,1)S(1)} %get-tuple-element.70), channel_id=1, source_target_pairs={{6,0},{56,32},{70,64},{120,96},{7,1},{57,33},{71,65},{121,97},{0,2... | collective-permute-start | bytes 393224 | tf_op jit(solution)/shard_map/ppermute | solution.py:493
  32.1 1.8 %collective-permute-start.4 = (bf16[64,1024]{1,0:T(8,128)(2,1)S(1)}, bf16[64,1024]{1,0:T(8,128)(2,1)S(1)}, u32[]{:S(2)}, u32[]{:S(2)}) collective-permute-start(bf16[64,1024]{1,0:T(8,128)(2,1)S(1)} %get-tuple-element.71), channel_id=1, source_target_pairs={{2,0},{40,32},{66,64},{104,96},{3,1},{41,33},{67,65},{105,97},{4,2... | collective-permute-start | bytes 393224 | tf_op jit(solution)/shard_map/ppermute | solution.py:493
  33.9 1.4 %collective-permute-start.5 = (bf16[64,1024]{1,0:T(8,128)(2,1)S(1)}, bf16[64,1024]{1,0:T(8,128)(2,1)S(1)}, u32[]{:S(2)}, u32[]{:S(2)}) collective-permute-start(bf16[64,1024]{1,0:T(8,128)(2,1)S(1)} %get-tuple-element.72), channel_id=1, source_target_pairs={{4,0},{48,32},{68,64},{112,96},{5,1},{49,33},{69,65},{113,97},{6,2... | collective-permute-start | bytes 393224 | tf_op jit(solution)/shard_map/ppermute | solution.py:493
  35.3 13.3 %spectra.3 = bf16[128,16,512]{2,1,0:T(8,128)(2,1)} custom-call(bf16[16,110592]{1,0:T(8,128)(2,1)} %refs_0_.1, bf16[16,110592]{1,0:T(8,128)(2,1)} %refs_1_.1, f32[16,4096]{1,0:T(8,128)} %refs_2_.1, f32[32,128]{1,0:T(8,128)} %constant.28.clone.refs_3_, f32[32,128]{1,0:T(8,128)} %constant.29.clone.refs_4_, bf16[256,256]{1,0:T(8,128)(2,1)} %constant.30.clone.refs_5_), custom_call_target="tpu_custom_call" | custom-call | flops 1600000000 | bytes 32000000 | tf_op jit(solution)/shard_map/spectra/pallas_call | solution.py:190
  48.6 0.0 collective-permute-done.3.refs_1_
  48.6 0.0 collective-permute-done.4.refs_2_
  48.6 0.3 collective-permute-done.5.refs_3_
  48.9 1.0 all-to-all-done
  49.9 0.7 pick_second.1.refs_0_
  50.6 0.3 collective-permute-start.6
  50.9 2.4 %collective-permute-start.7 = (bf16[64,1024]{1,0:T(8,128)(2,1)S(1)}, bf16[64,1024]{1,0:T(8,128)(2,1)S(1)}, u32[]{:S(2)}, u32[]{:S(2)}) collective-permute-start(bf16[64,1024]{1,0:T(8,128)(2,1)S(1)} %pick_second.1.refs_0_), channel_id=1, source_target_pairs={{64,0},{96,32},{1,64},{33,96},{65,1},{97,33},{0,65},{32,97},{66,2}... | collective-permute-start | bytes 393224 | tf_op jit(solution)/shard_map/ppermute | solution.py:493
  53.3 0.4 collective-permute-start.8
  53.7 3.1 %collective-permute-done.6.refs_1_ = bf16[64,1024]{1,0:T(8,128)(2,1)S(1)} collective-permute-done((bf16[64,1024]{1,0:T(8,128)(2,1)S(1)}, bf16[64,1024]{1,0:T(8,128)(2,1)S(1)}, u32[]{:S(2)}, u32[]{:S(2)}) %collective-permute-start.6) | collective-permute-done | bytes 131104 | tf_op jit(solution)/shard_map/ppermute | solution.py:493
  56.8 1.9 %collective-permute-done.7.refs_2_ = bf16[64,1024]{1,0:T(8,128)(2,1)S(1)} collective-permute-done((bf16[64,1024]{1,0:T(8,128)(2,1)S(1)}, bf16[64,1024]{1,0:T(8,128)(2,1)S(1)}, u32[]{:S(2)}, u32[]{:S(2)}) %collective-permute-start.7) | collective-permute-done | bytes 131104 | tf_op jit(solution)/shard_map/ppermute | solution.py:493
  58.6 0.4 collective-permute-done.8.refs_3_
  59.1 0.8 pick_third.1
  59.9 1.7 %collective-permute-start.9 = (bf16[64,1024]{1,0:T(8,128)(2,1)S(1)}, bf16[64,1024]{1,0:T(8,128)(2,1)S(1)}, u32[]{:S(2)}, u32[]{:S(2)}) collective-permute-start(bf16[64,1024]{1,0:T(8,128)(2,1)S(1)} %get-tuple-element.82), channel_id=1, source_target_pairs={{0,32},{32,0},{64,96},{96,64},{1,33},{33,1},{65,97},{97,65},{2,34}... | collective-permute-start | bytes 393224 | tf_op jit(solution)/shard_map/ppermute | solution.py:523
  61.6 1.0 collective-permute-done.9.refs_1_
  62.6 1.0 collective-permute-start.10
  63.6 1.8 %collective-permute-start.11 = (bf16[64,2048]{1,0:T(8,128)(2,1)S(1)}, bf16[64,2048]{1,0:T(8,128)(2,1)S(1)}, u32[]{:S(2)}, u32[]{:S(2)}) collective-permute-start(bf16[64,2048]{1,0:T(8,128)(2,1)S(1)} %join.2.refs_0_), channel_id=1, source_target_pairs={{2,0},{40,32},{66,64},{104,96},{3,1},{41,33},{67,65},{105,97},{4,2... | collective-permute-start | bytes 786440 | tf_op jit(solution)/shard_map/ppermute | solution.py:493
  65.4 1.1 collective-permute-start.12
  66.4 3.0 %collective-permute-done.10.refs_1_ = bf16[64,2048]{1,0:T(8,128)(2,1)S(1)} collective-permute-done((bf16[64,2048]{1,0:T(8,128)(2,1)S(1)}, bf16[64,2048]{1,0:T(8,128)(2,1)S(1)}, u32[]{:S(2)}, u32[]{:S(2)}) %collective-permute-start.10) | collective-permute-done | bytes 262176 | tf_op jit(solution)/shard_map/ppermute | solution.py:493
  69.4 2.1 %collective-permute-done.11.refs_2_ = bf16[64,2048]{1,0:T(8,128)(2,1)S(1)} collective-permute-done((bf16[64,2048]{1,0:T(8,128)(2,1)S(1)}, bf16[64,2048]{1,0:T(8,128)(2,1)S(1)}, u32[]{:S(2)}, u32[]{:S(2)}) %collective-permute-start.11) | collective-permute-done | bytes 262176 | tf_op jit(solution)/shard_map/ppermute | solution.py:493
  71.5 1.5 %collective-permute-done.12.refs_3_ = bf16[64,2048]{1,0:T(8,128)(2,1)S(1)} collective-permute-done((bf16[64,2048]{1,0:T(8,128)(2,1)S(1)}, bf16[64,2048]{1,0:T(8,128)(2,1)S(1)}, u32[]{:S(2)}, u32[]{:S(2)}) %collective-permute-start.12) | collective-permute-done | bytes 262176 | tf_op jit(solution)/shard_map/ppermute | solution.py:493
  73.0 0.1 join.3.w0
  73.0 0.0 copy-start
  73.1 1.0 copy-done
  74.0 0.0 copy-start.3
  74.0 7.9 %all-to-all-start.1 = ((bf16[128,16,512]{2,1,0:T(8,128)(2,1)}), bf16[128,16,512]{2,1,0:T(8,128)(2,1)S(1)}, u32[]{:S(2)}, u32[]{:S(2)}) async-start(bf16[128,16,512]{2,1,0:T(8,128)(2,1)} %spectra.3), calls=%async_computation.1 | async-start | bytes 4194304 | tf_op jit(solution)/shard_map/all_to_all | solution.py:505
  81.9 1.5 %collective-permute-start.13 = (bf16[256,2048]{1,0:T(8,128)(2,1)}, bf16[256,2048]{1,0:T(8,128)(2,1)}, u32[]{:S(2)}, u32[]{:S(2)}) collective-permute-start(bf16[256,2048]{1,0:T(8,128)(2,1)} %copy-done), channel_id=1, source_target_pairs={{24,0},{38,32},{88,64},{102,96},{25,1},{39,33},{89,65},{103,97},{2... | collective-permute-start | bytes 3145736 | tf_op jit(solution)/shard_map/ppermute | solution.py:493
  83.4 1.3 collective-permute-start.14
  84.7 1.7 %collective-permute-start.15 = (bf16[256,2048]{1,0:T(8,128)(2,1)}, bf16[256,2048]{1,0:T(8,128)(2,1)}, u32[]{:S(2)}, u32[]{:S(2)}) collective-permute-start(bf16[256,2048]{1,0:T(8,128)(2,1)} %copy-done), channel_id=1, source_target_pairs={{16,0},{36,32},{80,64},{100,96},{17,1},{37,33},{81,65},{101,97},{1... | collective-permute-start | bytes 3145736 | tf_op jit(solution)/shard_map/ppermute | solution.py:493
  86.4 32.6 %collective-permute-done.13.w1 = bf16[256,2048]{1,0:T(8,128)(2,1)} collective-permute-done((bf16[256,2048]{1,0:T(8,128)(2,1)}, bf16[256,2048]{1,0:T(8,128)(2,1)}, u32[]{:S(2)}, u32[]{:S(2)}) %collective-permute-start.13) | collective-permute-done | bytes 1048608 | tf_op jit(solution)/shard_map/ppermute | solution.py:493
  118.9 0.0 all-to-all-done.1
  118.9 0.0 copy-start.1
  118.9 1.2 copy-done.1
  120.2 3.0 %early.1 = f32[512,768]{1,0:T(8,128)S(1)} custom-call(bf16[256,2048]{1,0:T(8,128)(2,1)S(1)} %copy-done.1, bf16[256,2048]{1,0:T(8,128)(2,1)} %collective-permute-done.13.w1, bf16[2048,512]{1,0:T(8,128)(2,1)S(1)} %bitcast.8, bf16[2048,256]{1,0:T(8,128)(2,1)S(1)} %bitcast.10), custom_call_target="tpu_custom_call" | custom-call | flops 1700000000 | bytes 8000000 | tf_op jit(solution)/shard_map/early/pallas_call | solution.py:410
  123.2 0.0 collective-permute-done.14.w2
  123.2 7.3 %collective-permute-done.15.w3 = bf16[256,2048]{1,0:T(8,128)(2,1)} collective-permute-done((bf16[256,2048]{1,0:T(8,128)(2,1)}, bf16[256,2048]{1,0:T(8,128)(2,1)}, u32[]{:S(2)}, u32[]{:S(2)}) %collective-permute-start.15) | collective-permute-done | bytes 1048608 | tf_op jit(solution)/shard_map/ppermute | solution.py:493
  130.4 0.0 copy-done.3
  130.5 4.3 %beams.1 = f32[64,512]{1,0:T(8,128)S(1)} custom-call(f32[512,768]{1,0:T(8,128)S(1)} %early.1, bf16[256,2048]{1,0:T(8,128)(2,1)} %collective-permute-done.14.w2, bf16[256,2048]{1,0:T(8,128)(2,1)} %collective-permute-done.15.w3, bf16[2048,512]{1,0:T(8,128)(2,1)S(1)} %bitcast.9, bf16[2048,256]{1,0:T(8,128)(2,1)S(1)} %bitcast.11, f32[64,384]{1,0:T(8,128)S(1)} %copy-done.3), custom_call_target="tpu_custom_call" | custom-call | flops 1700000000 | bytes 8000000 | tf_op jit(solution)/shard_map/beams/pallas_call | solution.py:460
  134.8 1.9 %collective-permute-start.16 = (f32[32,512]{1,0:T(8,128)S(1)}, f32[32,512]{1,0:T(8,128)S(1)}, u32[]{:S(2)}, u32[]{:S(2)}) collective-permute-start(f32[32,512]{1,0:T(8,128)S(1)} %get-tuple-element.88), channel_id=1, source_target_pairs={{0,32},{32,0},{64,96},{96,64},{1,33},{33,1},{65,97},{97,65},{2,34}... | collective-permute-start | bytes 196616 | tf_op jit(solution)/shard_map/ppermute | solution.py:536
  136.7 0.9 collective-permute-done.16
  137.6 0.7 maximum_select_fusion
  (2 shorter events, 0.0 us)
Async XLA Ops:
  5.6 14.1 %copy-start.2 = (bf16[128,1024]{1,0:T(8,128)(2,1)S(1)}, bf16[128,1024]{1,0:T(8,128)(2,1)}, u32[]{:S(2)}) copy-start(bf16[128,1024]{1,0:T(8,128)(2,1)} %get-tuple-element.57.refs_0_) | copy-start | bytes 786436
  5.6 14.1 %copy-start.4 = (s32[2]{0:T(128)S(1)}, s32[2]{0:T(128)}, u32[]{:S(2)}) copy-start(s32[2]{0:T(128)} %owners.5) | copy-start | bytes 28
  5.6 14.0 %collective-permute-start = (bf16[128,1024]{1,0:T(8,128)(2,1)}, bf16[128,1024]{1,0:T(8,128)(2,1)S(1)}, u32[]{:S(2)}, u32[]{:S(2)}) collective-permute-start(bf16[128,1024]{1,0:T(8,128)(2,1)} %get-tuple-element.51), channel_id=1, source_target_pairs={{24,0},{38,32},{88,64},{102,96},{25,1},{39,33},{89,65},{103,97},{2... | collective-permute-start | bytes 786440 | tf_op jit(solution)/shard_map/ppermute | solution.py:493
  7.7 11.9 %collective-permute-start.1 = (bf16[128,1024]{1,0:T(8,128)(2,1)}, bf16[128,1024]{1,0:T(8,128)(2,1)S(1)}, u32[]{:S(2)}, u32[]{:S(2)}) collective-permute-start(bf16[128,1024]{1,0:T(8,128)(2,1)} %get-tuple-element.52), channel_id=1, source_target_pairs={{8,0},{34,32},{72,64},{98,96},{9,1},{35,33},{73,65},{99,97},{10,2}... | collective-permute-start | bytes 786440 | tf_op jit(solution)/shard_map/ppermute | solution.py:493
  9.1 10.6 %collective-permute-start.2 = (bf16[128,1024]{1,0:T(8,128)(2,1)}, bf16[128,1024]{1,0:T(8,128)(2,1)S(1)}, u32[]{:S(2)}, u32[]{:S(2)}) collective-permute-start(bf16[128,1024]{1,0:T(8,128)(2,1)} %get-tuple-element.53), channel_id=1, source_target_pairs={{16,0},{36,32},{80,64},{100,96},{17,1},{37,33},{81,65},{101,97},{1... | collective-permute-start | bytes 786440 | tf_op jit(solution)/shard_map/ppermute | solution.py:493
  20.4 29.5 %all-to-all-start = ((bf16[128,16,256]{2,1,0:T(8,128)(2,1)}), bf16[128,16,256]{2,1,0:T(8,128)(2,1)S(1)}, u32[]{:S(2)}, u32[]{:S(2)}) async-start(bf16[128,16,256]{2,1,0:T(8,128)(2,1)} %spectra.2), calls=%async_computation | async-start | bytes 2097152 | tf_op jit(solution)/shard_map/all_to_all | solution.py:505
  30.5 18.1 %collective-permute-start.3 = (bf16[64,1024]{1,0:T(8,128)(2,1)S(1)}, bf16[64,1024]{1,0:T(8,128)(2,1)S(1)}, u32[]{:S(2)}, u32[]{:S(2)}) collective-permute-start(bf16[64,1024]{1,0:T(8,128)(2,1)S(1)} %get-tuple-element.70), channel_id=1, source_target_pairs={{6,0},{56,32},{70,64},{120,96},{7,1},{57,33},{71,65},{121,97},{0,2... | collective-permute-start | bytes 393224 | tf_op jit(solution)/shard_map/ppermute | solution.py:493
  32.1 16.5 %collective-permute-start.4 = (bf16[64,1024]{1,0:T(8,128)(2,1)S(1)}, bf16[64,1024]{1,0:T(8,128)(2,1)S(1)}, u32[]{:S(2)}, u32[]{:S(2)}) collective-permute-start(bf16[64,1024]{1,0:T(8,128)(2,1)S(1)} %get-tuple-element.71), channel_id=1, source_target_pairs={{2,0},{40,32},{66,64},{104,96},{3,1},{41,33},{67,65},{105,97},{4,2... | collective-permute-start | bytes 393224 | tf_op jit(solution)/shard_map/ppermute | solution.py:493
  33.9 15.0 %collective-permute-start.5 = (bf16[64,1024]{1,0:T(8,128)(2,1)S(1)}, bf16[64,1024]{1,0:T(8,128)(2,1)S(1)}, u32[]{:S(2)}, u32[]{:S(2)}) collective-permute-start(bf16[64,1024]{1,0:T(8,128)(2,1)S(1)} %get-tuple-element.72), channel_id=1, source_target_pairs={{4,0},{48,32},{68,64},{112,96},{5,1},{49,33},{69,65},{113,97},{6,2... | collective-permute-start | bytes 393224 | tf_op jit(solution)/shard_map/ppermute | solution.py:493
  50.6 6.2 %collective-permute-start.6 = (bf16[64,1024]{1,0:T(8,128)(2,1)S(1)}, bf16[64,1024]{1,0:T(8,128)(2,1)S(1)}, u32[]{:S(2)}, u32[]{:S(2)}) collective-permute-start(bf16[64,1024]{1,0:T(8,128)(2,1)S(1)} %pick_second.1.refs_0_), channel_id=1, source_target_pairs={{65,0},{97,32},{0,64},{32,96},{64,1},{96,33},{1,65},{33,97},{67,2}... | collective-permute-start | bytes 393224 | tf_op jit(solution)/shard_map/ppermute | solution.py:493
  50.9 7.7 %collective-permute-start.7 = (bf16[64,1024]{1,0:T(8,128)(2,1)S(1)}, bf16[64,1024]{1,0:T(8,128)(2,1)S(1)}, u32[]{:S(2)}, u32[]{:S(2)}) collective-permute-start(bf16[64,1024]{1,0:T(8,128)(2,1)S(1)} %pick_second.1.refs_0_), channel_id=1, source_target_pairs={{64,0},{96,32},{1,64},{33,96},{65,1},{97,33},{0,65},{32,97},{66,2}... | collective-permute-start | bytes 393224 | tf_op jit(solution)/shard_map/ppermute | solution.py:493
  53.3 5.7 %collective-permute-start.8 = (bf16[64,1024]{1,0:T(8,128)(2,1)S(1)}, bf16[64,1024]{1,0:T(8,128)(2,1)S(1)}, u32[]{:S(2)}, u32[]{:S(2)}) collective-permute-start(bf16[64,1024]{1,0:T(8,128)(2,1)S(1)} %pick_second.1.refs_0_), channel_id=1, source_target_pairs={{1,0},{33,32},{65,64},{97,96},{0,1},{32,33},{64,65},{96,97},{3,2},... | collective-permute-start | bytes 393224 | tf_op jit(solution)/shard_map/ppermute | solution.py:493
  59.9 2.7 %collective-permute-start.9 = (bf16[64,1024]{1,0:T(8,128)(2,1)S(1)}, bf16[64,1024]{1,0:T(8,128)(2,1)S(1)}, u32[]{:S(2)}, u32[]{:S(2)}) collective-permute-start(bf16[64,1024]{1,0:T(8,128)(2,1)S(1)} %get-tuple-element.82), channel_id=1, source_target_pairs={{0,32},{32,0},{64,96},{96,64},{1,33},{33,1},{65,97},{97,65},{2,34}... | collective-permute-start | bytes 393224 | tf_op jit(solution)/shard_map/ppermute | solution.py:523
  62.6 6.8 %collective-permute-start.10 = (bf16[64,2048]{1,0:T(8,128)(2,1)S(1)}, bf16[64,2048]{1,0:T(8,128)(2,1)S(1)}, u32[]{:S(2)}, u32[]{:S(2)}) collective-permute-start(bf16[64,2048]{1,0:T(8,128)(2,1)S(1)} %join.2.refs_0_), channel_id=1, source_target_pairs={{6,0},{56,32},{70,64},{120,96},{7,1},{57,33},{71,65},{121,97},{0,2... | collective-permute-start | bytes 786440 | tf_op jit(solution)/shard_map/ppermute | solution.py:493
  63.6 7.9 %collective-permute-start.11 = (bf16[64,2048]{1,0:T(8,128)(2,1)S(1)}, bf16[64,2048]{1,0:T(8,128)(2,1)S(1)}, u32[]{:S(2)}, u32[]{:S(2)}) collective-permute-start(bf16[64,2048]{1,0:T(8,128)(2,1)S(1)} %join.2.refs_0_), channel_id=1, source_target_pairs={{2,0},{40,32},{66,64},{104,96},{3,1},{41,33},{67,65},{105,97},{4,2... | collective-permute-start | bytes 786440 | tf_op jit(solution)/shard_map/ppermute | solution.py:493
  65.4 7.6 %collective-permute-start.12 = (bf16[64,2048]{1,0:T(8,128)(2,1)S(1)}, bf16[64,2048]{1,0:T(8,128)(2,1)S(1)}, u32[]{:S(2)}, u32[]{:S(2)}) collective-permute-start(bf16[64,2048]{1,0:T(8,128)(2,1)S(1)} %join.2.refs_0_), channel_id=1, source_target_pairs={{4,0},{48,32},{68,64},{112,96},{5,1},{49,33},{69,65},{113,97},{6,2... | collective-permute-start | bytes 786440 | tf_op jit(solution)/shard_map/ppermute | solution.py:493
  73.0 1.0 copy-start
  74.0 56.4 %copy-start.3 = (f32[64,384]{1,0:T(8,128)S(1)}, f32[64,384]{1,0:T(8,128)}, u32[]{:S(2)}) copy-start(f32[64,384]{1,0:T(8,128)} %constant.31.clone.choose) | copy-start | bytes 294916
  74.0 44.9 %all-to-all-start.1 = ((bf16[128,16,512]{2,1,0:T(8,128)(2,1)}), bf16[128,16,512]{2,1,0:T(8,128)(2,1)S(1)}, u32[]{:S(2)}, u32[]{:S(2)}) async-start(bf16[128,16,512]{2,1,0:T(8,128)(2,1)} %spectra.3), calls=%async_computation.1 | async-start | bytes 4194304 | tf_op jit(solution)/shard_map/all_to_all | solution.py:505
  81.9 37.0 %collective-permute-start.13 = (bf16[256,2048]{1,0:T(8,128)(2,1)}, bf16[256,2048]{1,0:T(8,128)(2,1)}, u32[]{:S(2)}, u32[]{:S(2)}) collective-permute-start(bf16[256,2048]{1,0:T(8,128)(2,1)} %copy-done), channel_id=1, source_target_pairs={{24,0},{38,32},{88,64},{102,96},{25,1},{39,33},{89,65},{103,97},{2... | collective-permute-start | bytes 3145736 | tf_op jit(solution)/shard_map/ppermute | solution.py:493
  83.4 39.8 %collective-permute-start.14 = (bf16[256,2048]{1,0:T(8,128)(2,1)}, bf16[256,2048]{1,0:T(8,128)(2,1)}, u32[]{:S(2)}, u32[]{:S(2)}) collective-permute-start(bf16[256,2048]{1,0:T(8,128)(2,1)} %copy-done), channel_id=1, source_target_pairs={{8,0},{34,32},{72,64},{98,96},{9,1},{35,33},{73,65},{99,97},{10,2}... | collective-permute-start | bytes 3145736 | tf_op jit(solution)/shard_map/ppermute | solution.py:493
  84.7 45.8 %collective-permute-start.15 = (bf16[256,2048]{1,0:T(8,128)(2,1)}, bf16[256,2048]{1,0:T(8,128)(2,1)}, u32[]{:S(2)}, u32[]{:S(2)}) collective-permute-start(bf16[256,2048]{1,0:T(8,128)(2,1)} %copy-done), channel_id=1, source_target_pairs={{16,0},{36,32},{80,64},{100,96},{17,1},{37,33},{81,65},{101,97},{1... | collective-permute-start | bytes 3145736 | tf_op jit(solution)/shard_map/ppermute | solution.py:493
  118.9 1.2 copy-start.1
  134.8 2.8 %collective-permute-start.16 = (f32[32,512]{1,0:T(8,128)S(1)}, f32[32,512]{1,0:T(8,128)S(1)}, u32[]{:S(2)}, u32[]{:S(2)}) collective-permute-start(f32[32,512]{1,0:T(8,128)S(1)} %get-tuple-element.88), channel_id=1, source_target_pairs={{0,32},{32,0},{64,96},{96,64},{1,33},{33,1},{65,97},{97,65},{2,34}... | collective-permute-start | bytes 196616 | tf_op jit(solution)/shard_map/ppermute | solution.py:536

commit v7 on v3

--- a/solution.py
+++ b/solution.py
@@ -21,7 +21,7 @@
 DEVICES = 128
 ROW_STRIDE = 24
 GROUPS = ((0, 1, 6, 7), (2, 3, 8, 9), (4, 5, 10, 11))
-MESSAGES = ((2,), (0, 1))
+MESSAGES = ((0, 1, 2),)
 ALL = ("grp", "dev")
 MIB = 1 << 20
 
@@ -337,48 +337,41 @@
     near = pl.ds(pl.multiple_of(core * half, half), half)
     far = pl.ds(pl.multiple_of((1 - core) * half, half), half)
     left, right = part[:, :half], part[:, half:]
-    return [
-        jnp.dot(left, z[near, :], preferred_element_type=jnp.float32)
-        + jnp.dot(right, z[far, :], preferred_element_type=jnp.float32)
-        for z in spectra
-    ]
-
-
-def early_kernel(w0, w1, za, zb, out):
+    return jnp.dot(left, spectra[near, :], preferred_element_type=jnp.float32) + jnp.dot(
+        right, spectra[far, :], preferred_element_type=jnp.float32
+    )
+
+
+def early_kernel(w0, w1, za, out):
     core = lax.axis_index("grp") % 2
-    wide = za.shape[1]
+    n = w0.shape[0]
     for i, part in enumerate((w0, w1)):
-        n = part.shape[0]
-        first, second = products(core, part, (za, zb))
-        out[i * n : (i + 1) * n, :wide] = first
-        out[i * n : (i + 1) * n, wide:] = second
+        out[i * n : (i + 1) * n, :] = products(core, part, za)
 
 
 def early_of(w0, w1, spectra, interpret=False):
     return pl.pallas_call(
         early_kernel,
         out_shape=jax.ShapeDtypeStruct((2 * w0.shape[0], 768), jnp.float32),
-        in_specs=[pl.BlockSpec(memory_space=pltpu.VMEM)] * 4,
+        in_specs=[pl.BlockSpec(memory_space=pltpu.VMEM)] * 3,
         out_specs=pl.BlockSpec(memory_space=pltpu.VMEM),
         compiler_params=pltpu.CompilerParams(vmem_limit_bytes=24 * MIB),
         cost_estimate=pl.CostEstimate(flops=17 * 10**8, bytes_accessed=8 * 10**6, transcendentals=0),
         interpret=interpret,
         name="early",
-    )(w0, w1, *spectra)
-
-
-def beams_kernel(places, early, w2, w3, za, zb, choose, out, sums):
+    )(w0, w1, spectra)
+
+
+def beams_kernel(places, early, w2, w3, za, choose, out, sums):
     for k in range(32):
         at = pl.multiple_of(places[k], 16)
         sums[pl.ds(at, 16), :] = early[k * 16 : (k + 1) * 16, :]
     core = lax.axis_index("grp") % 2
-    wide = za.shape[1]
     for i, part in enumerate((w2, w3)):
-        first, second = products(core, part, (za, zb))
+        result = products(core, part, za)
         for k in range(16):
             at = pl.multiple_of(places[(i + 2) * 16 + k], 16)
-            sums[pl.ds(at, 16), :wide] = first[k * 16 : (k + 1) * 16, :]
-            sums[pl.ds(at, 16), wide:] = second[k * 16 : (k + 1) * 16, :]
+            sums[pl.ds(at, 16), :] = result[k * 16 : (k + 1) * 16, :]
     beams = sums.shape[0] // 2
     powers = []
     for g in range(3):
@@ -401,14 +394,14 @@
     return pl.pallas_call(
         beams_kernel,
         out_shape=jax.ShapeDtypeStruct((64, rows // 2), jnp.float32),
-        in_specs=[pl.BlockSpec(memory_space=pltpu.SMEM)] + [pl.BlockSpec(memory_space=pltpu.VMEM)] * 6,
+        in_specs=[pl.BlockSpec(memory_space=pltpu.SMEM)] + [pl.BlockSpec(memory_space=pltpu.VMEM)] * 5,
         out_specs=pl.BlockSpec(memory_space=pltpu.VMEM),
         scratch_shapes=[pltpu.VMEM((rows, 768), jnp.float32)],
         compiler_params=pltpu.CompilerParams(vmem_limit_bytes=32 * MIB),
         cost_estimate=pl.CostEstimate(flops=17 * 10**8, bytes_accessed=8 * 10**6, transcendentals=0),
         interpret=interpret,
         name="beams",
-    )(places, early, w2, w3, *spectra, jnp.asarray(choose_matrix()))
+    )(places, early, w2, w3, spectra, jnp.asarray(choose_matrix()))
 
 
 def index_of(z, x, y, core):
@@ -462,20 +455,15 @@
 
     volts = (voltage_real, voltage_imaginary, filter_taps)
     quarter, *volts = lax.optimization_barrier((quarter, *volts))
-    messages = spectra_of(MESSAGES, *volts)
-
-    def turn(message):
-        moved = lax.all_to_all(message, ALL, split_axis=0, concat_axis=0, tiled=True)
-        return moved.reshape(DEVICES * SLOTS, -1)
-
-    message, offers = lax.optimization_barrier((messages[0], offers))
-    spectra = [turn(message)]
+    (message,) = spectra_of(MESSAGES, *volts)
+    message, offers = lax.optimization_barrier((message, offers))
+    spectra = lax.all_to_all(message, ALL, split_axis=0, concat_axis=0, tiled=True)
+    spectra = spectra.reshape(DEVICES * SLOTS, -1)
+
     mine, other = pick_of(owners, offers)
     other = lax.ppermute(other, "grp", SWAP)
     block = join_of([mine, other], 1)
     block = join_of(gather_stage(block, 0), 0)
-    block, message, spectra[0] = lax.optimization_barrier((block, messages[1], spectra[0]))
-    spectra.append(turn(message))
     block = join_of(gather_stage(block, 1), 0)
     parts = gather_stage(block, 2)
 

time: 137 us -> 132 us (0.964)
  waiting for transfers between devices: 58.1 us -> 55.3 us
  starting transfers between devices: 42.1 us -> 39.7 us
    all_to_all x2 -> x1, starting transfers between devices: 13.9 us -> 9.49 us  [on_device(): lax.all_to_all(message, ALL, split_axis=0, concat_axis=0, tiled=True)]
    all_to_all x2 -> x1, waiting for transfers between devices: 2.34 us -> 0.01 us  [on_device(): lax.all_to_all(message, ALL, split_axis=0, concat_axis=0, tiled=True)]
  transfers between devices with their start and end apart: 14 -> 13, of which waited for: 10 -> 11; matrix products, arithmetic and copies ran while one was open for 0% -> 0% of each run, Pallas kernels for 18% -> 18%
where the time goes in v7:
time: 132 us
  waiting for transfers between devices  55.3 us (42%)
  starting transfers between devices  39.7 us (30%)
  Pallas kernels  34.1 us (26%)
  local copies, waits for them, and re-layouts  1.89 us (1%)
    ppermute x9, waiting for transfers between devices, gather_stage(): lax.ppermute(block, ALL, permutation(stage, shift))  52.8 us
    pallas_call x1, Pallas kernels, spectra_of(): pl.pallas_call(functools.partial(spectra_kernel, messages), out_shape=[ja...  17.7 us
    ppermute x9, starting transfers between devices, gather_stage(): lax.ppermute(block, ALL, permutation(stage, shift))  14.7 us
    all_to_all x1, starting transfers between devices, on_device(): lax.all_to_all(quarter.reshape(32, 16, -1), 'dev', split_axis=0, concat_a...  11.4 us
    all_to_all x1, starting transfers between devices, on_device(): lax.all_to_all(message, ALL, split_axis=0, concat_axis=0, tiled=True)  9.49 us
    pallas_call x1, Pallas kernels, quarter_of(): pl.pallas_call(quarter_kernel, in_specs=[pl.BlockSpec(memory_space=pltpu....  5.56 us
    pallas_call x1, Pallas kernels, beams_of(): pl.pallas_call(beams_kernel, out_shape=jax.ShapeDtypeStruct((64, rows //...  4.33 us
    pallas_call x1, Pallas kernels, early_of(): pl.pallas_call(early_kernel, out_shape=jax.ShapeDtypeStruct((2 * w0.shape...  3.33 us
  transfers between devices with their start and end apart: 13, of which 11 were waited for; matrix products, arithmetic and copies ran while one was open for 0% of the time, Pallas kernels for 18%

profile of v7, /device:TPU:1, one launch (start us, length us, event | category | flops | bytes accessed | tf_op | source)
XLA Modules:
  0.0 131.9 jit_solution(5984061314032363163)
XLA Ops:
  0.0 5.6 %quarter.1 = bf16[512,1024]{1,0:T(8,128)(2,1)} custom-call(f32[2048,512]{1,0:T(8,128)} %bitcast.10, f32[2048,512]{1,0:T(8,128)} %bitcast.11, s32[2,1,1024]{2,1,0:T(1,128)} %bitcast.14), custom_call_target="tpu_custom_call" | custom-call | flops 2000000000 | bytes 6000000 | tf_op jit(solution)/shard_map/quarter/pallas_call | solution.py:257
  5.6 11.4 %all-to-all-start = ((bf16[32,16,1024]{2,1,0:T(8,128)(2,1)}), bf16[32,16,1024]{2,1,0:T(8,128)(2,1)S(1)}, u32[]{:S(2)}, u32[]{:S(2)}) async-start(bf16[32,16,1024]{2,1,0:T(8,128)(2,1)} %bitcast.12), calls=%async_computation | async-start | bytes 2097152 | tf_op jit(solution)/shard_map/all_to_all | solution.py:454
  16.9 17.7 %spectra.1 = bf16[128,16,768]{2,1,0:T(8,128)(2,1)} custom-call(bf16[16,110592]{1,0:T(8,128)(2,1)} %refs_0_, bf16[16,110592]{1,0:T(8,128)(2,1)} %refs_1_, f32[16,4096]{1,0:T(8,128)} %refs_2_, f32[32,128]{1,0:T(8,128)} %constant.121.clone.refs_3_, f32[32,128]{1,0:T(8,128)} %constant.122.clone.refs_4_, bf16[256,256]{1,0:T(8,128)(2,1)} %constant.123.clone.refs_5_), custom_call_target="tpu_custom_call" | custom-call | flops 2400000000 | bytes 48000000 | tf_op jit(solution)/shard_map/spectra/pallas_call | solution.py:190
  34.6 0.5 all-to-all-done.offers
  35.1 0.0 copy-start.2
  35.1 1.0 copy-done.2
  36.0 9.5 %all-to-all-start.1 = ((bf16[128,16,768]{2,1,0:T(8,128)(2,1)}), bf16[128,16,768]{2,1,0:T(8,128)(2,1)S(1)}, u32[]{:S(2)}, u32[]{:S(2)}) async-start(bf16[128,16,768]{2,1,0:T(8,128)(2,1)} %spectra.1), calls=%async_computation.1 | async-start | bytes 6291456 | tf_op jit(solution)/shard_map/all_to_all | solution.py:460
  45.5 0.0 copy-start.3
  45.5 0.0 copy-start.4
  45.6 0.0 copy-start.5
  45.6 2.2 %pick.1 = (bf16[16,1024]{1,0:T(8,128)(2,1)}, bf16[16,1024]{1,0:T(8,128)(2,1)}) custom-call(s32[2]{0:T(128)} %owners.1, bf16[32,16,1024]{2,1,0:T(8,128)(2,1)} %copy-done.2), custom_call_target="tpu_custom_call" | custom-call | tf_op jit(solution)/shard_map/pick/pallas_call | solution.py:289
  47.8 1.1 collective-permute-start
  48.9 1.1 collective-permute-done.refs_1_
  50.0 0.0 copy-start.1
  50.0 0.8 copy-done.1
  50.8 0.8 collective-permute-start.1
  51.6 1.9 %collective-permute-start.2 = (bf16[16,2048]{1,0:T(8,128)(2,1)S(1)}, bf16[16,2048]{1,0:T(8,128)(2,1)S(1)}, u32[]{:S(2)}, u32[]{:S(2)}) collective-permute-start(bf16[16,2048]{1,0:T(8,128)(2,1)S(1)} %join.3.refs_0_), channel_id=1, source_target_pairs={{64,0},{40,32},{1,64},{104,96},{65,1},{41,33},{0,65},{105,97},{66,... | collective-permute-start | bytes 196616 | tf_op jit(solution)/shard_map/ppermute | solution.py:427
  53.5 1.4 %collective-permute-start.3 = (bf16[16,2048]{1,0:T(8,128)(2,1)S(1)}, bf16[16,2048]{1,0:T(8,128)(2,1)S(1)}, u32[]{:S(2)}, u32[]{:S(2)}) collective-permute-start(bf16[16,2048]{1,0:T(8,128)(2,1)S(1)} %join.3.refs_0_), channel_id=1, source_target_pairs={{1,0},{48,32},{65,64},{112,96},{0,1},{49,33},{64,65},{113,97},{3,2... | collective-permute-start | bytes 196616 | tf_op jit(solution)/shard_map/ppermute | solution.py:427
  54.8 13.4 %collective-permute-done.1.refs_1_ = bf16[16,2048]{1,0:T(8,128)(2,1)S(1)} collective-permute-done((bf16[16,2048]{1,0:T(8,128)(2,1)S(1)}, bf16[16,2048]{1,0:T(8,128)(2,1)S(1)}, u32[]{:S(2)}, u32[]{:S(2)}) %collective-permute-start.1) | collective-permute-done | bytes 65568 | tf_op jit(solution)/shard_map/ppermute | solution.py:427
  68.3 3.4 %collective-permute-done.2.refs_2_ = bf16[16,2048]{1,0:T(8,128)(2,1)S(1)} collective-permute-done((bf16[16,2048]{1,0:T(8,128)(2,1)S(1)}, bf16[16,2048]{1,0:T(8,128)(2,1)S(1)}, u32[]{:S(2)}, u32[]{:S(2)}) %collective-permute-start.2) | collective-permute-done | bytes 65568 | tf_op jit(solution)/shard_map/ppermute | solution.py:427
  71.7 11.8 %collective-permute-done.3.refs_3_ = bf16[16,2048]{1,0:T(8,128)(2,1)S(1)} collective-permute-done((bf16[16,2048]{1,0:T(8,128)(2,1)S(1)}, bf16[16,2048]{1,0:T(8,128)(2,1)S(1)}, u32[]{:S(2)}, u32[]{:S(2)}) %collective-permute-start.3) | collective-permute-done | bytes 65568 | tf_op jit(solution)/shard_map/ppermute | solution.py:427
  83.6 0.3 collective-permute-start.4
  83.8 2.5 %collective-permute-start.5 = (bf16[64,2048]{1,0:T(8,128)(2,1)S(1)}, bf16[64,2048]{1,0:T(8,128)(2,1)S(1)}, u32[]{:S(2)}, u32[]{:S(2)}) collective-permute-start(bf16[64,2048]{1,0:T(8,128)(2,1)S(1)} %join.4.refs_0_), channel_id=1, source_target_pairs={{2,0},{96,32},{66,64},{33,96},{3,1},{97,33},{67,65},{32,97},{4,2},... | collective-permute-start | bytes 786440 | tf_op jit(solution)/shard_map/ppermute | solution.py:427
  86.3 1.3 %collective-permute-start.6 = (bf16[64,2048]{1,0:T(8,128)(2,1)S(1)}, bf16[64,2048]{1,0:T(8,128)(2,1)S(1)}, u32[]{:S(2)}, u32[]{:S(2)}) collective-permute-start(bf16[64,2048]{1,0:T(8,128)(2,1)S(1)} %join.4.refs_0_), channel_id=1, source_target_pairs={{4,0},{33,32},{68,64},{97,96},{5,1},{32,33},{69,65},{96,97},{6,2},... | collective-permute-start | bytes 786440 | tf_op jit(solution)/shard_map/ppermute | solution.py:427
  87.6 2.7 %collective-permute-done.4.refs_1_ = bf16[64,2048]{1,0:T(8,128)(2,1)S(1)} collective-permute-done((bf16[64,2048]{1,0:T(8,128)(2,1)S(1)}, bf16[64,2048]{1,0:T(8,128)(2,1)S(1)}, u32[]{:S(2)}, u32[]{:S(2)}) %collective-permute-start.4) | collective-permute-done | bytes 262176 | tf_op jit(solution)/shard_map/ppermute | solution.py:427
  90.3 2.1 %collective-permute-done.5.refs_2_ = bf16[64,2048]{1,0:T(8,128)(2,1)S(1)} collective-permute-done((bf16[64,2048]{1,0:T(8,128)(2,1)S(1)}, bf16[64,2048]{1,0:T(8,128)(2,1)S(1)}, u32[]{:S(2)}, u32[]{:S(2)}) %collective-permute-start.5) | collective-permute-done | bytes 262176 | tf_op jit(solution)/shard_map/ppermute | solution.py:427
  92.4 1.6 %collective-permute-done.6.refs_3_ = bf16[64,2048]{1,0:T(8,128)(2,1)S(1)} collective-permute-done((bf16[64,2048]{1,0:T(8,128)(2,1)S(1)}, bf16[64,2048]{1,0:T(8,128)(2,1)S(1)}, u32[]{:S(2)}, u32[]{:S(2)}) %collective-permute-start.6) | collective-permute-done | bytes 262176 | tf_op jit(solution)/shard_map/ppermute | solution.py:427
  94.0 1.0 join.5.w0
  95.0 0.0 copy-start
  95.0 3.9 %collective-permute-start.7 = (bf16[256,2048]{1,0:T(8,128)(2,1)}, bf16[256,2048]{1,0:T(8,128)(2,1)}, u32[]{:S(2)}, u32[]{:S(2)}) collective-permute-start(bf16[256,2048]{1,0:T(8,128)(2,1)} %join.5.w0), channel_id=1, source_target_pairs={{16,0},{36,32},{80,64},{100,96},{17,1},{37,33},{81,65},{101,97},{1... | collective-permute-start | bytes 3145736 | tf_op jit(solution)/shard_map/ppermute | solution.py:427
  99.0 0.0 collective-permute-start.8
  99.0 2.7 %collective-permute-start.9 = (bf16[256,2048]{1,0:T(8,128)(2,1)}, bf16[256,2048]{1,0:T(8,128)(2,1)}, u32[]{:S(2)}, u32[]{:S(2)}) collective-permute-start(bf16[256,2048]{1,0:T(8,128)(2,1)} %join.5.w0), channel_id=1, source_target_pairs={{8,0},{34,32},{72,64},{98,96},{9,1},{35,33},{73,65},{99,97},{10,2}... | collective-permute-start | bytes 3145736 | tf_op jit(solution)/shard_map/ppermute | solution.py:427
  101.6 0.0 copy-done.3
  101.7 0.0 copy-done.4
  101.7 0.0 copy-done.5
  101.7 0.1 slice.21
  101.8 0.1 fusion.16
  101.8 0.1 pad_add_fusion.places
  101.9 9.9 %collective-permute-done.7.w1 = bf16[256,2048]{1,0:T(8,128)(2,1)} collective-permute-done((bf16[256,2048]{1,0:T(8,128)(2,1)}, bf16[256,2048]{1,0:T(8,128)(2,1)}, u32[]{:S(2)}, u32[]{:S(2)}) %collective-permute-start.7) | collective-permute-done | bytes 1048608 | tf_op jit(solution)/shard_map/ppermute | solution.py:427
  111.8 0.0 all-to-all-done.1
  111.8 3.3 %early.1 = f32[512,768]{1,0:T(8,128)S(1)} custom-call(bf16[256,2048]{1,0:T(8,128)(2,1)} %join.5.w0, bf16[256,2048]{1,0:T(8,128)(2,1)} %collective-permute-done.7.w1, bf16[2048,768]{1,0:T(8,128)(2,1)S(1)} %bitcast.8), custom_call_target="tpu_custom_call" | custom-call | flops 1700000000 | bytes 8000000 | tf_op jit(solution)/shard_map/early/pallas_call | solution.py:353
  115.2 7.9 %collective-permute-done.8.w2 = bf16[256,2048]{1,0:T(8,128)(2,1)} collective-permute-done((bf16[256,2048]{1,0:T(8,128)(2,1)}, bf16[256,2048]{1,0:T(8,128)(2,1)}, u32[]{:S(2)}, u32[]{:S(2)}) %collective-permute-start.8) | collective-permute-done | bytes 1048608 | tf_op jit(solution)/shard_map/ppermute | solution.py:427
  123.0 0.0 collective-permute-done.9.w3
  123.0 0.0 copy-done
  123.0 4.3 %beams.1 = f32[64,512]{1,0:T(8,128)S(1)} custom-call(s32[64]{0:T(128)S(1)} %pad_add_fusion.places, f32[512,768]{1,0:T(8,128)S(1)} %early.1, bf16[256,2048]{1,0:T(8,128)(2,1)} %collective-permute-done.8.w2, bf16[256,2048]{1,0:T(8,128)(2,1)} %collective-permute-done.9.w3, bf16[2048,768]{1,0:T(8,128)(2,1)S(1)} %bitcast.9, f32[64,384]{1,0:T(8,128)S(1)} %copy-done), custom_call_target="tpu_custom_call" | custom-call | flops 1700000000 | bytes 8000000 | tf_op jit(solution)/shard_map/beams/pallas_call | solution.py:394
  127.4 3.0 %collective-permute-start.10 = (f32[32,512]{1,0:T(8,128)S(1)}, f32[32,512]{1,0:T(8,128)S(1)}, u32[]{:S(2)}, u32[]{:S(2)}) collective-permute-start(f32[32,512]{1,0:T(8,128)S(1)} %get-tuple-element.20), channel_id=1, source_target_pairs={{0,32},{32,0},{64,96},{96,64},{1,33},{33,1},{65,97},{97,65},{2,34}... | collective-permute-start | bytes 196616 | tf_op jit(solution)/shard_map/ppermute | solution.py:477
  130.3 0.9 collective-permute-done.10
  131.3 0.7 maximum_select_fusion
  (4 shorter events, 0.1 us)
Async XLA Ops:
  5.6 29.5 %all-to-all-start = ((bf16[32,16,1024]{2,1,0:T(8,128)(2,1)}), bf16[32,16,1024]{2,1,0:T(8,128)(2,1)S(1)}, u32[]{:S(2)}, u32[]{:S(2)}) async-start(bf16[32,16,1024]{2,1,0:T(8,128)(2,1)} %bitcast.12), calls=%async_computation | async-start | bytes 2097152 | tf_op jit(solution)/shard_map/all_to_all | solution.py:454
  35.1 1.0 copy-start.2
  36.0 75.8 %all-to-all-start.1 = ((bf16[128,16,768]{2,1,0:T(8,128)(2,1)}), bf16[128,16,768]{2,1,0:T(8,128)(2,1)S(1)}, u32[]{:S(2)}, u32[]{:S(2)}) async-start(bf16[128,16,768]{2,1,0:T(8,128)(2,1)} %spectra.1), calls=%async_computation.1 | async-start | bytes 6291456 | tf_op jit(solution)/shard_map/all_to_all | solution.py:460
  45.5 56.1 %copy-start.3 = (s32[64]{0:T(128)S(1)}, s32[64]{0:T(128)}, u32[]{:S(2)}) copy-start(s32[64]{0:T(128)} %constant.124.clone) | copy-start | bytes 772
  45.5 56.1 %copy-start.4 = (s32[64]{0:T(128)S(1)}, s32[64]{0:T(128)}, u32[]{:S(2)}) copy-start(s32[64]{0:T(128)} %constant.125.clone) | copy-start | bytes 772
  45.6 56.1 %copy-start.5 = (s32[64]{0:T(128)S(1)}, s32[64]{0:T(128)}, u32[]{:S(2)}) copy-start(s32[64]{0:T(128)} %constant.126.clone) | copy-start | bytes 772
  47.8 2.2 %collective-permute-start = (bf16[16,1024]{1,0:T(8,128)(2,1)}, bf16[16,1024]{1,0:T(8,128)(2,1)S(1)}, u32[]{:S(2)}, u32[]{:S(2)}) collective-permute-start(bf16[16,1024]{1,0:T(8,128)(2,1)} %get-tuple-element.17), channel_id=1, source_target_pairs={{0,32},{32,0},{64,96},{96,64},{1,33},{33,1},{65,97},{97,65},{2,34}... | collective-permute-start | bytes 98312 | tf_op jit(solution)/shard_map/ppermute | solution.py:464
  50.0 0.8 copy-start.1
  50.8 17.5 %collective-permute-start.1 = (bf16[16,2048]{1,0:T(8,128)(2,1)S(1)}, bf16[16,2048]{1,0:T(8,128)(2,1)S(1)}, u32[]{:S(2)}, u32[]{:S(2)}) collective-permute-start(bf16[16,2048]{1,0:T(8,128)(2,1)S(1)} %join.3.refs_0_), channel_id=1, source_target_pairs={{65,0},{56,32},{0,64},{120,96},{64,1},{57,33},{1,65},{121,97},{67,... | collective-permute-start | bytes 196616 | tf_op jit(solution)/shard_map/ppermute | solution.py:427
  51.6 20.1 %collective-permute-start.2 = (bf16[16,2048]{1,0:T(8,128)(2,1)S(1)}, bf16[16,2048]{1,0:T(8,128)(2,1)S(1)}, u32[]{:S(2)}, u32[]{:S(2)}) collective-permute-start(bf16[16,2048]{1,0:T(8,128)(2,1)S(1)} %join.3.refs_0_), channel_id=1, source_target_pairs={{64,0},{40,32},{1,64},{104,96},{65,1},{41,33},{0,65},{105,97},{66,... | collective-permute-start | bytes 196616 | tf_op jit(solution)/shard_map/ppermute | solution.py:427
  53.5 30.1 %collective-permute-start.3 = (bf16[16,2048]{1,0:T(8,128)(2,1)S(1)}, bf16[16,2048]{1,0:T(8,128)(2,1)S(1)}, u32[]{:S(2)}, u32[]{:S(2)}) collective-permute-start(bf16[16,2048]{1,0:T(8,128)(2,1)S(1)} %join.3.refs_0_), channel_id=1, source_target_pairs={{1,0},{48,32},{65,64},{112,96},{0,1},{49,33},{64,65},{113,97},{3,2... | collective-permute-start | bytes 196616 | tf_op jit(solution)/shard_map/ppermute | solution.py:427
  83.6 6.8 %collective-permute-start.4 = (bf16[64,2048]{1,0:T(8,128)(2,1)S(1)}, bf16[64,2048]{1,0:T(8,128)(2,1)S(1)}, u32[]{:S(2)}, u32[]{:S(2)}) collective-permute-start(bf16[64,2048]{1,0:T(8,128)(2,1)S(1)} %join.4.refs_0_), channel_id=1, source_target_pairs={{6,0},{97,32},{70,64},{32,96},{7,1},{96,33},{71,65},{33,97},{0,2},... | collective-permute-start | bytes 786440 | tf_op jit(solution)/shard_map/ppermute | solution.py:427
  83.8 8.6 %collective-permute-start.5 = (bf16[64,2048]{1,0:T(8,128)(2,1)S(1)}, bf16[64,2048]{1,0:T(8,128)(2,1)S(1)}, u32[]{:S(2)}, u32[]{:S(2)}) collective-permute-start(bf16[64,2048]{1,0:T(8,128)(2,1)S(1)} %join.4.refs_0_), channel_id=1, source_target_pairs={{2,0},{96,32},{66,64},{33,96},{3,1},{97,33},{67,65},{32,97},{4,2},... | collective-permute-start | bytes 786440 | tf_op jit(solution)/shard_map/ppermute | solution.py:427
  86.3 7.7 %collective-permute-start.6 = (bf16[64,2048]{1,0:T(8,128)(2,1)S(1)}, bf16[64,2048]{1,0:T(8,128)(2,1)S(1)}, u32[]{:S(2)}, u32[]{:S(2)}) collective-permute-start(bf16[64,2048]{1,0:T(8,128)(2,1)S(1)} %join.4.refs_0_), channel_id=1, source_target_pairs={{4,0},{33,32},{68,64},{97,96},{5,1},{32,33},{69,65},{96,97},{6,2},... | collective-permute-start | bytes 786440 | tf_op jit(solution)/shard_map/ppermute | solution.py:427
  95.0 28.0 %copy-start = (f32[64,384]{1,0:T(8,128)S(1)}, f32[64,384]{1,0:T(8,128)}, u32[]{:S(2)}) copy-start(f32[64,384]{1,0:T(8,128)} %constant.127.clone.choose) | copy-start | bytes 294916
  95.0 16.8 %collective-permute-start.7 = (bf16[256,2048]{1,0:T(8,128)(2,1)}, bf16[256,2048]{1,0:T(8,128)(2,1)}, u32[]{:S(2)}, u32[]{:S(2)}) collective-permute-start(bf16[256,2048]{1,0:T(8,128)(2,1)} %join.5.w0), channel_id=1, source_target_pairs={{16,0},{36,32},{80,64},{100,96},{17,1},{37,33},{81,65},{101,97},{1... | collective-permute-start | bytes 3145736 | tf_op jit(solution)/shard_map/ppermute | solution.py:427
  99.0 24.0 %collective-permute-start.8 = (bf16[256,2048]{1,0:T(8,128)(2,1)}, bf16[256,2048]{1,0:T(8,128)(2,1)}, u32[]{:S(2)}, u32[]{:S(2)}) collective-permute-start(bf16[256,2048]{1,0:T(8,128)(2,1)} %join.5.w0), channel_id=1, source_target_pairs={{24,0},{38,32},{88,64},{102,96},{25,1},{39,33},{89,65},{103,97},{2... | collective-permute-start | bytes 3145736 | tf_op jit(solution)/shard_map/ppermute | solution.py:427
  99.0 24.0 %collective-permute-start.9 = (bf16[256,2048]{1,0:T(8,128)(2,1)}, bf16[256,2048]{1,0:T(8,128)(2,1)}, u32[]{:S(2)}, u32[]{:S(2)}) collective-permute-start(bf16[256,2048]{1,0:T(8,128)(2,1)} %join.5.w0), channel_id=1, source_target_pairs={{8,0},{34,32},{72,64},{98,96},{9,1},{35,33},{73,65},{99,97},{10,2}... | collective-permute-start | bytes 3145736 | tf_op jit(solution)/shard_map/ppermute | solution.py:427
  127.4 3.9 %collective-permute-start.10 = (f32[32,512]{1,0:T(8,128)S(1)}, f32[32,512]{1,0:T(8,128)S(1)}, u32[]{:S(2)}, u32[]{:S(2)}) collective-permute-start(f32[32,512]{1,0:T(8,128)S(1)} %get-tuple-element.20), channel_id=1, source_target_pairs={{0,32},{32,0},{64,96},{96,64},{1,33},{33,1},{65,97},{97,65},{2,34}... | collective-permute-start | bytes 196616 | tf_op jit(solution)/shard_map/ppermute | solution.py:477

commit v8 on v7

--- a/solution.py
+++ b/solution.py
@@ -272,27 +272,20 @@
     )(wre, wim, antenna_map.reshape(2, 1, half))
 
 
-def pick_kernel(owners, offers, mine, other, sems):
+def pick_kernel(owners, offers, mine, other):
     core = lax.axis_index("grp") % 2
-    copies = [
-        pltpu.make_async_copy(offers.at[owners[core]], mine, sems.at[0]),
-        pltpu.make_async_copy(offers.at[owners[1 - core]], other, sems.at[1]),
-    ]
-    for copy in copies:
-        copy.start()
-    for copy in copies:
-        copy.wait()
+    mine[...] = offers[owners[core]]
+    other[...] = offers[owners[1 - core]]
 
 
 def pick_of(owners, offers, interpret=False):
     _, rows, columns = offers.shape
     return pl.pallas_call(
         pick_kernel,
-        in_specs=[pl.BlockSpec(memory_space=pltpu.SMEM), pl.BlockSpec(memory_space=pltpu.HBM)],
+        in_specs=[pl.BlockSpec(memory_space=pltpu.SMEM), pl.BlockSpec(memory_space=pltpu.VMEM)],
         out_specs=[pl.BlockSpec(memory_space=pltpu.VMEM)] * 2,
         out_shape=[jax.ShapeDtypeStruct((rows, columns), offers.dtype)] * 2,
-        scratch_shapes=[pltpu.SemaphoreType.DMA((2,))],
-        compiler_params=pltpu.CompilerParams(vmem_limit_bytes=58 * MIB),
+        compiler_params=pltpu.CompilerParams(vmem_limit_bytes=8 * MIB),
         interpret=interpret,
         name="pick",
     )(owners, offers)
@@ -427,20 +420,19 @@
     return [block] + [lax.ppermute(block, ALL, permutation(stage, shift)) for shift in SHIFTS[1:]]
 
 
+def plane_groups():
+    groups = [[index_of(z, x, y, 0) for y in range(4) for x in range(4)] for z in range(4)]
+    return groups + [[index_of(z, x, y, 1) for y in range(4) for z in range(4)] for x in range(4)]
+
+
 def block_places(grp, dev):
     core = grp % 2
-    z, x, y = dev // 8, dev // 2 % 4, dev % 2 * 2 + grp // 2
+    z, x = dev // 8, dev // 2 % 4
     k = np.arange(64)
-    shift = np.array(SHIFTS)
-    first, second, third = shift[k % 4], shift[k // 4 % 4], shift[k // 16]
-    by_core = []
-    for order in ORDER:
-        moved = dict(zip(order, (first, second, third)))
-        by_core.append([moved[axis] for axis in "zxy"])
-    is_first = core == 0
-    mz, mx, my = [jnp.where(is_first, jnp.asarray(a), jnp.asarray(b)) for a, b in zip(*by_core)]
-    fz, fx, fy = (z + mz + 4) % 4, (x + mx + 4) % 4, (y + my + 4) % 4
-    return (((fy % 2) * 32 + fz * 8 + fx * 2 + fy // 2) * 16).astype(jnp.int32)
+    shift, y, other = np.array(SHIFTS)[k // 16], k % 16 // 4, k % 4
+    fz = jnp.where(core == 0, (z + shift + 4) % 4, other)
+    fx = jnp.where(core == 0, other, (x + shift + 4) % 4)
+    return (((y % 2) * 32 + fz * 8 + fx * 2 + y // 2) * 16).astype(jnp.int32)
 
 
 SWAP = [(0, 1), (1, 0), (2, 3), (3, 2)]
@@ -463,8 +455,7 @@
     mine, other = pick_of(owners, offers)
     other = lax.ppermute(other, "grp", SWAP)
     block = join_of([mine, other], 1)
-    block = join_of(gather_stage(block, 0), 0)
-    block = join_of(gather_stage(block, 1), 0)
+    block = lax.all_gather(block, ALL, axis=0, tiled=True, axis_index_groups=plane_groups())
     parts = gather_stage(block, 2)
 
     early = early_of(parts[0], parts[3], spectra)

time: 132 us -> 178 us (1.35)
  waiting for transfers between devices: 55.3 us -> 97.9 us
  between operations: 0.1 us -> 13.5 us
  starting transfers between devices: 39.7 us -> 29.6 us
  Pallas kernels: 34.1 us -> 31.8 us
    all_gather x0 -> x1, waiting for transfers between devices: none -> 78.4 us  [on_device(): lax.all_gather(block, ALL, axis=0, tiled=True, axis_index_groups=plane_gr...]
    ppermute x9 -> x3, waiting for transfers between devices: 52.8 us -> 17.3 us  [gather_stage(): lax.ppermute(block, ALL, permutation(stage, shift))]
    ppermute x9 -> x3, starting transfers between devices: 14.7 us -> 5.67 us  [gather_stage(): lax.ppermute(block, ALL, permutation(stage, shift))]
  transfers between devices with their start and end apart: 13 -> 8, of which waited for: 11 -> 7; matrix products, arithmetic and copies ran while one was open for 0% -> 0% of each run, Pallas kernels for 18% -> 12%
where the time goes in v8:
time: 178 us; the launch traced here: 177 us
  waiting for transfers between devices  97.9 us (55%)
  Pallas kernels  31.8 us (18%)
  starting transfers between devices  29.6 us (17%)
  between operations  13.5 us (8%)
  local copies, waits for them, and re-layouts  3.59 us (2%)
    all_gather x1, waiting for transfers between devices, on_device(): lax.all_gather(block, ALL, axis=0, tiled=True, axis_index_groups=plane_gr...  78.4 us
    pallas_call x1, Pallas kernels, spectra_of(): pl.pallas_call(functools.partial(spectra_kernel, messages), out_shape=[ja...  17.7 us
    ppermute x3, waiting for transfers between devices, gather_stage(): lax.ppermute(block, ALL, permutation(stage, shift))  17.3 us
    all_to_all x1, starting transfers between devices, on_device(): lax.all_to_all(quarter.reshape(32, 16, -1), 'dev', split_axis=0, concat_a...  11.4 us
    all_to_all x1, starting transfers between devices, on_device(): lax.all_to_all(message, ALL, split_axis=0, concat_axis=0, tiled=True)  9.54 us
    ppermute x3, starting transfers between devices, gather_stage(): lax.ppermute(block, ALL, permutation(stage, shift))  5.67 us
    pallas_call x1, Pallas kernels, quarter_of(): pl.pallas_call(quarter_kernel, in_specs=[pl.BlockSpec(memory_space=pltpu....  5.56 us
    pallas_call x1, Pallas kernels, beams_of(): pl.pallas_call(beams_kernel, out_shape=jax.ShapeDtypeStruct((64, rows //...  4.33 us
  transfers between devices with their start and end apart: 8, of which 7 were waited for; matrix products, arithmetic and copies ran while one was open for 0% of the time, Pallas kernels for 12%

profile of v8, /device:TPU:1, one launch (start us, length us, event | category | flops | bytes accessed | tf_op | source)
XLA Modules:
  0.0 177.1 jit_solution(17204748265339399502)
XLA Ops:
  6.5 5.6 %quarter.1 = bf16[512,1024]{1,0:T(8,128)(2,1)} custom-call(f32[2048,512]{1,0:T(8,128)} %bitcast.10, f32[2048,512]{1,0:T(8,128)} %bitcast.11, s32[2,1,1024]{2,1,0:T(1,128)} %bitcast.14), custom_call_target="tpu_custom_call" | custom-call | flops 2000000000 | bytes 6000000 | tf_op jit(solution)/shard_map/quarter/pallas_call | solution.py:257
  12.1 11.4 %all-to-all-start = ((bf16[32,16,1024]{2,1,0:T(8,128)(2,1)}), bf16[32,16,1024]{2,1,0:T(8,128)(2,1)S(1)}, u32[]{:S(2)}, u32[]{:S(2)}) async-start(bf16[32,16,1024]{2,1,0:T(8,128)(2,1)} %bitcast.12), calls=%async_computation | async-start | bytes 2097152 | tf_op jit(solution)/shard_map/all_to_all | solution.py:446
  23.5 17.7 %spectra.1 = bf16[128,16,768]{2,1,0:T(8,128)(2,1)} custom-call(bf16[16,110592]{1,0:T(8,128)(2,1)} %refs_0_, bf16[16,110592]{1,0:T(8,128)(2,1)} %refs_1_, f32[16,4096]{1,0:T(8,128)} %refs_2_, f32[32,128]{1,0:T(8,128)} %constant.91.clone.refs_3_, f32[32,128]{1,0:T(8,128)} %constant.92.clone.refs_4_, bf16[256,256]{1,0:T(8,128)(2,1)} %constant.93.clone.refs_5_), custom_call_target="tpu_custom_call" | custom-call | flops 2400000000 | bytes 48000000 | tf_op jit(solution)/shard_map/spectra/pallas_call | solution.py:190
  41.1 0.0 copy-start.4
  41.1 0.0 copy-start.5
  41.2 0.0 copy-start.6
  41.2 0.0 copy-start.7
  41.2 0.0 copy-start.8
  41.2 0.4 all-to-all-done.offers
  41.6 0.0 copy-start
  41.6 1.0 copy-done
  42.6 9.5 %all-to-all-start.1 = ((bf16[128,16,768]{2,1,0:T(8,128)(2,1)}), bf16[128,16,768]{2,1,0:T(8,128)(2,1)S(1)}, u32[]{:S(2)}, u32[]{:S(2)}) async-start(bf16[128,16,768]{2,1,0:T(8,128)(2,1)} %spectra.1), calls=%async_computation.1 | async-start | bytes 6291456 | tf_op jit(solution)/shard_map/all_to_all | solution.py:452
  52.1 0.0 all-gather.2.cloned.1.call-start
  52.2 0.0 copy-done.4
  52.2 0.0 copy-start.1
  52.2 1.2 copy-done.1
  53.4 0.6 pick.1
  54.0 1.1 collective-permute-start
  55.1 0.9 collective-permute-done.refs_1_
  56.0 0.0 copy-start.3
  56.0 0.6 join.1
  56.6 0.0 all-gather.2.cloned.1.call-update
  56.6 78.4 %all-gather.2.cloned.1.call-done.w0 = bf16[256,2048]{1,0:T(8,128)(2,1)} async-done(((bf16[16,2048]{1,0:T(8,128)(2,1)}), bf16[256,2048]{1,0:T(8,128)(2,1)}) %all-gather.2.cloned.1.call-update) | async-done | bytes 1048592 | tf_op jit(solution)/shard_map/all_gather | solution.py:458
  135.0 3.0 %collective-permute-start.1 = (bf16[256,2048]{1,0:T(8,128)(2,1)}, bf16[256,2048]{1,0:T(8,128)(2,1)}, u32[]{:S(2)}, u32[]{:S(2)}) collective-permute-start(bf16[256,2048]{1,0:T(8,128)(2,1)} %all-gather.2.cloned.1.call-done.w0), channel_id=1, source_target_pairs={{16,0},{36,32},{80,64},{100,96},{17,1},{37,33},{81,65},{101,97},{1... | collective-permute-start | bytes 3145736 | tf_op jit(solution)/shard_map/ppermute | solution.py:420
  138.0 0.4 collective-permute-start.2
  138.4 2.3 %collective-permute-start.3 = (bf16[256,2048]{1,0:T(8,128)(2,1)}, bf16[256,2048]{1,0:T(8,128)(2,1)}, u32[]{:S(2)}, u32[]{:S(2)}) collective-permute-start(bf16[256,2048]{1,0:T(8,128)(2,1)} %all-gather.2.cloned.1.call-done.w0), channel_id=1, source_target_pairs={{8,0},{34,32},{72,64},{98,96},{9,1},{35,33},{73,65},{99,97},{10,2}... | collective-permute-start | bytes 3145736 | tf_op jit(solution)/shard_map/ppermute | solution.py:420
  140.7 0.0 copy-done.5
  140.7 0.0 copy-done.6
  140.7 0.0 copy-done.7
  140.7 0.0 copy-done.8
  140.7 0.1 slice.21
  140.8 0.1 fusion.4
  140.9 0.1 pad_add_fusion.places
  141.0 9.9 %collective-permute-done.1.w1 = bf16[256,2048]{1,0:T(8,128)(2,1)} collective-permute-done((bf16[256,2048]{1,0:T(8,128)(2,1)}, bf16[256,2048]{1,0:T(8,128)(2,1)}, u32[]{:S(2)}, u32[]{:S(2)}) %collective-permute-start.1) | collective-permute-done | bytes 1048608 | tf_op jit(solution)/shard_map/ppermute | solution.py:420
  150.9 0.0 all-to-all-done.1
  150.9 0.0 copy-start.2
  150.9 1.2 copy-done.2
  152.1 3.0 %early.1 = f32[512,768]{1,0:T(8,128)S(1)} custom-call(bf16[256,2048]{1,0:T(8,128)(2,1)S(1)} %copy-done.2, bf16[256,2048]{1,0:T(8,128)(2,1)} %collective-permute-done.1.w1, bf16[2048,768]{1,0:T(8,128)(2,1)S(1)} %bitcast.8), custom_call_target="tpu_custom_call" | custom-call | flops 1700000000 | bytes 8000000 | tf_op jit(solution)/shard_map/early/pallas_call | solution.py:346
  155.1 6.9 %collective-permute-done.2.w2 = bf16[256,2048]{1,0:T(8,128)(2,1)} collective-permute-done((bf16[256,2048]{1,0:T(8,128)(2,1)}, bf16[256,2048]{1,0:T(8,128)(2,1)}, u32[]{:S(2)}, u32[]{:S(2)}) %collective-permute-start.2) | collective-permute-done | bytes 1048608 | tf_op jit(solution)/shard_map/ppermute | solution.py:420
  162.1 0.4 collective-permute-done.3.w3
  162.5 0.0 copy-done.3
  162.5 4.3 %beams.1 = f32[64,512]{1,0:T(8,128)S(1)} custom-call(s32[64]{0:T(128)S(1)} %pad_add_fusion.places, f32[512,768]{1,0:T(8,128)S(1)} %early.1, bf16[256,2048]{1,0:T(8,128)(2,1)} %collective-permute-done.2.w2, bf16[256,2048]{1,0:T(8,128)(2,1)} %collective-permute-done.3.w3, bf16[2048,768]{1,0:T(8,128)(2,1)S(1)} %bitcast.9, f32[64,384]{1,0:T(8,128)S(1)} %copy-done.3), custom_call_target="tpu_custom_call" | custom-call | flops 1700000000 | bytes 8000000 | tf_op jit(solution)/shard_map/beams/pallas_call | solution.py:387
  166.8 1.9 %collective-permute-start.4 = (f32[32,512]{1,0:T(8,128)S(1)}, f32[32,512]{1,0:T(8,128)S(1)}, u32[]{:S(2)}, u32[]{:S(2)}) collective-permute-start(f32[32,512]{1,0:T(8,128)S(1)} %get-tuple-element.20), channel_id=1, source_target_pairs={{0,32},{32,0},{64,96},{96,64},{1,33},{33,1},{65,97},{97,65},{2,34}... | collective-permute-start | bytes 196616 | tf_op jit(solution)/shard_map/ppermute | solution.py:468
  168.7 0.9 collective-permute-done.4
  169.6 0.7 maximum_select_fusion
  (2 shorter events, 0.0 us)
Async XLA Ops:
  12.1 29.5 %all-to-all-start = ((bf16[32,16,1024]{2,1,0:T(8,128)(2,1)}), bf16[32,16,1024]{2,1,0:T(8,128)(2,1)S(1)}, u32[]{:S(2)}, u32[]{:S(2)}) async-start(bf16[32,16,1024]{2,1,0:T(8,128)(2,1)} %bitcast.12), calls=%async_computation | async-start | bytes 2097152 | tf_op jit(solution)/shard_map/all_to_all | solution.py:446
  41.1 11.0 %copy-start.4 = (s32[2]{0:T(128)S(1)}, s32[2]{0:T(128)}, u32[]{:S(2)}) copy-start(s32[2]{0:T(128)} %owners.1) | copy-start | bytes 28
  41.1 99.6 %copy-start.5 = (s32[64]{0:T(128)S(1)}, s32[64]{0:T(128)}, u32[]{:S(2)}) copy-start(s32[64]{0:T(128)} %constant.94.clone) | copy-start | bytes 772
  41.2 99.5 %copy-start.6 = (s32[64]{0:T(128)S(1)}, s32[64]{0:T(128)}, u32[]{:S(2)}) copy-start(s32[64]{0:T(128)} %constant.95.clone) | copy-start | bytes 772
  41.2 99.5 %copy-start.7 = (s32[64]{0:T(128)S(1)}, s32[64]{0:T(128)}, u32[]{:S(2)}) copy-start(s32[64]{0:T(128)} %constant.96.clone) | copy-start | bytes 772
  41.2 99.5 %copy-start.8 = (s32[64]{0:T(128)S(1)}, s32[64]{0:T(128)}, u32[]{:S(2)}) copy-start(s32[64]{0:T(128)} %constant.97.clone) | copy-start | bytes 772
  41.6 1.0 copy-start
  42.6 108.3 %all-to-all-start.1 = ((bf16[128,16,768]{2,1,0:T(8,128)(2,1)}), bf16[128,16,768]{2,1,0:T(8,128)(2,1)S(1)}, u32[]{:S(2)}, u32[]{:S(2)}) async-start(bf16[128,16,768]{2,1,0:T(8,128)(2,1)} %spectra.1), calls=%async_computation.1 | async-start | bytes 6291456 | tf_op jit(solution)/shard_map/all_to_all | solution.py:452
  52.1 82.9 %all-gather.2.cloned.1.call-start = ((), (), s32[]{:S(2)}) async-start(), calls=%async_computation.2 | async-start | bytes 1114112 | tf_op jit(solution)/shard_map/all_gather | solution.py:458
  52.2 1.2 copy-start.1
  54.0 2.0 %collective-permute-start = (bf16[16,1024]{1,0:T(8,128)(2,1)S(1)}, bf16[16,1024]{1,0:T(8,128)(2,1)S(1)}, u32[]{:S(2)}, u32[]{:S(2)}) collective-permute-start(bf16[16,1024]{1,0:T(8,128)(2,1)S(1)} %get-tuple-element.17), channel_id=1, source_target_pairs={{0,32},{32,0},{64,96},{96,64},{1,33},{33,1},{65,97},{97,65},{2,34}... | collective-permute-start | bytes 98312 | tf_op jit(solution)/shard_map/ppermute | solution.py:456
  56.0 106.5 %copy-start.3 = (f32[64,384]{1,0:T(8,128)S(1)}, f32[64,384]{1,0:T(8,128)}, u32[]{:S(2)}) copy-start(f32[64,384]{1,0:T(8,128)} %constant.98.clone.choose) | copy-start | bytes 294916
  135.0 15.8 %collective-permute-start.1 = (bf16[256,2048]{1,0:T(8,128)(2,1)}, bf16[256,2048]{1,0:T(8,128)(2,1)}, u32[]{:S(2)}, u32[]{:S(2)}) collective-permute-start(bf16[256,2048]{1,0:T(8,128)(2,1)} %all-gather.2.cloned.1.call-done.w0), channel_id=1, source_target_pairs={{16,0},{36,32},{80,64},{100,96},{17,1},{37,33},{81,65},{101,97},{1... | collective-permute-start | bytes 3145736 | tf_op jit(solution)/shard_map/ppermute | solution.py:420
  138.0 24.0 %collective-permute-start.2 = (bf16[256,2048]{1,0:T(8,128)(2,1)}, bf16[256,2048]{1,0:T(8,128)(2,1)}, u32[]{:S(2)}, u32[]{:S(2)}) collective-permute-start(bf16[256,2048]{1,0:T(8,128)(2,1)} %all-gather.2.cloned.1.call-done.w0), channel_id=1, source_target_pairs={{24,0},{38,32},{88,64},{102,96},{25,1},{39,33},{89,65},{103,97},{2... | collective-permute-start | bytes 3145736 | tf_op jit(solution)/shard_map/ppermute | solution.py:420
  138.4 24.1 %collective-permute-start.3 = (bf16[256,2048]{1,0:T(8,128)(2,1)}, bf16[256,2048]{1,0:T(8,128)(2,1)}, u32[]{:S(2)}, u32[]{:S(2)}) collective-permute-start(bf16[256,2048]{1,0:T(8,128)(2,1)} %all-gather.2.cloned.1.call-done.w0), channel_id=1, source_target_pairs={{8,0},{34,32},{72,64},{98,96},{9,1},{35,33},{73,65},{99,97},{10,2}... | collective-permute-start | bytes 3145736 | tf_op jit(solution)/shard_map/ppermute | solution.py:420
  150.9 1.2 copy-start.2
  166.8 2.8 %collective-permute-start.4 = (f32[32,512]{1,0:T(8,128)S(1)}, f32[32,512]{1,0:T(8,128)S(1)}, u32[]{:S(2)}, u32[]{:S(2)}) collective-permute-start(f32[32,512]{1,0:T(8,128)S(1)} %get-tuple-element.20), channel_id=1, source_target_pairs={{0,32},{32,0},{64,96},{96,64},{1,33},{33,1},{65,97},{97,65},{2,34}... | collective-permute-start | bytes 196616 | tf_op jit(solution)/shard_map/ppermute | solution.py:468
Sparse Core Ops, SparseCore 0:
  56.8 78.2 all-gather.1

commit v9 on v7

--- a/solution.py
+++ b/solution.py
@@ -132,17 +132,21 @@
 
     lax.fori_loop(0, 2 * len(chosen), outer, 0)
 
-    matrix = mat[...]
+    matrix, matrix_low = mat[:256, :], mat[256:, :]
     lane = lax.broadcasted_iota(jnp.int32, (32, INNER), 1)
 
     def inner(a, _):
         base = pl.multiple_of(a * slot_stride, 8)
         rows = jnp.concatenate(
             [turned[0, pl.ds(base, rows_per_slot), :], turned[1, pl.ds(base, rows_per_slot), :]], axis=1
-        ).astype(jnp.bfloat16)
-        spec = lax.dot_general(
-            matrix, rows, (((1,), (1,)), ((), ())), preferred_element_type=jnp.float32
         )
+        high = rows.astype(jnp.bfloat16)
+        low = (rows - high.astype(jnp.float32)).astype(jnp.bfloat16)
+
+        def product(left, right):
+            return lax.dot_general(left, right, (((1,), (1,)), ((), ())), preferred_element_type=jnp.float32)
+
+        spec = product(matrix, high) + (product(matrix_low, high) + product(matrix, low))
         for g in range(count):
             for y in range(2):
                 for c in range(2):
@@ -181,7 +185,9 @@
 
 def spectra_of(messages, vre, vim, taps, interpret=False):
     cos_t, sin_t = twist_tables()
-    mat = inner_matrix().astype(jnp.bfloat16)
+    mat = inner_matrix()
+    high = mat.astype(jnp.bfloat16)
+    mat = np.concatenate([high, (mat - high.astype(np.float32)).astype(jnp.bfloat16)])
     groups = [group for message in messages for group in message]
     count = len(groups)
     many = 4 * count
@@ -198,7 +204,7 @@
             pltpu.VMEM((TAPS, CHANNELS), jnp.float32),
             pltpu.VMEM((OUTER, INNER), jnp.float32),
             pltpu.VMEM((OUTER, INNER), jnp.float32),
-            pltpu.VMEM((256, 256), jnp.bfloat16),
+            pltpu.VMEM((512, 256), jnp.bfloat16),
             pltpu.VMEM((2, many, OUTER, SLOTS, INNER), jnp.float32),
             pltpu.VMEM((2, SLOTS * (32 * many + 8), INNER), jnp.float32),
             pltpu.VMEM((2 * count, DEVICES * ROW_STRIDE, INNER), jnp.float32),
@@ -362,7 +368,7 @@
     )(w0, w1, spectra)
 
 
-def beams_kernel(places, early, w2, w3, za, choose, out, sums):
+def beams_kernel(places, early, w2, w3, za, choose, own, given, sums):
     for k in range(32):
         at = pl.multiple_of(places[k], 16)
         sums[pl.ds(at, 16), :] = early[k * 16 : (k + 1) * 16, :]
@@ -386,16 +392,18 @@
         preferred_element_type=jnp.float32,
         precision=lax.Precision.HIGHEST,
     )
-    out[...] = total * (1.0 / SPECTRA)
+    total = total * (1.0 / SPECTRA)
+    own[...] = jnp.where(core == 0, total[:32], total[32:])
+    given[...] = jnp.where(core == 0, total[32:], total[:32])
 
 
 def beams_of(places, early, w2, w3, spectra, interpret=False):
     rows = early.shape[0] + 2 * w2.shape[0]
     return pl.pallas_call(
         beams_kernel,
-        out_shape=jax.ShapeDtypeStruct((64, rows // 2), jnp.float32),
+        out_shape=[jax.ShapeDtypeStruct((32, rows // 2), jnp.float32)] * 2,
         in_specs=[pl.BlockSpec(memory_space=pltpu.SMEM)] + [pl.BlockSpec(memory_space=pltpu.VMEM)] * 5,
-        out_specs=pl.BlockSpec(memory_space=pltpu.VMEM),
+        out_specs=[pl.BlockSpec(memory_space=pltpu.VMEM)] * 2,
         scratch_shapes=[pltpu.VMEM((rows, 768), jnp.float32)],
         compiler_params=pltpu.CompilerParams(vmem_limit_bytes=32 * MIB),
         cost_estimate=pl.CostEstimate(flops=17 * 10**8, bytes_accessed=8 * 10**6, transcendentals=0),
@@ -470,10 +478,7 @@
     early = early_of(parts[0], parts[3], spectra)
     places = block_places(grp, dev)
     places = jnp.concatenate([places[:16], places[48:], places[16:48]])
-    power = beams_of(places, early, parts[1], parts[2], spectra)
-    power = power.reshape(2, 32, -1)
-    own = jnp.where(core == 0, power[0], power[1])
-    given = jnp.where(core == 0, power[1], power[0])
+    own, given = beams_of(places, early, parts[1], parts[2], spectra)
     taken = lax.ppermute(given, "grp", SWAP)
     return jnp.where(core == 0, jnp.stack([own, taken]), jnp.stack([taken, own]))
 

time: 132 us -> 134 us (1.015)
  Pallas kernels: 34.1 us -> 35.9 us
    pallas_call x1, Pallas kernels: 17.7 us -> 19.4 us  [spectra_of(): pl.pallas_call(functools.partial(spectra_kernel, messages), out_shape=[ja...]
  transfers between devices with their start and end apart: 13 -> 13, of which waited for: 11 -> 10; matrix products, arithmetic and copies ran while one was open for 0% -> 0% of each run, Pallas kernels for 18% -> 19%
where the time goes in v9:
time: 134 us
  waiting for transfers between devices  54.8 us (41%)
  starting transfers between devices  40.2 us (30%)
  Pallas kernels  35.9 us (27%)
  local copies, waits for them, and re-layouts  1.88 us (1%)
    ppermute x9, waiting for transfers between devices, gather_stage(): lax.ppermute(block, ALL, permutation(stage, shift))  52.8 us
    pallas_call x1, Pallas kernels, spectra_of(): pl.pallas_call(functools.partial(spectra_kernel, messages), out_shape=[ja...  19.4 us
    ppermute x9, starting transfers between devices, gather_stage(): lax.ppermute(block, ALL, permutation(stage, shift))  14.7 us
    all_to_all x1, starting transfers between devices, on_device(): lax.all_to_all(quarter.reshape(32, 16, -1), 'dev', split_axis=0, concat_a...  11.4 us
    all_to_all x1, starting transfers between devices, on_device(): lax.all_to_all(message, ALL, split_axis=0, concat_axis=0, tiled=True)  9.95 us
    pallas_call x1, Pallas kernels, quarter_of(): pl.pallas_call(quarter_kernel, in_specs=[pl.BlockSpec(memory_space=pltpu....  5.56 us
    pallas_call x1, Pallas kernels, beams_of(): pl.pallas_call(beams_kernel, out_shape=[jax.ShapeDtypeStruct((32, rows //...  4.33 us
    pallas_call x1, Pallas kernels, early_of(): pl.pallas_call(early_kernel, out_shape=jax.ShapeDtypeStruct((2 * w0.shape...  3.33 us
  transfers between devices with their start and end apart: 13, of which 10 were waited for; matrix products, arithmetic and copies ran while one was open for 0% of the time, Pallas kernels for 19%

profile of v9, /device:TPU:1, one launch (start us, length us, event | category | flops | bytes accessed | tf_op | source)
XLA Modules:
  0.0 133.7 jit_solution(13800435930608339394)
XLA Ops:
  0.0 5.6 %quarter.1 = bf16[512,1024]{1,0:T(8,128)(2,1)} custom-call(f32[2048,512]{1,0:T(8,128)} %bitcast.10, f32[2048,512]{1,0:T(8,128)} %bitcast.11, s32[2,1,1024]{2,1,0:T(1,128)} %bitcast.14), custom_call_target="tpu_custom_call" | custom-call | flops 2000000000 | bytes 6000000 | tf_op jit(solution)/shard_map/quarter/pallas_call | solution.py:263
  5.6 11.4 %all-to-all-start = ((bf16[32,16,1024]{2,1,0:T(8,128)(2,1)}), bf16[32,16,1024]{2,1,0:T(8,128)(2,1)S(1)}, u32[]{:S(2)}, u32[]{:S(2)}) async-start(bf16[32,16,1024]{2,1,0:T(8,128)(2,1)} %bitcast.12), calls=%async_computation | async-start | bytes 2097152 | tf_op jit(solution)/shard_map/all_to_all | solution.py:462
  16.9 19.4 %spectra.1 = bf16[128,16,768]{2,1,0:T(8,128)(2,1)} custom-call(bf16[16,110592]{1,0:T(8,128)(2,1)} %refs_0_, bf16[16,110592]{1,0:T(8,128)(2,1)} %refs_1_, f32[16,4096]{1,0:T(8,128)} %refs_2_, f32[32,128]{1,0:T(8,128)} %constant.121.clone.refs_3_, f32[32,128]{1,0:T(8,128)} %constant.122.clone.refs_4_, bf16[512,256]{1,0:T(8,128)(2,1)} %constant.123.clone.refs_5_), custom_call_target="tpu_custom_call" | custom-call | flops 2400000000 | bytes 48000000 | tf_op jit(solution)/shard_map/spectra/pallas_call | solution.py:196
  36.4 0.0 all-to-all-done.offers
  36.4 0.0 copy-start.2
  36.4 1.0 copy-done.2
  37.3 9.9 %all-to-all-start.1 = ((bf16[128,16,768]{2,1,0:T(8,128)(2,1)}), bf16[128,16,768]{2,1,0:T(8,128)(2,1)S(1)}, u32[]{:S(2)}, u32[]{:S(2)}) async-start(bf16[128,16,768]{2,1,0:T(8,128)(2,1)} %spectra.1), calls=%async_computation.1 | async-start | bytes 6291456 | tf_op jit(solution)/shard_map/all_to_all | solution.py:468
  47.3 0.0 copy-start.3
  47.3 0.0 copy-start.4
  47.3 0.0 copy-start.5
  47.3 2.2 %pick.1 = (bf16[16,1024]{1,0:T(8,128)(2,1)}, bf16[16,1024]{1,0:T(8,128)(2,1)}) custom-call(s32[2]{0:T(128)} %owners.1, bf16[32,16,1024]{2,1,0:T(8,128)(2,1)} %copy-done.2), custom_call_target="tpu_custom_call" | custom-call | tf_op jit(solution)/shard_map/pick/pallas_call | solution.py:295
  49.6 1.1 collective-permute-start
  50.7 1.1 collective-permute-done.refs_1_
  51.8 0.0 copy-start.1
  51.8 0.8 copy-done.1
  52.5 0.8 collective-permute-start.1
  53.3 1.9 %collective-permute-start.2 = (bf16[16,2048]{1,0:T(8,128)(2,1)S(1)}, bf16[16,2048]{1,0:T(8,128)(2,1)S(1)}, u32[]{:S(2)}, u32[]{:S(2)}) collective-permute-start(bf16[16,2048]{1,0:T(8,128)(2,1)S(1)} %join.3.refs_0_), channel_id=1, source_target_pairs={{64,0},{40,32},{1,64},{104,96},{65,1},{41,33},{0,65},{105,97},{66,... | collective-permute-start | bytes 196616 | tf_op jit(solution)/shard_map/ppermute | solution.py:435
  55.2 1.4 %collective-permute-start.3 = (bf16[16,2048]{1,0:T(8,128)(2,1)S(1)}, bf16[16,2048]{1,0:T(8,128)(2,1)S(1)}, u32[]{:S(2)}, u32[]{:S(2)}) collective-permute-start(bf16[16,2048]{1,0:T(8,128)(2,1)S(1)} %join.3.refs_0_), channel_id=1, source_target_pairs={{1,0},{48,32},{65,64},{112,96},{0,1},{49,33},{64,65},{113,97},{3,2... | collective-permute-start | bytes 196616 | tf_op jit(solution)/shard_map/ppermute | solution.py:435
  56.6 13.4 %collective-permute-done.1.refs_1_ = bf16[16,2048]{1,0:T(8,128)(2,1)S(1)} collective-permute-done((bf16[16,2048]{1,0:T(8,128)(2,1)S(1)}, bf16[16,2048]{1,0:T(8,128)(2,1)S(1)}, u32[]{:S(2)}, u32[]{:S(2)}) %collective-permute-start.1) | collective-permute-done | bytes 65568 | tf_op jit(solution)/shard_map/ppermute | solution.py:435
  70.0 3.4 %collective-permute-done.2.refs_2_ = bf16[16,2048]{1,0:T(8,128)(2,1)S(1)} collective-permute-done((bf16[16,2048]{1,0:T(8,128)(2,1)S(1)}, bf16[16,2048]{1,0:T(8,128)(2,1)S(1)}, u32[]{:S(2)}, u32[]{:S(2)}) %collective-permute-start.2) | collective-permute-done | bytes 65568 | tf_op jit(solution)/shard_map/ppermute | solution.py:435
  73.5 11.8 %collective-permute-done.3.refs_3_ = bf16[16,2048]{1,0:T(8,128)(2,1)S(1)} collective-permute-done((bf16[16,2048]{1,0:T(8,128)(2,1)S(1)}, bf16[16,2048]{1,0:T(8,128)(2,1)S(1)}, u32[]{:S(2)}, u32[]{:S(2)}) %collective-permute-start.3) | collective-permute-done | bytes 65568 | tf_op jit(solution)/shard_map/ppermute | solution.py:435
  85.3 0.3 collective-permute-start.4
  85.6 2.5 %collective-permute-start.5 = (bf16[64,2048]{1,0:T(8,128)(2,1)S(1)}, bf16[64,2048]{1,0:T(8,128)(2,1)S(1)}, u32[]{:S(2)}, u32[]{:S(2)}) collective-permute-start(bf16[64,2048]{1,0:T(8,128)(2,1)S(1)} %join.4.refs_0_), channel_id=1, source_target_pairs={{2,0},{96,32},{66,64},{33,96},{3,1},{97,33},{67,65},{32,97},{4,2},... | collective-permute-start | bytes 786440 | tf_op jit(solution)/shard_map/ppermute | solution.py:435
  88.1 1.3 %collective-permute-start.6 = (bf16[64,2048]{1,0:T(8,128)(2,1)S(1)}, bf16[64,2048]{1,0:T(8,128)(2,1)S(1)}, u32[]{:S(2)}, u32[]{:S(2)}) collective-permute-start(bf16[64,2048]{1,0:T(8,128)(2,1)S(1)} %join.4.refs_0_), channel_id=1, source_target_pairs={{4,0},{33,32},{68,64},{97,96},{5,1},{32,33},{69,65},{96,97},{6,2},... | collective-permute-start | bytes 786440 | tf_op jit(solution)/shard_map/ppermute | solution.py:435
  89.4 2.7 %collective-permute-done.4.refs_1_ = bf16[64,2048]{1,0:T(8,128)(2,1)S(1)} collective-permute-done((bf16[64,2048]{1,0:T(8,128)(2,1)S(1)}, bf16[64,2048]{1,0:T(8,128)(2,1)S(1)}, u32[]{:S(2)}, u32[]{:S(2)}) %collective-permute-start.4) | collective-permute-done | bytes 262176 | tf_op jit(solution)/shard_map/ppermute | solution.py:435
  92.1 2.1 %collective-permute-done.5.refs_2_ = bf16[64,2048]{1,0:T(8,128)(2,1)S(1)} collective-permute-done((bf16[64,2048]{1,0:T(8,128)(2,1)S(1)}, bf16[64,2048]{1,0:T(8,128)(2,1)S(1)}, u32[]{:S(2)}, u32[]{:S(2)}) %collective-permute-start.5) | collective-permute-done | bytes 262176 | tf_op jit(solution)/shard_map/ppermute | solution.py:435
  94.2 1.6 %collective-permute-done.6.refs_3_ = bf16[64,2048]{1,0:T(8,128)(2,1)S(1)} collective-permute-done((bf16[64,2048]{1,0:T(8,128)(2,1)S(1)}, bf16[64,2048]{1,0:T(8,128)(2,1)S(1)}, u32[]{:S(2)}, u32[]{:S(2)}) %collective-permute-start.6) | collective-permute-done | bytes 262176 | tf_op jit(solution)/shard_map/ppermute | solution.py:435
  95.8 1.0 join.5.w0
  96.8 0.0 copy-start
  96.8 3.9 %collective-permute-start.7 = (bf16[256,2048]{1,0:T(8,128)(2,1)}, bf16[256,2048]{1,0:T(8,128)(2,1)}, u32[]{:S(2)}, u32[]{:S(2)}) collective-permute-start(bf16[256,2048]{1,0:T(8,128)(2,1)} %join.5.w0), channel_id=1, source_target_pairs={{16,0},{36,32},{80,64},{100,96},{17,1},{37,33},{81,65},{101,97},{1... | collective-permute-start | bytes 3145736 | tf_op jit(solution)/shard_map/ppermute | solution.py:435
  100.7 0.0 collective-permute-start.8
  100.7 2.7 %collective-permute-start.9 = (bf16[256,2048]{1,0:T(8,128)(2,1)}, bf16[256,2048]{1,0:T(8,128)(2,1)}, u32[]{:S(2)}, u32[]{:S(2)}) collective-permute-start(bf16[256,2048]{1,0:T(8,128)(2,1)} %join.5.w0), channel_id=1, source_target_pairs={{8,0},{34,32},{72,64},{98,96},{9,1},{35,33},{73,65},{99,97},{10,2}... | collective-permute-start | bytes 3145736 | tf_op jit(solution)/shard_map/ppermute | solution.py:435
  103.4 0.0 copy-done.3
  103.4 0.0 copy-done.4
  103.4 0.0 copy-done.5
  103.5 0.1 slice.11
  103.5 0.1 fusion.16
  103.6 0.1 pad_add_fusion.places
  103.7 9.9 %collective-permute-done.7.w1 = bf16[256,2048]{1,0:T(8,128)(2,1)} collective-permute-done((bf16[256,2048]{1,0:T(8,128)(2,1)}, bf16[256,2048]{1,0:T(8,128)(2,1)}, u32[]{:S(2)}, u32[]{:S(2)}) %collective-permute-start.7) | collective-permute-done | bytes 1048608 | tf_op jit(solution)/shard_map/ppermute | solution.py:435
  113.6 0.0 all-to-all-done.1
  113.6 3.3 %early.1 = f32[512,768]{1,0:T(8,128)S(1)} custom-call(bf16[256,2048]{1,0:T(8,128)(2,1)} %join.5.w0, bf16[256,2048]{1,0:T(8,128)(2,1)} %collective-permute-done.7.w1, bf16[2048,768]{1,0:T(8,128)(2,1)S(1)} %bitcast.7), custom_call_target="tpu_custom_call" | custom-call | flops 1700000000 | bytes 8000000 | tf_op jit(solution)/shard_map/early/pallas_call | solution.py:359
  116.9 7.9 %collective-permute-done.8.w2 = bf16[256,2048]{1,0:T(8,128)(2,1)} collective-permute-done((bf16[256,2048]{1,0:T(8,128)(2,1)}, bf16[256,2048]{1,0:T(8,128)(2,1)}, u32[]{:S(2)}, u32[]{:S(2)}) %collective-permute-start.8) | collective-permute-done | bytes 1048608 | tf_op jit(solution)/shard_map/ppermute | solution.py:435
  124.8 0.0 collective-permute-done.9.w3
  124.8 0.0 copy-done
  124.8 4.3 %beams.1 = (f32[32,512]{1,0:T(8,128)S(1)}, f32[32,512]{1,0:T(8,128)S(1)}) custom-call(s32[64]{0:T(128)S(1)} %pad_add_fusion.places, f32[512,768]{1,0:T(8,128)S(1)} %early.1, bf16[256,2048]{1,0:T(8,128)(2,1)} %collective-permute-done.8.w2, bf16[256,2048]{1,0:T(8,128)(2,1)} %collective-permute-done.9.w3, bf16[2048,768]{1,0:T(8,128)(2,1)S(1)} %bitcast.8, ...), custom_call_target="tpu_custom_call" | custom-call | flops 1700000000 | bytes 8000000 | tf_op jit(solution)/shard_map/beams/pallas_call | solution.py:402
  129.1 3.0 %collective-permute-start.10 = (f32[32,512]{1,0:T(8,128)S(1)}, f32[32,512]{1,0:T(8,128)S(1)}, u32[]{:S(2)}, u32[]{:S(2)}) collective-permute-start(f32[32,512]{1,0:T(8,128)S(1)} %get-tuple-element.22), channel_id=1, source_target_pairs={{0,32},{32,0},{64,96},{96,64},{1,33},{33,1},{65,97},{97,65},{2,34}... | collective-permute-start | bytes 196616 | tf_op jit(solution)/shard_map/ppermute | solution.py:482
  132.1 0.9 collective-permute-done.10
  133.0 0.7 maximum_select_fusion
  (3 shorter events, 0.0 us)
Async XLA Ops:
  5.6 30.8 %all-to-all-start = ((bf16[32,16,1024]{2,1,0:T(8,128)(2,1)}), bf16[32,16,1024]{2,1,0:T(8,128)(2,1)S(1)}, u32[]{:S(2)}, u32[]{:S(2)}) async-start(bf16[32,16,1024]{2,1,0:T(8,128)(2,1)} %bitcast.12), calls=%async_computation | async-start | bytes 2097152 | tf_op jit(solution)/shard_map/all_to_all | solution.py:462
  36.4 1.0 copy-start.2
  37.3 76.2 %all-to-all-start.1 = ((bf16[128,16,768]{2,1,0:T(8,128)(2,1)}), bf16[128,16,768]{2,1,0:T(8,128)(2,1)S(1)}, u32[]{:S(2)}, u32[]{:S(2)}) async-start(bf16[128,16,768]{2,1,0:T(8,128)(2,1)} %spectra.1), calls=%async_computation.1 | async-start | bytes 6291456 | tf_op jit(solution)/shard_map/all_to_all | solution.py:468
  47.3 56.1 %copy-start.3 = (s32[64]{0:T(128)S(1)}, s32[64]{0:T(128)}, u32[]{:S(2)}) copy-start(s32[64]{0:T(128)} %constant.124.clone) | copy-start | bytes 772
  47.3 56.1 %copy-start.4 = (s32[64]{0:T(128)S(1)}, s32[64]{0:T(128)}, u32[]{:S(2)}) copy-start(s32[64]{0:T(128)} %constant.125.clone) | copy-start | bytes 772
  47.3 56.1 %copy-start.5 = (s32[64]{0:T(128)S(1)}, s32[64]{0:T(128)}, u32[]{:S(2)}) copy-start(s32[64]{0:T(128)} %constant.126.clone) | copy-start | bytes 772
  49.6 2.2 %collective-permute-start = (bf16[16,1024]{1,0:T(8,128)(2,1)}, bf16[16,1024]{1,0:T(8,128)(2,1)S(1)}, u32[]{:S(2)}, u32[]{:S(2)}) collective-permute-start(bf16[16,1024]{1,0:T(8,128)(2,1)} %get-tuple-element.19), channel_id=1, source_target_pairs={{0,32},{32,0},{64,96},{96,64},{1,33},{33,1},{65,97},{97,65},{2,34}... | collective-permute-start | bytes 98312 | tf_op jit(solution)/shard_map/ppermute | solution.py:472
  51.8 0.8 copy-start.1
  52.5 17.5 %collective-permute-start.1 = (bf16[16,2048]{1,0:T(8,128)(2,1)S(1)}, bf16[16,2048]{1,0:T(8,128)(2,1)S(1)}, u32[]{:S(2)}, u32[]{:S(2)}) collective-permute-start(bf16[16,2048]{1,0:T(8,128)(2,1)S(1)} %join.3.refs_0_), channel_id=1, source_target_pairs={{65,0},{56,32},{0,64},{120,96},{64,1},{57,33},{1,65},{121,97},{67,... | collective-permute-start | bytes 196616 | tf_op jit(solution)/shard_map/ppermute | solution.py:435
  53.3 20.1 %collective-permute-start.2 = (bf16[16,2048]{1,0:T(8,128)(2,1)S(1)}, bf16[16,2048]{1,0:T(8,128)(2,1)S(1)}, u32[]{:S(2)}, u32[]{:S(2)}) collective-permute-start(bf16[16,2048]{1,0:T(8,128)(2,1)S(1)} %join.3.refs_0_), channel_id=1, source_target_pairs={{64,0},{40,32},{1,64},{104,96},{65,1},{41,33},{0,65},{105,97},{66,... | collective-permute-start | bytes 196616 | tf_op jit(solution)/shard_map/ppermute | solution.py:435
  55.2 30.1 %collective-permute-start.3 = (bf16[16,2048]{1,0:T(8,128)(2,1)S(1)}, bf16[16,2048]{1,0:T(8,128)(2,1)S(1)}, u32[]{:S(2)}, u32[]{:S(2)}) collective-permute-start(bf16[16,2048]{1,0:T(8,128)(2,1)S(1)} %join.3.refs_0_), channel_id=1, source_target_pairs={{1,0},{48,32},{65,64},{112,96},{0,1},{49,33},{64,65},{113,97},{3,2... | collective-permute-start | bytes 196616 | tf_op jit(solution)/shard_map/ppermute | solution.py:435
  85.3 6.8 %collective-permute-start.4 = (bf16[64,2048]{1,0:T(8,128)(2,1)S(1)}, bf16[64,2048]{1,0:T(8,128)(2,1)S(1)}, u32[]{:S(2)}, u32[]{:S(2)}) collective-permute-start(bf16[64,2048]{1,0:T(8,128)(2,1)S(1)} %join.4.refs_0_), channel_id=1, source_target_pairs={{6,0},{97,32},{70,64},{32,96},{7,1},{96,33},{71,65},{33,97},{0,2},... | collective-permute-start | bytes 786440 | tf_op jit(solution)/shard_map/ppermute | solution.py:435
  85.6 8.6 %collective-permute-start.5 = (bf16[64,2048]{1,0:T(8,128)(2,1)S(1)}, bf16[64,2048]{1,0:T(8,128)(2,1)S(1)}, u32[]{:S(2)}, u32[]{:S(2)}) collective-permute-start(bf16[64,2048]{1,0:T(8,128)(2,1)S(1)} %join.4.refs_0_), channel_id=1, source_target_pairs={{2,0},{96,32},{66,64},{33,96},{3,1},{97,33},{67,65},{32,97},{4,2},... | collective-permute-start | bytes 786440 | tf_op jit(solution)/shard_map/ppermute | solution.py:435
  88.1 7.7 %collective-permute-start.6 = (bf16[64,2048]{1,0:T(8,128)(2,1)S(1)}, bf16[64,2048]{1,0:T(8,128)(2,1)S(1)}, u32[]{:S(2)}, u32[]{:S(2)}) collective-permute-start(bf16[64,2048]{1,0:T(8,128)(2,1)S(1)} %join.4.refs_0_), channel_id=1, source_target_pairs={{4,0},{33,32},{68,64},{97,96},{5,1},{32,33},{69,65},{96,97},{6,2},... | collective-permute-start | bytes 786440 | tf_op jit(solution)/shard_map/ppermute | solution.py:435
  96.8 28.0 %copy-start = (f32[64,384]{1,0:T(8,128)S(1)}, f32[64,384]{1,0:T(8,128)}, u32[]{:S(2)}) copy-start(f32[64,384]{1,0:T(8,128)} %constant.127.clone.choose) | copy-start | bytes 294916
  96.8 16.8 %collective-permute-start.7 = (bf16[256,2048]{1,0:T(8,128)(2,1)}, bf16[256,2048]{1,0:T(8,128)(2,1)}, u32[]{:S(2)}, u32[]{:S(2)}) collective-permute-start(bf16[256,2048]{1,0:T(8,128)(2,1)} %join.5.w0), channel_id=1, source_target_pairs={{16,0},{36,32},{80,64},{100,96},{17,1},{37,33},{81,65},{101,97},{1... | collective-permute-start | bytes 3145736 | tf_op jit(solution)/shard_map/ppermute | solution.py:435
  100.7 24.0 %collective-permute-start.8 = (bf16[256,2048]{1,0:T(8,128)(2,1)}, bf16[256,2048]{1,0:T(8,128)(2,1)}, u32[]{:S(2)}, u32[]{:S(2)}) collective-permute-start(bf16[256,2048]{1,0:T(8,128)(2,1)} %join.5.w0), channel_id=1, source_target_pairs={{24,0},{38,32},{88,64},{102,96},{25,1},{39,33},{89,65},{103,97},{2... | collective-permute-start | bytes 3145736 | tf_op jit(solution)/shard_map/ppermute | solution.py:435
  100.7 24.0 %collective-permute-start.9 = (bf16[256,2048]{1,0:T(8,128)(2,1)}, bf16[256,2048]{1,0:T(8,128)(2,1)}, u32[]{:S(2)}, u32[]{:S(2)}) collective-permute-start(bf16[256,2048]{1,0:T(8,128)(2,1)} %join.5.w0), channel_id=1, source_target_pairs={{8,0},{34,32},{72,64},{98,96},{9,1},{35,33},{73,65},{99,97},{10,2}... | collective-permute-start | bytes 3145736 | tf_op jit(solution)/shard_map/ppermute | solution.py:435
  129.1 3.9 %collective-permute-start.10 = (f32[32,512]{1,0:T(8,128)S(1)}, f32[32,512]{1,0:T(8,128)S(1)}, u32[]{:S(2)}, u32[]{:S(2)}) collective-permute-start(f32[32,512]{1,0:T(8,128)S(1)} %get-tuple-element.22), channel_id=1, source_target_pairs={{0,32},{32,0},{64,96},{96,64},{1,33},{33,1},{65,97},{97,65},{2,34}... | collective-permute-start | bytes 196616 | tf_op jit(solution)/shard_map/ppermute | solution.py:482

commit v10 on v7

--- a/solution.py
+++ b/solution.py
@@ -108,7 +108,7 @@
                 frames[c, i, n1] = total
             return 0
 
-        lax.fori_loop(0, OUTER, fir, 0)
+        lax.fori_loop(0, OUTER, fir, 0, unroll=2)
 
     for load in loads[3:]:
         load.wait()
@@ -130,7 +130,7 @@
             turned[1, pl.ds(at, 8, stride=slot_stride), :] = im
         return 0
 
-    lax.fori_loop(0, 2 * len(chosen), outer, 0)
+    lax.fori_loop(0, 2 * len(chosen), outer, 0, unroll=2)
 
     matrix = mat[...]
     lane = lax.broadcasted_iota(jnp.int32, (32, INNER), 1)
@@ -153,7 +153,7 @@
                     packed[g * 2 + c, to[1], :] = jnp.where(lane < 64, pltpu.roll(mixed[0], 64, 1), mixed[1])
         return 0
 
-    lax.fori_loop(0, SLOTS, inner, 0, unroll=4)
+    lax.fori_loop(0, SLOTS, inner, 0, unroll=8)
 
     stores = []
     tile = 0
@@ -272,27 +272,20 @@
     )(wre, wim, antenna_map.reshape(2, 1, half))
 
 
-def pick_kernel(owners, offers, mine, other, sems):
+def pick_kernel(owners, offers, mine, other):
     core = lax.axis_index("grp") % 2
-    copies = [
-        pltpu.make_async_copy(offers.at[owners[core]], mine, sems.at[0]),
-        pltpu.make_async_copy(offers.at[owners[1 - core]], other, sems.at[1]),
-    ]
-    for copy in copies:
-        copy.start()
-    for copy in copies:
-        copy.wait()
+    mine[...] = offers[owners[core]]
+    other[...] = offers[owners[1 - core]]
 
 
 def pick_of(owners, offers, interpret=False):
     _, rows, columns = offers.shape
     return pl.pallas_call(
         pick_kernel,
-        in_specs=[pl.BlockSpec(memory_space=pltpu.SMEM), pl.BlockSpec(memory_space=pltpu.HBM)],
+        in_specs=[pl.BlockSpec(memory_space=pltpu.SMEM), pl.BlockSpec(memory_space=pltpu.VMEM)],
         out_specs=[pl.BlockSpec(memory_space=pltpu.VMEM)] * 2,
         out_shape=[jax.ShapeDtypeStruct((rows, columns), offers.dtype)] * 2,
-        scratch_shapes=[pltpu.SemaphoreType.DMA((2,))],
-        compiler_params=pltpu.CompilerParams(vmem_limit_bytes=58 * MIB),
+        compiler_params=pltpu.CompilerParams(vmem_limit_bytes=8 * MIB),
         interpret=interpret,
         name="pick",
     )(owners, offers)
@@ -362,7 +355,7 @@
     )(w0, w1, spectra)
 
 
-def beams_kernel(places, early, w2, w3, za, choose, out, sums):
+def beams_kernel(places, early, w2, w3, za, choose, own, given, sums):
     for k in range(32):
         at = pl.multiple_of(places[k], 16)
         sums[pl.ds(at, 16), :] = early[k * 16 : (k + 1) * 16, :]
@@ -386,16 +379,18 @@
         preferred_element_type=jnp.float32,
         precision=lax.Precision.HIGHEST,
     )
-    out[...] = total * (1.0 / SPECTRA)
+    total = total * (1.0 / SPECTRA)
+    own[...] = jnp.where(core == 0, total[:32], total[32:])
+    given[...] = jnp.where(core == 0, total[32:], total[:32])
 
 
 def beams_of(places, early, w2, w3, spectra, interpret=False):
     rows = early.shape[0] + 2 * w2.shape[0]
     return pl.pallas_call(
         beams_kernel,
-        out_shape=jax.ShapeDtypeStruct((64, rows // 2), jnp.float32),
+        out_shape=[jax.ShapeDtypeStruct((32, rows // 2), jnp.float32)] * 2,
         in_specs=[pl.BlockSpec(memory_space=pltpu.SMEM)] + [pl.BlockSpec(memory_space=pltpu.VMEM)] * 5,
-        out_specs=pl.BlockSpec(memory_space=pltpu.VMEM),
+        out_specs=[pl.BlockSpec(memory_space=pltpu.VMEM)] * 2,
         scratch_shapes=[pltpu.VMEM((rows, 768), jnp.float32)],
         compiler_params=pltpu.CompilerParams(vmem_limit_bytes=32 * MIB),
         cost_estimate=pl.CostEstimate(flops=17 * 10**8, bytes_accessed=8 * 10**6, transcendentals=0),
@@ -457,10 +452,11 @@
     quarter, *volts = lax.optimization_barrier((quarter, *volts))
     (message,) = spectra_of(MESSAGES, *volts)
     message, offers = lax.optimization_barrier((message, offers))
+    mine, other = pick_of(owners, offers)
+    message, mine, other = lax.optimization_barrier((message, mine, other))
     spectra = lax.all_to_all(message, ALL, split_axis=0, concat_axis=0, tiled=True)
     spectra = spectra.reshape(DEVICES * SLOTS, -1)
 
-    mine, other = pick_of(owners, offers)
     other = lax.ppermute(other, "grp", SWAP)
     block = join_of([mine, other], 1)
     block = join_of(gather_stage(block, 0), 0)
@@ -470,10 +466,7 @@
     early = early_of(parts[0], parts[3], spectra)
     places = block_places(grp, dev)
     places = jnp.concatenate([places[:16], places[48:], places[16:48]])
-    power = beams_of(places, early, parts[1], parts[2], spectra)
-    power = power.reshape(2, 32, -1)
-    own = jnp.where(core == 0, power[0], power[1])
-    given = jnp.where(core == 0, power[1], power[0])
+    own, given = beams_of(places, early, parts[1], parts[2], spectra)
     taken = lax.ppermute(given, "grp", SWAP)
     return jnp.where(core == 0, jnp.stack([own, taken]), jnp.stack([taken, own]))
 

time: 132 us -> 131 us (level)
  starting transfers between devices: 39.7 us -> 53.3 us
  waiting for transfers between devices: 55.3 us -> 44.7 us
  Pallas kernels: 34.1 us -> 31.7 us
  local copies, waits for them, and re-layouts: 1.89 us -> 0.18 us
    ppermute x9, starting transfers between devices: 14.7 us -> 29.1 us  [gather_stage(): lax.ppermute(block, ALL, permutation(stage, shift))]
    ppermute x9, waiting for transfers between devices: 52.8 us -> 41.7 us  [gather_stage(): lax.ppermute(block, ALL, permutation(stage, shift))]
    unnamed x12 -> x10, local copies, waits for them, and re-layouts: 1.74 us -> 0.03 us
    pallas_call x1, Pallas kernels: 2.22 us -> 0.56 us  [pick_of(): pl.pallas_call(pick_kernel, in_specs=[pl.BlockSpec(memory_space=pltpu.SME...]
  transfers between devices with their start and end apart: 13 -> 13, of which waited for: 11 -> 11; matrix products, arithmetic and copies ran while one was open for 0% -> 0% of each run, Pallas kernels for 18% -> 16%
where the time goes in v10:
time: 131 us
  starting transfers between devices  53.3 us (41%)
  waiting for transfers between devices  44.7 us (34%)
  Pallas kernels  31.7 us (24%)
    ppermute x9, waiting for transfers between devices, gather_stage(): lax.ppermute(block, ALL, permutation(stage, shift))  41.7 us
    ppermute x9, starting transfers between devices, gather_stage(): lax.ppermute(block, ALL, permutation(stage, shift))  29.1 us
    pallas_call x1, Pallas kernels, spectra_of(): pl.pallas_call(functools.partial(spectra_kernel, messages), out_shape=[ja...  16.8 us
    all_to_all x1, starting transfers between devices, on_device(): lax.all_to_all(quarter.reshape(32, 16, -1), 'dev', split_axis=0, concat_a...  11.4 us
    all_to_all x1, starting transfers between devices, on_device(): lax.all_to_all(message, ALL, split_axis=0, concat_axis=0, tiled=True)  8.66 us
    pallas_call x1, Pallas kernels, quarter_of(): pl.pallas_call(quarter_kernel, in_specs=[pl.BlockSpec(memory_space=pltpu....  5.57 us
    pallas_call x1, Pallas kernels, beams_of(): pl.pallas_call(beams_kernel, out_shape=[jax.ShapeDtypeStruct((32, rows //...  4.33 us
    pallas_call x1, Pallas kernels, early_of(): pl.pallas_call(early_kernel, out_shape=jax.ShapeDtypeStruct((2 * w0.shape...  3.33 us
  transfers between devices with their start and end apart: 13, of which 11 were waited for; matrix products, arithmetic and copies ran while one was open for 0% of the time, Pallas kernels for 16%

profile of v10, /device:TPU:1, one launch (start us, length us, event | category | flops | bytes accessed | tf_op | source)
XLA Modules:
  0.0 130.7 jit_solution(4615342555091195126)
XLA Ops:
  0.0 5.6 %quarter.1 = bf16[512,1024]{1,0:T(8,128)(2,1)} custom-call(f32[2048,512]{1,0:T(8,128)} %bitcast.10, f32[2048,512]{1,0:T(8,128)} %bitcast.11, s32[2,1,1024]{2,1,0:T(1,128)} %bitcast.14), custom_call_target="tpu_custom_call" | custom-call | flops 2000000000 | bytes 6000000 | tf_op jit(solution)/shard_map/quarter/pallas_call | solution.py:257
  5.6 11.4 %all-to-all-start = ((bf16[32,16,1024]{2,1,0:T(8,128)(2,1)}), bf16[32,16,1024]{2,1,0:T(8,128)(2,1)S(1)}, u32[]{:S(2)}, u32[]{:S(2)}) async-start(bf16[32,16,1024]{2,1,0:T(8,128)(2,1)} %bitcast.12), calls=%async_computation | async-start | bytes 2097152 | tf_op jit(solution)/shard_map/all_to_all | solution.py:449
  16.9 0.0 copy-start.1
  17.0 16.8 %spectra.1 = bf16[128,16,768]{2,1,0:T(8,128)(2,1)} custom-call(bf16[16,110592]{1,0:T(8,128)(2,1)} %refs_0_, bf16[16,110592]{1,0:T(8,128)(2,1)} %refs_1_, f32[16,4096]{1,0:T(8,128)} %refs_2_, f32[32,128]{1,0:T(8,128)} %constant.121.clone.refs_3_, f32[32,128]{1,0:T(8,128)} %constant.122.clone.refs_4_, bf16[256,256]{1,0:T(8,128)(2,1)} %constant.123.clone.refs_5_), custom_call_target="tpu_custom_call" | custom-call | flops 2400000000 | bytes 48000000 | tf_op jit(solution)/shard_map/spectra/pallas_call | solution.py:190
  33.8 1.3 %all-to-all-done.offers = bf16[32,16,1024]{2,1,0:T(8,128)(2,1)S(1)} async-done(((bf16[32,16,1024]{2,1,0:T(8,128)(2,1)}), bf16[32,16,1024]{2,1,0:T(8,128)(2,1)S(1)}, u32[]{:S(2)}, u32[]{:S(2)}) %all-to-all-start) | async-done | bytes 1048608 | tf_op jit(solution)/shard_map/all_to_all | solution.py:449
  35.1 0.0 copy-done.1
  35.1 0.6 pick.1
  35.7 0.0 copy-start.2
  35.7 0.0 copy-start.3
  35.7 0.0 copy-start.4
  35.7 8.7 %all-to-all-start.1 = ((bf16[128,16,768]{2,1,0:T(8,128)(2,1)}), bf16[128,16,768]{2,1,0:T(8,128)(2,1)S(1)}, u32[]{:S(2)}, u32[]{:S(2)}) async-start(bf16[128,16,768]{2,1,0:T(8,128)(2,1)} %spectra.1), calls=%async_computation.1 | async-start | bytes 6291456 | tf_op jit(solution)/shard_map/all_to_all | solution.py:457
  44.4 1.1 collective-permute-start
  45.5 0.9 collective-permute-done.refs_1_
  46.4 0.8 collective-permute-start.1
  47.2 1.9 %collective-permute-start.2 = (bf16[16,2048]{1,0:T(8,128)(2,1)S(1)}, bf16[16,2048]{1,0:T(8,128)(2,1)S(1)}, u32[]{:S(2)}, u32[]{:S(2)}) collective-permute-start(bf16[16,2048]{1,0:T(8,128)(2,1)S(1)} %join.3.refs_0_), channel_id=1, source_target_pairs={{64,0},{40,32},{1,64},{104,96},{65,1},{41,33},{0,65},{105,97},{66,... | collective-permute-start | bytes 196616 | tf_op jit(solution)/shard_map/ppermute | solution.py:422
  49.0 1.4 %collective-permute-start.3 = (bf16[16,2048]{1,0:T(8,128)(2,1)S(1)}, bf16[16,2048]{1,0:T(8,128)(2,1)S(1)}, u32[]{:S(2)}, u32[]{:S(2)}) collective-permute-start(bf16[16,2048]{1,0:T(8,128)(2,1)S(1)} %join.3.refs_0_), channel_id=1, source_target_pairs={{1,0},{48,32},{65,64},{112,96},{0,1},{49,33},{64,65},{113,97},{3,2... | collective-permute-start | bytes 196616 | tf_op jit(solution)/shard_map/ppermute | solution.py:422
  50.4 1.9 %collective-permute-done.1.refs_1_ = bf16[16,2048]{1,0:T(8,128)(2,1)S(1)} collective-permute-done((bf16[16,2048]{1,0:T(8,128)(2,1)S(1)}, bf16[16,2048]{1,0:T(8,128)(2,1)S(1)}, u32[]{:S(2)}, u32[]{:S(2)}) %collective-permute-start.1) | collective-permute-done | bytes 65568 | tf_op jit(solution)/shard_map/ppermute | solution.py:422
  52.3 0.9 collective-permute-done.2.refs_2_
  53.2 14.2 %collective-permute-done.3.refs_3_ = bf16[16,2048]{1,0:T(8,128)(2,1)S(1)} collective-permute-done((bf16[16,2048]{1,0:T(8,128)(2,1)S(1)}, bf16[16,2048]{1,0:T(8,128)(2,1)S(1)}, u32[]{:S(2)}, u32[]{:S(2)}) %collective-permute-start.3) | collective-permute-done | bytes 65568 | tf_op jit(solution)/shard_map/ppermute | solution.py:422
  67.5 10.7 %collective-permute-start.4 = (bf16[64,2048]{1,0:T(8,128)(2,1)S(1)}, bf16[64,2048]{1,0:T(8,128)(2,1)S(1)}, u32[]{:S(2)}, u32[]{:S(2)}) collective-permute-start(bf16[64,2048]{1,0:T(8,128)(2,1)S(1)} %join.4.refs_0_), channel_id=1, source_target_pairs={{6,0},{97,32},{70,64},{32,96},{7,1},{96,33},{71,65},{33,97},{0,2},... | collective-permute-start | bytes 786440 | tf_op jit(solution)/shard_map/ppermute | solution.py:422
  78.2 6.4 %collective-permute-start.5 = (bf16[64,2048]{1,0:T(8,128)(2,1)S(1)}, bf16[64,2048]{1,0:T(8,128)(2,1)S(1)}, u32[]{:S(2)}, u32[]{:S(2)}) collective-permute-start(bf16[64,2048]{1,0:T(8,128)(2,1)S(1)} %join.4.refs_0_), channel_id=1, source_target_pairs={{2,0},{96,32},{66,64},{33,96},{3,1},{97,33},{67,65},{32,97},{4,2},... | collective-permute-start | bytes 786440 | tf_op jit(solution)/shard_map/ppermute | solution.py:422
  84.6 1.1 collective-permute-start.6
  85.7 2.9 %collective-permute-done.4.refs_1_ = bf16[64,2048]{1,0:T(8,128)(2,1)S(1)} collective-permute-done((bf16[64,2048]{1,0:T(8,128)(2,1)S(1)}, bf16[64,2048]{1,0:T(8,128)(2,1)S(1)}, u32[]{:S(2)}, u32[]{:S(2)}) %collective-permute-start.4) | collective-permute-done | bytes 262176 | tf_op jit(solution)/shard_map/ppermute | solution.py:422
  88.6 2.2 %collective-permute-done.5.refs_2_ = bf16[64,2048]{1,0:T(8,128)(2,1)S(1)} collective-permute-done((bf16[64,2048]{1,0:T(8,128)(2,1)S(1)}, bf16[64,2048]{1,0:T(8,128)(2,1)S(1)}, u32[]{:S(2)}, u32[]{:S(2)}) %collective-permute-start.5) | collective-permute-done | bytes 262176 | tf_op jit(solution)/shard_map/ppermute | solution.py:422
  90.7 1.8 %collective-permute-done.6.refs_3_ = bf16[64,2048]{1,0:T(8,128)(2,1)S(1)} collective-permute-done((bf16[64,2048]{1,0:T(8,128)(2,1)S(1)}, bf16[64,2048]{1,0:T(8,128)(2,1)S(1)}, u32[]{:S(2)}, u32[]{:S(2)}) %collective-permute-start.6) | collective-permute-done | bytes 262176 | tf_op jit(solution)/shard_map/ppermute | solution.py:422
  92.6 1.0 join.5.w0
  93.6 0.0 copy-start
  93.6 4.2 %collective-permute-start.7 = (bf16[256,2048]{1,0:T(8,128)(2,1)}, bf16[256,2048]{1,0:T(8,128)(2,1)}, u32[]{:S(2)}, u32[]{:S(2)}) collective-permute-start(bf16[256,2048]{1,0:T(8,128)(2,1)} %join.5.w0), channel_id=1, source_target_pairs={{16,0},{36,32},{80,64},{100,96},{17,1},{37,33},{81,65},{101,97},{1... | collective-permute-start | bytes 3145736 | tf_op jit(solution)/shard_map/ppermute | solution.py:422
  97.8 0.0 collective-permute-start.8
  97.8 2.7 %collective-permute-start.9 = (bf16[256,2048]{1,0:T(8,128)(2,1)}, bf16[256,2048]{1,0:T(8,128)(2,1)}, u32[]{:S(2)}, u32[]{:S(2)}) collective-permute-start(bf16[256,2048]{1,0:T(8,128)(2,1)} %join.5.w0), channel_id=1, source_target_pairs={{8,0},{34,32},{72,64},{98,96},{9,1},{35,33},{73,65},{99,97},{10,2}... | collective-permute-start | bytes 3145736 | tf_op jit(solution)/shard_map/ppermute | solution.py:422
  100.5 0.0 copy-done.2
  100.5 0.0 copy-done.3
  100.5 0.0 copy-done.4
  100.5 0.1 slice.11
  100.6 0.1 fusion.16
  100.7 0.1 pad_add_fusion.places
  100.8 9.9 %collective-permute-done.7.w1 = bf16[256,2048]{1,0:T(8,128)(2,1)} collective-permute-done((bf16[256,2048]{1,0:T(8,128)(2,1)}, bf16[256,2048]{1,0:T(8,128)(2,1)}, u32[]{:S(2)}, u32[]{:S(2)}) %collective-permute-start.7) | collective-permute-done | bytes 1048608 | tf_op jit(solution)/shard_map/ppermute | solution.py:422
  110.7 0.0 all-to-all-done.1
  110.7 3.3 %early.1 = f32[512,768]{1,0:T(8,128)S(1)} custom-call(bf16[256,2048]{1,0:T(8,128)(2,1)} %join.5.w0, bf16[256,2048]{1,0:T(8,128)(2,1)} %collective-permute-done.7.w1, bf16[2048,768]{1,0:T(8,128)(2,1)S(1)} %bitcast.7), custom_call_target="tpu_custom_call" | custom-call | flops 1700000000 | bytes 8000000 | tf_op jit(solution)/shard_map/early/pallas_call | solution.py:346
  114.0 7.9 %collective-permute-done.8.w2 = bf16[256,2048]{1,0:T(8,128)(2,1)} collective-permute-done((bf16[256,2048]{1,0:T(8,128)(2,1)}, bf16[256,2048]{1,0:T(8,128)(2,1)}, u32[]{:S(2)}, u32[]{:S(2)}) %collective-permute-start.8) | collective-permute-done | bytes 1048608 | tf_op jit(solution)/shard_map/ppermute | solution.py:422
  121.8 0.0 collective-permute-done.9.w3
  121.8 0.0 copy-done
  121.9 4.3 %beams.1 = (f32[32,512]{1,0:T(8,128)S(1)}, f32[32,512]{1,0:T(8,128)S(1)}) custom-call(s32[64]{0:T(128)S(1)} %pad_add_fusion.places, f32[512,768]{1,0:T(8,128)S(1)} %early.1, bf16[256,2048]{1,0:T(8,128)(2,1)} %collective-permute-done.8.w2, bf16[256,2048]{1,0:T(8,128)(2,1)} %collective-permute-done.9.w3, bf16[2048,768]{1,0:T(8,128)(2,1)S(1)} %bitcast.8, ...), custom_call_target="tpu_custom_call" | custom-call | flops 1700000000 | bytes 8000000 | tf_op jit(solution)/shard_map/beams/pallas_call | solution.py:389
  126.2 3.0 %collective-permute-start.10 = (f32[32,512]{1,0:T(8,128)S(1)}, f32[32,512]{1,0:T(8,128)S(1)}, u32[]{:S(2)}, u32[]{:S(2)}) collective-permute-start(f32[32,512]{1,0:T(8,128)S(1)} %get-tuple-element.28), channel_id=1, source_target_pairs={{0,32},{32,0},{64,96},{96,64},{1,33},{33,1},{65,97},{97,65},{2,34}... | collective-permute-start | bytes 196616 | tf_op jit(solution)/shard_map/ppermute | solution.py:470
  129.2 0.9 collective-permute-done.10
  130.1 0.7 maximum_select_fusion
  (3 shorter events, 0.0 us)
Async XLA Ops:
  5.6 29.5 %all-to-all-start = ((bf16[32,16,1024]{2,1,0:T(8,128)(2,1)}), bf16[32,16,1024]{2,1,0:T(8,128)(2,1)S(1)}, u32[]{:S(2)}, u32[]{:S(2)}) async-start(bf16[32,16,1024]{2,1,0:T(8,128)(2,1)} %bitcast.12), calls=%async_computation | async-start | bytes 2097152 | tf_op jit(solution)/shard_map/all_to_all | solution.py:449
  16.9 18.1 %copy-start.1 = (s32[2]{0:T(128)S(1)}, s32[2]{0:T(128)}, u32[]{:S(2)}) copy-start(s32[2]{0:T(128)} %owners.1) | copy-start | bytes 28
  35.7 64.8 %copy-start.2 = (s32[64]{0:T(128)S(1)}, s32[64]{0:T(128)}, u32[]{:S(2)}) copy-start(s32[64]{0:T(128)} %constant.124.clone) | copy-start | bytes 772
  35.7 64.8 %copy-start.3 = (s32[64]{0:T(128)S(1)}, s32[64]{0:T(128)}, u32[]{:S(2)}) copy-start(s32[64]{0:T(128)} %constant.125.clone) | copy-start | bytes 772
  35.7 64.8 %copy-start.4 = (s32[64]{0:T(128)S(1)}, s32[64]{0:T(128)}, u32[]{:S(2)}) copy-start(s32[64]{0:T(128)} %constant.126.clone) | copy-start | bytes 772
  35.7 75.0 %all-to-all-start.1 = ((bf16[128,16,768]{2,1,0:T(8,128)(2,1)}), bf16[128,16,768]{2,1,0:T(8,128)(2,1)S(1)}, u32[]{:S(2)}, u32[]{:S(2)}) async-start(bf16[128,16,768]{2,1,0:T(8,128)(2,1)} %spectra.1), calls=%async_computation.1 | async-start | bytes 6291456 | tf_op jit(solution)/shard_map/all_to_all | solution.py:457
  44.4 2.0 %collective-permute-start = (bf16[16,1024]{1,0:T(8,128)(2,1)S(1)}, bf16[16,1024]{1,0:T(8,128)(2,1)S(1)}, u32[]{:S(2)}, u32[]{:S(2)}) collective-permute-start(bf16[16,1024]{1,0:T(8,128)(2,1)S(1)} %get-tuple-element.25), channel_id=1, source_target_pairs={{0,32},{32,0},{64,96},{96,64},{1,33},{33,1},{65,97},{97,65},{2,34}... | collective-permute-start | bytes 98312 | tf_op jit(solution)/shard_map/ppermute | solution.py:460
  46.4 5.9 %collective-permute-start.1 = (bf16[16,2048]{1,0:T(8,128)(2,1)S(1)}, bf16[16,2048]{1,0:T(8,128)(2,1)S(1)}, u32[]{:S(2)}, u32[]{:S(2)}) collective-permute-start(bf16[16,2048]{1,0:T(8,128)(2,1)S(1)} %join.3.refs_0_), channel_id=1, source_target_pairs={{65,0},{56,32},{0,64},{120,96},{64,1},{57,33},{1,65},{121,97},{67,... | collective-permute-start | bytes 196616 | tf_op jit(solution)/shard_map/ppermute | solution.py:422
  47.2 6.0 %collective-permute-start.2 = (bf16[16,2048]{1,0:T(8,128)(2,1)S(1)}, bf16[16,2048]{1,0:T(8,128)(2,1)S(1)}, u32[]{:S(2)}, u32[]{:S(2)}) collective-permute-start(bf16[16,2048]{1,0:T(8,128)(2,1)S(1)} %join.3.refs_0_), channel_id=1, source_target_pairs={{64,0},{40,32},{1,64},{104,96},{65,1},{41,33},{0,65},{105,97},{66,... | collective-permute-start | bytes 196616 | tf_op jit(solution)/shard_map/ppermute | solution.py:422
  49.0 18.4 %collective-permute-start.3 = (bf16[16,2048]{1,0:T(8,128)(2,1)S(1)}, bf16[16,2048]{1,0:T(8,128)(2,1)S(1)}, u32[]{:S(2)}, u32[]{:S(2)}) collective-permute-start(bf16[16,2048]{1,0:T(8,128)(2,1)S(1)} %join.3.refs_0_), channel_id=1, source_target_pairs={{1,0},{48,32},{65,64},{112,96},{0,1},{49,33},{64,65},{113,97},{3,2... | collective-permute-start | bytes 196616 | tf_op jit(solution)/shard_map/ppermute | solution.py:422
  67.5 21.1 %collective-permute-start.4 = (bf16[64,2048]{1,0:T(8,128)(2,1)S(1)}, bf16[64,2048]{1,0:T(8,128)(2,1)S(1)}, u32[]{:S(2)}, u32[]{:S(2)}) collective-permute-start(bf16[64,2048]{1,0:T(8,128)(2,1)S(1)} %join.4.refs_0_), channel_id=1, source_target_pairs={{6,0},{97,32},{70,64},{32,96},{7,1},{96,33},{71,65},{33,97},{0,2},... | collective-permute-start | bytes 786440 | tf_op jit(solution)/shard_map/ppermute | solution.py:422
  78.2 12.5 %collective-permute-start.5 = (bf16[64,2048]{1,0:T(8,128)(2,1)S(1)}, bf16[64,2048]{1,0:T(8,128)(2,1)S(1)}, u32[]{:S(2)}, u32[]{:S(2)}) collective-permute-start(bf16[64,2048]{1,0:T(8,128)(2,1)S(1)} %join.4.refs_0_), channel_id=1, source_target_pairs={{2,0},{96,32},{66,64},{33,96},{3,1},{97,33},{67,65},{32,97},{4,2},... | collective-permute-start | bytes 786440 | tf_op jit(solution)/shard_map/ppermute | solution.py:422
  84.6 8.0 %collective-permute-start.6 = (bf16[64,2048]{1,0:T(8,128)(2,1)S(1)}, bf16[64,2048]{1,0:T(8,128)(2,1)S(1)}, u32[]{:S(2)}, u32[]{:S(2)}) collective-permute-start(bf16[64,2048]{1,0:T(8,128)(2,1)S(1)} %join.4.refs_0_), channel_id=1, source_target_pairs={{4,0},{33,32},{68,64},{97,96},{5,1},{32,33},{69,65},{96,97},{6,2},... | collective-permute-start | bytes 786440 | tf_op jit(solution)/shard_map/ppermute | solution.py:422
  93.6 28.2 %copy-start = (f32[64,384]{1,0:T(8,128)S(1)}, f32[64,384]{1,0:T(8,128)}, u32[]{:S(2)}) copy-start(f32[64,384]{1,0:T(8,128)} %constant.127.clone.choose) | copy-start | bytes 294916
  93.6 17.0 %collective-permute-start.7 = (bf16[256,2048]{1,0:T(8,128)(2,1)}, bf16[256,2048]{1,0:T(8,128)(2,1)}, u32[]{:S(2)}, u32[]{:S(2)}) collective-permute-start(bf16[256,2048]{1,0:T(8,128)(2,1)} %join.5.w0), channel_id=1, source_target_pairs={{16,0},{36,32},{80,64},{100,96},{17,1},{37,33},{81,65},{101,97},{1... | collective-permute-start | bytes 3145736 | tf_op jit(solution)/shard_map/ppermute | solution.py:422
  97.8 24.0 %collective-permute-start.8 = (bf16[256,2048]{1,0:T(8,128)(2,1)}, bf16[256,2048]{1,0:T(8,128)(2,1)}, u32[]{:S(2)}, u32[]{:S(2)}) collective-permute-start(bf16[256,2048]{1,0:T(8,128)(2,1)} %join.5.w0), channel_id=1, source_target_pairs={{24,0},{38,32},{88,64},{102,96},{25,1},{39,33},{89,65},{103,97},{2... | collective-permute-start | bytes 3145736 | tf_op jit(solution)/shard_map/ppermute | solution.py:422
  97.8 24.0 %collective-permute-start.9 = (bf16[256,2048]{1,0:T(8,128)(2,1)}, bf16[256,2048]{1,0:T(8,128)(2,1)}, u32[]{:S(2)}, u32[]{:S(2)}) collective-permute-start(bf16[256,2048]{1,0:T(8,128)(2,1)} %join.5.w0), channel_id=1, source_target_pairs={{8,0},{34,32},{72,64},{98,96},{9,1},{35,33},{73,65},{99,97},{10,2}... | collective-permute-start | bytes 3145736 | tf_op jit(solution)/shard_map/ppermute | solution.py:422
  126.2 3.9 %collective-permute-start.10 = (f32[32,512]{1,0:T(8,128)S(1)}, f32[32,512]{1,0:T(8,128)S(1)}, u32[]{:S(2)}, u32[]{:S(2)}) collective-permute-start(f32[32,512]{1,0:T(8,128)S(1)} %get-tuple-element.28), channel_id=1, source_target_pairs={{0,32},{32,0},{64,96},{96,64},{1,33},{33,1},{65,97},{97,65},{2,34}... | collective-permute-start | bytes 196616 | tf_op jit(solution)/shard_map/ppermute | solution.py:470

commit v11 on v10

--- a/solution.py
+++ b/solution.py
@@ -132,17 +132,21 @@
 
     lax.fori_loop(0, 2 * len(chosen), outer, 0, unroll=2)
 
-    matrix = mat[...]
+    matrix, matrix_low = mat[:256, :], mat[256:, :]
     lane = lax.broadcasted_iota(jnp.int32, (32, INNER), 1)
 
     def inner(a, _):
         base = pl.multiple_of(a * slot_stride, 8)
         rows = jnp.concatenate(
             [turned[0, pl.ds(base, rows_per_slot), :], turned[1, pl.ds(base, rows_per_slot), :]], axis=1
-        ).astype(jnp.bfloat16)
-        spec = lax.dot_general(
-            matrix, rows, (((1,), (1,)), ((), ())), preferred_element_type=jnp.float32
         )
+        high = rows.astype(jnp.bfloat16)
+        low = (rows - high.astype(jnp.float32)).astype(jnp.bfloat16)
+
+        def product(left, right):
+            return lax.dot_general(left, right, (((1,), (1,)), ((), ())), preferred_element_type=jnp.float32)
+
+        spec = product(matrix, high) + (product(matrix_low, high) + product(matrix, low))
         for g in range(count):
             for y in range(2):
                 for c in range(2):
@@ -181,7 +185,9 @@
 
 def spectra_of(messages, vre, vim, taps, interpret=False):
     cos_t, sin_t = twist_tables()
-    mat = inner_matrix().astype(jnp.bfloat16)
+    mat = inner_matrix()
+    high = mat.astype(jnp.bfloat16)
+    mat = np.concatenate([high, (mat - high.astype(np.float32)).astype(jnp.bfloat16)])
     groups = [group for message in messages for group in message]
     count = len(groups)
     many = 4 * count
@@ -198,7 +204,7 @@
             pltpu.VMEM((TAPS, CHANNELS), jnp.float32),
             pltpu.VMEM((OUTER, INNER), jnp.float32),
             pltpu.VMEM((OUTER, INNER), jnp.float32),
-            pltpu.VMEM((256, 256), jnp.bfloat16),
+            pltpu.VMEM((512, 256), jnp.bfloat16),
             pltpu.VMEM((2, many, OUTER, SLOTS, INNER), jnp.float32),
             pltpu.VMEM((2, SLOTS * (32 * many + 8), INNER), jnp.float32),
             pltpu.VMEM((2 * count, DEVICES * ROW_STRIDE, INNER), jnp.float32),

time: 131 us -> 133 us (1.015)
  Pallas kernels: 31.7 us -> 33.3 us
    pallas_call x1, Pallas kernels: 16.8 us -> 18.4 us  [spectra_of(): pl.pallas_call(functools.partial(spectra_kernel, messages), out_shape=[ja...]
  transfers between devices with their start and end apart: 13 -> 13, of which waited for: 11 -> 10; matrix products, arithmetic and copies ran while one was open for 0% -> 0% of each run, Pallas kernels for 16% -> 17%
where the time goes in v11:
time: 133 us; the launch traced here: 132 us
  starting transfers between devices  54.6 us (41%)
  waiting for transfers between devices  43.4 us (33%)
  Pallas kernels  33.3 us (25%)
    ppermute x9, waiting for transfers between devices, gather_stage(): lax.ppermute(block, ALL, permutation(stage, shift))  41.7 us
    ppermute x9, starting transfers between devices, gather_stage(): lax.ppermute(block, ALL, permutation(stage, shift))  29.1 us
    pallas_call x1, Pallas kernels, spectra_of(): pl.pallas_call(functools.partial(spectra_kernel, messages), out_shape=[ja...  18.4 us
    all_to_all x1, starting transfers between devices, on_device(): lax.all_to_all(quarter.reshape(32, 16, -1), 'dev', split_axis=0, concat_a...  11.4 us
    all_to_all x1, starting transfers between devices, on_device(): lax.all_to_all(message, ALL, split_axis=0, concat_axis=0, tiled=True)  9.94 us
    pallas_call x1, Pallas kernels, quarter_of(): pl.pallas_call(quarter_kernel, in_specs=[pl.BlockSpec(memory_space=pltpu....  5.57 us
    pallas_call x1, Pallas kernels, beams_of(): pl.pallas_call(beams_kernel, out_shape=[jax.ShapeDtypeStruct((32, rows //...  4.33 us
    pallas_call x1, Pallas kernels, early_of(): pl.pallas_call(early_kernel, out_shape=jax.ShapeDtypeStruct((2 * w0.shape...  3.33 us
  transfers between devices with their start and end apart: 13, of which 10 were waited for; matrix products, arithmetic and copies ran while one was open for 0% of the time, Pallas kernels for 17%

profile of v11, /device:TPU:1, one launch (start us, length us, event | category | flops | bytes accessed | tf_op | source)
XLA Modules:
  0.0 132.4 jit_solution(5877799652775545956)
XLA Ops:
  0.0 5.6 %quarter.1 = bf16[512,1024]{1,0:T(8,128)(2,1)} custom-call(f32[2048,512]{1,0:T(8,128)} %bitcast.10, f32[2048,512]{1,0:T(8,128)} %bitcast.11, s32[2,1,1024]{2,1,0:T(1,128)} %bitcast.14), custom_call_target="tpu_custom_call" | custom-call | flops 2000000000 | bytes 6000000 | tf_op jit(solution)/shard_map/quarter/pallas_call | solution.py:263
  5.6 11.4 %all-to-all-start = ((bf16[32,16,1024]{2,1,0:T(8,128)(2,1)}), bf16[32,16,1024]{2,1,0:T(8,128)(2,1)S(1)}, u32[]{:S(2)}, u32[]{:S(2)}) async-start(bf16[32,16,1024]{2,1,0:T(8,128)(2,1)} %bitcast.12), calls=%async_computation | async-start | bytes 2097152 | tf_op jit(solution)/shard_map/all_to_all | solution.py:455
  16.9 0.0 copy-start.1
  17.0 18.4 %spectra.1 = bf16[128,16,768]{2,1,0:T(8,128)(2,1)} custom-call(bf16[16,110592]{1,0:T(8,128)(2,1)} %refs_0_, bf16[16,110592]{1,0:T(8,128)(2,1)} %refs_1_, f32[16,4096]{1,0:T(8,128)} %refs_2_, f32[32,128]{1,0:T(8,128)} %constant.121.clone.refs_3_, f32[32,128]{1,0:T(8,128)} %constant.122.clone.refs_4_, bf16[512,256]{1,0:T(8,128)(2,1)} %constant.123.clone.refs_5_), custom_call_target="tpu_custom_call" | custom-call | flops 2400000000 | bytes 48000000 | tf_op jit(solution)/shard_map/spectra/pallas_call | solution.py:196
  35.4 0.0 all-to-all-done.offers
  35.4 0.0 copy-done.1
  35.4 0.6 pick.1
  36.0 0.0 copy-start.2
  36.0 0.0 copy-start.3
  36.0 0.0 copy-start.4
  36.0 9.9 %all-to-all-start.1 = ((bf16[128,16,768]{2,1,0:T(8,128)(2,1)}), bf16[128,16,768]{2,1,0:T(8,128)(2,1)S(1)}, u32[]{:S(2)}, u32[]{:S(2)}) async-start(bf16[128,16,768]{2,1,0:T(8,128)(2,1)} %spectra.1), calls=%async_computation.1 | async-start | bytes 6291456 | tf_op jit(solution)/shard_map/all_to_all | solution.py:463
  46.0 1.1 collective-permute-start
  47.1 0.9 collective-permute-done.refs_1_
  48.0 0.8 collective-permute-start.1
  48.8 1.9 %collective-permute-start.2 = (bf16[16,2048]{1,0:T(8,128)(2,1)S(1)}, bf16[16,2048]{1,0:T(8,128)(2,1)S(1)}, u32[]{:S(2)}, u32[]{:S(2)}) collective-permute-start(bf16[16,2048]{1,0:T(8,128)(2,1)S(1)} %join.3.refs_0_), channel_id=1, source_target_pairs={{64,0},{40,32},{1,64},{104,96},{65,1},{41,33},{0,65},{105,97},{66,... | collective-permute-start | bytes 196616 | tf_op jit(solution)/shard_map/ppermute | solution.py:428
  50.7 1.4 %collective-permute-start.3 = (bf16[16,2048]{1,0:T(8,128)(2,1)S(1)}, bf16[16,2048]{1,0:T(8,128)(2,1)S(1)}, u32[]{:S(2)}, u32[]{:S(2)}) collective-permute-start(bf16[16,2048]{1,0:T(8,128)(2,1)S(1)} %join.3.refs_0_), channel_id=1, source_target_pairs={{1,0},{48,32},{65,64},{112,96},{0,1},{49,33},{64,65},{113,97},{3,2... | collective-permute-start | bytes 196616 | tf_op jit(solution)/shard_map/ppermute | solution.py:428
  52.0 1.9 %collective-permute-done.1.refs_1_ = bf16[16,2048]{1,0:T(8,128)(2,1)S(1)} collective-permute-done((bf16[16,2048]{1,0:T(8,128)(2,1)S(1)}, bf16[16,2048]{1,0:T(8,128)(2,1)S(1)}, u32[]{:S(2)}, u32[]{:S(2)}) %collective-permute-start.1) | collective-permute-done | bytes 65568 | tf_op jit(solution)/shard_map/ppermute | solution.py:428
  53.9 0.9 collective-permute-done.2.refs_2_
  54.8 14.2 %collective-permute-done.3.refs_3_ = bf16[16,2048]{1,0:T(8,128)(2,1)S(1)} collective-permute-done((bf16[16,2048]{1,0:T(8,128)(2,1)S(1)}, bf16[16,2048]{1,0:T(8,128)(2,1)S(1)}, u32[]{:S(2)}, u32[]{:S(2)}) %collective-permute-start.3) | collective-permute-done | bytes 65568 | tf_op jit(solution)/shard_map/ppermute | solution.py:428
  69.1 10.7 %collective-permute-start.4 = (bf16[64,2048]{1,0:T(8,128)(2,1)S(1)}, bf16[64,2048]{1,0:T(8,128)(2,1)S(1)}, u32[]{:S(2)}, u32[]{:S(2)}) collective-permute-start(bf16[64,2048]{1,0:T(8,128)(2,1)S(1)} %join.4.refs_0_), channel_id=1, source_target_pairs={{6,0},{97,32},{70,64},{32,96},{7,1},{96,33},{71,65},{33,97},{0,2},... | collective-permute-start | bytes 786440 | tf_op jit(solution)/shard_map/ppermute | solution.py:428
  79.8 6.4 %collective-permute-start.5 = (bf16[64,2048]{1,0:T(8,128)(2,1)S(1)}, bf16[64,2048]{1,0:T(8,128)(2,1)S(1)}, u32[]{:S(2)}, u32[]{:S(2)}) collective-permute-start(bf16[64,2048]{1,0:T(8,128)(2,1)S(1)} %join.4.refs_0_), channel_id=1, source_target_pairs={{2,0},{96,32},{66,64},{33,96},{3,1},{97,33},{67,65},{32,97},{4,2},... | collective-permute-start | bytes 786440 | tf_op jit(solution)/shard_map/ppermute | solution.py:428
  86.2 1.1 collective-permute-start.6
  87.3 2.9 %collective-permute-done.4.refs_1_ = bf16[64,2048]{1,0:T(8,128)(2,1)S(1)} collective-permute-done((bf16[64,2048]{1,0:T(8,128)(2,1)S(1)}, bf16[64,2048]{1,0:T(8,128)(2,1)S(1)}, u32[]{:S(2)}, u32[]{:S(2)}) %collective-permute-start.4) | collective-permute-done | bytes 262176 | tf_op jit(solution)/shard_map/ppermute | solution.py:428
  90.2 2.2 %collective-permute-done.5.refs_2_ = bf16[64,2048]{1,0:T(8,128)(2,1)S(1)} collective-permute-done((bf16[64,2048]{1,0:T(8,128)(2,1)S(1)}, bf16[64,2048]{1,0:T(8,128)(2,1)S(1)}, u32[]{:S(2)}, u32[]{:S(2)}) %collective-permute-start.5) | collective-permute-done | bytes 262176 | tf_op jit(solution)/shard_map/ppermute | solution.py:428
  92.3 1.8 %collective-permute-done.6.refs_3_ = bf16[64,2048]{1,0:T(8,128)(2,1)S(1)} collective-permute-done((bf16[64,2048]{1,0:T(8,128)(2,1)S(1)}, bf16[64,2048]{1,0:T(8,128)(2,1)S(1)}, u32[]{:S(2)}, u32[]{:S(2)}) %collective-permute-start.6) | collective-permute-done | bytes 262176 | tf_op jit(solution)/shard_map/ppermute | solution.py:428
  94.2 1.0 join.5.w0
  95.2 0.0 copy-start
  95.2 4.2 %collective-permute-start.7 = (bf16[256,2048]{1,0:T(8,128)(2,1)}, bf16[256,2048]{1,0:T(8,128)(2,1)}, u32[]{:S(2)}, u32[]{:S(2)}) collective-permute-start(bf16[256,2048]{1,0:T(8,128)(2,1)} %join.5.w0), channel_id=1, source_target_pairs={{16,0},{36,32},{80,64},{100,96},{17,1},{37,33},{81,65},{101,97},{1... | collective-permute-start | bytes 3145736 | tf_op jit(solution)/shard_map/ppermute | solution.py:428
  99.4 0.0 collective-permute-start.8
  99.4 2.7 %collective-permute-start.9 = (bf16[256,2048]{1,0:T(8,128)(2,1)}, bf16[256,2048]{1,0:T(8,128)(2,1)}, u32[]{:S(2)}, u32[]{:S(2)}) collective-permute-start(bf16[256,2048]{1,0:T(8,128)(2,1)} %join.5.w0), channel_id=1, source_target_pairs={{8,0},{34,32},{72,64},{98,96},{9,1},{35,33},{73,65},{99,97},{10,2}... | collective-permute-start | bytes 3145736 | tf_op jit(solution)/shard_map/ppermute | solution.py:428
  102.1 0.0 copy-done.2
  102.1 0.0 copy-done.3
  102.1 0.0 copy-done.4
  102.1 0.1 slice.11
  102.2 0.1 fusion.16
  102.3 0.1 pad_add_fusion.places
  102.4 9.9 %collective-permute-done.7.w1 = bf16[256,2048]{1,0:T(8,128)(2,1)} collective-permute-done((bf16[256,2048]{1,0:T(8,128)(2,1)}, bf16[256,2048]{1,0:T(8,128)(2,1)}, u32[]{:S(2)}, u32[]{:S(2)}) %collective-permute-start.7) | collective-permute-done | bytes 1048608 | tf_op jit(solution)/shard_map/ppermute | solution.py:428
  112.3 0.0 all-to-all-done.1
  112.3 3.3 %early.1 = f32[512,768]{1,0:T(8,128)S(1)} custom-call(bf16[256,2048]{1,0:T(8,128)(2,1)} %join.5.w0, bf16[256,2048]{1,0:T(8,128)(2,1)} %collective-permute-done.7.w1, bf16[2048,768]{1,0:T(8,128)(2,1)S(1)} %bitcast.7), custom_call_target="tpu_custom_call" | custom-call | flops 1700000000 | bytes 8000000 | tf_op jit(solution)/shard_map/early/pallas_call | solution.py:352
  115.6 7.9 %collective-permute-done.8.w2 = bf16[256,2048]{1,0:T(8,128)(2,1)} collective-permute-done((bf16[256,2048]{1,0:T(8,128)(2,1)}, bf16[256,2048]{1,0:T(8,128)(2,1)}, u32[]{:S(2)}, u32[]{:S(2)}) %collective-permute-start.8) | collective-permute-done | bytes 1048608 | tf_op jit(solution)/shard_map/ppermute | solution.py:428
  123.5 0.0 collective-permute-done.9.w3
  123.5 0.0 copy-done
  123.5 4.3 %beams.1 = (f32[32,512]{1,0:T(8,128)S(1)}, f32[32,512]{1,0:T(8,128)S(1)}) custom-call(s32[64]{0:T(128)S(1)} %pad_add_fusion.places, f32[512,768]{1,0:T(8,128)S(1)} %early.1, bf16[256,2048]{1,0:T(8,128)(2,1)} %collective-permute-done.8.w2, bf16[256,2048]{1,0:T(8,128)(2,1)} %collective-permute-done.9.w3, bf16[2048,768]{1,0:T(8,128)(2,1)S(1)} %bitcast.8, ...), custom_call_target="tpu_custom_call" | custom-call | flops 1700000000 | bytes 8000000 | tf_op jit(solution)/shard_map/beams/pallas_call | solution.py:395
  127.8 3.0 %collective-permute-start.10 = (f32[32,512]{1,0:T(8,128)S(1)}, f32[32,512]{1,0:T(8,128)S(1)}, u32[]{:S(2)}, u32[]{:S(2)}) collective-permute-start(f32[32,512]{1,0:T(8,128)S(1)} %get-tuple-element.28), channel_id=1, source_target_pairs={{0,32},{32,0},{64,96},{96,64},{1,33},{33,1},{65,97},{97,65},{2,34}... | collective-permute-start | bytes 196616 | tf_op jit(solution)/shard_map/ppermute | solution.py:476
  130.8 0.9 collective-permute-done.10
  131.7 0.7 maximum_select_fusion
  (3 shorter events, 0.0 us)
Async XLA Ops:
  5.6 29.8 %all-to-all-start = ((bf16[32,16,1024]{2,1,0:T(8,128)(2,1)}), bf16[32,16,1024]{2,1,0:T(8,128)(2,1)S(1)}, u32[]{:S(2)}, u32[]{:S(2)}) async-start(bf16[32,16,1024]{2,1,0:T(8,128)(2,1)} %bitcast.12), calls=%async_computation | async-start | bytes 2097152 | tf_op jit(solution)/shard_map/all_to_all | solution.py:455
  16.9 18.5 %copy-start.1 = (s32[2]{0:T(128)S(1)}, s32[2]{0:T(128)}, u32[]{:S(2)}) copy-start(s32[2]{0:T(128)} %owners.1) | copy-start | bytes 28
  36.0 66.1 %copy-start.2 = (s32[64]{0:T(128)S(1)}, s32[64]{0:T(128)}, u32[]{:S(2)}) copy-start(s32[64]{0:T(128)} %constant.124.clone) | copy-start | bytes 772
  36.0 66.1 %copy-start.3 = (s32[64]{0:T(128)S(1)}, s32[64]{0:T(128)}, u32[]{:S(2)}) copy-start(s32[64]{0:T(128)} %constant.125.clone) | copy-start | bytes 772
  36.0 66.1 %copy-start.4 = (s32[64]{0:T(128)S(1)}, s32[64]{0:T(128)}, u32[]{:S(2)}) copy-start(s32[64]{0:T(128)} %constant.126.clone) | copy-start | bytes 772
  36.0 76.2 %all-to-all-start.1 = ((bf16[128,16,768]{2,1,0:T(8,128)(2,1)}), bf16[128,16,768]{2,1,0:T(8,128)(2,1)S(1)}, u32[]{:S(2)}, u32[]{:S(2)}) async-start(bf16[128,16,768]{2,1,0:T(8,128)(2,1)} %spectra.1), calls=%async_computation.1 | async-start | bytes 6291456 | tf_op jit(solution)/shard_map/all_to_all | solution.py:463
  46.0 2.0 %collective-permute-start = (bf16[16,1024]{1,0:T(8,128)(2,1)S(1)}, bf16[16,1024]{1,0:T(8,128)(2,1)S(1)}, u32[]{:S(2)}, u32[]{:S(2)}) collective-permute-start(bf16[16,1024]{1,0:T(8,128)(2,1)S(1)} %get-tuple-element.25), channel_id=1, source_target_pairs={{0,32},{32,0},{64,96},{96,64},{1,33},{33,1},{65,97},{97,65},{2,34}... | collective-permute-start | bytes 98312 | tf_op jit(solution)/shard_map/ppermute | solution.py:466
  48.0 5.9 %collective-permute-start.1 = (bf16[16,2048]{1,0:T(8,128)(2,1)S(1)}, bf16[16,2048]{1,0:T(8,128)(2,1)S(1)}, u32[]{:S(2)}, u32[]{:S(2)}) collective-permute-start(bf16[16,2048]{1,0:T(8,128)(2,1)S(1)} %join.3.refs_0_), channel_id=1, source_target_pairs={{65,0},{56,32},{0,64},{120,96},{64,1},{57,33},{1,65},{121,97},{67,... | collective-permute-start | bytes 196616 | tf_op jit(solution)/shard_map/ppermute | solution.py:428
  48.8 6.0 %collective-permute-start.2 = (bf16[16,2048]{1,0:T(8,128)(2,1)S(1)}, bf16[16,2048]{1,0:T(8,128)(2,1)S(1)}, u32[]{:S(2)}, u32[]{:S(2)}) collective-permute-start(bf16[16,2048]{1,0:T(8,128)(2,1)S(1)} %join.3.refs_0_), channel_id=1, source_target_pairs={{64,0},{40,32},{1,64},{104,96},{65,1},{41,33},{0,65},{105,97},{66,... | collective-permute-start | bytes 196616 | tf_op jit(solution)/shard_map/ppermute | solution.py:428
  50.7 18.4 %collective-permute-start.3 = (bf16[16,2048]{1,0:T(8,128)(2,1)S(1)}, bf16[16,2048]{1,0:T(8,128)(2,1)S(1)}, u32[]{:S(2)}, u32[]{:S(2)}) collective-permute-start(bf16[16,2048]{1,0:T(8,128)(2,1)S(1)} %join.3.refs_0_), channel_id=1, source_target_pairs={{1,0},{48,32},{65,64},{112,96},{0,1},{49,33},{64,65},{113,97},{3,2... | collective-permute-start | bytes 196616 | tf_op jit(solution)/shard_map/ppermute | solution.py:428
  69.1 21.1 %collective-permute-start.4 = (bf16[64,2048]{1,0:T(8,128)(2,1)S(1)}, bf16[64,2048]{1,0:T(8,128)(2,1)S(1)}, u32[]{:S(2)}, u32[]{:S(2)}) collective-permute-start(bf16[64,2048]{1,0:T(8,128)(2,1)S(1)} %join.4.refs_0_), channel_id=1, source_target_pairs={{6,0},{97,32},{70,64},{32,96},{7,1},{96,33},{71,65},{33,97},{0,2},... | collective-permute-start | bytes 786440 | tf_op jit(solution)/shard_map/ppermute | solution.py:428
  79.8 12.5 %collective-permute-start.5 = (bf16[64,2048]{1,0:T(8,128)(2,1)S(1)}, bf16[64,2048]{1,0:T(8,128)(2,1)S(1)}, u32[]{:S(2)}, u32[]{:S(2)}) collective-permute-start(bf16[64,2048]{1,0:T(8,128)(2,1)S(1)} %join.4.refs_0_), channel_id=1, source_target_pairs={{2,0},{96,32},{66,64},{33,96},{3,1},{97,33},{67,65},{32,97},{4,2},... | collective-permute-start | bytes 786440 | tf_op jit(solution)/shard_map/ppermute | solution.py:428
  86.2 8.0 %collective-permute-start.6 = (bf16[64,2048]{1,0:T(8,128)(2,1)S(1)}, bf16[64,2048]{1,0:T(8,128)(2,1)S(1)}, u32[]{:S(2)}, u32[]{:S(2)}) collective-permute-start(bf16[64,2048]{1,0:T(8,128)(2,1)S(1)} %join.4.refs_0_), channel_id=1, source_target_pairs={{4,0},{33,32},{68,64},{97,96},{5,1},{32,33},{69,65},{96,97},{6,2},... | collective-permute-start | bytes 786440 | tf_op jit(solution)/shard_map/ppermute | solution.py:428
  95.2 28.2 %copy-start = (f32[64,384]{1,0:T(8,128)S(1)}, f32[64,384]{1,0:T(8,128)}, u32[]{:S(2)}) copy-start(f32[64,384]{1,0:T(8,128)} %constant.127.clone.choose) | copy-start | bytes 294916
  95.2 17.0 %collective-permute-start.7 = (bf16[256,2048]{1,0:T(8,128)(2,1)}, bf16[256,2048]{1,0:T(8,128)(2,1)}, u32[]{:S(2)}, u32[]{:S(2)}) collective-permute-start(bf16[256,2048]{1,0:T(8,128)(2,1)} %join.5.w0), channel_id=1, source_target_pairs={{16,0},{36,32},{80,64},{100,96},{17,1},{37,33},{81,65},{101,97},{1... | collective-permute-start | bytes 3145736 | tf_op jit(solution)/shard_map/ppermute | solution.py:428
  99.4 24.0 %collective-permute-start.8 = (bf16[256,2048]{1,0:T(8,128)(2,1)}, bf16[256,2048]{1,0:T(8,128)(2,1)}, u32[]{:S(2)}, u32[]{:S(2)}) collective-permute-start(bf16[256,2048]{1,0:T(8,128)(2,1)} %join.5.w0), channel_id=1, source_target_pairs={{24,0},{38,32},{88,64},{102,96},{25,1},{39,33},{89,65},{103,97},{2... | collective-permute-start | bytes 3145736 | tf_op jit(solution)/shard_map/ppermute | solution.py:428
  99.4 24.0 %collective-permute-start.9 = (bf16[256,2048]{1,0:T(8,128)(2,1)}, bf16[256,2048]{1,0:T(8,128)(2,1)}, u32[]{:S(2)}, u32[]{:S(2)}) collective-permute-start(bf16[256,2048]{1,0:T(8,128)(2,1)} %join.5.w0), channel_id=1, source_target_pairs={{8,0},{34,32},{72,64},{98,96},{9,1},{35,33},{73,65},{99,97},{10,2}... | collective-permute-start | bytes 3145736 | tf_op jit(solution)/shard_map/ppermute | solution.py:428
  127.8 3.9 %collective-permute-start.10 = (f32[32,512]{1,0:T(8,128)S(1)}, f32[32,512]{1,0:T(8,128)S(1)}, u32[]{:S(2)}, u32[]{:S(2)}) collective-permute-start(f32[32,512]{1,0:T(8,128)S(1)} %get-tuple-element.28), channel_id=1, source_target_pairs={{0,32},{32,0},{64,96},{96,64},{1,33},{33,1},{65,97},{97,65},{2,34}... | collective-permute-start | bytes 196616 | tf_op jit(solution)/shard_map/ppermute | solution.py:476

commit v12 on v10

--- a/solution.py
+++ b/solution.py
@@ -335,36 +335,35 @@
     )
 
 
-def early_kernel(w0, w1, za, out):
+def early_kernel(w0, w1, w2, za, out):
     core = lax.axis_index("grp") % 2
     n = w0.shape[0]
-    for i, part in enumerate((w0, w1)):
+    for i, part in enumerate((w0, w1, w2)):
         out[i * n : (i + 1) * n, :] = products(core, part, za)
 
 
-def early_of(w0, w1, spectra, interpret=False):
+def early_of(w0, w1, w2, spectra, interpret=False):
     return pl.pallas_call(
         early_kernel,
-        out_shape=jax.ShapeDtypeStruct((2 * w0.shape[0], 768), jnp.float32),
-        in_specs=[pl.BlockSpec(memory_space=pltpu.VMEM)] * 3,
+        out_shape=jax.ShapeDtypeStruct((3 * w0.shape[0], 768), jnp.float32),
+        in_specs=[pl.BlockSpec(memory_space=pltpu.VMEM)] * 4,
         out_specs=pl.BlockSpec(memory_space=pltpu.VMEM),
         compiler_params=pltpu.CompilerParams(vmem_limit_bytes=24 * MIB),
         cost_estimate=pl.CostEstimate(flops=17 * 10**8, bytes_accessed=8 * 10**6, transcendentals=0),
         interpret=interpret,
         name="early",
-    )(w0, w1, spectra)
-
-
-def beams_kernel(places, early, w2, w3, za, choose, own, given, sums):
-    for k in range(32):
+    )(w0, w1, w2, spectra)
+
+
+def beams_kernel(places, early, w3, za, choose, own, given, sums):
+    for k in range(48):
         at = pl.multiple_of(places[k], 16)
         sums[pl.ds(at, 16), :] = early[k * 16 : (k + 1) * 16, :]
     core = lax.axis_index("grp") % 2
-    for i, part in enumerate((w2, w3)):
-        result = products(core, part, za)
-        for k in range(16):
-            at = pl.multiple_of(places[(i + 2) * 16 + k], 16)
-            sums[pl.ds(at, 16), :] = result[k * 16 : (k + 1) * 16, :]
+    result = products(core, w3, za)
+    for k in range(16):
+        at = pl.multiple_of(places[48 + k], 16)
+        sums[pl.ds(at, 16), :] = result[k * 16 : (k + 1) * 16, :]
     beams = sums.shape[0] // 2
     powers = []
     for g in range(3):
@@ -384,19 +383,19 @@
     given[...] = jnp.where(core == 0, total[32:], total[:32])
 
 
-def beams_of(places, early, w2, w3, spectra, interpret=False):
-    rows = early.shape[0] + 2 * w2.shape[0]
+def beams_of(places, early, w3, spectra, interpret=False):
+    rows = early.shape[0] + w3.shape[0]
     return pl.pallas_call(
         beams_kernel,
         out_shape=[jax.ShapeDtypeStruct((32, rows // 2), jnp.float32)] * 2,
-        in_specs=[pl.BlockSpec(memory_space=pltpu.SMEM)] + [pl.BlockSpec(memory_space=pltpu.VMEM)] * 5,
+        in_specs=[pl.BlockSpec(memory_space=pltpu.SMEM)] + [pl.BlockSpec(memory_space=pltpu.VMEM)] * 4,
         out_specs=[pl.BlockSpec(memory_space=pltpu.VMEM)] * 2,
         scratch_shapes=[pltpu.VMEM((rows, 768), jnp.float32)],
         compiler_params=pltpu.CompilerParams(vmem_limit_bytes=32 * MIB),
         cost_estimate=pl.CostEstimate(flops=17 * 10**8, bytes_accessed=8 * 10**6, transcendentals=0),
         interpret=interpret,
         name="beams",
-    )(places, early, w2, w3, spectra, jnp.asarray(choose_matrix()))
+    )(places, early, w3, spectra, jnp.asarray(choose_matrix()))
 
 
 def index_of(z, x, y, core):
@@ -463,10 +462,9 @@
     block = join_of(gather_stage(block, 1), 0)
     parts = gather_stage(block, 2)
 
-    early = early_of(parts[0], parts[3], spectra)
+    early = early_of(*parts[:3], spectra)
     places = block_places(grp, dev)
-    places = jnp.concatenate([places[:16], places[48:], places[16:48]])
-    own, given = beams_of(places, early, parts[1], parts[2], spectra)
+    own, given = beams_of(places, early, parts[3], spectra)
     taken = lax.ppermute(given, "grp", SWAP)
     return jnp.where(core == 0, jnp.stack([own, taken]), jnp.stack([taken, own]))
 

time: 131 us -> 132 us (level); the launches traced: 131 us -> 130 us
  transfers between devices with their start and end apart: 13 -> 13, of which waited for: 11 -> 12; matrix products, arithmetic and copies ran while one was open for 0% -> 0% of each run, Pallas kernels for 16% -> 17%
where the time goes in v12:
time: 132 us; the launch traced here: 130 us
  starting transfers between devices  52.1 us (39%)
  waiting for transfers between devices  45.5 us (34%)
  Pallas kernels  31.7 us (24%)
    ppermute x9, waiting for transfers between devices, gather_stage(): lax.ppermute(block, ALL, permutation(stage, shift))  42.5 us
    ppermute x9, starting transfers between devices, gather_stage(): lax.ppermute(block, ALL, permutation(stage, shift))  27.9 us
    pallas_call x1, Pallas kernels, spectra_of(): pl.pallas_call(functools.partial(spectra_kernel, messages), out_shape=[ja...  16.8 us
    all_to_all x1, starting transfers between devices, on_device(): lax.all_to_all(quarter.reshape(32, 16, -1), 'dev', split_axis=0, concat_a...  11.4 us
    all_to_all x1, starting transfers between devices, on_device(): lax.all_to_all(message, ALL, split_axis=0, concat_axis=0, tiled=True)  8.66 us
    pallas_call x1, Pallas kernels, quarter_of(): pl.pallas_call(quarter_kernel, in_specs=[pl.BlockSpec(memory_space=pltpu....  5.57 us
    pallas_call x1, Pallas kernels, early_of(): pl.pallas_call(early_kernel, out_shape=jax.ShapeDtypeStruct((3 * w0.shape...  4.49 us
    pallas_call x1, Pallas kernels, beams_of(): pl.pallas_call(beams_kernel, out_shape=[jax.ShapeDtypeStruct((32, rows //...  3.24 us
  transfers between devices with their start and end apart: 13, of which 12 were waited for; matrix products, arithmetic and copies ran while one was open for 0% of the time, Pallas kernels for 17%

profile of v12, /device:TPU:1, one launch (start us, length us, event | category | flops | bytes accessed | tf_op | source)
XLA Modules:
  0.0 130.2 jit_solution(5744820100646501279)
XLA Ops:
  0.0 5.6 %quarter.1 = bf16[512,1024]{1,0:T(8,128)(2,1)} custom-call(f32[2048,512]{1,0:T(8,128)} %bitcast.10, f32[2048,512]{1,0:T(8,128)} %bitcast.11, s32[2,1,1024]{2,1,0:T(1,128)} %bitcast.14), custom_call_target="tpu_custom_call" | custom-call | flops 2000000000 | bytes 6000000 | tf_op jit(solution)/shard_map/quarter/pallas_call | solution.py:257
  5.6 11.4 %all-to-all-start = ((bf16[32,16,1024]{2,1,0:T(8,128)(2,1)}), bf16[32,16,1024]{2,1,0:T(8,128)(2,1)S(1)}, u32[]{:S(2)}, u32[]{:S(2)}) async-start(bf16[32,16,1024]{2,1,0:T(8,128)(2,1)} %bitcast.12), calls=%async_computation | async-start | bytes 2097152 | tf_op jit(solution)/shard_map/all_to_all | solution.py:448
  16.9 0.0 copy-start.1
  17.0 16.8 %spectra.1 = bf16[128,16,768]{2,1,0:T(8,128)(2,1)} custom-call(bf16[16,110592]{1,0:T(8,128)(2,1)} %refs_0_, bf16[16,110592]{1,0:T(8,128)(2,1)} %refs_1_, f32[16,4096]{1,0:T(8,128)} %refs_2_, f32[32,128]{1,0:T(8,128)} %constant.121.clone.refs_3_, f32[32,128]{1,0:T(8,128)} %constant.122.clone.refs_4_, bf16[256,256]{1,0:T(8,128)(2,1)} %constant.123.clone.refs_5_), custom_call_target="tpu_custom_call" | custom-call | flops 2400000000 | bytes 48000000 | tf_op jit(solution)/shard_map/spectra/pallas_call | solution.py:190
  33.8 1.3 %all-to-all-done.offers = bf16[32,16,1024]{2,1,0:T(8,128)(2,1)S(1)} async-done(((bf16[32,16,1024]{2,1,0:T(8,128)(2,1)}), bf16[32,16,1024]{2,1,0:T(8,128)(2,1)S(1)}, u32[]{:S(2)}, u32[]{:S(2)}) %all-to-all-start) | async-done | bytes 1048608 | tf_op jit(solution)/shard_map/all_to_all | solution.py:448
  35.1 0.0 copy-done.1
  35.1 0.6 pick.1
  35.7 0.0 copy-start.2
  35.7 0.0 copy-start.3
  35.7 0.0 copy-start.4
  35.7 8.7 %all-to-all-start.1 = ((bf16[128,16,768]{2,1,0:T(8,128)(2,1)}), bf16[128,16,768]{2,1,0:T(8,128)(2,1)S(1)}, u32[]{:S(2)}, u32[]{:S(2)}) async-start(bf16[128,16,768]{2,1,0:T(8,128)(2,1)} %spectra.1), calls=%async_computation.1 | async-start | bytes 6291456 | tf_op jit(solution)/shard_map/all_to_all | solution.py:456
  44.4 1.1 collective-permute-start
  45.5 0.9 collective-permute-done.refs_1_
  46.4 0.8 collective-permute-start.1
  47.2 1.9 %collective-permute-start.2 = (bf16[16,2048]{1,0:T(8,128)(2,1)S(1)}, bf16[16,2048]{1,0:T(8,128)(2,1)S(1)}, u32[]{:S(2)}, u32[]{:S(2)}) collective-permute-start(bf16[16,2048]{1,0:T(8,128)(2,1)S(1)} %join.3.refs_0_), channel_id=1, source_target_pairs={{64,0},{40,32},{1,64},{104,96},{65,1},{41,33},{0,65},{105,97},{66,... | collective-permute-start | bytes 196616 | tf_op jit(solution)/shard_map/ppermute | solution.py:421
  49.1 1.4 %collective-permute-start.3 = (bf16[16,2048]{1,0:T(8,128)(2,1)S(1)}, bf16[16,2048]{1,0:T(8,128)(2,1)S(1)}, u32[]{:S(2)}, u32[]{:S(2)}) collective-permute-start(bf16[16,2048]{1,0:T(8,128)(2,1)S(1)} %join.3.refs_0_), channel_id=1, source_target_pairs={{1,0},{48,32},{65,64},{112,96},{0,1},{49,33},{64,65},{113,97},{3,2... | collective-permute-start | bytes 196616 | tf_op jit(solution)/shard_map/ppermute | solution.py:421
  50.4 1.9 %collective-permute-done.1.refs_1_ = bf16[16,2048]{1,0:T(8,128)(2,1)S(1)} collective-permute-done((bf16[16,2048]{1,0:T(8,128)(2,1)S(1)}, bf16[16,2048]{1,0:T(8,128)(2,1)S(1)}, u32[]{:S(2)}, u32[]{:S(2)}) %collective-permute-start.1) | collective-permute-done | bytes 65568 | tf_op jit(solution)/shard_map/ppermute | solution.py:421
  52.3 0.9 collective-permute-done.2.refs_2_
  53.2 14.2 %collective-permute-done.3.refs_3_ = bf16[16,2048]{1,0:T(8,128)(2,1)S(1)} collective-permute-done((bf16[16,2048]{1,0:T(8,128)(2,1)S(1)}, bf16[16,2048]{1,0:T(8,128)(2,1)S(1)}, u32[]{:S(2)}, u32[]{:S(2)}) %collective-permute-start.3) | collective-permute-done | bytes 65568 | tf_op jit(solution)/shard_map/ppermute | solution.py:421
  67.5 10.7 %collective-permute-start.4 = (bf16[64,2048]{1,0:T(8,128)(2,1)S(1)}, bf16[64,2048]{1,0:T(8,128)(2,1)S(1)}, u32[]{:S(2)}, u32[]{:S(2)}) collective-permute-start(bf16[64,2048]{1,0:T(8,128)(2,1)S(1)} %join.4.refs_0_), channel_id=1, source_target_pairs={{6,0},{97,32},{70,64},{32,96},{7,1},{96,33},{71,65},{33,97},{0,2},... | collective-permute-start | bytes 786440 | tf_op jit(solution)/shard_map/ppermute | solution.py:421
  78.2 6.4 %collective-permute-start.5 = (bf16[64,2048]{1,0:T(8,128)(2,1)S(1)}, bf16[64,2048]{1,0:T(8,128)(2,1)S(1)}, u32[]{:S(2)}, u32[]{:S(2)}) collective-permute-start(bf16[64,2048]{1,0:T(8,128)(2,1)S(1)} %join.4.refs_0_), channel_id=1, source_target_pairs={{2,0},{96,32},{66,64},{33,96},{3,1},{97,33},{67,65},{32,97},{4,2},... | collective-permute-start | bytes 786440 | tf_op jit(solution)/shard_map/ppermute | solution.py:421
  84.6 1.1 collective-permute-start.6
  85.7 2.9 %collective-permute-done.4.refs_1_ = bf16[64,2048]{1,0:T(8,128)(2,1)S(1)} collective-permute-done((bf16[64,2048]{1,0:T(8,128)(2,1)S(1)}, bf16[64,2048]{1,0:T(8,128)(2,1)S(1)}, u32[]{:S(2)}, u32[]{:S(2)}) %collective-permute-start.4) | collective-permute-done | bytes 262176 | tf_op jit(solution)/shard_map/ppermute | solution.py:421
  88.6 2.2 %collective-permute-done.5.refs_2_ = bf16[64,2048]{1,0:T(8,128)(2,1)S(1)} collective-permute-done((bf16[64,2048]{1,0:T(8,128)(2,1)S(1)}, bf16[64,2048]{1,0:T(8,128)(2,1)S(1)}, u32[]{:S(2)}, u32[]{:S(2)}) %collective-permute-start.5) | collective-permute-done | bytes 262176 | tf_op jit(solution)/shard_map/ppermute | solution.py:421
  90.7 1.8 %collective-permute-done.6.refs_3_ = bf16[64,2048]{1,0:T(8,128)(2,1)S(1)} collective-permute-done((bf16[64,2048]{1,0:T(8,128)(2,1)S(1)}, bf16[64,2048]{1,0:T(8,128)(2,1)S(1)}, u32[]{:S(2)}, u32[]{:S(2)}) %collective-permute-start.6) | collective-permute-done | bytes 262176 | tf_op jit(solution)/shard_map/ppermute | solution.py:421
  92.6 1.0 join.5.w0
  93.6 2.6 %collective-permute-start.7 = (bf16[256,2048]{1,0:T(8,128)(2,1)}, bf16[256,2048]{1,0:T(8,128)(2,1)}, u32[]{:S(2)}, u32[]{:S(2)}) collective-permute-start(bf16[256,2048]{1,0:T(8,128)(2,1)} %join.5.w0), channel_id=1, source_target_pairs={{24,0},{38,32},{88,64},{102,96},{25,1},{39,33},{89,65},{103,97},{2... | collective-permute-start | bytes 3145736 | tf_op jit(solution)/shard_map/ppermute | solution.py:421
  96.2 1.0 collective-permute-start.8
  97.2 2.1 %collective-permute-start.9 = (bf16[256,2048]{1,0:T(8,128)(2,1)}, bf16[256,2048]{1,0:T(8,128)(2,1)}, u32[]{:S(2)}, u32[]{:S(2)}) collective-permute-start(bf16[256,2048]{1,0:T(8,128)(2,1)} %join.5.w0), channel_id=1, source_target_pairs={{16,0},{36,32},{80,64},{100,96},{17,1},{37,33},{81,65},{101,97},{1... | collective-permute-start | bytes 3145736 | tf_op jit(solution)/shard_map/ppermute | solution.py:421
  99.3 0.0 copy-done.2
  99.3 0.0 copy-done.3
  99.3 0.0 copy-done.4
  99.3 10.7 %collective-permute-done.7.w1 = bf16[256,2048]{1,0:T(8,128)(2,1)} collective-permute-done((bf16[256,2048]{1,0:T(8,128)(2,1)}, bf16[256,2048]{1,0:T(8,128)(2,1)}, u32[]{:S(2)}, u32[]{:S(2)}) %collective-permute-start.7) | collective-permute-done | bytes 1048608 | tf_op jit(solution)/shard_map/ppermute | solution.py:421
  110.0 0.5 collective-permute-done.8.w2
  110.5 0.0 all-to-all-done.1
  110.5 0.0 copy-start
  110.5 4.5 %early.1 = f32[768,768]{1,0:T(8,128)S(1)} custom-call(bf16[256,2048]{1,0:T(8,128)(2,1)} %join.5.w0, bf16[256,2048]{1,0:T(8,128)(2,1)} %collective-permute-done.7.w1, bf16[256,2048]{1,0:T(8,128)(2,1)} %collective-permute-done.8.w2, bf16[2048,768]{1,0:T(8,128)(2,1)S(1)} %bitcast.7), custom_call_target="tpu_custom_call" | custom-call | flops 1700000000 | bytes 8000000 | tf_op jit(solution)/shard_map/early/pallas_call | solution.py:346
  115.0 7.4 %collective-permute-done.9.w3 = bf16[256,2048]{1,0:T(8,128)(2,1)} collective-permute-done((bf16[256,2048]{1,0:T(8,128)(2,1)}, bf16[256,2048]{1,0:T(8,128)(2,1)}, u32[]{:S(2)}, u32[]{:S(2)}) %collective-permute-start.9) | collective-permute-done | bytes 1048608 | tf_op jit(solution)/shard_map/ppermute | solution.py:421
  122.4 0.0 copy-done
  122.4 3.2 %beams.1 = (f32[32,512]{1,0:T(8,128)S(1)}, f32[32,512]{1,0:T(8,128)S(1)}) custom-call(s32[64]{0:T(128)S(1)} %fusion.15.places, f32[768,768]{1,0:T(8,128)S(1)} %early.1, bf16[256,2048]{1,0:T(8,128)(2,1)} %collective-permute-done.9.w3, bf16[2048,768]{1,0:T(8,128)(2,1)S(1)} %bitcast.8, f32[64,384]{1,0:T(8,128)S(1)} %copy-done), custom_call_target="tpu_custom_call" | custom-call | flops 1700000000 | bytes 8000000 | tf_op jit(solution)/shard_map/beams/pallas_call | solution.py:388
  125.6 3.0 %collective-permute-start.10 = (f32[32,512]{1,0:T(8,128)S(1)}, f32[32,512]{1,0:T(8,128)S(1)}, u32[]{:S(2)}, u32[]{:S(2)}) collective-permute-start(f32[32,512]{1,0:T(8,128)S(1)} %get-tuple-element.28), channel_id=1, source_target_pairs={{0,32},{32,0},{64,96},{96,64},{1,33},{33,1},{65,97},{97,65},{2,34}... | collective-permute-start | bytes 196616 | tf_op jit(solution)/shard_map/ppermute | solution.py:468
  128.7 0.9 collective-permute-done.10
  129.6 0.7 maximum_select_fusion
  (3 shorter events, 0.0 us)
Async XLA Ops:
  5.6 29.5 %all-to-all-start = ((bf16[32,16,1024]{2,1,0:T(8,128)(2,1)}), bf16[32,16,1024]{2,1,0:T(8,128)(2,1)S(1)}, u32[]{:S(2)}, u32[]{:S(2)}) async-start(bf16[32,16,1024]{2,1,0:T(8,128)(2,1)} %bitcast.12), calls=%async_computation | async-start | bytes 2097152 | tf_op jit(solution)/shard_map/all_to_all | solution.py:448
  16.9 18.1 %copy-start.1 = (s32[2]{0:T(128)S(1)}, s32[2]{0:T(128)}, u32[]{:S(2)}) copy-start(s32[2]{0:T(128)} %owners.1) | copy-start | bytes 28
  35.7 63.6 %copy-start.2 = (s32[64]{0:T(128)S(1)}, s32[64]{0:T(128)}, u32[]{:S(2)}) copy-start(s32[64]{0:T(128)} %constant.124.clone) | copy-start | bytes 772
  35.7 63.6 %copy-start.3 = (s32[64]{0:T(128)S(1)}, s32[64]{0:T(128)}, u32[]{:S(2)}) copy-start(s32[64]{0:T(128)} %constant.125.clone) | copy-start | bytes 772
  35.7 63.6 %copy-start.4 = (s32[64]{0:T(128)S(1)}, s32[64]{0:T(128)}, u32[]{:S(2)}) copy-start(s32[64]{0:T(128)} %constant.126.clone) | copy-start | bytes 772
  35.7 74.8 %all-to-all-start.1 = ((bf16[128,16,768]{2,1,0:T(8,128)(2,1)}), bf16[128,16,768]{2,1,0:T(8,128)(2,1)S(1)}, u32[]{:S(2)}, u32[]{:S(2)}) async-start(bf16[128,16,768]{2,1,0:T(8,128)(2,1)} %spectra.1), calls=%async_computation.1 | async-start | bytes 6291456 | tf_op jit(solution)/shard_map/all_to_all | solution.py:456
  44.4 2.0 %collective-permute-start = (bf16[16,1024]{1,0:T(8,128)(2,1)S(1)}, bf16[16,1024]{1,0:T(8,128)(2,1)S(1)}, u32[]{:S(2)}, u32[]{:S(2)}) collective-permute-start(bf16[16,1024]{1,0:T(8,128)(2,1)S(1)} %get-tuple-element.25), channel_id=1, source_target_pairs={{0,32},{32,0},{64,96},{96,64},{1,33},{33,1},{65,97},{97,65},{2,34}... | collective-permute-start | bytes 98312 | tf_op jit(solution)/shard_map/ppermute | solution.py:459
  46.4 5.9 %collective-permute-start.1 = (bf16[16,2048]{1,0:T(8,128)(2,1)S(1)}, bf16[16,2048]{1,0:T(8,128)(2,1)S(1)}, u32[]{:S(2)}, u32[]{:S(2)}) collective-permute-start(bf16[16,2048]{1,0:T(8,128)(2,1)S(1)} %join.3.refs_0_), channel_id=1, source_target_pairs={{65,0},{56,32},{0,64},{120,96},{64,1},{57,33},{1,65},{121,97},{67,... | collective-permute-start | bytes 196616 | tf_op jit(solution)/shard_map/ppermute | solution.py:421
  47.2 6.0 %collective-permute-start.2 = (bf16[16,2048]{1,0:T(8,128)(2,1)S(1)}, bf16[16,2048]{1,0:T(8,128)(2,1)S(1)}, u32[]{:S(2)}, u32[]{:S(2)}) collective-permute-start(bf16[16,2048]{1,0:T(8,128)(2,1)S(1)} %join.3.refs_0_), channel_id=1, source_target_pairs={{64,0},{40,32},{1,64},{104,96},{65,1},{41,33},{0,65},{105,97},{66,... | collective-permute-start | bytes 196616 | tf_op jit(solution)/shard_map/ppermute | solution.py:421
  49.1 18.4 %collective-permute-start.3 = (bf16[16,2048]{1,0:T(8,128)(2,1)S(1)}, bf16[16,2048]{1,0:T(8,128)(2,1)S(1)}, u32[]{:S(2)}, u32[]{:S(2)}) collective-permute-start(bf16[16,2048]{1,0:T(8,128)(2,1)S(1)} %join.3.refs_0_), channel_id=1, source_target_pairs={{1,0},{48,32},{65,64},{112,96},{0,1},{49,33},{64,65},{113,97},{3,2... | collective-permute-start | bytes 196616 | tf_op jit(solution)/shard_map/ppermute | solution.py:421
  67.5 21.1 %collective-permute-start.4 = (bf16[64,2048]{1,0:T(8,128)(2,1)S(1)}, bf16[64,2048]{1,0:T(8,128)(2,1)S(1)}, u32[]{:S(2)}, u32[]{:S(2)}) collective-permute-start(bf16[64,2048]{1,0:T(8,128)(2,1)S(1)} %join.4.refs_0_), channel_id=1, source_target_pairs={{6,0},{97,32},{70,64},{32,96},{7,1},{96,33},{71,65},{33,97},{0,2},... | collective-permute-start | bytes 786440 | tf_op jit(solution)/shard_map/ppermute | solution.py:421
  78.2 12.5 %collective-permute-start.5 = (bf16[64,2048]{1,0:T(8,128)(2,1)S(1)}, bf16[64,2048]{1,0:T(8,128)(2,1)S(1)}, u32[]{:S(2)}, u32[]{:S(2)}) collective-permute-start(bf16[64,2048]{1,0:T(8,128)(2,1)S(1)} %join.4.refs_0_), channel_id=1, source_target_pairs={{2,0},{96,32},{66,64},{33,96},{3,1},{97,33},{67,65},{32,97},{4,2},... | collective-permute-start | bytes 786440 | tf_op jit(solution)/shard_map/ppermute | solution.py:421
  84.6 8.0 %collective-permute-start.6 = (bf16[64,2048]{1,0:T(8,128)(2,1)S(1)}, bf16[64,2048]{1,0:T(8,128)(2,1)S(1)}, u32[]{:S(2)}, u32[]{:S(2)}) collective-permute-start(bf16[64,2048]{1,0:T(8,128)(2,1)S(1)} %join.4.refs_0_), channel_id=1, source_target_pairs={{4,0},{33,32},{68,64},{97,96},{5,1},{32,33},{69,65},{96,97},{6,2},... | collective-permute-start | bytes 786440 | tf_op jit(solution)/shard_map/ppermute | solution.py:421
  93.6 16.4 %collective-permute-start.7 = (bf16[256,2048]{1,0:T(8,128)(2,1)}, bf16[256,2048]{1,0:T(8,128)(2,1)}, u32[]{:S(2)}, u32[]{:S(2)}) collective-permute-start(bf16[256,2048]{1,0:T(8,128)(2,1)} %join.5.w0), channel_id=1, source_target_pairs={{24,0},{38,32},{88,64},{102,96},{25,1},{39,33},{89,65},{103,97},{2... | collective-permute-start | bytes 3145736 | tf_op jit(solution)/shard_map/ppermute | solution.py:421
  96.2 14.3 %collective-permute-start.8 = (bf16[256,2048]{1,0:T(8,128)(2,1)}, bf16[256,2048]{1,0:T(8,128)(2,1)}, u32[]{:S(2)}, u32[]{:S(2)}) collective-permute-start(bf16[256,2048]{1,0:T(8,128)(2,1)} %join.5.w0), channel_id=1, source_target_pairs={{8,0},{34,32},{72,64},{98,96},{9,1},{35,33},{73,65},{99,97},{10,2}... | collective-permute-start | bytes 3145736 | tf_op jit(solution)/shard_map/ppermute | solution.py:421
  97.2 25.2 %collective-permute-start.9 = (bf16[256,2048]{1,0:T(8,128)(2,1)}, bf16[256,2048]{1,0:T(8,128)(2,1)}, u32[]{:S(2)}, u32[]{:S(2)}) collective-permute-start(bf16[256,2048]{1,0:T(8,128)(2,1)} %join.5.w0), channel_id=1, source_target_pairs={{16,0},{36,32},{80,64},{100,96},{17,1},{37,33},{81,65},{101,97},{1... | collective-permute-start | bytes 3145736 | tf_op jit(solution)/shard_map/ppermute | solution.py:421
  110.5 11.9 %copy-start = (f32[64,384]{1,0:T(8,128)S(1)}, f32[64,384]{1,0:T(8,128)}, u32[]{:S(2)}) copy-start(f32[64,384]{1,0:T(8,128)} %constant.127.clone.choose) | copy-start | bytes 294916
  125.6 3.9 %collective-permute-start.10 = (f32[32,512]{1,0:T(8,128)S(1)}, f32[32,512]{1,0:T(8,128)S(1)}, u32[]{:S(2)}, u32[]{:S(2)}) collective-permute-start(f32[32,512]{1,0:T(8,128)S(1)} %get-tuple-element.28), channel_id=1, source_target_pairs={{0,32},{32,0},{64,96},{96,64},{1,33},{33,1},{65,97},{97,65},{2,34}... | collective-permute-start | bytes 196616 | tf_op jit(solution)/shard_map/ppermute | solution.py:468

commit v13 on v12

--- a/solution.py
+++ b/solution.py
@@ -214,7 +214,7 @@
     )(vre, vim, taps, jnp.asarray(cos_t), jnp.asarray(sin_t), jnp.asarray(mat))
 
 
-def quarter_kernel(wre, wim, slots, out, buf, names, chosen, sems):
+def quarter_kernel(wre, wim, slots, out, buf, names, chosen, ready, sems):
     grp = lax.axis_index("grp")
     y_lo, core = grp // 2, grp % 2
     antennas, beams = wre.shape
@@ -235,7 +235,7 @@
         antenna = lax.broadcasted_iota(jnp.int32, (16, half), 0) + i * 16
         chosen[pl.ds(pl.multiple_of(i * 16, 16), 16), :] = jnp.where(antenna == row, 1.0, 0.0).astype(jnp.bfloat16)
         return 0
-    lax.fori_loop(0, antennas // 16, build, 0, unroll=4)
+    lax.fori_loop(0, antennas // 16, build, 0, unroll=8)
     for y, source in ((0, wre), (1, wim)):
 
         @pl.when(y_lo == y)
@@ -243,12 +243,18 @@
             for i in range(4):
                 part = pl.ds(i * half // 2, half // 2)
                 pltpu.make_async_copy(source.at[part], buf.at[part], sems.at[i]).wait()
+    stores = []
     for j in range(0, beams, 256):
         w = buf[:, j : j + 256].astype(jnp.bfloat16)
         for k in range(0, half, 512):
-            out[j : j + 256, k : k + 512] = lax.dot_general(
+            ready[j : j + 256, k : k + 512] = lax.dot_general(
                 w, chosen[:, k : k + 512], (((0,), (0,)), ((), ())), preferred_element_type=jnp.float32
             ).astype(jnp.bfloat16)
+        part = pl.ds(j, 256)
+        stores.append(pltpu.make_async_copy(ready.at[part], out.at[part], sems.at[5 + len(stores)]))
+        stores[-1].start()
+    for store in stores:
+        store.wait()
 
 
 def quarter_of(wre, wim, antenna_map, interpret=False):
@@ -257,13 +263,14 @@
     return pl.pallas_call(
         quarter_kernel,
         in_specs=[pl.BlockSpec(memory_space=pltpu.HBM)] * 3,
-        out_specs=pl.BlockSpec(memory_space=pltpu.VMEM),
+        out_specs=pl.BlockSpec(memory_space=pltpu.HBM),
         out_shape=jax.ShapeDtypeStruct((beams, half), jnp.bfloat16),
         scratch_shapes=[
             pltpu.VMEM((antennas, beams), jnp.float32),
             pltpu.VMEM((1, half), jnp.int32),
             pltpu.VMEM((antennas, half), jnp.bfloat16),
-            pltpu.SemaphoreType.DMA((5,)),
+            pltpu.VMEM((beams, half), jnp.bfloat16),
+            pltpu.SemaphoreType.DMA((7,)),
         ],
         compiler_params=pltpu.CompilerParams(vmem_limit_bytes=58 * MIB),
         cost_estimate=pl.CostEstimate(flops=2 * 10**9, bytes_accessed=6 * 10**6, transcendentals=0),

time: 132 us -> 132 us (level)
  no operation moved by 1% of the time
where the time goes in v13:
time: 132 us; the launch traced here: 130 us
  starting transfers between devices  52.1 us (39%)
  waiting for transfers between devices  45.5 us (34%)
  Pallas kernels  31.6 us (24%)
    ppermute x9, waiting for transfers between devices, gather_stage(): lax.ppermute(block, ALL, permutation(stage, shift))  42.5 us
    ppermute x9, starting transfers between devices, gather_stage(): lax.ppermute(block, ALL, permutation(stage, shift))  27.9 us
    pallas_call x1, Pallas kernels, spectra_of(): pl.pallas_call(functools.partial(spectra_kernel, messages), out_shape=[ja...  16.8 us
    all_to_all x1, starting transfers between devices, on_device(): lax.all_to_all(quarter.reshape(32, 16, -1), 'dev', split_axis=0, concat_a...  11.4 us
    all_to_all x1, starting transfers between devices, on_device(): lax.all_to_all(message, ALL, split_axis=0, concat_axis=0, tiled=True)  8.66 us
    pallas_call x1, Pallas kernels, quarter_of(): pl.pallas_call(quarter_kernel, in_specs=[pl.BlockSpec(memory_space=pltpu....  5.4 us
    pallas_call x1, Pallas kernels, early_of(): pl.pallas_call(early_kernel, out_shape=jax.ShapeDtypeStruct((3 * w0.shape...  4.49 us
    pallas_call x1, Pallas kernels, beams_of(): pl.pallas_call(beams_kernel, out_shape=[jax.ShapeDtypeStruct((32, rows //...  3.24 us
  transfers between devices with their start and end apart: 13, of which 12 were waited for; matrix products, arithmetic and copies ran while one was open for 0% of the time, Pallas kernels for 17%

profile of v13, /device:TPU:1, one launch (start us, length us, event | category | flops | bytes accessed | tf_op | source)
XLA Modules:
  0.0 130.1 jit_solution(2481517248183926340)
XLA Ops:
  0.0 5.4 %quarter.1 = bf16[512,1024]{1,0:T(8,128)(2,1)} custom-call(f32[2048,512]{1,0:T(8,128)} %bitcast.10, f32[2048,512]{1,0:T(8,128)} %bitcast.11, s32[2,1,1024]{2,1,0:T(1,128)} %bitcast.14), custom_call_target="tpu_custom_call" | custom-call | flops 2000000000 | bytes 6000000 | tf_op jit(solution)/shard_map/quarter/pallas_call | solution.py:263
  5.4 11.4 %all-to-all-start = ((bf16[32,16,1024]{2,1,0:T(8,128)(2,1)}), bf16[32,16,1024]{2,1,0:T(8,128)(2,1)S(1)}, u32[]{:S(2)}, u32[]{:S(2)}) async-start(bf16[32,16,1024]{2,1,0:T(8,128)(2,1)} %bitcast.12), calls=%async_computation | async-start | bytes 2097152 | tf_op jit(solution)/shard_map/all_to_all | solution.py:455
  16.8 0.0 copy-start.1
  16.8 16.8 %spectra.1 = bf16[128,16,768]{2,1,0:T(8,128)(2,1)} custom-call(bf16[16,110592]{1,0:T(8,128)(2,1)} %refs_0_, bf16[16,110592]{1,0:T(8,128)(2,1)} %refs_1_, f32[16,4096]{1,0:T(8,128)} %refs_2_, f32[32,128]{1,0:T(8,128)} %constant.121.clone.refs_3_, f32[32,128]{1,0:T(8,128)} %constant.122.clone.refs_4_, bf16[256,256]{1,0:T(8,128)(2,1)} %constant.123.clone.refs_5_), custom_call_target="tpu_custom_call" | custom-call | flops 2400000000 | bytes 48000000 | tf_op jit(solution)/shard_map/spectra/pallas_call | solution.py:190
  33.6 1.3 %all-to-all-done.offers = bf16[32,16,1024]{2,1,0:T(8,128)(2,1)S(1)} async-done(((bf16[32,16,1024]{2,1,0:T(8,128)(2,1)}), bf16[32,16,1024]{2,1,0:T(8,128)(2,1)S(1)}, u32[]{:S(2)}, u32[]{:S(2)}) %all-to-all-start) | async-done | bytes 1048608 | tf_op jit(solution)/shard_map/all_to_all | solution.py:455
  34.9 0.0 copy-done.1
  34.9 0.6 pick.1
  35.5 0.0 copy-start.2
  35.5 0.0 copy-start.3
  35.5 0.0 copy-start.4
  35.5 8.7 %all-to-all-start.1 = ((bf16[128,16,768]{2,1,0:T(8,128)(2,1)}), bf16[128,16,768]{2,1,0:T(8,128)(2,1)S(1)}, u32[]{:S(2)}, u32[]{:S(2)}) async-start(bf16[128,16,768]{2,1,0:T(8,128)(2,1)} %spectra.1), calls=%async_computation.1 | async-start | bytes 6291456 | tf_op jit(solution)/shard_map/all_to_all | solution.py:463
  44.2 1.1 collective-permute-start
  45.3 0.9 collective-permute-done.refs_1_
  46.2 0.8 collective-permute-start.1
  47.0 1.9 %collective-permute-start.2 = (bf16[16,2048]{1,0:T(8,128)(2,1)S(1)}, bf16[16,2048]{1,0:T(8,128)(2,1)S(1)}, u32[]{:S(2)}, u32[]{:S(2)}) collective-permute-start(bf16[16,2048]{1,0:T(8,128)(2,1)S(1)} %join.3.refs_0_), channel_id=1, source_target_pairs={{64,0},{40,32},{1,64},{104,96},{65,1},{41,33},{0,65},{105,97},{66,... | collective-permute-start | bytes 196616 | tf_op jit(solution)/shard_map/ppermute | solution.py:428
  48.9 1.4 %collective-permute-start.3 = (bf16[16,2048]{1,0:T(8,128)(2,1)S(1)}, bf16[16,2048]{1,0:T(8,128)(2,1)S(1)}, u32[]{:S(2)}, u32[]{:S(2)}) collective-permute-start(bf16[16,2048]{1,0:T(8,128)(2,1)S(1)} %join.3.refs_0_), channel_id=1, source_target_pairs={{1,0},{48,32},{65,64},{112,96},{0,1},{49,33},{64,65},{113,97},{3,2... | collective-permute-start | bytes 196616 | tf_op jit(solution)/shard_map/ppermute | solution.py:428
  50.3 1.9 %collective-permute-done.1.refs_1_ = bf16[16,2048]{1,0:T(8,128)(2,1)S(1)} collective-permute-done((bf16[16,2048]{1,0:T(8,128)(2,1)S(1)}, bf16[16,2048]{1,0:T(8,128)(2,1)S(1)}, u32[]{:S(2)}, u32[]{:S(2)}) %collective-permute-start.1) | collective-permute-done | bytes 65568 | tf_op jit(solution)/shard_map/ppermute | solution.py:428
  52.1 0.9 collective-permute-done.2.refs_2_
  53.1 14.2 %collective-permute-done.3.refs_3_ = bf16[16,2048]{1,0:T(8,128)(2,1)S(1)} collective-permute-done((bf16[16,2048]{1,0:T(8,128)(2,1)S(1)}, bf16[16,2048]{1,0:T(8,128)(2,1)S(1)}, u32[]{:S(2)}, u32[]{:S(2)}) %collective-permute-start.3) | collective-permute-done | bytes 65568 | tf_op jit(solution)/shard_map/ppermute | solution.py:428
  67.3 10.7 %collective-permute-start.4 = (bf16[64,2048]{1,0:T(8,128)(2,1)S(1)}, bf16[64,2048]{1,0:T(8,128)(2,1)S(1)}, u32[]{:S(2)}, u32[]{:S(2)}) collective-permute-start(bf16[64,2048]{1,0:T(8,128)(2,1)S(1)} %join.4.refs_0_), channel_id=1, source_target_pairs={{6,0},{97,32},{70,64},{32,96},{7,1},{96,33},{71,65},{33,97},{0,2},... | collective-permute-start | bytes 786440 | tf_op jit(solution)/shard_map/ppermute | solution.py:428
  78.0 6.4 %collective-permute-start.5 = (bf16[64,2048]{1,0:T(8,128)(2,1)S(1)}, bf16[64,2048]{1,0:T(8,128)(2,1)S(1)}, u32[]{:S(2)}, u32[]{:S(2)}) collective-permute-start(bf16[64,2048]{1,0:T(8,128)(2,1)S(1)} %join.4.refs_0_), channel_id=1, source_target_pairs={{2,0},{96,32},{66,64},{33,96},{3,1},{97,33},{67,65},{32,97},{4,2},... | collective-permute-start | bytes 786440 | tf_op jit(solution)/shard_map/ppermute | solution.py:428
  84.4 1.1 collective-permute-start.6
  85.5 2.9 %collective-permute-done.4.refs_1_ = bf16[64,2048]{1,0:T(8,128)(2,1)S(1)} collective-permute-done((bf16[64,2048]{1,0:T(8,128)(2,1)S(1)}, bf16[64,2048]{1,0:T(8,128)(2,1)S(1)}, u32[]{:S(2)}, u32[]{:S(2)}) %collective-permute-start.4) | collective-permute-done | bytes 262176 | tf_op jit(solution)/shard_map/ppermute | solution.py:428
  88.4 2.2 %collective-permute-done.5.refs_2_ = bf16[64,2048]{1,0:T(8,128)(2,1)S(1)} collective-permute-done((bf16[64,2048]{1,0:T(8,128)(2,1)S(1)}, bf16[64,2048]{1,0:T(8,128)(2,1)S(1)}, u32[]{:S(2)}, u32[]{:S(2)}) %collective-permute-start.5) | collective-permute-done | bytes 262176 | tf_op jit(solution)/shard_map/ppermute | solution.py:428
  90.6 1.8 %collective-permute-done.6.refs_3_ = bf16[64,2048]{1,0:T(8,128)(2,1)S(1)} collective-permute-done((bf16[64,2048]{1,0:T(8,128)(2,1)S(1)}, bf16[64,2048]{1,0:T(8,128)(2,1)S(1)}, u32[]{:S(2)}, u32[]{:S(2)}) %collective-permute-start.6) | collective-permute-done | bytes 262176 | tf_op jit(solution)/shard_map/ppermute | solution.py:428
  92.4 1.0 join.5.w0
  93.4 2.6 %collective-permute-start.7 = (bf16[256,2048]{1,0:T(8,128)(2,1)}, bf16[256,2048]{1,0:T(8,128)(2,1)}, u32[]{:S(2)}, u32[]{:S(2)}) collective-permute-start(bf16[256,2048]{1,0:T(8,128)(2,1)} %join.5.w0), channel_id=1, source_target_pairs={{24,0},{38,32},{88,64},{102,96},{25,1},{39,33},{89,65},{103,97},{2... | collective-permute-start | bytes 3145736 | tf_op jit(solution)/shard_map/ppermute | solution.py:428
  96.0 1.0 collective-permute-start.8
  97.0 2.1 %collective-permute-start.9 = (bf16[256,2048]{1,0:T(8,128)(2,1)}, bf16[256,2048]{1,0:T(8,128)(2,1)}, u32[]{:S(2)}, u32[]{:S(2)}) collective-permute-start(bf16[256,2048]{1,0:T(8,128)(2,1)} %join.5.w0), channel_id=1, source_target_pairs={{16,0},{36,32},{80,64},{100,96},{17,1},{37,33},{81,65},{101,97},{1... | collective-permute-start | bytes 3145736 | tf_op jit(solution)/shard_map/ppermute | solution.py:428
  99.1 0.0 copy-done.2
  99.1 0.0 copy-done.3
  99.1 0.0 copy-done.4
  99.2 10.7 %collective-permute-done.7.w1 = bf16[256,2048]{1,0:T(8,128)(2,1)} collective-permute-done((bf16[256,2048]{1,0:T(8,128)(2,1)}, bf16[256,2048]{1,0:T(8,128)(2,1)}, u32[]{:S(2)}, u32[]{:S(2)}) %collective-permute-start.7) | collective-permute-done | bytes 1048608 | tf_op jit(solution)/shard_map/ppermute | solution.py:428
  109.8 0.5 collective-permute-done.8.w2
  110.3 0.0 all-to-all-done.1
  110.3 0.0 copy-start
  110.3 4.5 %early.1 = f32[768,768]{1,0:T(8,128)S(1)} custom-call(bf16[256,2048]{1,0:T(8,128)(2,1)} %join.5.w0, bf16[256,2048]{1,0:T(8,128)(2,1)} %collective-permute-done.7.w1, bf16[256,2048]{1,0:T(8,128)(2,1)} %collective-permute-done.8.w2, bf16[2048,768]{1,0:T(8,128)(2,1)S(1)} %bitcast.7), custom_call_target="tpu_custom_call" | custom-call | flops 1700000000 | bytes 8000000 | tf_op jit(solution)/shard_map/early/pallas_call | solution.py:353
  114.8 7.4 %collective-permute-done.9.w3 = bf16[256,2048]{1,0:T(8,128)(2,1)} collective-permute-done((bf16[256,2048]{1,0:T(8,128)(2,1)}, bf16[256,2048]{1,0:T(8,128)(2,1)}, u32[]{:S(2)}, u32[]{:S(2)}) %collective-permute-start.9) | collective-permute-done | bytes 1048608 | tf_op jit(solution)/shard_map/ppermute | solution.py:428
  122.2 0.0 copy-done
  122.2 3.2 %beams.1 = (f32[32,512]{1,0:T(8,128)S(1)}, f32[32,512]{1,0:T(8,128)S(1)}) custom-call(s32[64]{0:T(128)S(1)} %fusion.15.places, f32[768,768]{1,0:T(8,128)S(1)} %early.1, bf16[256,2048]{1,0:T(8,128)(2,1)} %collective-permute-done.9.w3, bf16[2048,768]{1,0:T(8,128)(2,1)S(1)} %bitcast.8, f32[64,384]{1,0:T(8,128)S(1)} %copy-done), custom_call_target="tpu_custom_call" | custom-call | flops 1700000000 | bytes 8000000 | tf_op jit(solution)/shard_map/beams/pallas_call | solution.py:395
  125.5 3.0 %collective-permute-start.10 = (f32[32,512]{1,0:T(8,128)S(1)}, f32[32,512]{1,0:T(8,128)S(1)}, u32[]{:S(2)}, u32[]{:S(2)}) collective-permute-start(f32[32,512]{1,0:T(8,128)S(1)} %get-tuple-element.28), channel_id=1, source_target_pairs={{0,32},{32,0},{64,96},{96,64},{1,33},{33,1},{65,97},{97,65},{2,34}... | collective-permute-start | bytes 196616 | tf_op jit(solution)/shard_map/ppermute | solution.py:475
  128.5 0.9 collective-permute-done.10
  129.4 0.7 maximum_select_fusion
  (3 shorter events, 0.0 us)
Async XLA Ops:
  5.4 29.5 %all-to-all-start = ((bf16[32,16,1024]{2,1,0:T(8,128)(2,1)}), bf16[32,16,1024]{2,1,0:T(8,128)(2,1)S(1)}, u32[]{:S(2)}, u32[]{:S(2)}) async-start(bf16[32,16,1024]{2,1,0:T(8,128)(2,1)} %bitcast.12), calls=%async_computation | async-start | bytes 2097152 | tf_op jit(solution)/shard_map/all_to_all | solution.py:455
  16.8 18.1 %copy-start.1 = (s32[2]{0:T(128)S(1)}, s32[2]{0:T(128)}, u32[]{:S(2)}) copy-start(s32[2]{0:T(128)} %owners.1) | copy-start | bytes 28
  35.5 63.6 %copy-start.2 = (s32[64]{0:T(128)S(1)}, s32[64]{0:T(128)}, u32[]{:S(2)}) copy-start(s32[64]{0:T(128)} %constant.124.clone) | copy-start | bytes 772
  35.5 63.6 %copy-start.3 = (s32[64]{0:T(128)S(1)}, s32[64]{0:T(128)}, u32[]{:S(2)}) copy-start(s32[64]{0:T(128)} %constant.125.clone) | copy-start | bytes 772
  35.5 63.6 %copy-start.4 = (s32[64]{0:T(128)S(1)}, s32[64]{0:T(128)}, u32[]{:S(2)}) copy-start(s32[64]{0:T(128)} %constant.126.clone) | copy-start | bytes 772
  35.5 74.8 %all-to-all-start.1 = ((bf16[128,16,768]{2,1,0:T(8,128)(2,1)}), bf16[128,16,768]{2,1,0:T(8,128)(2,1)S(1)}, u32[]{:S(2)}, u32[]{:S(2)}) async-start(bf16[128,16,768]{2,1,0:T(8,128)(2,1)} %spectra.1), calls=%async_computation.1 | async-start | bytes 6291456 | tf_op jit(solution)/shard_map/all_to_all | solution.py:463
  44.2 2.0 %collective-permute-start = (bf16[16,1024]{1,0:T(8,128)(2,1)S(1)}, bf16[16,1024]{1,0:T(8,128)(2,1)S(1)}, u32[]{:S(2)}, u32[]{:S(2)}) collective-permute-start(bf16[16,1024]{1,0:T(8,128)(2,1)S(1)} %get-tuple-element.25), channel_id=1, source_target_pairs={{0,32},{32,0},{64,96},{96,64},{1,33},{33,1},{65,97},{97,65},{2,34}... | collective-permute-start | bytes 98312 | tf_op jit(solution)/shard_map/ppermute | solution.py:466
  46.2 5.9 %collective-permute-start.1 = (bf16[16,2048]{1,0:T(8,128)(2,1)S(1)}, bf16[16,2048]{1,0:T(8,128)(2,1)S(1)}, u32[]{:S(2)}, u32[]{:S(2)}) collective-permute-start(bf16[16,2048]{1,0:T(8,128)(2,1)S(1)} %join.3.refs_0_), channel_id=1, source_target_pairs={{65,0},{56,32},{0,64},{120,96},{64,1},{57,33},{1,65},{121,97},{67,... | collective-permute-start | bytes 196616 | tf_op jit(solution)/shard_map/ppermute | solution.py:428
  47.0 6.0 %collective-permute-start.2 = (bf16[16,2048]{1,0:T(8,128)(2,1)S(1)}, bf16[16,2048]{1,0:T(8,128)(2,1)S(1)}, u32[]{:S(2)}, u32[]{:S(2)}) collective-permute-start(bf16[16,2048]{1,0:T(8,128)(2,1)S(1)} %join.3.refs_0_), channel_id=1, source_target_pairs={{64,0},{40,32},{1,64},{104,96},{65,1},{41,33},{0,65},{105,97},{66,... | collective-permute-start | bytes 196616 | tf_op jit(solution)/shard_map/ppermute | solution.py:428
  48.9 18.4 %collective-permute-start.3 = (bf16[16,2048]{1,0:T(8,128)(2,1)S(1)}, bf16[16,2048]{1,0:T(8,128)(2,1)S(1)}, u32[]{:S(2)}, u32[]{:S(2)}) collective-permute-start(bf16[16,2048]{1,0:T(8,128)(2,1)S(1)} %join.3.refs_0_), channel_id=1, source_target_pairs={{1,0},{48,32},{65,64},{112,96},{0,1},{49,33},{64,65},{113,97},{3,2... | collective-permute-start | bytes 196616 | tf_op jit(solution)/shard_map/ppermute | solution.py:428
  67.3 21.1 %collective-permute-start.4 = (bf16[64,2048]{1,0:T(8,128)(2,1)S(1)}, bf16[64,2048]{1,0:T(8,128)(2,1)S(1)}, u32[]{:S(2)}, u32[]{:S(2)}) collective-permute-start(bf16[64,2048]{1,0:T(8,128)(2,1)S(1)} %join.4.refs_0_), channel_id=1, source_target_pairs={{6,0},{97,32},{70,64},{32,96},{7,1},{96,33},{71,65},{33,97},{0,2},... | collective-permute-start | bytes 786440 | tf_op jit(solution)/shard_map/ppermute | solution.py:428
  78.0 12.5 %collective-permute-start.5 = (bf16[64,2048]{1,0:T(8,128)(2,1)S(1)}, bf16[64,2048]{1,0:T(8,128)(2,1)S(1)}, u32[]{:S(2)}, u32[]{:S(2)}) collective-permute-start(bf16[64,2048]{1,0:T(8,128)(2,1)S(1)} %join.4.refs_0_), channel_id=1, source_target_pairs={{2,0},{96,32},{66,64},{33,96},{3,1},{97,33},{67,65},{32,97},{4,2},... | collective-permute-start | bytes 786440 | tf_op jit(solution)/shard_map/ppermute | solution.py:428
  84.4 8.0 %collective-permute-start.6 = (bf16[64,2048]{1,0:T(8,128)(2,1)S(1)}, bf16[64,2048]{1,0:T(8,128)(2,1)S(1)}, u32[]{:S(2)}, u32[]{:S(2)}) collective-permute-start(bf16[64,2048]{1,0:T(8,128)(2,1)S(1)} %join.4.refs_0_), channel_id=1, source_target_pairs={{4,0},{33,32},{68,64},{97,96},{5,1},{32,33},{69,65},{96,97},{6,2},... | collective-permute-start | bytes 786440 | tf_op jit(solution)/shard_map/ppermute | solution.py:428
  93.4 16.4 %collective-permute-start.7 = (bf16[256,2048]{1,0:T(8,128)(2,1)}, bf16[256,2048]{1,0:T(8,128)(2,1)}, u32[]{:S(2)}, u32[]{:S(2)}) collective-permute-start(bf16[256,2048]{1,0:T(8,128)(2,1)} %join.5.w0), channel_id=1, source_target_pairs={{24,0},{38,32},{88,64},{102,96},{25,1},{39,33},{89,65},{103,97},{2... | collective-permute-start | bytes 3145736 | tf_op jit(solution)/shard_map/ppermute | solution.py:428
  96.0 14.3 %collective-permute-start.8 = (bf16[256,2048]{1,0:T(8,128)(2,1)}, bf16[256,2048]{1,0:T(8,128)(2,1)}, u32[]{:S(2)}, u32[]{:S(2)}) collective-permute-start(bf16[256,2048]{1,0:T(8,128)(2,1)} %join.5.w0), channel_id=1, source_target_pairs={{8,0},{34,32},{72,64},{98,96},{9,1},{35,33},{73,65},{99,97},{10,2}... | collective-permute-start | bytes 3145736 | tf_op jit(solution)/shard_map/ppermute | solution.py:428
  97.0 25.2 %collective-permute-start.9 = (bf16[256,2048]{1,0:T(8,128)(2,1)}, bf16[256,2048]{1,0:T(8,128)(2,1)}, u32[]{:S(2)}, u32[]{:S(2)}) collective-permute-start(bf16[256,2048]{1,0:T(8,128)(2,1)} %join.5.w0), channel_id=1, source_target_pairs={{16,0},{36,32},{80,64},{100,96},{17,1},{37,33},{81,65},{101,97},{1... | collective-permute-start | bytes 3145736 | tf_op jit(solution)/shard_map/ppermute | solution.py:428
  110.3 11.9 %copy-start = (f32[64,384]{1,0:T(8,128)S(1)}, f32[64,384]{1,0:T(8,128)}, u32[]{:S(2)}) copy-start(f32[64,384]{1,0:T(8,128)} %constant.127.clone.choose) | copy-start | bytes 294916
  125.5 3.9 %collective-permute-start.10 = (f32[32,512]{1,0:T(8,128)S(1)}, f32[32,512]{1,0:T(8,128)S(1)}, u32[]{:S(2)}, u32[]{:S(2)}) collective-permute-start(f32[32,512]{1,0:T(8,128)S(1)} %get-tuple-element.28), channel_id=1, source_target_pairs={{0,32},{32,0},{64,96},{96,64},{1,33},{33,1},{65,97},{97,65},{2,34}... | collective-permute-start | bytes 196616 | tf_op jit(solution)/shard_map/ppermute | solution.py:475

commit v14 on v10

--- a/solution.py
+++ b/solution.py
@@ -214,7 +214,7 @@
     )(vre, vim, taps, jnp.asarray(cos_t), jnp.asarray(sin_t), jnp.asarray(mat))
 
 
-def quarter_kernel(wre, wim, slots, out, buf, names, chosen, sems):
+def quarter_kernel(wre, wim, slots, out, buf, names, chosen, ready, sems):
     grp = lax.axis_index("grp")
     y_lo, core = grp // 2, grp % 2
     antennas, beams = wre.shape
@@ -235,7 +235,7 @@
         antenna = lax.broadcasted_iota(jnp.int32, (16, half), 0) + i * 16
         chosen[pl.ds(pl.multiple_of(i * 16, 16), 16), :] = jnp.where(antenna == row, 1.0, 0.0).astype(jnp.bfloat16)
         return 0
-    lax.fori_loop(0, antennas // 16, build, 0, unroll=4)
+    lax.fori_loop(0, antennas // 16, build, 0, unroll=8)
     for y, source in ((0, wre), (1, wim)):
 
         @pl.when(y_lo == y)
@@ -243,12 +243,18 @@
             for i in range(4):
                 part = pl.ds(i * half // 2, half // 2)
                 pltpu.make_async_copy(source.at[part], buf.at[part], sems.at[i]).wait()
+    stores = []
     for j in range(0, beams, 256):
         w = buf[:, j : j + 256].astype(jnp.bfloat16)
         for k in range(0, half, 512):
-            out[j : j + 256, k : k + 512] = lax.dot_general(
+            ready[j : j + 256, k : k + 512] = lax.dot_general(
                 w, chosen[:, k : k + 512], (((0,), (0,)), ((), ())), preferred_element_type=jnp.float32
             ).astype(jnp.bfloat16)
+        part = pl.ds(j, 256)
+        stores.append(pltpu.make_async_copy(ready.at[part], out.at[part], sems.at[5 + len(stores)]))
+        stores[-1].start()
+    for store in stores:
+        store.wait()
 
 
 def quarter_of(wre, wim, antenna_map, interpret=False):
@@ -257,13 +263,14 @@
     return pl.pallas_call(
         quarter_kernel,
         in_specs=[pl.BlockSpec(memory_space=pltpu.HBM)] * 3,
-        out_specs=pl.BlockSpec(memory_space=pltpu.VMEM),
+        out_specs=pl.BlockSpec(memory_space=pltpu.HBM),
         out_shape=jax.ShapeDtypeStruct((beams, half), jnp.bfloat16),
         scratch_shapes=[
             pltpu.VMEM((antennas, beams), jnp.float32),
             pltpu.VMEM((1, half), jnp.int32),
             pltpu.VMEM((antennas, half), jnp.bfloat16),
-            pltpu.SemaphoreType.DMA((5,)),
+            pltpu.VMEM((beams, half), jnp.bfloat16),
+            pltpu.SemaphoreType.DMA((7,)),
         ],
         compiler_params=pltpu.CompilerParams(vmem_limit_bytes=58 * MIB),
         cost_estimate=pl.CostEstimate(flops=2 * 10**9, bytes_accessed=6 * 10**6, transcendentals=0),

time: 131 us -> 131 us (level)
  no operation moved by 1% of the time
where the time goes in v14:
time: 131 us
  starting transfers between devices  53.3 us (41%)
  waiting for transfers between devices  44.7 us (34%)
  Pallas kernels  31.5 us (24%)
    ppermute x9, waiting for transfers between devices, gather_stage(): lax.ppermute(block, ALL, permutation(stage, shift))  41.7 us
    ppermute x9, starting transfers between devices, gather_stage(): lax.ppermute(block, ALL, permutation(stage, shift))  29.1 us
    pallas_call x1, Pallas kernels, spectra_of(): pl.pallas_call(functools.partial(spectra_kernel, messages), out_shape=[ja...  16.8 us
    all_to_all x1, starting transfers between devices, on_device(): lax.all_to_all(quarter.reshape(32, 16, -1), 'dev', split_axis=0, concat_a...  11.4 us
    all_to_all x1, starting transfers between devices, on_device(): lax.all_to_all(message, ALL, split_axis=0, concat_axis=0, tiled=True)  8.67 us
    pallas_call x1, Pallas kernels, quarter_of(): pl.pallas_call(quarter_kernel, in_specs=[pl.BlockSpec(memory_space=pltpu....  5.41 us
    pallas_call x1, Pallas kernels, beams_of(): pl.pallas_call(beams_kernel, out_shape=[jax.ShapeDtypeStruct((32, rows //...  4.33 us
    pallas_call x1, Pallas kernels, early_of(): pl.pallas_call(early_kernel, out_shape=jax.ShapeDtypeStruct((2 * w0.shape...  3.33 us
  transfers between devices with their start and end apart: 13, of which 11 were waited for; matrix products, arithmetic and copies ran while one was open for 0% of the time, Pallas kernels for 16%

profile of v14, /device:TPU:1, one launch (start us, length us, event | category | flops | bytes accessed | tf_op | source)
XLA Modules:
  0.0 130.6 jit_solution(14973837461051285374)
XLA Ops:
  0.0 5.4 %quarter.1 = bf16[512,1024]{1,0:T(8,128)(2,1)} custom-call(f32[2048,512]{1,0:T(8,128)} %bitcast.10, f32[2048,512]{1,0:T(8,128)} %bitcast.11, s32[2,1,1024]{2,1,0:T(1,128)} %bitcast.14), custom_call_target="tpu_custom_call" | custom-call | flops 2000000000 | bytes 6000000 | tf_op jit(solution)/shard_map/quarter/pallas_call | solution.py:263
  5.4 11.4 %all-to-all-start = ((bf16[32,16,1024]{2,1,0:T(8,128)(2,1)}), bf16[32,16,1024]{2,1,0:T(8,128)(2,1)S(1)}, u32[]{:S(2)}, u32[]{:S(2)}) async-start(bf16[32,16,1024]{2,1,0:T(8,128)(2,1)} %bitcast.12), calls=%async_computation | async-start | bytes 2097152 | tf_op jit(solution)/shard_map/all_to_all | solution.py:456
  16.8 0.0 copy-start.1
  16.8 16.8 %spectra.1 = bf16[128,16,768]{2,1,0:T(8,128)(2,1)} custom-call(bf16[16,110592]{1,0:T(8,128)(2,1)} %refs_0_, bf16[16,110592]{1,0:T(8,128)(2,1)} %refs_1_, f32[16,4096]{1,0:T(8,128)} %refs_2_, f32[32,128]{1,0:T(8,128)} %constant.121.clone.refs_3_, f32[32,128]{1,0:T(8,128)} %constant.122.clone.refs_4_, bf16[256,256]{1,0:T(8,128)(2,1)} %constant.123.clone.refs_5_), custom_call_target="tpu_custom_call" | custom-call | flops 2400000000 | bytes 48000000 | tf_op jit(solution)/shard_map/spectra/pallas_call | solution.py:190
  33.6 1.3 all-to-all-done.offers
  34.9 0.0 copy-done.1
  34.9 0.6 pick.1
  35.5 0.0 copy-start.2
  35.5 0.0 copy-start.3
  35.5 0.0 copy-start.4
  35.5 8.7 %all-to-all-start.1 = ((bf16[128,16,768]{2,1,0:T(8,128)(2,1)}), bf16[128,16,768]{2,1,0:T(8,128)(2,1)S(1)}, u32[]{:S(2)}, u32[]{:S(2)}) async-start(bf16[128,16,768]{2,1,0:T(8,128)(2,1)} %spectra.1), calls=%async_computation.1 | async-start | bytes 6291456 | tf_op jit(solution)/shard_map/all_to_all | solution.py:464
  44.2 1.1 collective-permute-start
  45.3 0.9 collective-permute-done.refs_1_
  46.2 0.8 collective-permute-start.1
  47.0 1.9 %collective-permute-start.2 = (bf16[16,2048]{1,0:T(8,128)(2,1)S(1)}, bf16[16,2048]{1,0:T(8,128)(2,1)S(1)}, u32[]{:S(2)}, u32[]{:S(2)}) collective-permute-start(bf16[16,2048]{1,0:T(8,128)(2,1)S(1)} %join.3.refs_0_), channel_id=1, source_target_pairs={{64,0},{40,32},{1,64},{104,96},{65,1},{41,33},{0,65},{105,97},{66,... | collective-permute-start | bytes 196616 | tf_op jit(solution)/shard_map/ppermute | solution.py:429
  48.9 1.4 %collective-permute-start.3 = (bf16[16,2048]{1,0:T(8,128)(2,1)S(1)}, bf16[16,2048]{1,0:T(8,128)(2,1)S(1)}, u32[]{:S(2)}, u32[]{:S(2)}) collective-permute-start(bf16[16,2048]{1,0:T(8,128)(2,1)S(1)} %join.3.refs_0_), channel_id=1, source_target_pairs={{1,0},{48,32},{65,64},{112,96},{0,1},{49,33},{64,65},{113,97},{3,2... | collective-permute-start | bytes 196616 | tf_op jit(solution)/shard_map/ppermute | solution.py:429
  50.3 1.9 %collective-permute-done.1.refs_1_ = bf16[16,2048]{1,0:T(8,128)(2,1)S(1)} collective-permute-done((bf16[16,2048]{1,0:T(8,128)(2,1)S(1)}, bf16[16,2048]{1,0:T(8,128)(2,1)S(1)}, u32[]{:S(2)}, u32[]{:S(2)}) %collective-permute-start.1) | collective-permute-done | bytes 65568 | tf_op jit(solution)/shard_map/ppermute | solution.py:429
  52.1 0.9 collective-permute-done.2.refs_2_
  53.1 14.2 %collective-permute-done.3.refs_3_ = bf16[16,2048]{1,0:T(8,128)(2,1)S(1)} collective-permute-done((bf16[16,2048]{1,0:T(8,128)(2,1)S(1)}, bf16[16,2048]{1,0:T(8,128)(2,1)S(1)}, u32[]{:S(2)}, u32[]{:S(2)}) %collective-permute-start.3) | collective-permute-done | bytes 65568 | tf_op jit(solution)/shard_map/ppermute | solution.py:429
  67.3 10.7 %collective-permute-start.4 = (bf16[64,2048]{1,0:T(8,128)(2,1)S(1)}, bf16[64,2048]{1,0:T(8,128)(2,1)S(1)}, u32[]{:S(2)}, u32[]{:S(2)}) collective-permute-start(bf16[64,2048]{1,0:T(8,128)(2,1)S(1)} %join.4.refs_0_), channel_id=1, source_target_pairs={{6,0},{97,32},{70,64},{32,96},{7,1},{96,33},{71,65},{33,97},{0,2},... | collective-permute-start | bytes 786440 | tf_op jit(solution)/shard_map/ppermute | solution.py:429
  78.0 6.4 %collective-permute-start.5 = (bf16[64,2048]{1,0:T(8,128)(2,1)S(1)}, bf16[64,2048]{1,0:T(8,128)(2,1)S(1)}, u32[]{:S(2)}, u32[]{:S(2)}) collective-permute-start(bf16[64,2048]{1,0:T(8,128)(2,1)S(1)} %join.4.refs_0_), channel_id=1, source_target_pairs={{2,0},{96,32},{66,64},{33,96},{3,1},{97,33},{67,65},{32,97},{4,2},... | collective-permute-start | bytes 786440 | tf_op jit(solution)/shard_map/ppermute | solution.py:429
  84.4 1.1 collective-permute-start.6
  85.5 2.9 %collective-permute-done.4.refs_1_ = bf16[64,2048]{1,0:T(8,128)(2,1)S(1)} collective-permute-done((bf16[64,2048]{1,0:T(8,128)(2,1)S(1)}, bf16[64,2048]{1,0:T(8,128)(2,1)S(1)}, u32[]{:S(2)}, u32[]{:S(2)}) %collective-permute-start.4) | collective-permute-done | bytes 262176 | tf_op jit(solution)/shard_map/ppermute | solution.py:429
  88.4 2.2 %collective-permute-done.5.refs_2_ = bf16[64,2048]{1,0:T(8,128)(2,1)S(1)} collective-permute-done((bf16[64,2048]{1,0:T(8,128)(2,1)S(1)}, bf16[64,2048]{1,0:T(8,128)(2,1)S(1)}, u32[]{:S(2)}, u32[]{:S(2)}) %collective-permute-start.5) | collective-permute-done | bytes 262176 | tf_op jit(solution)/shard_map/ppermute | solution.py:429
  90.6 1.8 %collective-permute-done.6.refs_3_ = bf16[64,2048]{1,0:T(8,128)(2,1)S(1)} collective-permute-done((bf16[64,2048]{1,0:T(8,128)(2,1)S(1)}, bf16[64,2048]{1,0:T(8,128)(2,1)S(1)}, u32[]{:S(2)}, u32[]{:S(2)}) %collective-permute-start.6) | collective-permute-done | bytes 262176 | tf_op jit(solution)/shard_map/ppermute | solution.py:429
  92.4 1.0 join.5.w0
  93.4 0.0 copy-start
  93.5 4.2 %collective-permute-start.7 = (bf16[256,2048]{1,0:T(8,128)(2,1)}, bf16[256,2048]{1,0:T(8,128)(2,1)}, u32[]{:S(2)}, u32[]{:S(2)}) collective-permute-start(bf16[256,2048]{1,0:T(8,128)(2,1)} %join.5.w0), channel_id=1, source_target_pairs={{16,0},{36,32},{80,64},{100,96},{17,1},{37,33},{81,65},{101,97},{1... | collective-permute-start | bytes 3145736 | tf_op jit(solution)/shard_map/ppermute | solution.py:429
  97.7 0.0 collective-permute-start.8
  97.7 2.7 %collective-permute-start.9 = (bf16[256,2048]{1,0:T(8,128)(2,1)}, bf16[256,2048]{1,0:T(8,128)(2,1)}, u32[]{:S(2)}, u32[]{:S(2)}) collective-permute-start(bf16[256,2048]{1,0:T(8,128)(2,1)} %join.5.w0), channel_id=1, source_target_pairs={{8,0},{34,32},{72,64},{98,96},{9,1},{35,33},{73,65},{99,97},{10,2}... | collective-permute-start | bytes 3145736 | tf_op jit(solution)/shard_map/ppermute | solution.py:429
  100.3 0.0 copy-done.2
  100.3 0.0 copy-done.3
  100.3 0.0 copy-done.4
  100.4 0.1 slice.11
  100.4 0.1 fusion.16
  100.5 0.1 pad_add_fusion.places
  100.6 9.9 %collective-permute-done.7.w1 = bf16[256,2048]{1,0:T(8,128)(2,1)} collective-permute-done((bf16[256,2048]{1,0:T(8,128)(2,1)}, bf16[256,2048]{1,0:T(8,128)(2,1)}, u32[]{:S(2)}, u32[]{:S(2)}) %collective-permute-start.7) | collective-permute-done | bytes 1048608 | tf_op jit(solution)/shard_map/ppermute | solution.py:429
  110.5 0.0 all-to-all-done.1
  110.5 3.3 %early.1 = f32[512,768]{1,0:T(8,128)S(1)} custom-call(bf16[256,2048]{1,0:T(8,128)(2,1)} %join.5.w0, bf16[256,2048]{1,0:T(8,128)(2,1)} %collective-permute-done.7.w1, bf16[2048,768]{1,0:T(8,128)(2,1)S(1)} %bitcast.7), custom_call_target="tpu_custom_call" | custom-call | flops 1700000000 | bytes 8000000 | tf_op jit(solution)/shard_map/early/pallas_call | solution.py:353
  113.8 7.9 %collective-permute-done.8.w2 = bf16[256,2048]{1,0:T(8,128)(2,1)} collective-permute-done((bf16[256,2048]{1,0:T(8,128)(2,1)}, bf16[256,2048]{1,0:T(8,128)(2,1)}, u32[]{:S(2)}, u32[]{:S(2)}) %collective-permute-start.8) | collective-permute-done | bytes 1048608 | tf_op jit(solution)/shard_map/ppermute | solution.py:429
  121.7 0.0 collective-permute-done.9.w3
  121.7 0.0 copy-done
  121.7 4.3 %beams.1 = (f32[32,512]{1,0:T(8,128)S(1)}, f32[32,512]{1,0:T(8,128)S(1)}) custom-call(s32[64]{0:T(128)S(1)} %pad_add_fusion.places, f32[512,768]{1,0:T(8,128)S(1)} %early.1, bf16[256,2048]{1,0:T(8,128)(2,1)} %collective-permute-done.8.w2, bf16[256,2048]{1,0:T(8,128)(2,1)} %collective-permute-done.9.w3, bf16[2048,768]{1,0:T(8,128)(2,1)S(1)} %bitcast.8, ...), custom_call_target="tpu_custom_call" | custom-call | flops 1700000000 | bytes 8000000 | tf_op jit(solution)/shard_map/beams/pallas_call | solution.py:396
  126.0 3.0 %collective-permute-start.10 = (f32[32,512]{1,0:T(8,128)S(1)}, f32[32,512]{1,0:T(8,128)S(1)}, u32[]{:S(2)}, u32[]{:S(2)}) collective-permute-start(f32[32,512]{1,0:T(8,128)S(1)} %get-tuple-element.28), channel_id=1, source_target_pairs={{0,32},{32,0},{64,96},{96,64},{1,33},{33,1},{65,97},{97,65},{2,34}... | collective-permute-start | bytes 196616 | tf_op jit(solution)/shard_map/ppermute | solution.py:477
  129.0 0.9 collective-permute-done.10
  129.9 0.7 maximum_select_fusion
  (3 shorter events, 0.0 us)
Async XLA Ops:
  5.4 29.5 %all-to-all-start = ((bf16[32,16,1024]{2,1,0:T(8,128)(2,1)}), bf16[32,16,1024]{2,1,0:T(8,128)(2,1)S(1)}, u32[]{:S(2)}, u32[]{:S(2)}) async-start(bf16[32,16,1024]{2,1,0:T(8,128)(2,1)} %bitcast.12), calls=%async_computation | async-start | bytes 2097152 | tf_op jit(solution)/shard_map/all_to_all | solution.py:456
  16.8 18.1 %copy-start.1 = (s32[2]{0:T(128)S(1)}, s32[2]{0:T(128)}, u32[]{:S(2)}) copy-start(s32[2]{0:T(128)} %owners.1) | copy-start | bytes 28
  35.5 64.8 %copy-start.2 = (s32[64]{0:T(128)S(1)}, s32[64]{0:T(128)}, u32[]{:S(2)}) copy-start(s32[64]{0:T(128)} %constant.124.clone) | copy-start | bytes 772
  35.5 64.8 %copy-start.3 = (s32[64]{0:T(128)S(1)}, s32[64]{0:T(128)}, u32[]{:S(2)}) copy-start(s32[64]{0:T(128)} %constant.125.clone) | copy-start | bytes 772
  35.5 64.8 %copy-start.4 = (s32[64]{0:T(128)S(1)}, s32[64]{0:T(128)}, u32[]{:S(2)}) copy-start(s32[64]{0:T(128)} %constant.126.clone) | copy-start | bytes 772
  35.5 75.0 %all-to-all-start.1 = ((bf16[128,16,768]{2,1,0:T(8,128)(2,1)}), bf16[128,16,768]{2,1,0:T(8,128)(2,1)S(1)}, u32[]{:S(2)}, u32[]{:S(2)}) async-start(bf16[128,16,768]{2,1,0:T(8,128)(2,1)} %spectra.1), calls=%async_computation.1 | async-start | bytes 6291456 | tf_op jit(solution)/shard_map/all_to_all | solution.py:464
  44.2 2.0 %collective-permute-start = (bf16[16,1024]{1,0:T(8,128)(2,1)S(1)}, bf16[16,1024]{1,0:T(8,128)(2,1)S(1)}, u32[]{:S(2)}, u32[]{:S(2)}) collective-permute-start(bf16[16,1024]{1,0:T(8,128)(2,1)S(1)} %get-tuple-element.25), channel_id=1, source_target_pairs={{0,32},{32,0},{64,96},{96,64},{1,33},{33,1},{65,97},{97,65},{2,34}... | collective-permute-start | bytes 98312 | tf_op jit(solution)/shard_map/ppermute | solution.py:467
  46.2 5.9 %collective-permute-start.1 = (bf16[16,2048]{1,0:T(8,128)(2,1)S(1)}, bf16[16,2048]{1,0:T(8,128)(2,1)S(1)}, u32[]{:S(2)}, u32[]{:S(2)}) collective-permute-start(bf16[16,2048]{1,0:T(8,128)(2,1)S(1)} %join.3.refs_0_), channel_id=1, source_target_pairs={{65,0},{56,32},{0,64},{120,96},{64,1},{57,33},{1,65},{121,97},{67,... | collective-permute-start | bytes 196616 | tf_op jit(solution)/shard_map/ppermute | solution.py:429
  47.0 6.0 %collective-permute-start.2 = (bf16[16,2048]{1,0:T(8,128)(2,1)S(1)}, bf16[16,2048]{1,0:T(8,128)(2,1)S(1)}, u32[]{:S(2)}, u32[]{:S(2)}) collective-permute-start(bf16[16,2048]{1,0:T(8,128)(2,1)S(1)} %join.3.refs_0_), channel_id=1, source_target_pairs={{64,0},{40,32},{1,64},{104,96},{65,1},{41,33},{0,65},{105,97},{66,... | collective-permute-start | bytes 196616 | tf_op jit(solution)/shard_map/ppermute | solution.py:429
  48.9 18.4 %collective-permute-start.3 = (bf16[16,2048]{1,0:T(8,128)(2,1)S(1)}, bf16[16,2048]{1,0:T(8,128)(2,1)S(1)}, u32[]{:S(2)}, u32[]{:S(2)}) collective-permute-start(bf16[16,2048]{1,0:T(8,128)(2,1)S(1)} %join.3.refs_0_), channel_id=1, source_target_pairs={{1,0},{48,32},{65,64},{112,96},{0,1},{49,33},{64,65},{113,97},{3,2... | collective-permute-start | bytes 196616 | tf_op jit(solution)/shard_map/ppermute | solution.py:429
  67.3 21.1 %collective-permute-start.4 = (bf16[64,2048]{1,0:T(8,128)(2,1)S(1)}, bf16[64,2048]{1,0:T(8,128)(2,1)S(1)}, u32[]{:S(2)}, u32[]{:S(2)}) collective-permute-start(bf16[64,2048]{1,0:T(8,128)(2,1)S(1)} %join.4.refs_0_), channel_id=1, source_target_pairs={{6,0},{97,32},{70,64},{32,96},{7,1},{96,33},{71,65},{33,97},{0,2},... | collective-permute-start | bytes 786440 | tf_op jit(solution)/shard_map/ppermute | solution.py:429
  78.0 12.5 %collective-permute-start.5 = (bf16[64,2048]{1,0:T(8,128)(2,1)S(1)}, bf16[64,2048]{1,0:T(8,128)(2,1)S(1)}, u32[]{:S(2)}, u32[]{:S(2)}) collective-permute-start(bf16[64,2048]{1,0:T(8,128)(2,1)S(1)} %join.4.refs_0_), channel_id=1, source_target_pairs={{2,0},{96,32},{66,64},{33,96},{3,1},{97,33},{67,65},{32,97},{4,2},... | collective-permute-start | bytes 786440 | tf_op jit(solution)/shard_map/ppermute | solution.py:429
  84.4 8.0 %collective-permute-start.6 = (bf16[64,2048]{1,0:T(8,128)(2,1)S(1)}, bf16[64,2048]{1,0:T(8,128)(2,1)S(1)}, u32[]{:S(2)}, u32[]{:S(2)}) collective-permute-start(bf16[64,2048]{1,0:T(8,128)(2,1)S(1)} %join.4.refs_0_), channel_id=1, source_target_pairs={{4,0},{33,32},{68,64},{97,96},{5,1},{32,33},{69,65},{96,97},{6,2},... | collective-permute-start | bytes 786440 | tf_op jit(solution)/shard_map/ppermute | solution.py:429
  93.4 28.2 %copy-start = (f32[64,384]{1,0:T(8,128)S(1)}, f32[64,384]{1,0:T(8,128)}, u32[]{:S(2)}) copy-start(f32[64,384]{1,0:T(8,128)} %constant.127.clone.choose) | copy-start | bytes 294916
  93.5 17.0 %collective-permute-start.7 = (bf16[256,2048]{1,0:T(8,128)(2,1)}, bf16[256,2048]{1,0:T(8,128)(2,1)}, u32[]{:S(2)}, u32[]{:S(2)}) collective-permute-start(bf16[256,2048]{1,0:T(8,128)(2,1)} %join.5.w0), channel_id=1, source_target_pairs={{16,0},{36,32},{80,64},{100,96},{17,1},{37,33},{81,65},{101,97},{1... | collective-permute-start | bytes 3145736 | tf_op jit(solution)/shard_map/ppermute | solution.py:429
  97.7 24.0 %collective-permute-start.8 = (bf16[256,2048]{1,0:T(8,128)(2,1)}, bf16[256,2048]{1,0:T(8,128)(2,1)}, u32[]{:S(2)}, u32[]{:S(2)}) collective-permute-start(bf16[256,2048]{1,0:T(8,128)(2,1)} %join.5.w0), channel_id=1, source_target_pairs={{24,0},{38,32},{88,64},{102,96},{25,1},{39,33},{89,65},{103,97},{2... | collective-permute-start | bytes 3145736 | tf_op jit(solution)/shard_map/ppermute | solution.py:429
  97.7 24.0 %collective-permute-start.9 = (bf16[256,2048]{1,0:T(8,128)(2,1)}, bf16[256,2048]{1,0:T(8,128)(2,1)}, u32[]{:S(2)}, u32[]{:S(2)}) collective-permute-start(bf16[256,2048]{1,0:T(8,128)(2,1)} %join.5.w0), channel_id=1, source_target_pairs={{8,0},{34,32},{72,64},{98,96},{9,1},{35,33},{73,65},{99,97},{10,2}... | collective-permute-start | bytes 3145736 | tf_op jit(solution)/shard_map/ppermute | solution.py:429
  126.0 3.9 %collective-permute-start.10 = (f32[32,512]{1,0:T(8,128)S(1)}, f32[32,512]{1,0:T(8,128)S(1)}, u32[]{:S(2)}, u32[]{:S(2)}) collective-permute-start(f32[32,512]{1,0:T(8,128)S(1)} %get-tuple-element.28), channel_id=1, source_target_pairs={{0,32},{32,0},{64,96},{96,64},{1,33},{33,1},{65,97},{97,65},{2,34}... | collective-permute-start | bytes 196616 | tf_op jit(solution)/shard_map/ppermute | solution.py:477
